TPU v7x, 32 devices: a whole 2x2x4 slice. The times are simulated.
32 devices in a mesh: dp: 2 (over x), seq: 8 (over z, core), tp: 2 (over y).
Axes of the slice: x: 2, y: 2, z: 4, core: 2. Of those that a mesh axis runs over, the one named last changes fastest.
Arguments:
- block_input: bfloat16 [8, 1024, 2048], P('dp', 'seq'), may hold values from -6 to 6
- initial_state: float32 [8, 32, 64, 64], P('dp', 'tp'), may hold values from -6 to 6
- norm_gains: bfloat16 [2, 2048], P(None, ('dp', 'seq')), may hold values from 0.5 to 1.5
- norm_biases: bfloat16 [2, 2048], P(None, ('dp', 'seq')), may hold values from -1.5 to 1.5
- mixing_coefficients: bfloat16 [8, 2048], P(None, ('dp', 'seq')), may hold values from 0 to 1
- mix_down: bfloat16 [2048, 160], P(('dp', 'seq')), may hold values from -0.125 to 0.125
- mixing_up_weight: bfloat16 [160, 2048], P(None, ('dp', 'seq')), may hold values from -0.5 to 0.5
- decay_down: bfloat16 [2048, 64], P(('dp', 'seq')), may hold values from -0.125 to 0.125
- decay_up: bfloat16 [64, 32, 64], P(None, 'tp', ('dp', 'seq')), may hold values from -0.5 to 0.5
- proj_weights: bfloat16 [4, 2048, 2048], P(None, ('dp', 'seq'), 'tp'), may hold values from -0.125 to 0.125
- out_weight: bfloat16 [2048, 2048], P('tp', ('dp', 'seq')), may hold values from -0.25 to 0.25
- time_decay: bfloat16 [32, 64], P('tp', ('dp', 'seq')), may hold values from -12 to -2
- time_first: bfloat16 [32, 64], P('tp', ('dp', 'seq')), may hold values from -0.5 to 1.5
- group_gain: bfloat16 [32, 64], P('tp', ('dp', 'seq')), may hold values from 0.5 to 1.5
- group_bias: bfloat16 [32, 64], P('tp', ('dp', 'seq')), may hold values from -1.5 to 1.5
- channel_key: bfloat16 [2048, 7168], P(None, 'tp'), may hold values from -0.125 to 0.125
- channel_value: bfloat16 [7168, 2048], P('tp'), may hold values from -0.0625 to 0.0625
- channel_recept: bfloat16 [2048, 2048], P(None, 'tp'), may hold values from -0.125 to 0.125
- out_grad: bfloat16 [8, 1024, 2048], P('dp', 'seq', 'tp'), may hold values from -6 to 6
Outputs:
- output: bfloat16 [8, 1024, 2048], P('dp', 'seq', 'tp')
- input_grad: float32 [8, 1024, 2048], P('dp', 'seq', 'tp')
- state_grad: float32 [8, 32, 64, 64], P('dp', 'tp')
- norm_gains_grad: float32 [2, 2048], P(None, ('dp', 'seq'))
- norm_biases_grad: float32 [2, 2048], P(None, ('dp', 'seq'))
- mix_coeffs_grad: float32 [7, 2048], P(None, ('dp', 'seq'))
- decay_coeff_grad: float32 [1, 2048], P(None, ('dp', 'seq'))
- mix_down_grad: float32 [2048, 160], P(('dp', 'seq'))
- mix_up_grad: float32 [160, 2048], P(None, ('dp', 'seq'))
- decay_down_grad: float32 [2048, 64], P(('dp', 'seq'))
- decay_up_grad: float32 [64, 32, 64], P(None, 'tp', ('dp', 'seq'))
- proj_weights_grad: float32 [4, 2048, 2048], P(None, ('dp', 'seq'), 'tp')
- out_weight_grad: float32 [2048, 2048], P('tp', ('dp', 'seq'))
- time_decay_grad: float32 [32, 64], P('tp', ('dp', 'seq'))
- time_first_grad: float32 [32, 64], P('tp', ('dp', 'seq'))
- group_gain_grad: float32 [32, 64], P('tp', ('dp', 'seq'))
- group_bias_grad: float32 [32, 64], P('tp', ('dp', 'seq'))
- channel_key_grad: float32 [2048, 7168], P(('dp', 'seq'), 'tp')
- channel_value_grad: float32 [7168, 2048], P('tp', ('dp', 'seq'))
- channel_recept_grad: float32 [2048, 2048], P(('dp', 'seq'), 'tp')
- decay_min: float32 [8, 32], P('dp', 'tp')
- decay_max: float32 [8, 32], P('dp', 'tp')
All inputs are finite; a program needn't handle non-finite values.
Results may differ from a plain program's by a relative error of at most 0.015.
The roundings to bfloat16 on the way count: a program that leaves them out, or rounds other values in their place, can miss the bound.
Values may be sent and summed in bfloat16 or wider, within the bound.
A program may use at most 512 MiB of HBM per device.

v0:
```python
import jax
import jax.numpy as jnp
from jax import lax
from jax.sharding import PartitionSpec as P

PRECISION_TOP = lax.Precision.HIGHEST
NORM_EPS = 1e-05
GROUP_EPS = 0.00064


def from_behind(block, axis, distance):
    devices = range(lax.axis_size(axis))
    route = [(i - distance, i) for i in devices if i - distance in devices]
    return lax.ppermute(block, axis, route)


def entering(array, axis, combine, identity):
    devices, place = (lax.axis_size(axis), lax.axis_index(axis))
    everything = jax.tree.map(lambda part: lax.all_gather(part, axis), array)
    start = jax.tree.map(
        lambda part, zero: jnp.broadcast_to(jnp.asarray(zero, part.dtype), part.shape),
        array,
        identity,
    )

    def turn(k, before):
        reached = k < place
        new = combine(before, jax.tree.map(lambda part: part[k], everything))
        return jax.tree.map(lambda a, b: jnp.where(reached, a, b), new, before)

    return lax.fori_loop(0, devices, turn, start)


def for_sending(array):

    def short(part):
        return part.astype(jnp.bfloat16) if part.dtype == jnp.float32 else part

    return jax.tree.map(short, array)


def entering_2(array, axis, combine, identity):
    devices, place = (lax.axis_size(axis), lax.axis_index(axis))
    everything = jax.tree.map(
        lambda part, kind: lax.all_gather(part.astype(kind), axis),
        array,
        jax.tree.map(lambda a: jnp.bfloat16 if a.dtype == jnp.float32 else a.dtype, array),
    )
    start = jax.tree.map(
        lambda part, zero: jnp.broadcast_to(jnp.asarray(zero, part.dtype), part.shape),
        array,
        identity,
    )

    def turn(k, before):
        at = devices - 1 - k
        reached = at > place
        new = combine(
            before, jax.tree.map(lambda part, own: part[at].astype(own.dtype), everything, array)
        )
        return jax.tree.map(lambda a, b: jnp.where(reached, a, b), new, before)

    return lax.fori_loop(0, devices, turn, start)


def joined(array, axis, combine):
    everything = jax.tree.map(
        lambda part, kind: lax.all_gather(part.astype(kind), axis),
        array,
        jax.tree.map(lambda a: jnp.bfloat16 if a.dtype == jnp.float32 else a.dtype, array),
    )

    def take(k):
        return jax.tree.map(lambda part, own: part[k].astype(own.dtype), everything, array)

    return lax.fori_loop(
        1, lax.axis_size(axis), lambda k, so_far: combine(so_far, take(k)), take(0)
    )


def dense_single_float(left, right):
    return jnp.einsum(
        "...i,ij->...j", left, right, precision=PRECISION_TOP, preferred_element_type=jnp.float32
    )


def layer_norm(values, scale_row, shift_row):
    mean_val = jnp.mean(values, axis=-1, keepdims=True)
    centered = values - mean_val
    variance = jnp.mean(centered * centered, axis=-1, keepdims=True)
    return centered * lax.rsqrt(variance + NORM_EPS) * scale_row + shift_row


def group_norm(values, scale_rows, shift_rows):
    mean_val = jnp.mean(values, axis=-1, keepdims=True)
    centered = values - mean_val
    variance = jnp.mean(centered * centered, axis=-1, keepdims=True)
    return (
        centered * lax.rsqrt(variance + GROUP_EPS) * scale_rows[None, :, None, :]
        + shift_rows[None, :, None, :]
    )


def token_mixture(
    normalized_rows, preceding_row, shift_coefficient, lowrank_down, lowrank_up, decay_projection
):
    earlier = jnp.concatenate([preceding_row[:, None, :], normalized_rows[:, :-1, :]], axis=1)
    shift_difference = earlier - normalized_rows
    base_value = normalized_rows + shift_difference * shift_coefficient[0]
    hidden_mixture = jnp.tanh(dense_single_float(base_value, lowrank_down))
    seq_count, length, feature_columns = normalized_rows.shape
    rank_count = lowrank_up.shape[0] // 5
    lowrank_map = jnp.einsum(
        "stri,rid->rstd",
        hidden_mixture.reshape(seq_count, length, 5, rank_count),
        lowrank_up.reshape(5, rank_count, feature_columns),
        precision=PRECISION_TOP,
    )
    mixed_input = [
        normalized_rows
        + shift_difference * (shift_coefficient[1 + branch_output] + lowrank_map[branch_output])
        for branch_output in range(5)
    ]
    hidden_decay = jnp.tanh(dense_single_float(mixed_input[0], decay_projection))
    return (mixed_input[3], mixed_input[1], mixed_input[2], mixed_input[4], hidden_decay)


def decay_rates(hidden_decay, decay_lift, decay_base):
    return decay_base + dense_single_float(hidden_decay, decay_lift)


def channel_mix(normalized_rows, preceding_row, shift_coefficient):
    earlier = jnp.concatenate([preceding_row[:, None, :], normalized_rows[:, :-1, :]], axis=1)
    shift_difference = earlier - normalized_rows
    return (
        normalized_rows + shift_difference * shift_coefficient[6],
        normalized_rows + shift_difference * shift_coefficient[7],
    )


def span_totals(lookup_array_entries, payload_array_entries, natural_log_fading):
    cumulative = jnp.cumsum(-jnp.exp(natural_log_fading), axis=2)
    final_cum = cumulative[:, :, -1:, :]
    carried = jnp.einsum(
        "shtk,shtv->shkv",
        lookup_array_entries * jnp.exp(final_cum - cumulative),
        payload_array_entries,
        precision=PRECISION_TOP,
    )
    return (jnp.exp(final_cum[:, :, 0, :]), carried)


def segment_output(
    acceptance_entries_list,
    lookup_array_entries,
    payload_array_entries,
    natural_log_fading,
    initial_reward_vector,
    arriving_carry_tensor,
):
    decrement = -jnp.exp(natural_log_fading)
    cumulative = jnp.cumsum(decrement, axis=2)
    before = cumulative - decrement
    length = acceptance_entries_list.shape[2]
    middle = before[:, :, length // 2 : length // 2 + 1, :]
    carried = jnp.einsum(
        "shtk,shkv->shtv",
        acceptance_entries_list * jnp.exp(before),
        arriving_carry_tensor,
        precision=PRECISION_TOP,
    )
    scores = jnp.einsum(
        "shtk,shuk->shtu",
        acceptance_entries_list * jnp.exp(before - middle),
        lookup_array_entries * jnp.exp(middle - cumulative),
        precision=PRECISION_TOP,
    )
    positions = lax.broadcasted_iota(jnp.int32, (length, length), 0)
    sources = lax.broadcasted_iota(jnp.int32, (length, length), 1)
    scores = jnp.where(positions > sources, scores, 0.0)
    within = jnp.einsum("shtu,shuv->shtv", scores, payload_array_entries, precision=PRECISION_TOP)
    current = (
        jnp.sum(
            acceptance_entries_list
            * initial_reward_vector[None, :, None, :]
            * lookup_array_entries,
            axis=-1,
            keepdims=True,
        )
        * payload_array_entries
    )
    return carried + within + current


def chain_link(earlier, later_part):
    return (earlier[0] * later_part[0], later_part[0][..., None] * earlier[1] + later_part[1])


def merge_totals(left_side, right_side):
    return (
        left_side[0] + right_side[0],
        jnp.minimum(left_side[1], right_side[1]),
        jnp.maximum(left_side[2], right_side[2]),
    )


def gather_params(
    norm_gains,
    norm_biases,
    mixing_coefficients,
    mix_down,
    mixing_up_weight,
    decay_down,
    decay_up,
    proj_weights,
    out_weight,
    time_decay,
    time_first,
    group_gain,
    group_bias,
):
    return (
        lax.all_gather(norm_gains, ("dp", "seq"), axis=1, tiled=True),
        lax.all_gather(norm_biases, ("dp", "seq"), axis=1, tiled=True),
        lax.all_gather(mixing_coefficients, ("dp", "seq"), axis=1, tiled=True),
        lax.all_gather(mix_down, ("dp", "seq"), axis=0, tiled=True),
        lax.all_gather(mixing_up_weight, ("dp", "seq"), axis=1, tiled=True),
        lax.all_gather(decay_down, ("dp", "seq"), axis=0, tiled=True),
        lax.all_gather(decay_up, ("dp", "seq"), axis=2, tiled=True),
        lax.all_gather(proj_weights, ("dp", "seq"), axis=1, tiled=True),
        lax.all_gather(out_weight, ("dp", "seq"), axis=1, tiled=True),
        lax.all_gather(time_decay, ("dp", "seq"), axis=1, tiled=True),
        lax.all_gather(time_first, ("dp", "seq"), axis=1, tiled=True),
        lax.all_gather(group_gain, ("dp", "seq"), axis=1, tiled=True),
        lax.all_gather(group_bias, ("dp", "seq"), axis=1, tiled=True),
    )


def per_device(
    block_input,
    initial_state,
    norm_gains,
    norm_biases,
    mixing_coefficients,
    mix_down,
    mixing_up_weight,
    decay_down,
    decay_up,
    proj_weights,
    out_weight,
    time_decay,
    time_first,
    group_gain,
    group_bias,
    channel_key,
    channel_value,
    channel_recept,
    out_grad,
):
    gathered_parameter_list = gather_params(
        norm_gains,
        norm_biases,
        mixing_coefficients,
        mix_down,
        mixing_up_weight,
        decay_down,
        decay_up,
        proj_weights,
        out_weight,
        time_decay,
        time_first,
        group_gain,
        group_bias,
    )
    gains_all = gathered_parameter_list[0].astype(jnp.float32)
    biases_all = gathered_parameter_list[1].astype(jnp.float32)
    shift_coefficient = gathered_parameter_list[2].astype(jnp.float32)
    lowrank_down = gathered_parameter_list[3].astype(jnp.float32)
    lowrank_up = gathered_parameter_list[4].astype(jnp.float32)
    decay_projection = gathered_parameter_list[5].astype(jnp.float32)
    decay_lift = gathered_parameter_list[6]
    projections = gathered_parameter_list[7]
    out_proj = gathered_parameter_list[8]
    decay_base = gathered_parameter_list[9]
    reward_array_entries = gathered_parameter_list[10].astype(jnp.float32)
    group_scale = gathered_parameter_list[11].astype(jnp.float32)
    group_shift = gathered_parameter_list[12].astype(jnp.float32)
    seq_count, length, feature_columns = block_input.shape
    heads_here, head_size = decay_base.shape
    head_cols = heads_here * head_size
    tokens = seq_count * length
    own_cols = channel_recept.shape[1]

    def split_heads(rows):
        return rows.reshape(seq_count, length, heads_here, head_size).transpose(0, 2, 1, 3)

    def join_heads(rows):
        return rows.transpose(0, 2, 1, 3).reshape(seq_count, length, head_cols)

    input_f = block_input.astype(jnp.float32)
    normalized_first, norm_one_back = jax.vjp(layer_norm, input_f, gains_all[0], biases_all[0])
    preceding_first = from_behind(normalized_first[:, -1, :].astype(jnp.bfloat16), "seq", 1).astype(
        jnp.float32
    )
    mixed_input, mix_back = jax.vjp(
        token_mixture,
        normalized_first,
        preceding_first,
        shift_coefficient,
        lowrank_down,
        lowrank_up,
        decay_projection,
    )
    log_rows, decay_back = jax.vjp(
        decay_rates,
        mixed_input[4],
        decay_lift.astype(jnp.float32).reshape(decay_lift.shape[0], head_cols),
        decay_base.astype(jnp.float32).reshape(head_cols),
    )
    stacked = jnp.stack(mixed_input[:4]).astype(jnp.bfloat16).reshape(4, tokens, feature_columns)
    projected = jnp.einsum("ntd,nde->nte", stacked, projections, preferred_element_type=jnp.float32)
    acceptance_entries_list = split_heads(projected[0])
    lookup_array_entries = split_heads(projected[1])
    payload_array_entries = split_heads(projected[2])
    gate_pre = projected[3].reshape(seq_count, length, head_cols)
    gate_act = jax.nn.silu(gate_pre)
    logarithm_heads = split_heads(log_rows)
    (decay_prod, carried), totals_back = jax.vjp(
        span_totals, lookup_array_entries, payload_array_entries, logarithm_heads
    )
    prefix_decay, prefix_state = entering(
        (decay_prod, carried),
        "seq",
        chain_link,
        (jnp.ones_like(decay_prod), jnp.zeros_like(carried)),
    )
    arriving_carry_tensor = prefix_decay[..., None] * initial_state + prefix_state
    wkv, output_back = jax.vjp(
        segment_output,
        acceptance_entries_list,
        lookup_array_entries,
        payload_array_entries,
        logarithm_heads,
        reward_array_entries,
        arriving_carry_tensor,
    )
    normed_heads, group_back = jax.vjp(group_norm, wkv, group_scale, group_shift)
    normed_rows = join_heads(normed_heads)
    mixer_in = (normed_rows * gate_act).astype(jnp.bfloat16)
    mixer_part = jnp.einsum("std,de->ste", mixer_in, out_proj, preferred_element_type=jnp.float32)
    residual = input_f + lax.psum(mixer_part, "tp")
    normed_two, norm_two_back = jax.vjp(layer_norm, residual, gains_all[1], biases_all[1])
    prev_two = from_behind(normed_two[:, -1, :].astype(jnp.bfloat16), "seq", 1).astype(jnp.float32)
    (chan_key, chan_recept), chan_back = jax.vjp(
        channel_mix, normed_two, prev_two, shift_coefficient
    )
    chan_key_b = chan_key.astype(jnp.bfloat16)
    chan_recept_b = chan_recept.astype(jnp.bfloat16)
    key_pre = jnp.einsum("std,df->stf", chan_key_b, channel_key, preferred_element_type=jnp.float32)
    hidden = jnp.square(jnp.maximum(key_pre, 0.0)).astype(jnp.bfloat16)
    value_part = jnp.einsum(
        "stf,fd->std", hidden, channel_value, preferred_element_type=jnp.float32
    )
    recept_pre = jnp.einsum(
        "std,de->ste", chan_recept_b, channel_recept, preferred_element_type=jnp.float32
    )
    kv_rows = lax.psum_scatter(
        value_part.astype(jnp.bfloat16), "tp", scatter_dimension=2, tiled=True
    ).astype(jnp.float32)
    gate_chan = jax.nn.sigmoid(recept_pre)
    own_residual = lax.dynamic_slice_in_dim(residual, lax.axis_index("tp") * own_cols, own_cols, 2)
    output = (own_residual + gate_chan * kv_rows).astype(jnp.bfloat16)
    decay_heads = jnp.exp(-jnp.exp(logarithm_heads))
    stat_least = jnp.min(decay_heads, axis=(2, 3))
    stat_most = jnp.max(decay_heads, axis=(2, 3))
    grad_out = out_grad.astype(jnp.float32)
    grad_value = (grad_out * gate_chan).astype(jnp.bfloat16)
    grad_recept = (grad_out * kv_rows * gate_chan * (1.0 - gate_chan)).astype(jnp.bfloat16)
    full_out, full_value = (
        lax.all_gather(out_grad, "tp", axis=2, tiled=True),
        lax.all_gather(grad_value, "tp", axis=2, tiled=True),
    )
    grad_hidden = jnp.einsum(
        "std,fd->stf", full_value, channel_value, preferred_element_type=jnp.float32
    )
    grad_key = (grad_hidden * 2.0 * jnp.maximum(key_pre, 0.0)).astype(jnp.bfloat16)
    part_key = jnp.einsum("stf,df->std", grad_key, channel_key, preferred_element_type=jnp.float32)
    part_recept = jnp.einsum(
        "ste,de->std", grad_recept, channel_recept, preferred_element_type=jnp.float32
    )
    grad_chan_key, grad_chan_recept = (
        lax.psum(part_key.astype(jnp.bfloat16), "tp").astype(jnp.float32),
        lax.psum(part_recept.astype(jnp.bfloat16), "tp").astype(jnp.float32),
    )
    grad_normed_two, grad_prev_two, grad_coeffs_chan = chan_back((grad_chan_key, grad_chan_recept))
    from_next_two = from_behind(for_sending(grad_prev_two), "seq", -1).astype(grad_prev_two.dtype)
    grad_normed_two = grad_normed_two.at[:, -1, :].add(from_next_two)
    grad_residual, grad_gain_two, grad_bias_two = norm_two_back(grad_normed_two)
    grad_residual = grad_residual + full_out.astype(jnp.float32)
    regather = lax.optimization_barrier(
        (
            (
                norm_gains,
                norm_biases,
                mixing_coefficients,
                mix_down,
                mixing_up_weight,
                decay_down,
                decay_up,
                proj_weights,
                out_weight,
                time_decay,
                time_first,
                group_gain,
                group_bias,
            ),
            grad_residual,
        )
    )[0]
    again_params = gather_params(
        regather[0],
        regather[1],
        regather[2],
        regather[3],
        regather[4],
        regather[5],
        regather[6],
        regather[7],
        regather[8],
        regather[9],
        regather[10],
        regather[11],
        regather[12],
    )
    projections = again_params[7]
    out_proj = again_params[8]
    grad_branch = grad_residual.astype(jnp.bfloat16)
    out_weight_grad = jnp.einsum(
        "std,ste->de", mixer_in, grad_branch, preferred_element_type=jnp.float32
    )
    grad_mixer = jnp.einsum(
        "ste,de->std", grad_branch, out_proj, preferred_element_type=jnp.float32
    )
    grad_normed_rows = grad_mixer * gate_act
    gate_sig = jax.nn.sigmoid(gate_pre)
    grad_gate = grad_mixer * normed_rows * gate_sig * (1.0 + gate_pre * (1.0 - gate_sig))
    grad_wkv, group_gain_grad, group_bias_grad = group_back(split_heads(grad_normed_rows))
    (
        receptance_gradient,
        key_gradient_output,
        value_gradient_output,
        logarithm_gradient_output,
        reward_cotangent_term,
        incoming_gradient,
    ) = output_back(grad_wkv)
    later_decay, later_grad = entering_2(
        (decay_prod, incoming_gradient),
        "seq",
        chain_link,
        (jnp.ones_like(decay_prod), jnp.zeros_like(incoming_gradient)),
    )
    grad_decay_prod = jnp.sum(later_grad * arriving_carry_tensor, axis=-1)
    grad_keys_tot, grad_values_tot, grad_logs_tot = totals_back((grad_decay_prod, later_grad))
    state_term = prefix_decay[..., None] * incoming_gradient
    state_grad, total_least, total_most = joined(
        (state_term, stat_least, stat_most), "seq", merge_totals
    )
    grad_proj = jnp.stack(
        [
            join_heads(receptance_gradient).reshape(tokens, head_cols),
            join_heads(key_gradient_output + grad_keys_tot).reshape(tokens, head_cols),
            join_heads(value_gradient_output + grad_values_tot).reshape(tokens, head_cols),
            grad_gate.reshape(tokens, head_cols),
        ]
    ).astype(jnp.bfloat16)
    proj_grad = jnp.einsum("ntd,nte->nde", stacked, grad_proj, preferred_element_type=jnp.float32)
    part_inputs = jnp.einsum(
        "nte,nde->ntd", grad_proj, projections, preferred_element_type=jnp.float32
    )
    grad_hdec_part, lift_grad, base_grad = decay_back(
        join_heads(logarithm_gradient_output + grad_logs_tot)
    )
    grad_inputs, grad_hdec = (
        lax.psum(part_inputs.astype(jnp.bfloat16), "tp").astype(jnp.float32),
        lax.psum(grad_hdec_part.astype(jnp.bfloat16), "tp").astype(jnp.float32),
    )
    grad_normed_one, grad_prev_one, grad_coeffs_time, down_grad, up_grad, decay_proj_grad = (
        mix_back(
            (
                grad_inputs[0].reshape(seq_count, length, feature_columns),
                grad_inputs[1].reshape(seq_count, length, feature_columns),
                grad_inputs[2].reshape(seq_count, length, feature_columns),
                grad_inputs[3].reshape(seq_count, length, feature_columns),
                grad_hdec,
            )
        )
    )
    from_next_one = from_behind(for_sending(grad_prev_one), "seq", -1).astype(grad_prev_one.dtype)
    grad_normed_one = grad_normed_one.at[:, -1, :].add(from_next_one)
    grad_block, grad_gain_one, grad_bias_one = norm_one_back(grad_normed_one)
    grad_block = grad_block + grad_residual
    input_grad = lax.dynamic_slice_in_dim(grad_block, lax.axis_index("tp") * own_cols, own_cols, 2)
    time_terms = (
        jnp.stack([grad_gain_one, grad_gain_two]),
        jnp.stack([grad_bias_one, grad_bias_two]),
        grad_coeffs_time + grad_coeffs_chan,
        down_grad,
        up_grad,
        decay_proj_grad,
        lift_grad.reshape(decay_lift.shape),
        proj_grad,
        out_weight_grad,
        base_grad.reshape(decay_base.shape),
        reward_cotangent_term,
        group_gain_grad,
        group_bias_grad,
    )
    value_weight_grad = jnp.einsum(
        "stf,std->fd", hidden, full_value, preferred_element_type=jnp.float32
    )
    key_weight_grad = jnp.einsum(
        "std,stf->df", chan_key_b, grad_key, preferred_element_type=jnp.float32
    )
    recept_weight_grad = jnp.einsum(
        "std,ste->de", chan_recept_b, grad_recept, preferred_element_type=jnp.float32
    )
    all_terms = time_terms + (key_weight_grad, value_weight_grad, recept_weight_grad)
    summed = (
        lax.psum_scatter(all_terms[0], ("dp", "seq"), scatter_dimension=1, tiled=True),
        lax.psum_scatter(all_terms[1], ("dp", "seq"), scatter_dimension=1, tiled=True),
        lax.psum_scatter(all_terms[2], ("dp", "seq"), scatter_dimension=1, tiled=True),
        lax.psum_scatter(all_terms[3], ("dp", "seq"), scatter_dimension=0, tiled=True),
        lax.psum_scatter(all_terms[4], ("dp", "seq"), scatter_dimension=1, tiled=True),
        lax.psum_scatter(all_terms[5], ("dp", "seq"), scatter_dimension=0, tiled=True),
        lax.psum_scatter(all_terms[6], ("dp", "seq"), scatter_dimension=2, tiled=True),
        lax.psum_scatter(all_terms[7], ("dp", "seq"), scatter_dimension=1, tiled=True),
        lax.psum_scatter(all_terms[8], ("dp", "seq"), scatter_dimension=1, tiled=True),
        lax.psum_scatter(all_terms[9], ("dp", "seq"), scatter_dimension=1, tiled=True),
        lax.psum_scatter(all_terms[10], ("dp", "seq"), scatter_dimension=1, tiled=True),
        lax.psum_scatter(all_terms[11], ("dp", "seq"), scatter_dimension=1, tiled=True),
        lax.psum_scatter(all_terms[12], ("dp", "seq"), scatter_dimension=1, tiled=True),
        lax.psum_scatter(all_terms[13], ("dp", "seq"), scatter_dimension=0, tiled=True),
        lax.psum_scatter(all_terms[14], ("dp", "seq"), scatter_dimension=1, tiled=True),
        lax.psum_scatter(all_terms[15], ("dp", "seq"), scatter_dimension=0, tiled=True),
    )
    rest = summed[:13]
    key_sum, value_sum_rows, recept_sum = (summed[13], summed[14], summed[15])
    coeff_rows = jnp.concatenate([rest[2][:1], rest[2][2:]], axis=0)
    decay_row = rest[2][1:2]
    return (
        output,
        input_grad,
        state_grad,
        rest[0],
        rest[1],
        coeff_rows,
        decay_row,
        rest[3],
        rest[4],
        rest[5],
        rest[6],
        rest[7],
        rest[8],
        rest[9],
        rest[10],
        rest[11],
        rest[12],
        key_sum,
        value_sum_rows,
        recept_sum,
        total_least,
        total_most,
    )


def solution(mesh):
    return jax.shard_map(
        per_device,
        mesh=mesh,
        in_specs=(
            P("dp", "seq", None),
            P("dp", "tp", None, None),
            P(None, ("dp", "seq")),
            P(None, ("dp", "seq")),
            P(None, ("dp", "seq")),
            P(("dp", "seq"), None),
            P(None, ("dp", "seq")),
            P(("dp", "seq"), None),
            P(None, "tp", ("dp", "seq")),
            P(None, ("dp", "seq"), "tp"),
            P("tp", ("dp", "seq")),
            P("tp", ("dp", "seq")),
            P("tp", ("dp", "seq")),
            P("tp", ("dp", "seq")),
            P("tp", ("dp", "seq")),
            P(None, "tp"),
            P("tp", None),
            P(None, "tp"),
            P("dp", "seq", "tp"),
        ),
        out_specs=(
            P("dp", "seq", "tp"),
            P("dp", "seq", "tp"),
            P("dp", "tp", None, None),
            P(None, ("dp", "seq")),
            P(None, ("dp", "seq")),
            P(None, ("dp", "seq")),
            P(None, ("dp", "seq")),
            P(("dp", "seq"), None),
            P(None, ("dp", "seq")),
            P(("dp", "seq"), None),
            P(None, "tp", ("dp", "seq")),
            P(None, ("dp", "seq"), "tp"),
            P("tp", ("dp", "seq")),
            P("tp", ("dp", "seq")),
            P("tp", ("dp", "seq")),
            P("tp", ("dp", "seq")),
            P("tp", ("dp", "seq")),
            P(("dp", "seq"), "tp"),
            P("tp", ("dp", "seq")),
            P(("dp", "seq"), "tp"),
            P("dp", "tp"),
            P("dp", "tp"),
        ),
        check_vma=False,
    )
```

profile of v0, /device:TPU:0, one launch (start us, length us, event | category | flops | bytes accessed | tf_op | source)
XLA Modules:
  0.0 3084.7 jit_solution(9080356912012168600)
XLA Ops:
  8.0 23.2 all_gather.85
  31.2 17.7 all_gather.86
  59.2 19.5 all_gather.87
  78.7 22.1 all_gather.92
  100.8 28.4 all_gather.88
  129.1 26.0 all_gather.89
  155.9 20.4 all_gather.93
  179.4 20.0 all-gather.7
  202.1 20.0 all-gather.8
  269.3 16.4 fusion.139
  308.6 13.5 exponential_reduce_fusion
  355.8 18.4 all-gather.9
  374.3 24.3 all-gather.10
  411.4 17.3 all-gather
  439.7 66.8 %all-gather.35.cloned.1.call-done = f32[32,16,64,64]{3,2,1,0:T(8,128)} async-done(((f32[4,16,64,64]{3,2,1,0:T(8,128)}), f32[32,16,64,64]{3,2,1,0:T(8,128)}) %all-gather.35.cloned.1.call-update) | async-done | bytes 8388624 | tf_op jit(solution)/shard_map/all_gather | solution.py:19
  506.5 28.4 while.54
  566.7 106.3 %all-reduce.28.cloned.1.call-done = f32[4,128,2048]{2,1,0:T(8,128)} async-done(((f32[4,128,2048]{2,1,0:T(8,128)}), f32[4,128,2048]{2,1,0:T(8,128)}) %all-reduce.28.cloned.1.call-update) | async-done | bytes 4194320 | tf_op jit(solution)/shard_map/psum | solution.py:351
  684.1 13.0 fusion.10
  709.1 34.0 %reduce-scatter.18.cloned.1.call-done = bf16[4,128,1024]{2,1,0:T(8,128)(2,1)} async-done(((bf16[4,128,2048]{2,1,0:T(8,128)(2,1)}), bf16[4,128,1024]{2,1,0:T(8,128)(2,1)}) %reduce-scatter.18.cloned.1.call-update) | async-done | bytes 1048592 | tf_op jit(solution)/shard_map/reduce_scatter | solution.py:367
  757.4 27.1 all-gather.27.cloned.1.call-done
  784.5 12.8 multiply_convert_fusion
  799.1 12.1 fusion.73
  812.0 107.6 %all-reduce.32.cloned.1.call-done = (bf16[4,128,2048]{2,1,0:T(8,128)(2,1)}, bf16[4,128,2048]{2,1,0:T(8,128)(2,1)}) async-done(((bf16[4,128,2048]{2,1,0:T(8,128)(2,1)}, bf16[4,128,2048]{2,1,0:T(8,128)(2,1)}), (bf16[4,128,2048]{2,1,0:T(8,128)(2,1)}, bf16[4,128,2048]{2,1,0:T(8,128)(2,1)})) %all-reduce.32.cloned.1.call-update) | async-done | bytes 4194320 | tf_op jit(solution)/shard_map/psum | solution.py:392
  960.7 53.3 %all-gather.31.cloned.1.call-done = bf16[1024,2048]{1,0:T(8,128)(2,1)} async-done(((bf16[1024,128]{1,0:T(8,128)(2,1)}), bf16[1024,2048]{1,0:T(8,128)(2,1)}) %all-gather.31.cloned.1.call-update) | async-done | bytes 4194320 | tf_op jit(solution)/shard_map/all_gather | solution.py:231
  1042.4 14.6 all-gather.6
  1079.5 12.4 fusion.64
  1104.6 12.2 all-gather.37.cloned.1.call-done
  1116.8 25.3 while.55
  1244.9 15.2 convolution_convert_fusion
  1267.6 190.8 %all-reduce.30.cloned.1.call-done = (bf16[4,512,2048]{2,1,0:T(8,128)(2,1)}, bf16[4,128,64]{1,2,0:T(8,128)(2,1)}) async-done(((bf16[4,512,2048]{2,1,0:T(8,128)(2,1)}, bf16[4,128,64]{1,2,0:T(8,128)(2,1)}), (bf16[4,512,2048]{2,1,0:T(8,128)(2,1)}, bf16[4,128,64]{1,2,0:T(8,128)(2,1)})) %all-reduce.30.cloned.1.call-update) | async-done | bytes 8454160 | tf_op jit(solution)/shard_map/psum | solution.py:484
  1473.5 15.3 multiply_bitcast_fusion.4
  1488.9 14.2 convolution_bitcast_fusion.6
  1503.3 21.8 multiply_reduce_fusion.12
  1570.9 16.4 convolution_bitcast_fusion
  1587.8 15.8 convolution_bitcast_fusion.1
  1611.8 15.8 fusion.2
  1635.1 18.9 fusion.138
  1655.9 12.8 all-gather.12
  1677.8 61.0 %all-reduce.21 = (f32[16,64]{0,1:T(8,128)S(1)}, f32[16,64]{0,1:T(8,128)S(1)}, f32[16,64]{0,1:T(8,128)S(1)}, f32[16,64]{0,1:T(8,128)S(1)}) all-reduce(f32[16,64]{0,1:T(8,128)S(1)} %copy.489, f32[16,64]{0,1:T(8,128)S(1)} %copy.492, f32[16,64]{0,1:T(8,128)S(1)} %copy.493, ...), channel_id=19, replica_groups=mesh['dp'=2,'seq'=8,'tp'=2] {'dp','seq'}, use_global_device_ids=true, to_apply=%region_57.58.clone | all-reduce | flops 4096 | bytes 32768
  1742.8 25.5 while.53
  1780.4 103.5 %reduce-scatter.38.cloned.1.call-done = f32[128,1024]{1,0:T(8,128)} async-done(((f32[2048,1024]{1,0:T(8,128)}), f32[128,1024]{1,0:T(8,128)}) %reduce-scatter.38.cloned.1.call-update) | async-done | bytes 524304 | tf_op jit(solution)/shard_map/reduce_scatter | solution.py:544
  1883.9 109.8 %reduce-scatter.32.cloned.1.call-done = f32[1024,128]{1,0:T(8,128)} async-done(((f32[1024,2048]{1,0:T(8,128)}), f32[1024,128]{1,0:T(8,128)}) %reduce-scatter.32.cloned.1.call-update) | async-done | bytes 524304 | tf_op jit(solution)/shard_map/reduce_scatter | solution.py:537
  1993.7 282.6 %reduce-scatter.36.cloned.1.call-done = f32[3584,128]{1,0:T(8,128)} async-done(((f32[3584,2048]{1,0:T(8,128)}), f32[3584,128]{1,0:T(8,128)}) %reduce-scatter.36.cloned.1.call-update) | async-done | bytes 1835024 | tf_op jit(solution)/shard_map/reduce_scatter | solution.py:543
  2276.3 282.1 %reduce-scatter.34.cloned.1.call-done = f32[128,3584]{1,0:T(8,128)} async-done(((f32[2048,3584]{1,0:T(8,128)}), f32[128,3584]{1,0:T(8,128)}) %reduce-scatter.34.cloned.1.call-update) | async-done | bytes 1835024 | tf_op jit(solution)/shard_map/reduce_scatter | solution.py:542
  2558.4 59.4 %reduce-scatter.26.cloned.1.call-done = f32[128,64]{0,1:T(8,128)} async-done(((f32[2048,64]{0,1:T(8,128)}), f32[128,64]{0,1:T(8,128)}) %reduce-scatter.26.cloned.1.call-update) | async-done | bytes 32784 | tf_op jit(solution)/shard_map/reduce_scatter | solution.py:534
  2617.8 61.6 %reduce-scatter.24.cloned.1.call-done = f32[160,128]{1,0:T(8,128)} async-done(((f32[160,2048]{1,0:T(8,128)}), f32[160,128]{1,0:T(8,128)}) %reduce-scatter.24.cloned.1.call-update) | async-done | bytes 81936 | tf_op jit(solution)/shard_map/reduce_scatter | solution.py:533
  2679.4 61.9 %reduce-scatter.22.cloned.1.call-done = f32[128,160]{0,1:T(8,128)} async-done(((f32[2048,160]{0,1:T(8,128)}), f32[128,160]{0,1:T(8,128)}) %reduce-scatter.22.cloned.1.call-update) | async-done | bytes 81936 | tf_op jit(solution)/shard_map/reduce_scatter | solution.py:532
  2741.3 336.6 %reduce-scatter.30.cloned.1.call-done = f32[4,128,1024]{2,1,0:T(8,128)} async-done(((f32[4,2048,1024]{2,1,0:T(8,128)}), f32[4,128,1024]{2,1,0:T(8,128)}) %reduce-scatter.30.cloned.1.call-update) | async-done | bytes 2097168 | tf_op jit(solution)/shard_map/reduce_scatter | solution.py:536
  (553 shorter events, 612.8 us)
Async XLA Ops:
  7.2 43.6 %copy-start.2 = (bf16[4,128,2048]{2,1,0:T(8,128)(2,1)S(1)}, bf16[4,128,2048]{2,1,0:T(8,128)(2,1)}, u32[]{:S(2)}) copy-start(bf16[4,128,2048]{2,1,0:T(8,128)(2,1)} %param.29) | copy-start | bytes 6291460
  7.2 262.1 %all-gather.23.cloned.1.call-start = ((), (), s32[]{:S(2)}) async-start(), calls=%async_computation.13 | async-start | bytes 17825792 | tf_op jit(solution)/shard_map/all_gather | solution.py:230
  7.9 498.5 %all-gather.35.cloned.1.call-start = ((), (), s32[]{:S(2)}) async-start(), calls=%async_computation.31 | async-start | bytes 18874368 | tf_op jit(solution)/shard_map/all_gather | solution.py:19
  50.9 27.8 copy-start.122
  50.9 49.9 %copy-start.109 = (bf16[128,160]{0,1:T(8,128)(2,1)S(1)}, bf16[128,160]{0,1:T(8,128)(2,1)}, u32[]{:S(2)}) copy-start(bf16[128,160]{0,1:T(8,128)(2,1)} %param.34) | copy-start | bytes 122884
  51.6 77.5 %copy-start.110 = (bf16[160,128]{1,0:T(8,128)(2,1)S(1)}, bf16[160,128]{1,0:T(8,128)(2,1)}, u32[]{:S(2)}) copy-start(bf16[160,128]{1,0:T(8,128)(2,1)} %param.35) | copy-start | bytes 122884
  51.6 49.2 %copy-start.97 = (f32[4,128]{1,0:T(4,128)}, f32[4,128]{1,0:T(4,128)S(1)}, u32[]{:S(2)}) copy-start(f32[4,128]{1,0:T(4,128)S(1)} %fusion.178) | copy-start | bytes 6148
  52.2 205.0 %copy-start.64 = (f32[1,2048]{1,0:T(1,128)}, f32[1,2048]{1,0:T(1,128)S(1)}, u32[]{:S(2)}) copy-start(f32[1,2048]{1,0:T(1,128)S(1)} %get-tuple-element.765) | copy-start | bytes 24580
  52.8 47.9 %copy-start.70 = (f32[1,2048]{1,0:T(1,128)}, f32[1,2048]{1,0:T(1,128)S(1)}, u32[]{:S(2)}) copy-start(f32[1,2048]{1,0:T(1,128)S(1)} %get-tuple-element.767) | copy-start | bytes 24580
  56.3 167.1 %collective-permute-start = (bf16[4,2048]{1,0:T(4,128)(2,1)}, bf16[4,2048]{1,0:T(4,128)(2,1)}, u32[]{:S(2)}, u32[]{:S(2)}) collective-permute-start(bf16[4,2048]{1,0:T(4,128)(2,1)} %bitcast.472), channel_id=1, source_target_pairs={{0,2},{2,4},{4,6},{6,8},{8,10},{10,12},{12,14},{1,3},{3,5},{5,7},{... | collective-permute-start | bytes 49160 | tf_op jit(solution)/shard_map/ppermute | solution.py:14
  129.1 98.7 %copy-start.48 = (bf16[2048,160]{0,1:T(8,128)(2,1)}, bf16[2048,160]{0,1:T(8,128)(2,1)S(1)}, u32[]{:S(2)}) copy-start(bf16[2048,160]{0,1:T(8,128)(2,1)S(1)} %all_gather.88) | copy-start | bytes 1966084
  155.1 76.2 %copy-start.44 = (bf16[160,2048]{1,0:T(8,128)(2,1)}, bf16[160,2048]{1,0:T(8,128)(2,1)S(1)}, u32[]{:S(2)}) copy-start(bf16[160,2048]{1,0:T(8,128)(2,1)S(1)} %all_gather.89) | copy-start | bytes 1966084
  155.9 84.1 %copy-start.68 = (f32[1,2048]{1,0:T(1,128)}, f32[1,2048]{1,0:T(1,128)S(1)}, u32[]{:S(2)}) copy-start(f32[1,2048]{1,0:T(1,128)S(1)} %get-tuple-element.755) | copy-start | bytes 24580
  348.0 26.3 copy-start.128
  355.0 205.1 %all-gather.25.cloned.1.call-start = ((), (), s32[]{:S(2)}) async-start(), calls=%async_computation.14 | async-start | bytes 4456448 | tf_op jit(solution)/shard_map/all_gather | solution.py:231
  355.7 317.4 %all-reduce.28.cloned.1.call-start = ((), (), s32[]{:S(2)}) async-start(), calls=%async_computation.15 | async-start | bytes 8388608 | tf_op jit(solution)/shard_map/psum | solution.py:351
  374.3 654.4 %copy-start.91 = (f32[64,16]{0,1:T(8,128)}, f32[64,16]{0,1:T(8,128)S(1)}, u32[]{:S(2)}) copy-start(f32[64,16]{0,1:T(8,128)S(1)} %copy.451) | copy-start | bytes 12292
  411.4 140.0 %copy-start.83 = (f32[4,128,16]{1,2,0:T(8,128)}, f32[4,128,16]{1,2,0:T(8,128)S(1)}, u32[]{:S(2)}) copy-start(f32[4,128,16]{1,2,0:T(8,128)S(1)} %copy.448) | copy-start | bytes 98308
  566.7 176.5 %reduce-scatter.18.cloned.1.call-start = ((), (), s32[]{:S(2)}) async-start(), calls=%async_computation.16 | async-start | bytes 3145728 | tf_op jit(solution)/shard_map/reduce_scatter | solution.py:367
  677.4 2.6 collective-permute-start.1
  682.7 60.4 %copy-start.54 = (bf16[4,128,2048]{2,1,0:T(8,128)(2,1)}, bf16[4,128,2048]{2,1,0:T(8,128)(2,1)S(1)}, u32[]{:S(2)}) copy-start(bf16[4,128,2048]{2,1,0:T(8,128)(2,1)S(1)} %get-tuple-element.715) | copy-start | bytes 6291460
  697.2 46.0 %copy-start.61 = (bf16[4,128,1024]{2,1,0:T(8,128)(2,1)S(1)}, bf16[4,128,1024]{2,1,0:T(8,128)(2,1)}, u32[]{:S(2)}) copy-start(bf16[4,128,1024]{2,1,0:T(8,128)(2,1)} %param.47) | copy-start | bytes 3145732
  708.7 75.8 %all-gather.27.cloned.1.call-start = ((), (), s32[]{:S(2)}) async-start(), calls=%async_computation.17 | async-start | bytes 3145728 | tf_op jit(solution)/shard_map/all_gather | solution.py:381
  751.2 168.4 %all-reduce.32.cloned.1.call-start = ((), (), s32[]{:S(2)}) async-start(), calls=%async_computation.37 | async-start | bytes 8388608 | tf_op jit(solution)/shard_map/psum | solution.py:392
  811.2 143.2 %all-gather.29.cloned.1.call-start = ((), (), s32[]{:S(2)}) async-start(), calls=%async_computation.18 | async-start | bytes 3145728 | tf_op jit(solution)/shard_map/all_gather | solution.py:380
  812.0 202.0 %all-gather.31.cloned.1.call-start = ((), (), s32[]{:S(2)}) async-start(), calls=%async_computation.19 | async-start | bytes 4456448 | tf_op jit(solution)/shard_map/all_gather | solution.py:231
  926.8 3.4 collective-permute-start.2
  942.3 71.7 %copy-start.37 = (f32[4,128,1024]{2,1,0:T(8,128)S(1)}, f32[4,128,1024]{2,1,0:T(8,128)}, u32[]{:S(2)}) copy-start(f32[4,128,1024]{2,1,0:T(8,128)} %copy.453) | copy-start | bytes 6291460
  960.6 156.2 %all-gather.37.cloned.1.call-start = ((), (), s32[]{:S(2)}) async-start(), calls=%async_computation.32 | async-start | bytes 9437184 | tf_op jit(solution)/shard_map/all_gather | solution.py:45
  1035.5 209.4 %all-gather.33.cloned.1.call-start = ((), (), s32[]{:S(2)}) async-start(), calls=%async_computation.20 | async-start | bytes 17825792 | tf_op jit(solution)/shard_map/all_gather | solution.py:230
  1036.3 422.2 %all-reduce.30.cloned.1.call-start = ((), (), s32[]{:S(2)}) async-start(), calls=%async_computation.36 | async-start | bytes 16908288 | tf_op jit(solution)/shard_map/psum | solution.py:484
  1260.1 198.3 %copy-start.51 = (bf16[2048,64]{0,1:T(8,128)(2,1)S(1)}, bf16[2048,64]{0,1:T(8,128)(2,1)}, u32[]{:S(2)}) copy-start(bf16[2048,64]{0,1:T(8,128)(2,1)} %all_gather.92) | copy-start | bytes 786436
  1260.2 479.8 %all-gather.39.cloned.1.call-start = ((), (), s32[]{:S(2)}) async-start(), calls=%async_computation.33 | async-start | bytes 9437184 | tf_op jit(solution)/shard_map/all_gather | solution.py:68
  1260.9 507.4 %reduce-scatter.28.cloned.1.call-start = ((), (), s32[]{:S(2)}) async-start(), calls=%async_computation.25 | async-start | bytes 557056 | tf_op jit(solution)/shard_map/reduce_scatter | solution.py:535
  1267.6 507.3 %reduce-scatter.42.cloned.1.call-start = ((), (), s32[]{:S(2)}) async-start(), calls=%async_computation.35 | async-start | bytes 1114112
  1531.4 11.8 collective-permute-start.3
  1551.9 224.5 %reduce-scatter.40.cloned.1.call-start = ((), (), s32[]{:S(2)}) async-start(), calls=%async_computation.34 | async-start | bytes 1114112
  1553.4 224.5 %reduce-scatter.20.cloned.1.call-start = ((), (), s32[]{:S(2)}) async-start(), calls=%async_computation.21 | async-start | bytes 69632 | tf_op jit(solution)/shard_map/reduce_scatter | solution.py:531
  1554.2 329.7 %reduce-scatter.38.cloned.1.call-start = ((), (), s32[]{:S(2)}) async-start(), calls=%async_computation.30 | async-start | bytes 8912896 | tf_op jit(solution)/shard_map/reduce_scatter | solution.py:544
  1561.8 431.9 %reduce-scatter.32.cloned.1.call-start = ((), (), s32[]{:S(2)}) async-start(), calls=%async_computation.27 | async-start | bytes 8912896 | tf_op jit(solution)/shard_map/reduce_scatter | solution.py:537
  1570.9 705.4 %reduce-scatter.36.cloned.1.call-start = ((), (), s32[]{:S(2)}) async-start(), calls=%async_computation.29 | async-start | bytes 31195136 | tf_op jit(solution)/shard_map/reduce_scatter | solution.py:543
  1587.4 971.1 %reduce-scatter.34.cloned.1.call-start = ((), (), s32[]{:S(2)}) async-start(), calls=%async_computation.28 | async-start | bytes 31195136 | tf_op jit(solution)/shard_map/reduce_scatter | solution.py:542
  1603.7 1014.2 %reduce-scatter.26.cloned.1.call-start = ((), (), s32[]{:S(2)}) async-start(), calls=%async_computation.24 | async-start | bytes 557056 | tf_op jit(solution)/shard_map/reduce_scatter | solution.py:534
  1611.7 1067.7 %reduce-scatter.24.cloned.1.call-start = ((), (), s32[]{:S(2)}) async-start(), calls=%async_computation.23 | async-start | bytes 1392640 | tf_op jit(solution)/shard_map/reduce_scatter | solution.py:533
  1627.6 1113.7 %reduce-scatter.22.cloned.1.call-start = ((), (), s32[]{:S(2)}) async-start(), calls=%async_computation.22 | async-start | bytes 1392640 | tf_op jit(solution)/shard_map/reduce_scatter | solution.py:532
  1635.0 1442.9 %reduce-scatter.30.cloned.1.call-start = ((), (), s32[]{:S(2)}) async-start(), calls=%async_computation.26 | async-start | bytes 35651584 | tf_op jit(solution)/shard_map/reduce_scatter | solution.py:536
  1654.1 23.6 copy-start.115
  1742.8 26.9 copy-start.120
  (117 other events, 907.2 us)
Sparse Core Ops, SparseCore 0:
  10.3 140.6 all-gather.22
  355.1 151.3 all-gather.34
  508.6 51.4 all-gather.24
  566.8 106.2 all-reduce.27
  708.8 34.2 reduce-scatter.17
  751.3 33.1 all-gather.26
  811.3 108.2 all-reduce.31
  921.2 33.1 all-gather.28
  960.7 53.1 all-gather.30
  1035.7 81.1 all-gather.36
  1119.3 125.5 all-gather.32
  1260.3 198.1 all-reduce.29
  1460.1 82.2 all-gather.38
  1546.2 54.2 reduce-scatter.27
  1604.0 56.4 reduce-scatter.41
  1664.4 56.5 reduce-scatter.39
  1724.3 50.9 reduce-scatter.19
  1780.2 103.5 reduce-scatter.37
  1889.1 104.5 reduce-scatter.31
  1998.8 277.5 reduce-scatter.35
  2281.6 276.8 reduce-scatter.33
  2563.0 54.8 reduce-scatter.25
  2622.0 57.3 reduce-scatter.23
  2683.9 57.3 reduce-scatter.21
  2746.2 331.7 reduce-scatter.29
where the time goes:
time: 3090 us; the launch traced here: 3080 us
  waiting for transfers between devices  1920 us (62%)
  matrix products  367 us (12%)
  blocking collectives  354 us (11%)
  other arithmetic  244 us (8%)
  local copies, waits for them, and re-layouts  171 us (6%)
    reduce_scatter x1, waiting for transfers between devices, per_device(): lax.psum_scatter(all_terms[7], ('dp', 'seq'), scatter_dimension=1, tiled=...  337 us
    reduce_scatter x1, waiting for transfers between devices, per_device(): lax.psum_scatter(all_terms[14], ('dp', 'seq'), scatter_dimension=1, tiled...  283 us
    reduce_scatter x1, waiting for transfers between devices, per_device(): lax.psum_scatter(all_terms[13], ('dp', 'seq'), scatter_dimension=0, tiled...  282 us
    psum x1, waiting for transfers between devices, per_device(): lax.psum(part_inputs.astype(jnp.bfloat16), 'tp').astype(jnp.float32)  191 us
    reduce_scatter x1, waiting for transfers between devices, per_device(): lax.psum_scatter(all_terms[8], ('dp', 'seq'), scatter_dimension=1, tiled=...  110 us
    psum x1, waiting for transfers between devices, per_device(): lax.psum(part_key.astype(jnp.bfloat16), 'tp').astype(jnp.float32)  108 us
    psum x1, waiting for transfers between devices, per_device(): residual = input_f + lax.psum(mixer_part, 'tp')  106 us
    reduce_scatter x1, waiting for transfers between devices, per_device(): lax.psum_scatter(all_terms[15], ('dp', 'seq'), scatter_dimension=0, tiled...  103 us
  transfers between devices with their start and end apart: 29, of which 20 were waited for; matrix products, arithmetic and copies ran while one was open for 18% of the time, Pallas kernels for 0%

commit v1 on v0

v1 whole, which is shorter than its diff:
```python
import jax
import jax.numpy as jnp
from jax import lax
from jax.sharding import PartitionSpec as P

PRECISION_TOP = lax.Precision.HIGHEST
NORM_EPS = 1e-05
GROUP_EPS = 0.00064


def from_behind(block, axis, distance):
    devices = range(lax.axis_size(axis))
    route = [(i - distance, i) for i in devices if i - distance in devices]
    return lax.ppermute(block, axis, route)


def for_sending(array):

    def short(part):
        return part.astype(jnp.bfloat16) if part.dtype == jnp.float32 else part

    return jax.tree.map(short, array)


def dense_single_float(left, right):
    return jnp.einsum(
        "...i,ij->...j", left, right, precision=PRECISION_TOP, preferred_element_type=jnp.float32
    )


def layer_norm(values, scale_row, shift_row):
    mean_val = jnp.mean(values, axis=-1, keepdims=True)
    centered = values - mean_val
    variance = jnp.mean(centered * centered, axis=-1, keepdims=True)
    return centered * lax.rsqrt(variance + NORM_EPS) * scale_row + shift_row


def group_norm(values, scale_rows, shift_rows):
    mean_val = jnp.mean(values, axis=-1, keepdims=True)
    centered = values - mean_val
    variance = jnp.mean(centered * centered, axis=-1, keepdims=True)
    return (
        centered * lax.rsqrt(variance + GROUP_EPS) * scale_rows[None, :, None, :]
        + shift_rows[None, :, None, :]
    )


def token_mixture(
    normalized_rows, preceding_row, shift_coefficient, lowrank_down, lowrank_up, decay_projection
):
    earlier = jnp.concatenate([preceding_row[:, None, :], normalized_rows[:, :-1, :]], axis=1)
    shift_difference = earlier - normalized_rows
    base_value = normalized_rows + shift_difference * shift_coefficient[0]
    hidden_mixture = jnp.tanh(dense_single_float(base_value, lowrank_down))
    seq_count, length, feature_columns = normalized_rows.shape
    rank_count = lowrank_up.shape[0] // 5
    lowrank_map = jnp.einsum(
        "stri,rid->rstd",
        hidden_mixture.reshape(seq_count, length, 5, rank_count),
        lowrank_up.reshape(5, rank_count, feature_columns),
        precision=PRECISION_TOP,
    )
    mixed_input = [
        normalized_rows
        + shift_difference * (shift_coefficient[1 + branch_output] + lowrank_map[branch_output])
        for branch_output in range(5)
    ]
    hidden_decay = jnp.tanh(dense_single_float(mixed_input[0], decay_projection))
    return (mixed_input[3], mixed_input[1], mixed_input[2], mixed_input[4], hidden_decay)


def decay_rates(hidden_decay, decay_lift, decay_base):
    return decay_base + dense_single_float(hidden_decay, decay_lift)


def channel_mix(normalized_rows, preceding_row, shift_coefficient):
    earlier = jnp.concatenate([preceding_row[:, None, :], normalized_rows[:, :-1, :]], axis=1)
    shift_difference = earlier - normalized_rows
    return (
        normalized_rows + shift_difference * shift_coefficient[6],
        normalized_rows + shift_difference * shift_coefficient[7],
    )


def span_totals(lookup_array_entries, payload_array_entries, natural_log_fading):
    cumulative = jnp.cumsum(-jnp.exp(natural_log_fading), axis=2)
    final_cum = cumulative[:, :, -1:, :]
    carried = jnp.einsum(
        "shtk,shtv->shkv",
        lookup_array_entries * jnp.exp(final_cum - cumulative),
        payload_array_entries,
        precision=PRECISION_TOP,
    )
    return (jnp.exp(final_cum[:, :, 0, :]), carried)


def segment_output(
    acceptance_entries_list,
    lookup_array_entries,
    payload_array_entries,
    natural_log_fading,
    initial_reward_vector,
    arriving_carry_tensor,
):
    decrement = -jnp.exp(natural_log_fading)
    cumulative = jnp.cumsum(decrement, axis=2)
    before = cumulative - decrement
    length = acceptance_entries_list.shape[2]
    middle = before[:, :, length // 2 : length // 2 + 1, :]
    carried = jnp.einsum(
        "shtk,shkv->shtv",
        acceptance_entries_list * jnp.exp(before),
        arriving_carry_tensor,
        precision=PRECISION_TOP,
    )
    scores = jnp.einsum(
        "shtk,shuk->shtu",
        acceptance_entries_list * jnp.exp(before - middle),
        lookup_array_entries * jnp.exp(middle - cumulative),
        precision=PRECISION_TOP,
    )
    positions = lax.broadcasted_iota(jnp.int32, (length, length), 0)
    sources = lax.broadcasted_iota(jnp.int32, (length, length), 1)
    scores = jnp.where(positions > sources, scores, 0.0)
    within = jnp.einsum("shtu,shuv->shtv", scores, payload_array_entries, precision=PRECISION_TOP)
    current = (
        jnp.sum(
            acceptance_entries_list
            * initial_reward_vector[None, :, None, :]
            * lookup_array_entries,
            axis=-1,
            keepdims=True,
        )
        * payload_array_entries
    )
    return carried + within + current


def packed_gather(pieces):
    flat = jnp.concatenate([part.reshape(-1) for part, _ in pieces])
    everything = lax.all_gather(flat, ("dp", "seq"))
    devices = everything.shape[0]
    out, at = [], 0
    for part, dim in pieces:
        piece = everything[:, at : at + part.size].reshape((devices,) + part.shape)
        at += part.size
        piece = jnp.moveaxis(piece, 0, dim)
        shape = list(part.shape)
        shape[dim] *= devices
        out.append(piece.reshape(shape))
    return out


def packed_scatter(pieces, devices):
    rows, shapes = [], []
    for whole, dim in pieces:
        shape = list(whole.shape)
        shape[dim] //= devices
        shapes.append(tuple(shape))
        cut = whole.reshape(whole.shape[:dim] + (devices, shape[dim]) + whole.shape[dim + 1 :])
        rows.append(jnp.moveaxis(cut, dim, 0).reshape(devices, -1))
    rows = jnp.concatenate(rows, axis=1)
    rows = jnp.pad(rows, ((0, 0), (0, -rows.shape[1] % 1024))).reshape(-1, 128)
    flat = lax.psum_scatter(rows, ("dp", "seq"), scatter_dimension=0, tiled=True).reshape(-1)
    out, at = [], 0
    for shape in shapes:
        size = 1
        for extent in shape:
            size *= extent
        out.append(flat[at : at + size].reshape(shape))
        at += size
    return out


def other_half(block):
    return lax.ppermute(block, "tp", [(0, 1), (1, 0)])


def big_scatter(whole, dim):
    return lax.psum_scatter(
        whole.astype(jnp.bfloat16), ("dp", "seq"), scatter_dimension=dim, tiled=True
    ).astype(jnp.float32)


def per_device(
    block_input,
    initial_state,
    norm_gains,
    norm_biases,
    mixing_coefficients,
    mix_down,
    mixing_up_weight,
    decay_down,
    decay_up,
    proj_weights,
    out_weight,
    time_decay,
    time_first,
    group_gain,
    group_bias,
    channel_key,
    channel_value,
    channel_recept,
    out_grad,
):
    blocks, place = lax.axis_size("seq"), lax.axis_index("seq")
    gathered = lax.axis_size("dp") * blocks
    half = lax.axis_index("tp")
    (
        gains_all,
        biases_all,
        shift_coefficient,
        lowrank_down,
        lowrank_up,
        decay_projection,
        decay_lift,
        decay_base,
        reward_array_entries,
        group_scale,
        group_shift,
    ) = [
        part.astype(jnp.float32)
        for part in packed_gather(
            [
                (norm_gains, 1),
                (norm_biases, 1),
                (mixing_coefficients, 1),
                (mix_down, 0),
                (mixing_up_weight, 1),
                (decay_down, 0),
                (decay_up, 2),
                (time_decay, 1),
                (time_first, 1),
                (group_gain, 1),
                (group_bias, 1),
            ]
        )
    ]
    projections = lax.all_gather(proj_weights, ("dp", "seq"), axis=1, tiled=True)
    out_proj = lax.all_gather(out_weight, ("dp", "seq"), axis=1, tiled=True)
    seq_count, length, feature_columns = block_input.shape
    heads_here, head_size = decay_base.shape
    head_cols = heads_here * head_size
    tokens = seq_count * length
    own_cols = channel_recept.shape[1]

    def split_heads(rows):
        return rows.reshape(seq_count, length, heads_here, head_size).transpose(0, 2, 1, 3)

    def join_heads(rows):
        return rows.transpose(0, 2, 1, 3).reshape(seq_count, length, head_cols)

    def both_halves(own):
        other = other_half(own)
        low = jnp.where(half == 0, own, other)
        high = jnp.where(half == 0, other, own)
        return jnp.concatenate([low, high], axis=-1)

    def own_half(rows):
        return lax.dynamic_slice_in_dim(rows, half * own_cols, own_cols, rows.ndim - 1)

    def half_sum(part):
        sent = lax.dynamic_slice_in_dim(part, (1 - half) * own_cols, own_cols, part.ndim - 1)
        return own_half(part) + other_half(sent.astype(jnp.bfloat16)).astype(jnp.float32)

    full_out = both_halves(out_grad)
    input_f = block_input.astype(jnp.float32)
    normalized_first, norm_one_back = jax.vjp(layer_norm, input_f, gains_all[0], biases_all[0])
    preceding_first = from_behind(normalized_first[:, -1, :].astype(jnp.bfloat16), "seq", 1).astype(
        jnp.float32
    )
    mixed_input, mix_back = jax.vjp(
        token_mixture,
        normalized_first,
        preceding_first,
        shift_coefficient,
        lowrank_down,
        lowrank_up,
        decay_projection,
    )
    log_rows, decay_back = jax.vjp(
        decay_rates,
        mixed_input[4],
        decay_lift.reshape(decay_lift.shape[0], head_cols),
        decay_base.reshape(head_cols),
    )
    stacked = jnp.stack(mixed_input[:4]).astype(jnp.bfloat16).reshape(4, tokens, feature_columns)
    projected = jnp.einsum("ntd,nde->nte", stacked, projections, preferred_element_type=jnp.float32)
    acceptance_entries_list = split_heads(projected[0])
    lookup_array_entries = split_heads(projected[1])
    payload_array_entries = split_heads(projected[2])
    gate_pre = projected[3].reshape(seq_count, length, head_cols)
    gate_act = jax.nn.silu(gate_pre)
    logarithm_heads = split_heads(log_rows)
    (decay_prod, carried), totals_back = jax.vjp(
        span_totals, lookup_array_entries, payload_array_entries, logarithm_heads
    )
    decay_heads = jnp.exp(-jnp.exp(logarithm_heads))
    stat_least = jnp.min(decay_heads, axis=(2, 3))
    stat_most = jnp.max(decay_heads, axis=(2, 3))
    small = jnp.concatenate(
        [decay_prod, stat_least[..., None], stat_most[..., None]], axis=-1
    )
    all_small = lax.all_gather(small, "seq")
    all_decay = all_small[..., :head_size]
    total_least = jnp.min(all_small[..., head_size], axis=0)
    total_most = jnp.max(all_small[..., head_size + 1], axis=0)
    all_carried = lax.all_gather(carried.astype(jnp.bfloat16), "seq")
    ahead = [jnp.ones_like(decay_prod)]
    for k in range(blocks):
        ahead.append(ahead[-1] * all_decay[k])
    prefix_decay = jnp.ones_like(decay_prod)
    prefix_state = jnp.zeros_like(carried)
    for k in range(blocks - 1):
        reached = k < place
        prefix_decay = jnp.where(reached, prefix_decay * all_decay[k], prefix_decay)
        prefix_state = jnp.where(
            reached,
            all_decay[k][..., None] * prefix_state + all_carried[k].astype(jnp.float32),
            prefix_state,
        )
    arriving_carry_tensor = prefix_decay[..., None] * initial_state + prefix_state
    wkv, output_back = jax.vjp(
        segment_output,
        acceptance_entries_list,
        lookup_array_entries,
        payload_array_entries,
        logarithm_heads,
        reward_array_entries,
        arriving_carry_tensor,
    )
    normed_heads, group_back = jax.vjp(group_norm, wkv, group_scale, group_shift)
    normed_rows = join_heads(normed_heads)
    mixer_in = (normed_rows * gate_act).astype(jnp.bfloat16)
    mixer_part = jnp.einsum("std,de->ste", mixer_in, out_proj, preferred_element_type=jnp.float32)
    residual = (
        input_f + mixer_part + other_half(mixer_part.astype(jnp.bfloat16)).astype(jnp.float32)
    )
    normed_two, norm_two_back = jax.vjp(layer_norm, residual, gains_all[1], biases_all[1])
    prev_two = from_behind(normed_two[:, -1, :].astype(jnp.bfloat16), "seq", 1).astype(jnp.float32)
    (chan_key, chan_recept), chan_back = jax.vjp(
        channel_mix, normed_two, prev_two, shift_coefficient
    )
    chan_key_b = chan_key.astype(jnp.bfloat16)
    chan_recept_b = chan_recept.astype(jnp.bfloat16)
    key_pre = jnp.einsum("std,df->stf", chan_key_b, channel_key, preferred_element_type=jnp.float32)
    hidden = jnp.square(jnp.maximum(key_pre, 0.0)).astype(jnp.bfloat16)
    value_part = jnp.einsum(
        "stf,fd->std", hidden, channel_value, preferred_element_type=jnp.float32
    )
    recept_pre = jnp.einsum(
        "std,de->ste", chan_recept_b, channel_recept, preferred_element_type=jnp.float32
    )
    kv_rows = half_sum(value_part)
    gate_chan = jax.nn.sigmoid(recept_pre)
    output = (own_half(residual) + gate_chan * kv_rows).astype(jnp.bfloat16)
    grad_out = out_grad.astype(jnp.float32)
    grad_value = (grad_out * gate_chan).astype(jnp.bfloat16)
    grad_recept = (grad_out * kv_rows * gate_chan * (1.0 - gate_chan)).astype(jnp.bfloat16)
    full_value = both_halves(grad_value)
    grad_hidden = jnp.einsum(
        "std,fd->stf", full_value, channel_value, preferred_element_type=jnp.float32
    )
    grad_key = (grad_hidden * 2.0 * jnp.maximum(key_pre, 0.0)).astype(jnp.bfloat16)
    part_key = jnp.einsum("stf,df->std", grad_key, channel_key, preferred_element_type=jnp.float32)
    part_recept = jnp.einsum(
        "ste,de->std", grad_recept, channel_recept, preferred_element_type=jnp.float32
    )
    part_normed_two, part_prev_two, grad_coeffs_chan = chan_back((part_key, part_recept))
    from_next_two = from_behind(for_sending(part_prev_two), "seq", -1).astype(jnp.float32)
    part_normed_two = part_normed_two.at[:, -1, :].add(from_next_two)
    grad_normed_two = part_normed_two + other_half(part_normed_two.astype(jnp.bfloat16)).astype(
        jnp.float32
    )
    grad_residual, grad_gain_two, grad_bias_two = norm_two_back(grad_normed_two)
    grad_residual = grad_residual + full_out.astype(jnp.float32)
    grad_branch = grad_residual.astype(jnp.bfloat16)
    out_weight_grad = jnp.einsum(
        "std,ste->de", mixer_in, grad_branch, preferred_element_type=jnp.float32
    )
    grad_mixer = jnp.einsum(
        "ste,de->std", grad_branch, out_proj, preferred_element_type=jnp.float32
    )
    grad_normed_rows = grad_mixer * gate_act
    gate_sig = jax.nn.sigmoid(gate_pre)
    grad_gate = grad_mixer * normed_rows * gate_sig * (1.0 + gate_pre * (1.0 - gate_sig))
    grad_wkv, group_gain_grad, group_bias_grad = group_back(split_heads(grad_normed_rows))
    (
        receptance_gradient,
        key_gradient_output,
        value_gradient_output,
        logarithm_gradient_output,
        reward_cotangent_term,
        incoming_gradient,
    ) = output_back(grad_wkv)
    all_incoming = lax.all_gather(incoming_gradient.astype(jnp.bfloat16), "seq")
    later_grad = jnp.zeros_like(incoming_gradient)
    state_grad = jnp.zeros_like(incoming_gradient)
    for k in range(blocks - 1, -1, -1):
        term = all_incoming[k].astype(jnp.float32)
        state_grad = state_grad + ahead[k][..., None] * term
        later_grad = jnp.where(k > place, all_decay[k][..., None] * later_grad + term, later_grad)
    grad_decay_prod = jnp.sum(later_grad * arriving_carry_tensor, axis=-1)
    grad_keys_tot, grad_values_tot, grad_logs_tot = totals_back((grad_decay_prod, later_grad))
    grad_proj = jnp.stack(
        [
            join_heads(receptance_gradient).reshape(tokens, head_cols),
            join_heads(key_gradient_output + grad_keys_tot).reshape(tokens, head_cols),
            join_heads(value_gradient_output + grad_values_tot).reshape(tokens, head_cols),
            grad_gate.reshape(tokens, head_cols),
        ]
    ).astype(jnp.bfloat16)
    proj_grad = jnp.einsum("ntd,nte->nde", stacked, grad_proj, preferred_element_type=jnp.float32)
    part_inputs = jnp.einsum(
        "nte,nde->ntd", grad_proj, projections, preferred_element_type=jnp.float32
    )
    part_hdec, lift_grad, base_grad = decay_back(join_heads(logarithm_gradient_output + grad_logs_tot))
    part_normed_one, part_prev_one, grad_coeffs_time, down_grad, up_grad, decay_proj_grad = mix_back(
        (
            part_inputs[0].reshape(seq_count, length, feature_columns),
            part_inputs[1].reshape(seq_count, length, feature_columns),
            part_inputs[2].reshape(seq_count, length, feature_columns),
            part_inputs[3].reshape(seq_count, length, feature_columns),
            part_hdec,
        )
    )
    from_next_one = from_behind(for_sending(part_prev_one), "seq", -1).astype(jnp.float32)
    part_normed_one = part_normed_one.at[:, -1, :].add(from_next_one)
    part_block, grad_gain_one, grad_bias_one = norm_one_back(part_normed_one)
    input_grad = own_half(grad_residual) + half_sum(part_block)
    value_weight_grad = jnp.einsum(
        "stf,std->fd", hidden, full_value, preferred_element_type=jnp.float32
    )
    key_weight_grad = jnp.einsum(
        "std,stf->df", chan_key_b, grad_key, preferred_element_type=jnp.float32
    )
    recept_weight_grad = jnp.einsum(
        "std,ste->de", chan_recept_b, grad_recept, preferred_element_type=jnp.float32
    )
    small_sums = packed_scatter(
        [
            (jnp.stack([grad_gain_one, 0.5 * grad_gain_two]), 1),
            (jnp.stack([grad_bias_one, 0.5 * grad_bias_two]), 1),
            (grad_coeffs_time + grad_coeffs_chan, 1),
            (down_grad, 0),
            (up_grad, 1),
            (decay_proj_grad, 0),
            (lift_grad.reshape(decay_lift.shape), 2),
            (base_grad.reshape(decay_base.shape), 1),
            (reward_cotangent_term, 1),
            (group_gain_grad, 1),
            (group_bias_grad, 1),
        ],
        gathered,
    )
    rest = [part + other_half(part) for part in small_sums[:6]] + small_sums[6:]
    proj_sum = big_scatter(proj_grad, 1)
    out_sum = big_scatter(out_weight_grad, 1)
    key_sum = big_scatter(key_weight_grad, 0)
    value_sum_rows = big_scatter(value_weight_grad, 1)
    recept_sum = big_scatter(recept_weight_grad, 0)
    coeff_rows = jnp.concatenate([rest[2][:1], rest[2][2:]], axis=0)
    decay_row = rest[2][1:2]
    return (
        output,
        input_grad,
        state_grad,
        rest[0],
        rest[1],
        coeff_rows,
        decay_row,
        rest[3],
        rest[4],
        rest[5],
        rest[6],
        proj_sum,
        out_sum,
        rest[7],
        rest[8],
        rest[9],
        rest[10],
        key_sum,
        value_sum_rows,
        recept_sum,
        total_least,
        total_most,
    )


def solution(mesh):
    return jax.shard_map(
        per_device,
        mesh=mesh,
        in_specs=(
            P("dp", "seq", None),
            P("dp", "tp", None, None),
            P(None, ("dp", "seq")),
            P(None, ("dp", "seq")),
            P(None, ("dp", "seq")),
            P(("dp", "seq"), None),
            P(None, ("dp", "seq")),
            P(("dp", "seq"), None),
            P(None, "tp", ("dp", "seq")),
            P(None, ("dp", "seq"), "tp"),
            P("tp", ("dp", "seq")),
            P("tp", ("dp", "seq")),
            P("tp", ("dp", "seq")),
            P("tp", ("dp", "seq")),
            P("tp", ("dp", "seq")),
            P(None, "tp"),
            P("tp", None),
            P(None, "tp"),
            P("dp", "seq", "tp"),
        ),
        out_specs=(
            P("dp", "seq", "tp"),
            P("dp", "seq", "tp"),
            P("dp", "tp", None, None),
            P(None, ("dp", "seq")),
            P(None, ("dp", "seq")),
            P(None, ("dp", "seq")),
            P(None, ("dp", "seq")),
            P(("dp", "seq"), None),
            P(None, ("dp", "seq")),
            P(("dp", "seq"), None),
            P(None, "tp", ("dp", "seq")),
            P(None, ("dp", "seq"), "tp"),
            P("tp", ("dp", "seq")),
            P("tp", ("dp", "seq")),
            P("tp", ("dp", "seq")),
            P("tp", ("dp", "seq")),
            P("tp", ("dp", "seq")),
            P(("dp", "seq"), "tp"),
            P("tp", ("dp", "seq")),
            P(("dp", "seq"), "tp"),
            P("dp", "tp"),
            P("dp", "tp"),
        ),
        check_vma=False,
    )
```

time: 3090 us -> 1660 us (0.54)
  waiting for transfers between devices: 1920 us -> 766 us
  blocking collectives: 354 us -> 16.6 us
  local copies, waits for them, and re-layouts: 171 us -> 274 us
  other arithmetic: 244 us -> 195 us
    reduce_scatter x11 -> x4, waiting for transfers between devices: 1330 us -> 329 us  [the longest x3 329 us: big_scatter(): lax.psum_scatter(whole.astype(jnp.bfloat16), ('dp', 'seq'), scatter_dimen...]
    psum x3 -> x0, waiting for transfers between devices: 405 us -> none  [the longest x1 191 us: per_device(): lax.psum(part_inputs.astype(jnp.bfloat16), 'tp').astype(jnp.float32)]
    all_gather x15 -> x1, blocking collectives: 293 us -> 16.6 us  [per_device(): all_small = lax.all_gather(small, 'seq')]
    ppermute x0 -> x12, waiting for transfers between devices: none -> 174 us  [other_half(): return lax.ppermute(block, 'tp', [(0, 1), (1, 0)])]
    unnamed x27 -> x13, waiting for transfers between devices: 3.77 us -> 96.3 us
    unnamed x1 -> x0, blocking collectives: 61 us -> none
    select_n x24 -> x3, other arithmetic: 53.3 us -> 1.53 us  [the longest x2 1.5 us: both_halves(): low = jnp.where(half == 0, own, other)]
    unnamed x285 -> x417, local copies, waits for them, and re-layouts: 34.7 us -> 83.3 us
  transfers between devices with their start and end apart: 29 -> 27, of which waited for: 20 -> 16; matrix products, arithmetic and copies ran while one was open for 18% -> 36% of each run, Pallas kernels for 0% -> 0%
where the time goes in v1:
time: 1660 us; the launch traced here: 1650 us
  waiting for transfers between devices  766 us (46%)
  matrix products  363 us (22%)
  local copies, waits for them, and re-layouts  274 us (17%)
  other arithmetic  195 us (12%)
  starting transfers between devices  21.8 us (1%)
  blocking collectives  16.6 us (1%)
  between operations  16.6 us (1%)
    reduce_scatter x3, waiting for transfers between devices, big_scatter(): lax.psum_scatter(whole.astype(jnp.bfloat16), ('dp', 'seq'), scatter_dimen...  329 us
    ppermute x12, waiting for transfers between devices, other_half(): return lax.ppermute(block, 'tp', [(0, 1), (1, 0)])  174 us
    unnamed x13, waiting for transfers between devices  96.3 us
    unnamed x417, local copies, waits for them, and re-layouts  83.3 us
    dot_general x9, matrix products, dense_single_float(): jnp.einsum('...i,ij->...j', left, right, precision=PRECISION_TOP, preferr...  63.6 us
    all_gather x1, waiting for transfers between devices, per_device(): lax.all_gather(proj_weights, ('dp', 'seq'), axis=1, tiled=True)  53.6 us
    all_gather x1, waiting for transfers between devices, packed_gather(): everything = lax.all_gather(flat, ('dp', 'seq'))  46.5 us
    dot_general x3, matrix products, token_mixture(): jnp.einsum('stri,rid->rstd', hidden_mixture.reshape(seq_count, length, 5,...  38.8 us
  transfers between devices with their start and end apart: 27, of which 16 were waited for; matrix products, arithmetic and copies ran while one was open for 36% of the time, Pallas kernels for 0%

profile of v1, /device:TPU:0, one launch (start us, length us, event | category | flops | bytes accessed | tf_op | source)
XLA Modules:
  0.0 1653.2 jit_solution(595480984506222102)
XLA Ops:
  22.4 46.5 %all-gather.19.cloned.1.call-done = bf16[16,1,55040]{2,1,0:T(2,128)(2,1)} async-done(((bf16[1,1,55040]{2,1,0:T(2,128)(2,1)}), bf16[16,1,55040]{2,1,0:T(2,128)(2,1)}) %all-gather.19.cloned.1.call-update) | async-done | bytes 1761296 | tf_op jit(solution)/shard_map/all_gather | solution.py:141
  104.2 8.8 fusion.167
  131.2 12.4 add_convert_fusion.5
  143.6 53.6 %all-gather.11.cloned.1.call-done = bf16[4,2048,1024]{2,1,0:T(8,128)(2,1)} async-done(((bf16[4,128,1024]{2,1,0:T(8,128)(2,1)}), bf16[4,2048,1024]{2,1,0:T(8,128)(2,1)}) %all-gather.11.cloned.1.call-update) | async-done | bytes 16777232 | tf_op jit(solution)/shard_map/all_gather | solution.py:239
  197.2 16.6 %fusion.151 = f32[4,512,1024]{2,1,0:T(8,128)S(1)} fusion(bf16[4,2048,1024]{2,1,0:T(8,128)(2,1)} %all-gather.11.cloned.1.call-done, bf16[1,512,2048]{2,1,0:T(8,128)(2,1)} %bitcast.589, bf16[1,512,2048]{2,1,0:T(8,128)(2,1)} %bitcast.591, bf16[1,512,2048]{2,1,0:T(8,128)(2,1)} %bitcast.593, bf16[1,512,2048]{2,1,0:T(8,128)(2,1)} %bitcast.587), kind=kOutput, calls=%fused_computation.267 | convolution fusion | flops 8602517504 | bytes 33554432 | tf_op jit(solution)/shard_map/ntd,nde->nte/dot_general | solution.py:288
  245.3 11.7 exponential_reduce_fusion.1
  257.8 8.8 fusion.36
  292.3 16.6 %all-gather.1 = f32[32,16,66]{2,1,0:T(8,128)S(1)} all-gather(f32[4,16,66]{2,1,0:T(8,128)S(1)} %pad_maximum_fusion.9), channel_id=3, replica_groups=mesh['dp'=2,'seq'=8,'tp'=2] {'seq'}, dimensions={0}, use_global_device_ids=true | all-gather | bytes 152064 | tf_op jit(solution)/shard_map/all_gather | solution.py:304
  310.3 11.0 fusion.238
  321.3 38.5 %all-gather.15.cloned.1.call-done = bf16[32,16,64,64]{3,2,1,0:T(8,128)(2,1)} async-done(((bf16[4,16,64,64]{3,2,1,0:T(8,128)(2,1)}), bf16[32,16,64,64]{3,2,1,0:T(8,128)(2,1)}) %all-gather.15.cloned.1.call-update) | async-done | bytes 4194320 | tf_op jit(solution)/shard_map/all_gather | solution.py:308
  359.9 9.1 fusion.113
  374.0 8.3 fusion.222
  391.2 22.4 %all-gather.13.cloned.1.call-done = bf16[1024,2048]{1,0:T(8,128)(2,1)} async-done(((bf16[1024,128]{1,0:T(8,128)(2,1)}), bf16[1024,2048]{1,0:T(8,128)(2,1)}) %all-gather.13.cloned.1.call-update) | async-done | bytes 4194320 | tf_op jit(solution)/shard_map/all_gather | solution.py:240
  419.7 46.3 %collective-permute-done.1 = bf16[4,128,2048]{2,1,0:T(8,128)(2,1)S(1)} collective-permute-done((bf16[4,128,2048]{2,1,0:T(8,128)(2,1)S(1)}, bf16[4,128,2048]{2,1,0:T(8,128)(2,1)S(1)}, u32[]{:S(2)}, u32[]{:S(2)}) %collective-permute-start.1) | collective-permute-done | bytes 2097184 | tf_op jit(solution)/shard_map/ppermute | solution.py:176
  479.8 13.0 fusion.8
  492.9 10.1 fusion.4
  507.7 24.3 %collective-permute-done.3 = bf16[4,128,1024]{2,1,0:T(8,128)(2,1)} collective-permute-done((bf16[4,128,1024]{2,1,0:T(8,128)(2,1)}, bf16[4,128,1024]{2,1,0:T(8,128)(2,1)}, u32[]{:S(2)}, u32[]{:S(2)}) %collective-permute-start.3) | collective-permute-done | bytes 1048608 | tf_op jit(solution)/shard_map/ppermute | solution.py:176
  531.9 8.9 fusion.68
  542.1 23.6 %collective-permute-done.4 = bf16[4,128,1024]{2,1,0:T(8,128)(2,1)S(1)} collective-permute-done((bf16[4,128,1024]{2,1,0:T(8,128)(2,1)}, bf16[4,128,1024]{2,1,0:T(8,128)(2,1)S(1)}, u32[]{:S(2)}, u32[]{:S(2)}) %collective-permute-start.4) | collective-permute-done | bytes 1048608 | tf_op jit(solution)/shard_map/ppermute | solution.py:176
  568.3 27.0 %multiply_convert_fusion = bf16[4,128,3584]{2,1,0:T(8,128)(2,1)} fusion(f32[4,128,3584]{2,1,0:T(8,128)} %fusion.8, bf16[3584,2048]{1,0:T(8,128)(2,1)} %param.39, bf16[4,128,1024]{2,1,0:T(8,128)(2,1)S(1)} %get-tuple-element.289, bf16[4,128,1024]{2,1,0:T(8,128)(2,1)S(1)} %get-tuple-element.288), kind=kOutput, calls=%fused_computation.17 | convolution fusion | flops 7527727104 | bytes 27787264 | tf_op jit(solution)/shard_map/std,fd->stf/dot_general | solution.py:361
  595.3 12.3 fusion.6
  625.9 68.8 %collective-permute-done.7 = bf16[4,128,1024]{2,1,0:T(8,128)(2,1)S(1)} collective-permute-done((bf16[4,128,1024]{2,1,0:T(8,128)(2,1)S(1)}, bf16[4,128,1024]{2,1,0:T(8,128)(2,1)S(1)}, u32[]{:S(2)}, u32[]{:S(2)}) %collective-permute-start.7) | collective-permute-done | bytes 1048608 | tf_op jit(solution)/shard_map/ppermute | solution.py:176
  736.1 8.5 fusion.101
  746.7 9.7 fusion.55
  800.5 9.4 multiply_reduce_fusion.7
  819.0 9.6 fusion.94
  832.6 11.3 fusion.215
  848.9 9.6 fusion.50
  858.5 12.5 fusion.236
  878.0 11.9 convolution_bitcast_fusion.1
  918.5 17.1 %fusion.165 = f32[4,512,2048]{2,1,0:T(8,128)} fusion(bf16[4,2048,1024]{2,1,0:T(8,128)(2,1)} %all-gather.11.cloned.1.call-done, bf16[1,512,1024]{2,1,0:T(8,128)(2,1)} %bitcast.688, bf16[1,512,1024]{2,1,0:T(8,128)(2,1)} %reshape.892, bf16[1,512,1024]{2,1,0:T(8,128)(2,1)S(1)} %reshape.891, bf16[1,512,1024]{2,1,0:T(8,128)(2,1)} %reshape.890), kind=kOutput, calls=%fused_computation.287 | convolution fusion | flops 8596226048 | bytes 37748736 | tf_op jit(solution)/shard_map/nte,nde->ntd/dot_general | solution.py:414
  935.6 13.2 fusion.225
  948.8 15.5 multiply_bitcast_fusion.4
  964.3 15.6 convolution_bitcast_fusion.2
  980.0 14.4 fusion
  995.3 20.7 %multiply_reduce_fusion.14 = (f32[2048]{0:T(1024)S(1)}, f32[2048]{0:T(1024)S(1)}, f32[2048]{0:T(1024)S(1)}, f32[2048]{0:T(1024)S(1)}, f32[2048]{0:T(1024)S(1)}, ...) fusion(f32[4,128,2048]{2,1,0:T(8,128)} %copy-done.4, f32[4,128,2048]{2,1,0:T(8,128)} %bitcast.546, ...), kind=kOutput, calls=%fused_computation.253 | convolution fusion | flops 2042613760 | bytes 55607296 | tf_op jit(solution)/shard_map/transpose(jvp(...i,ij->...j))/dot_general | solution.py:26
  1016.0 11.0 convolution_bitcast_fusion
  1032.1 10.9 pad_add_fusion.1
  1087.2 13.7 bitcast_convert_fusion
  1101.0 19.0 %copy.797 = bf16[3584,2048]{0,1:T(8,128)(2,1)} copy(bf16[3584,2048]{1,0:T(8,128)(2,1)} %bitcast_convert_fusion) | data formatting | bytes 29360128
  1120.0 13.2 bitcast_convert_fusion.1
  1134.5 16.1 convolution_convert_fusion
  1162.1 11.3 convert_add_fusion.4
  1173.5 8.4 collective-permute-done.9
  1192.7 9.1 slice.421
  1214.2 95.0 %reduce-scatter.21.cloned.1.call-done = bf16[128,3584]{1,0:T(8,128)(2,1)} async-done(((bf16[2048,3584]{1,0:T(8,128)(2,1)}), bf16[128,3584]{1,0:T(8,128)(2,1)}) %reduce-scatter.21.cloned.1.call-update) | async-done | bytes 917520
  1312.1 149.8 %reduce-scatter.15.cloned.1.call-done = bf16[128,3584]{1,0:T(8,128)(2,1)} async-done(((bf16[2048,3584]{1,0:T(8,128)(2,1)}), bf16[128,3584]{1,0:T(8,128)(2,1)}) %reduce-scatter.15.cloned.1.call-update) | async-done | bytes 917520 | tf_op jit(solution)/shard_map/reduce_scatter | solution.py:180
  1464.5 179.2 %reduce-scatter.13.cloned.1.call-done = bf16[4,128,1024]{2,1,0:T(8,128)(2,1)} async-done(((bf16[4,2048,1024]{2,1,0:T(8,128)(2,1)}), bf16[4,128,1024]{2,1,0:T(8,128)(2,1)}) %reduce-scatter.13.cloned.1.call-update) | async-done | bytes 1048592 | tf_op jit(solution)/shard_map/reduce_scatter | solution.py:180
  (675 shorter events, 422.5 us)
Async XLA Ops:
  7.2 61.7 %all-gather.19.cloned.1.call-start = ((), (), s32[]{:S(2)}) async-start(), calls=%async_computation.14 | async-start | bytes 3742720 | tf_op jit(solution)/shard_map/all_gather | solution.py:141
  18.9 178.3 %all-gather.11.cloned.1.call-start = ((), (), s32[]{:S(2)}) async-start(), calls=%async_computation.6 | async-start | bytes 17825792 | tf_op jit(solution)/shard_map/all_gather | solution.py:239
  19.7 340.2 %all-gather.15.cloned.1.call-start = ((), (), s32[]{:S(2)}) async-start(), calls=%async_computation.12 | async-start | bytes 9437184 | tf_op jit(solution)/shard_map/all_gather | solution.py:308
  21.7 53.7 %copy-start.143 = (f32[4,128]{1,0:T(4,128)}, f32[4,128]{1,0:T(4,128)S(1)}, u32[]{:S(2)}) copy-start(f32[4,128]{1,0:T(4,128)S(1)} %broadcast_multiply_fusion.5) | copy-start | bytes 6148
  22.4 48.7 %copy-start.182 = (f32[4,128]{1,0:T(4,128)}, f32[4,128]{1,0:T(4,128)S(1)}, u32[]{:S(2)}) copy-start(f32[4,128]{1,0:T(4,128)S(1)} %fusion.20) | copy-start | bytes 6148
  22.4 52.9 %copy-start.153 = (f32[4,128]{1,0:T(4,128)}, f32[4,128]{1,0:T(4,128)S(1)}, u32[]{:S(2)}) copy-start(f32[4,128]{1,0:T(4,128)S(1)} %fusion.184) | copy-start | bytes 6148
  73.9 57.3 %copy-start.95 = (f32[1,16,128]{2,0,1:T(1,128)}, f32[1,16,128]{2,0,1:T(1,128)S(1)}, u32[]{:S(2)}) copy-start(f32[1,16,128]{2,0,1:T(1,128)S(1)} %get-tuple-element.328) | copy-start | bytes 24580
  78.0 18.1 %collective-permute-start = (bf16[4,2048]{1,0:T(4,128)(2,1)}, bf16[4,2048]{1,0:T(4,128)(2,1)}, u32[]{:S(2)}, u32[]{:S(2)}) collective-permute-start(bf16[4,2048]{1,0:T(4,128)(2,1)} %bitcast.537), channel_id=1, source_target_pairs={{0,2},{2,4},{4,6},{6,8},{8,10},{10,12},{12,14},{1,3},{3,5},{5,7},{... | collective-permute-start | bytes 49160 | tf_op jit(solution)/shard_map/ppermute | solution.py:14
  81.4 31.6 %copy-start.104 = (f32[1,16,128]{2,0,1:T(1,128)}, f32[1,16,128]{2,0,1:T(1,128)S(1)}, u32[]{:S(2)}) copy-start(f32[1,16,128]{2,0,1:T(1,128)S(1)} %get-tuple-element.317) | copy-start | bytes 24580
  86.1 27.0 %copy-start.56 = (bf16[2048,64]{1,0:T(8,128)(2,1)}, bf16[2048,64]{1,0:T(8,128)(2,1)S(1)}, u32[]{:S(2)}) copy-start(bf16[2048,64]{1,0:T(8,128)(2,1)S(1)} %reshape_reshape.17) | copy-start | bytes 786436
  277.5 136.2 %all-gather.13.cloned.1.call-start = ((), (), s32[]{:S(2)}) async-start(), calls=%async_computation.7 | async-start | bytes 4456448 | tf_op jit(solution)/shard_map/all_gather | solution.py:240
  278.0 522.5 %all-gather.17.cloned.1.call-start = ((), (), s32[]{:S(2)}) async-start(), calls=%async_computation.13 | async-start | bytes 9437184 | tf_op jit(solution)/shard_map/all_gather | solution.py:396
  278.1 95.8 %copy-start.102 = (pred[128,128]{1,0:T(8,128)(4,1)}, pred[128,128]{1,0:T(8,128)(4,1)S(1)}, u32[]{:S(2)}) copy-start(pred[128,128]{1,0:T(8,128)(4,1)S(1)} %iota_compare_fusion) | copy-start | bytes 49156
  278.6 104.2 %copy-start.141 = (f32[16,64]{1,0:T(8,128)}, f32[16,64]{1,0:T(8,128)S(1)}, u32[]{:S(2)}) copy-start(f32[16,64]{1,0:T(8,128)S(1)} %copy.693) | copy-start | bytes 12292
  287.4 95.4 %copy-start.108 = (f32[4,128,16]{1,2,0:T(8,128)}, f32[4,128,16]{1,2,0:T(8,128)S(1)}, u32[]{:S(2)}) copy-start(f32[4,128,16]{1,2,0:T(8,128)S(1)} %copy.688) | copy-start | bytes 98308
  310.3 49.6 %copy-start.112 = (f32[4,16,64]{2,1,0:T(8,128)}, f32[4,16,64]{2,1,0:T(8,128)S(1)}, u32[]{:S(2)}) copy-start(f32[4,16,64]{2,1,0:T(8,128)S(1)} %get-tuple-element.303) | copy-start | bytes 49156
  310.3 49.6 %copy-start.114 = (f32[4,16,64]{2,1,0:T(8,128)}, f32[4,16,64]{2,1,0:T(8,128)S(1)}, u32[]{:S(2)}) copy-start(f32[4,16,64]{2,1,0:T(8,128)S(1)} %get-tuple-element.304) | copy-start | bytes 49156
  310.3 49.6 %copy-start.116 = (f32[4,16,64]{2,1,0:T(8,128)}, f32[4,16,64]{2,1,0:T(8,128)S(1)}, u32[]{:S(2)}) copy-start(f32[4,16,64]{2,1,0:T(8,128)S(1)} %get-tuple-element.305) | copy-start | bytes 49156
  310.3 49.6 %copy-start.118 = (f32[4,16,64]{2,1,0:T(8,128)}, f32[4,16,64]{2,1,0:T(8,128)S(1)}, u32[]{:S(2)}) copy-start(f32[4,16,64]{2,1,0:T(8,128)S(1)} %get-tuple-element.306) | copy-start | bytes 49156
  310.3 49.6 %copy-start.120 = (f32[4,16,64]{2,1,0:T(8,128)}, f32[4,16,64]{2,1,0:T(8,128)S(1)}, u32[]{:S(2)}) copy-start(f32[4,16,64]{2,1,0:T(8,128)S(1)} %get-tuple-element.307) | copy-start | bytes 49156
  310.3 49.6 %copy-start.122 = (f32[4,16,64]{2,1,0:T(8,128)}, f32[4,16,64]{2,1,0:T(8,128)S(1)}, u32[]{:S(2)}) copy-start(f32[4,16,64]{2,1,0:T(8,128)S(1)} %get-tuple-element.308) | copy-start | bytes 49156
  391.2 26.9 %copy-start.84 = (bf16[4,128,1024]{2,1,0:T(8,128)(2,1)}, bf16[4,128,1024]{2,1,0:T(8,128)(2,1)S(1)}, u32[]{:S(2)}) copy-start(bf16[4,128,1024]{2,1,0:T(8,128)(2,1)S(1)} %multiply_convert_fusion.3) | copy-start | bytes 3145732
  418.2 47.9 %collective-permute-start.1 = (bf16[4,128,2048]{2,1,0:T(8,128)(2,1)S(1)}, bf16[4,128,2048]{2,1,0:T(8,128)(2,1)S(1)}, u32[]{:S(2)}, u32[]{:S(2)}) collective-permute-start(bf16[4,128,2048]{2,1,0:T(8,128)(2,1)S(1)} %get-tuple-element.335), channel_id=1, source_target_pairs={{0,1},{1,0},{2,3},{3,2},{4,5},{5,4},{6,7},{7,6},{8,9},{9,8},{10,11... | collective-permute-start | bytes 6291464 | tf_op jit(solution)/shard_map/ppermute | solution.py:176
  471.4 2.2 collective-permute-start.2
  478.5 53.4 %copy-start.72 = (bf16[4,128,2048]{2,1,0:T(8,128)(2,1)}, bf16[4,128,2048]{2,1,0:T(8,128)(2,1)S(1)}, u32[]{:S(2)}) copy-start(bf16[4,128,2048]{2,1,0:T(8,128)(2,1)S(1)} %get-tuple-element.254) | copy-start | bytes 6291460
  492.9 39.0 %copy-start.80 = (bf16[4,128,1024]{2,1,0:T(8,128)(2,1)S(1)}, bf16[4,128,1024]{2,1,0:T(8,128)(2,1)}, u32[]{:S(2)}) copy-start(bf16[4,128,1024]{2,1,0:T(8,128)(2,1)} %param.41) | copy-start | bytes 3145732
  506.2 25.7 %collective-permute-start.3 = (bf16[4,128,1024]{2,1,0:T(8,128)(2,1)}, bf16[4,128,1024]{2,1,0:T(8,128)(2,1)}, u32[]{:S(2)}, u32[]{:S(2)}) collective-permute-start(bf16[4,128,1024]{2,1,0:T(8,128)(2,1)} %dynamic-slice_convert_fusion.1), channel_id=1, source_target_pairs={{0,1},{1,0},{2,3},{3,2},{4,5},{5,4},{6,7},{7,6},{8,9},{9,8},{10,11... | collective-permute-start | bytes 3145736 | tf_op jit(solution)/shard_map/ppermute | solution.py:176
  540.8 24.8 %collective-permute-start.4 = (bf16[4,128,1024]{2,1,0:T(8,128)(2,1)}, bf16[4,128,1024]{2,1,0:T(8,128)(2,1)S(1)}, u32[]{:S(2)}, u32[]{:S(2)}) collective-permute-start(bf16[4,128,1024]{2,1,0:T(8,128)(2,1)} %get-tuple-element.285), channel_id=1, source_target_pairs={{0,1},{1,0},{2,3},{3,2},{4,5},{5,4},{6,7},{7,6},{8,9},{9,8},{10,11... | collective-permute-start | bytes 3145736 | tf_op jit(solution)/shard_map/ppermute | solution.py:176
  614.5 3.1 collective-permute-start.5
  621.2 73.7 %copy-start.91 = (f32[4,16,128]{2,1,0:T(8,128)S(1)}, f32[4,16,128]{2,1,0:T(8,128)}, u32[]{:S(2)}) copy-start(f32[4,16,128]{2,1,0:T(8,128)} %copy-done.90) | copy-start | bytes 98308
  621.2 73.8 %copy-start.3 = (f32[4,128,2048]{2,1,0:T(8,128)S(1)}, f32[4,128,2048]{2,1,0:T(8,128)}, u32[]{:S(2)}) copy-start(f32[4,128,2048]{2,1,0:T(8,128)} %copy-done.2) | copy-start | bytes 12582916
  621.2 73.8 %copy-start.11 = (f32[4,128,2048]{2,1,0:T(8,128)S(1)}, f32[4,128,2048]{2,1,0:T(8,128)}, u32[]{:S(2)}) copy-start(f32[4,128,2048]{2,1,0:T(8,128)} %scatter-add.6) | copy-start | bytes 12582916
  623.8 71.1 %collective-permute-start.6 = (bf16[4,128,2048]{2,1,0:T(8,128)(2,1)S(1)}, bf16[4,128,2048]{2,1,0:T(8,128)(2,1)S(1)}, u32[]{:S(2)}, u32[]{:S(2)}) collective-permute-start(bf16[4,128,2048]{2,1,0:T(8,128)(2,1)S(1)} %convert_element_type.366), channel_id=1, source_target_pairs={{0,1},{1,0},{2,3},{3,2},{4,5},{5,4},{6,7},{7,6},{8,9},{9,8},{10,11... | collective-permute-start | bytes 6291464 | tf_op jit(solution)/shard_map/ppermute | solution.py:176
  625.2 69.6 %collective-permute-start.7 = (bf16[4,128,1024]{2,1,0:T(8,128)(2,1)S(1)}, bf16[4,128,1024]{2,1,0:T(8,128)(2,1)S(1)}, u32[]{:S(2)}, u32[]{:S(2)}) collective-permute-start(bf16[4,128,1024]{2,1,0:T(8,128)(2,1)S(1)} %copy-done.80), channel_id=1, source_target_pairs={{0,1},{1,0},{2,3},{3,2},{4,5},{5,4},{6,7},{7,6},{8,9},{9,8},{10,11... | collective-permute-start | bytes 3145736 | tf_op jit(solution)/shard_map/ppermute | solution.py:176
  719.2 439.1 %reduce-scatter.17.cloned.1.call-start = ((), (), s32[]{:S(2)}) async-start(), calls=%async_computation.11 | async-start | bytes 4456448 | tf_op jit(solution)/shard_map/reduce_scatter | solution.py:180
  724.0 436.1 %reduce-scatter.19.cloned.1.call-start = ((), (), s32[]{:S(2)}) async-start(), calls=%async_computation.15 | async-start | bytes 4456448
  795.9 387.9 %reduce-scatter.11.cloned.1.call-start = ((), (), s32[]{:S(2)}) async-start(), calls=%async_computation.8 | async-start | bytes 3760128 | tf_op jit(solution)/shard_map/reduce_scatter | solution.py:164
  1030.4 28.4 %collective-permute-start.8 = (bf16[4,2048]{1,0:T(4,128)(2,1)}, bf16[4,2048]{1,0:T(4,128)(2,1)}, u32[]{:S(2)}, u32[]{:S(2)}) collective-permute-start(bf16[4,2048]{1,0:T(4,128)(2,1)} %bitcast.539), channel_id=1, source_target_pairs={{2,0},{4,2},{6,4},{8,6},{10,8},{12,10},{14,12},{3,1},{5,3},{7,5},{... | collective-permute-start | bytes 49160 | tf_op jit(solution)/shard_map/ppermute | solution.py:14
  1087.2 222.0 %reduce-scatter.21.cloned.1.call-start = ((), (), s32[]{:S(2)}) async-start(), calls=%async_computation.16 | async-start | bytes 15597568
  1120.0 341.9 %reduce-scatter.15.cloned.1.call-start = ((), (), s32[]{:S(2)}) async-start(), calls=%async_computation.10 | async-start | bytes 15597568 | tf_op jit(solution)/shard_map/reduce_scatter | solution.py:180
  1133.3 510.4 %reduce-scatter.13.cloned.1.call-start = ((), (), s32[]{:S(2)}) async-start(), calls=%async_computation.9 | async-start | bytes 17825792 | tf_op jit(solution)/shard_map/reduce_scatter | solution.py:180
  1155.8 26.1 %collective-permute-start.9 = (bf16[4,128,1024]{2,1,0:T(8,128)(2,1)S(1)}, bf16[4,128,1024]{2,1,0:T(8,128)(2,1)S(1)}, u32[]{:S(2)}, u32[]{:S(2)}) collective-permute-start(bf16[4,128,1024]{2,1,0:T(8,128)(2,1)S(1)} %dynamic-slice_convert_fusion), channel_id=1, source_target_pairs={{0,1},{1,0},{2,3},{3,2},{4,5},{5,4},{6,7},{7,6},{8,9},{9,8},{10,11... | collective-permute-start | bytes 3145736 | tf_op jit(solution)/shard_map/ppermute | solution.py:176
  1184.6 21.9 %collective-permute-start.11 = (f32[2,128]{1,0:T(2,128)S(1)}, f32[2,128]{1,0:T(2,128)S(1)}, u32[]{:S(2)}, u32[]{:S(2)}) collective-permute-start(f32[2,128]{1,0:T(2,128)S(1)} %get-tuple-element.313), channel_id=1, source_target_pairs={{0,1},{1,0},{2,3},{3,2},{4,5},{5,4},{6,7},{7,6},{8,9},{9,8},{10,11... | collective-permute-start | bytes 3080 | tf_op jit(solution)/shard_map/ppermute | solution.py:176
  1186.2 20.4 %collective-permute-start.10 = (f32[2,128]{1,0:T(2,128)S(1)}, f32[2,128]{1,0:T(2,128)S(1)}, u32[]{:S(2)}, u32[]{:S(2)}) collective-permute-start(f32[2,128]{1,0:T(2,128)S(1)} %get-tuple-element.314), channel_id=1, source_target_pairs={{0,1},{1,0},{2,3},{3,2},{4,5},{5,4},{6,7},{7,6},{8,9},{9,8},{10,11... | collective-permute-start | bytes 3080 | tf_op jit(solution)/shard_map/ppermute | solution.py:176
  1187.3 19.8 %collective-permute-start.12 = (f32[8,128]{1,0:T(8,128)S(1)}, f32[8,128]{1,0:T(8,128)S(1)}, u32[]{:S(2)}, u32[]{:S(2)}) collective-permute-start(f32[8,128]{1,0:T(8,128)S(1)} %slice.512), channel_id=1, source_target_pairs={{0,1},{1,0},{2,3},{3,2},{4,5},{5,4},{6,7},{7,6},{8,9},{9,8},{10,11... | collective-permute-start | bytes 12296 | tf_op jit(solution)/shard_map/ppermute | solution.py:176
  1189.7 19.8 %collective-permute-start.15 = (f32[128,64]{1,0:T(8,128)S(1)}, f32[128,64]{1,0:T(8,128)S(1)}, u32[]{:S(2)}, u32[]{:S(2)}) collective-permute-start(f32[128,64]{1,0:T(8,128)S(1)} %reshape.785), channel_id=1, source_target_pairs={{0,1},{1,0},{2,3},{3,2},{4,5},{5,4},{6,7},{7,6},{8,9},{9,8},{10,11... | collective-permute-start | bytes 98312 | tf_op jit(solution)/shard_map/ppermute | solution.py:176
  1191.1 16.5 %collective-permute-start.14 = (f32[160,128]{1,0:T(8,128)S(1)}, f32[160,128]{1,0:T(8,128)S(1)}, u32[]{:S(2)}, u32[]{:S(2)}) collective-permute-start(f32[160,128]{1,0:T(8,128)S(1)} %slice.514), channel_id=1, source_target_pairs={{0,1},{1,0},{2,3},{3,2},{4,5},{5,4},{6,7},{7,6},{8,9},{9,8},{10,11... | collective-permute-start | bytes 245768 | tf_op jit(solution)/shard_map/ppermute | solution.py:176
  1208.4 5.0 collective-permute-start.13
  (169 other events, 1211.2 us)
Sparse Core Ops, SparseCore 0:
  19.0 49.8 all-gather.18
  71.1 125.9 all-gather.10
  277.6 82.2 all-gather.14
  361.8 51.7 all-gather.12
  719.3 81.1 all-gather.16
  804.2 71.1 reduce-scatter.16
  879.8 71.7 reduce-scatter.18
  1087.3 69.1 reduce-scatter.10
  1160.6 148.5 reduce-scatter.20
  1313.1 148.7 reduce-scatter.14
  1466.0 177.6 reduce-scatter.12

commit v2 on v1

--- a/solution.py
+++ b/solution.py
@@ -1,6 +1,10 @@
+import functools
+
 import jax
 import jax.numpy as jnp
 from jax import lax
+from jax.experimental import pallas as pl
+from jax.experimental.pallas import tpu as pltpu
 from jax.sharding import PartitionSpec as P
 
 PRECISION_TOP = lax.Precision.HIGHEST
@@ -176,10 +180,251 @@
     return lax.ppermute(block, "tp", [(0, 1), (1, 0)])
 
 
-def big_scatter(whole, dim):
-    return lax.psum_scatter(
-        whole.astype(jnp.bfloat16), ("dp", "seq"), scatter_dimension=dim, tiled=True
-    ).astype(jnp.float32)
+CORES = 2
+
+
+def ring_places(dp_size, seq_size):
+    per_row = seq_size // CORES
+    count = dp_size * per_row
+
+    def chip(position):
+        position = lax.rem(position + 2 * count, count)
+        row = lax.div(position, per_row)
+        column = lax.rem(position, per_row)
+        column = jnp.where(lax.rem(row, 2) == 0, column, per_row - 1 - column)
+        return row, column
+
+    def own():
+        row, column = lax.axis_index("dp"), lax.div(lax.axis_index("seq"), CORES)
+        return row * per_row + jnp.where(lax.rem(row, 2) == 0, column, per_row - 1 - column)
+
+    return count, chip, own
+
+
+def cut_rings(widths, rings):
+    each = sum(widths) // rings
+    runs, product, column = [], 0, 0
+    for _ in range(rings):
+        run, left = [], each
+        while left:
+            take = min(left, widths[product] - column)
+            run.append((product, column, take))
+            left, column = left - take, column + take
+            if column == widths[product]:
+                product, column = product + 1, 0
+        runs.append(run)
+    return runs
+
+
+def ring_kernel(dp_size, seq_size, rows, widths, runs, places, operands, *refs):
+    products = len(widths)
+    lefts = [(refs[left], lead) for left, _, lead in places]
+    rights = [(refs[right], lead) for _, right, lead in places]
+    totals, refs = refs[operands : operands + products], refs[operands + products :]
+    rings = len(runs)
+    mine, pair_out, pair_in, ring_out, ring_in = [
+        refs[k * rings : (k + 1) * rings] for k in range(5)
+    ]
+    pair_send, pair_recv, pair_free, ring_send, ring_recv, ring_free = refs[5 * rings :]
+    count, chip, own = ring_places(dp_size, seq_size)
+    position, core = own(), lax.rem(lax.axis_index("seq"), CORES)
+
+    def device(place, which):
+        row, column = chip(place)
+        return {"dp": row, "seq": column * CORES + which}
+
+    sibling = device(position, 1 - core)
+    after, before = device(position + 1, core), device(position - 1, core)
+    barrier = pltpu.get_barrier_semaphore()
+    for other in (sibling, after, before):
+        pl.semaphore_signal(barrier, inc=1, device_id=other, device_id_type=pl.DeviceIdType.MESH)
+    pl.semaphore_wait(barrier, 3)
+
+    def pair_copy(ring):
+        return pltpu.make_async_remote_copy(
+            src_ref=pair_out[ring],
+            dst_ref=pair_in[ring],
+            send_sem=pair_send.at[ring],
+            recv_sem=pair_recv.at[ring],
+            device_id=sibling,
+            device_id_type=pl.DeviceIdType.MESH,
+        )
+
+    def ring_copy(ring, slot):
+        return pltpu.make_async_remote_copy(
+            src_ref=ring_out[ring].at[slot],
+            dst_ref=ring_in[ring].at[slot],
+            send_sem=ring_send.at[ring, slot],
+            recv_sem=ring_recv.at[ring, slot],
+            device_id=after if ring % 2 == 0 else before,
+            device_id_type=pl.DeviceIdType.MESH,
+        )
+
+    def part(ring, place, which, put):
+        row, column = chip(place)
+        start = (row * seq_size + column * CORES + which) * rows
+        start = pl.multiple_of(start, rows)
+        at = 0
+        for product, first, wide in runs[ring]:
+            ref, lead = lefts[product]
+            if rows % 128 == 0:
+                left = ref[(*lead, slice(None), pl.ds(start, rows))]
+            else:
+                left = ref[(*lead, pl.ds(start, rows), slice(None))]
+            ref, lead = rights[product]
+            right = ref[(*lead, slice(None), pl.ds(first, wide))]
+            put(
+                at,
+                wide,
+                lax.dot_general(
+                    left,
+                    right,
+                    (((0 if rows % 128 == 0 else 1,), (0,)), ((), ())),
+                    preferred_element_type=jnp.float32,
+                ),
+            )
+            at += wide
+
+    def turn(step, carry):
+        slot = lax.rem(step, 2)
+        last = 1 - slot
+        for ring in range(rings):
+            place = position - 1 - step if ring % 2 == 0 else position + 1 + step
+
+            @pl.when(step >= 1)
+            def _():
+                pair_copy(ring).wait_send()
+
+            def put_out(at, wide, value):
+                pair_out[ring][:, at : at + wide] = value.astype(jnp.bfloat16)
+
+            part(ring, place, 1 - core, put_out)
+
+            @pl.when(step >= 1)
+            def _():
+                pl.semaphore_wait(pair_free.at[ring], 1)
+
+            pair_copy(ring).start()
+
+            def put_mine(at, wide, value):
+                mine[ring][:, at : at + wide] = value
+
+            part(ring, place, core, put_mine)
+        for ring in range(rings):
+            source = before if ring % 2 == 0 else after
+            pair_copy(ring).wait_recv()
+
+            @pl.when(step == 0)
+            def _():
+                ring_out[ring][slot] = (
+                    mine[ring][...] + pair_in[ring][...].astype(jnp.float32)
+                ).astype(jnp.bfloat16)
+
+            @pl.when(step >= 1)
+            def _():
+                ring_copy(ring, last).wait_recv()
+
+            @pl.when(jnp.logical_and(step >= 1, step < count - 1))
+            def _():
+                @pl.when(step >= 2)
+                def _():
+                    ring_copy(ring, slot).wait_send()
+
+                ring_out[ring][slot] = (
+                    mine[ring][...]
+                    + pair_in[ring][...].astype(jnp.float32)
+                    + ring_in[ring][last].astype(jnp.float32)
+                ).astype(jnp.bfloat16)
+
+            @pl.when(step == count - 1)
+            def _():
+                at = 0
+                for product, first, wide in runs[ring]:
+                    totals[product][:, first : first + wide] = (
+                        mine[ring][:, at : at + wide]
+                        + pair_in[ring][:, at : at + wide].astype(jnp.float32)
+                        + ring_in[ring][last, :, at : at + wide].astype(jnp.float32)
+                    )
+                    at += wide
+
+            @pl.when(step < count - 1)
+            def _():
+                @pl.when(step >= 2)
+                def _():
+                    pl.semaphore_wait(ring_free.at[ring], 1)
+
+                ring_copy(ring, slot).start()
+                pl.semaphore_signal(
+                    pair_free.at[ring],
+                    inc=1,
+                    device_id=sibling,
+                    device_id_type=pl.DeviceIdType.MESH,
+                )
+
+            @pl.when(jnp.logical_and(step >= 1, step < count - 2))
+            def _():
+                pl.semaphore_signal(
+                    ring_free.at[ring],
+                    inc=1,
+                    device_id=source,
+                    device_id_type=pl.DeviceIdType.MESH,
+                )
+
+        return carry
+
+    lax.fori_loop(0, count, turn, 0)
+    for ring in range(rings):
+        pair_copy(ring).wait_send()
+        for step in (count - 3, count - 2):
+            ring_copy(ring, step % 2).wait_send()
+
+
+def ring_sums(pairs, sizes, collective_id):
+    dp_size, seq_size = sizes
+    rows = pairs[0][0].shape[-1] // (dp_size * seq_size)
+    tokens = pairs[0][1].shape[-2]
+    operands, known, places = [], {}, []
+
+    def place_of(array, turned):
+        if id(array) not in known:
+            known[id(array)] = len(operands)
+            operands.append(jnp.swapaxes(array, -1, -2) if turned else array)
+        return known[id(array)]
+
+    for left, right, lead in pairs:
+        places.append((place_of(left, rows % 128 != 0), place_of(right, False), lead))
+    widths = [right.shape[-1] for _, right, _ in pairs]
+    rings = 4
+    runs = cut_rings(widths, rings)
+    each = sum(widths) // rings
+    low = jnp.bfloat16
+    return pl.pallas_call(
+        functools.partial(
+            ring_kernel, dp_size, seq_size, rows, widths, runs, places, len(operands)
+        ),
+        out_shape=[jax.ShapeDtypeStruct((rows, wide), jnp.float32) for wide in widths],
+        in_specs=[pl.BlockSpec(memory_space=pltpu.VMEM)] * len(operands),
+        out_specs=[pl.BlockSpec(memory_space=pltpu.VMEM)] * len(pairs),
+        scratch_shapes=[pltpu.VMEM((rows, each), jnp.float32)] * rings
+        + [pltpu.VMEM((rows, each), low)] * (2 * rings)
+        + [pltpu.VMEM((2, rows, each), low)] * (2 * rings)
+        + [
+            pltpu.SemaphoreType.DMA((rings,)),
+            pltpu.SemaphoreType.DMA((rings,)),
+            pltpu.SemaphoreType.REGULAR((rings,)),
+            pltpu.SemaphoreType.DMA((rings, 2)),
+            pltpu.SemaphoreType.DMA((rings, 2)),
+            pltpu.SemaphoreType.REGULAR((rings,)),
+        ],
+        compiler_params=pltpu.CompilerParams(
+            collective_id=collective_id, has_side_effects=True, vmem_limit_bytes=60 * 2**20
+        ),
+        cost_estimate=pl.CostEstimate(
+            flops=2 * tokens * rows * dp_size * seq_size * sum(widths),
+            bytes_accessed=2 * tokens * (2048 * len(pairs) + sum(widths)),
+            transcendentals=0,
+        ),
+    )(*operands)
 
 
 def per_device(
@@ -369,15 +614,23 @@
     part_normed_two, part_prev_two, grad_coeffs_chan = chan_back((part_key, part_recept))
     from_next_two = from_behind(for_sending(part_prev_two), "seq", -1).astype(jnp.float32)
     part_normed_two = part_normed_two.at[:, -1, :].add(from_next_two)
+    sizes = (lax.axis_size("dp"), blocks)
+    flat_value = full_value.reshape(tokens, -1)
+    key_sum, value_sum, recept_sum = ring_sums(
+        [
+            (chan_key_b.reshape(tokens, -1), grad_key.reshape(tokens, -1), ()),
+            (flat_value, hidden.reshape(tokens, -1), ()),
+            (chan_recept_b.reshape(tokens, -1), grad_recept.reshape(tokens, -1), ()),
+        ],
+        sizes,
+        0,
+    )
     grad_normed_two = part_normed_two + other_half(part_normed_two.astype(jnp.bfloat16)).astype(
         jnp.float32
     )
     grad_residual, grad_gain_two, grad_bias_two = norm_two_back(grad_normed_two)
     grad_residual = grad_residual + full_out.astype(jnp.float32)
     grad_branch = grad_residual.astype(jnp.bfloat16)
-    out_weight_grad = jnp.einsum(
-        "std,ste->de", mixer_in, grad_branch, preferred_element_type=jnp.float32
-    )
     grad_mixer = jnp.einsum(
         "ste,de->std", grad_branch, out_proj, preferred_element_type=jnp.float32
     )
@@ -410,7 +663,6 @@
             grad_gate.reshape(tokens, head_cols),
         ]
     ).astype(jnp.bfloat16)
-    proj_grad = jnp.einsum("ntd,nte->nde", stacked, grad_proj, preferred_element_type=jnp.float32)
     part_inputs = jnp.einsum(
         "nte,nde->ntd", grad_proj, projections, preferred_element_type=jnp.float32
     )
@@ -428,15 +680,6 @@
     part_normed_one = part_normed_one.at[:, -1, :].add(from_next_one)
     part_block, grad_gain_one, grad_bias_one = norm_one_back(part_normed_one)
     input_grad = own_half(grad_residual) + half_sum(part_block)
-    value_weight_grad = jnp.einsum(
-        "stf,std->fd", hidden, full_value, preferred_element_type=jnp.float32
-    )
-    key_weight_grad = jnp.einsum(
-        "std,stf->df", chan_key_b, grad_key, preferred_element_type=jnp.float32
-    )
-    recept_weight_grad = jnp.einsum(
-        "std,ste->de", chan_recept_b, grad_recept, preferred_element_type=jnp.float32
-    )
     small_sums = packed_scatter(
         [
             (jnp.stack([grad_gain_one, 0.5 * grad_gain_two]), 1),
@@ -454,11 +697,12 @@
         gathered,
     )
     rest = [part + other_half(part) for part in small_sums[:6]] + small_sums[6:]
-    proj_sum = big_scatter(proj_grad, 1)
-    out_sum = big_scatter(out_weight_grad, 1)
-    key_sum = big_scatter(key_weight_grad, 0)
-    value_sum_rows = big_scatter(value_weight_grad, 1)
-    recept_sum = big_scatter(recept_weight_grad, 0)
+    *proj_sums, out_sum = ring_sums(
+        [(stacked, grad_proj, (branch,)) for branch in range(4)]
+        + [(grad_branch.reshape(tokens, -1), mixer_in.reshape(tokens, -1), ())],
+        sizes,
+        1,
+    )
     coeff_rows = jnp.concatenate([rest[2][:1], rest[2][2:]], axis=0)
     decay_row = rest[2][1:2]
     return (
@@ -473,14 +717,14 @@
         rest[4],
         rest[5],
         rest[6],
-        proj_sum,
-        out_sum,
+        jnp.stack(proj_sums),
+        out_sum.T,
         rest[7],
         rest[8],
         rest[9],
         rest[10],
         key_sum,
-        value_sum_rows,
+        value_sum.T,
         recept_sum,
         total_least,
         total_most,

time: 1660 us -> 1480 us (0.89)
  waiting for transfers between devices: 766 us -> 341 us
  Pallas kernels: 0 us -> 307 us
  matrix products: 363 us -> 308 us
    reduce_scatter x3 -> x0, waiting for transfers between devices: 329 us -> none  [big_scatter(): lax.psum_scatter(whole.astype(jnp.bfloat16), ('dp', 'seq'), scatter_dimen...]
    pallas_call x0 -> x2, Pallas kernels: none -> 307 us  [ring_sums(): pl.pallas_call(functools.partial(ring_kernel, dp_size, seq_size, rows, wi...]
    unnamed x13 -> x6, waiting for transfers between devices: 96.3 us -> 1.28 us
    dot_general x5 -> x0, matrix products: 54 us -> none  [the longest x1 16.1 us: per_device(): jnp.einsum('ntd,nte->nde', stacked, grad_proj, preferred_element_type=jnp...]
    unnamed x417 -> x379, local copies, waits for them, and re-layouts: 83.3 us -> 61.1 us
  transfers between devices with their start and end apart: 27 -> 22, of which waited for: 16 -> 12; matrix products, arithmetic and copies ran while one was open for 36% -> 18% of each run, Pallas kernels for 0% -> 21%
where the time goes in v2:
time: 1480 us; the launch traced here: 1470 us
  waiting for transfers between devices  341 us (23%)
  matrix products  308 us (21%)
  Pallas kernels  307 us (21%)
  local copies, waits for them, and re-layouts  260 us (18%)
  other arithmetic  200 us (14%)
  starting transfers between devices  21.6 us (1%)
  between operations  16.8 us (1%)
  blocking collectives  16.4 us (1%)
    pallas_call x2, Pallas kernels, ring_sums(): pl.pallas_call(functools.partial(ring_kernel, dp_size, seq_size, rows, wi...  307 us
    ppermute x12, waiting for transfers between devices, other_half(): return lax.ppermute(block, 'tp', [(0, 1), (1, 0)])  165 us
    dot_general x9, matrix products, dense_single_float(): jnp.einsum('...i,ij->...j', left, right, precision=PRECISION_TOP, preferr...  63.9 us
    unnamed x379, local copies, waits for them, and re-layouts  61.1 us
    all_gather x1, waiting for transfers between devices, per_device(): lax.all_gather(proj_weights, ('dp', 'seq'), axis=1, tiled=True)  53.5 us
    all_gather x1, waiting for transfers between devices, packed_gather(): everything = lax.all_gather(flat, ('dp', 'seq'))  46.5 us
    all_gather x1, waiting for transfers between devices, per_device(): all_carried = lax.all_gather(carried.astype(jnp.bfloat16), 'seq')  38.7 us
    dot_general x3, matrix products, token_mixture(): jnp.einsum('stri,rid->rstd', hidden_mixture.reshape(seq_count, length, 5,...  38.6 us
  transfers between devices with their start and end apart: 22, of which 12 were waited for; matrix products, arithmetic and copies ran while one was open for 18% of the time, Pallas kernels for 21%

profile of v2, /device:TPU:0, one launch (start us, length us, event | category | flops | bytes accessed | tf_op | source)
XLA Modules:
  0.0 1470.2 jit_solution(4383191035593748405)
XLA Ops:
  22.4 46.5 %all-gather.19.cloned.1.call-done = bf16[16,1,55040]{2,1,0:T(2,128)(2,1)} async-done(((bf16[1,1,55040]{2,1,0:T(2,128)(2,1)}), bf16[16,1,55040]{2,1,0:T(2,128)(2,1)}) %all-gather.19.cloned.1.call-update) | async-done | bytes 1761296 | tf_op jit(solution)/shard_map/all_gather | solution.py:145
  104.5 8.6 fusion.168
  131.2 12.4 add_convert_fusion.5
  143.6 53.5 %all-gather.11.cloned.1.call-done = bf16[4,2048,1024]{2,1,0:T(8,128)(2,1)} async-done(((bf16[4,128,1024]{2,1,0:T(8,128)(2,1)}), bf16[4,2048,1024]{2,1,0:T(8,128)(2,1)}) %all-gather.11.cloned.1.call-update) | async-done | bytes 16777232 | tf_op jit(solution)/shard_map/all_gather | solution.py:484
  197.2 16.6 %fusion.205 = f32[4,512,1024]{2,1,0:T(8,128)S(1)} fusion(bf16[4,2048,1024]{2,1,0:T(8,128)(2,1)} %all-gather.11.cloned.1.call-done, bf16[1,512,2048]{2,1,0:T(8,128)(2,1)} %bitcast.587, bf16[1,512,2048]{2,1,0:T(8,128)(2,1)} %bitcast.589, bf16[1,512,2048]{2,1,0:T(8,128)(2,1)} %bitcast.591, bf16[1,512,2048]{2,1,0:T(8,128)(2,1)} %bitcast.585), kind=kOutput, calls=%fused_computation.394 | convolution fusion | flops 8602517504 | bytes 33554432 | tf_op jit(solution)/shard_map/ntd,nde->nte/dot_general | solution.py:533
  247.6 11.6 exponential_reduce_fusion.1
  260.0 8.7 fusion.36
  273.0 6.6 fusion.153
  294.6 16.4 %all-gather.1 = f32[32,16,66]{2,1,0:T(8,128)S(1)} all-gather(f32[4,16,66]{2,1,0:T(8,128)S(1)} %pad_maximum_fusion.4), channel_id=3, replica_groups=mesh['dp'=2,'seq'=8,'tp'=2] {'seq'}, dimensions={0}, use_global_device_ids=true | all-gather | bytes 152064 | tf_op jit(solution)/shard_map/all_gather | solution.py:549
  312.3 11.0 fusion.237
  323.3 38.7 %all-gather.15.cloned.1.call-done = bf16[32,16,64,64]{3,2,1,0:T(8,128)(2,1)} async-done(((bf16[4,16,64,64]{3,2,1,0:T(8,128)(2,1)}), bf16[32,16,64,64]{3,2,1,0:T(8,128)(2,1)}) %all-gather.15.cloned.1.call-update) | async-done | bytes 4194320 | tf_op jit(solution)/shard_map/all_gather | solution.py:553
  362.1 8.7 fusion.117
  375.8 8.3 fusion.221
  389.7 26.0 %all-gather.13.cloned.1.call-done = bf16[1024,2048]{1,0:T(8,128)(2,1)} async-done(((bf16[1024,128]{1,0:T(8,128)(2,1)}), bf16[1024,2048]{1,0:T(8,128)(2,1)}) %all-gather.13.cloned.1.call-update) | async-done | bytes 4194320 | tf_op jit(solution)/shard_map/all_gather | solution.py:485
  423.1 46.3 %collective-permute-done.1 = bf16[4,128,2048]{2,1,0:T(8,128)(2,1)S(1)} collective-permute-done((bf16[4,128,2048]{2,1,0:T(8,128)(2,1)S(1)}, bf16[4,128,2048]{2,1,0:T(8,128)(2,1)S(1)}, u32[]{:S(2)}, u32[]{:S(2)}) %collective-permute-start.1) | collective-permute-done | bytes 2097184 | tf_op jit(solution)/shard_map/ppermute | solution.py:180
  482.4 14.4 multiply_convert_fusion.1
  496.9 7.7 fusion.4
  509.2 24.2 %collective-permute-done.3 = bf16[4,128,1024]{2,1,0:T(8,128)(2,1)} collective-permute-done((bf16[4,128,1024]{2,1,0:T(8,128)(2,1)}, bf16[4,128,1024]{2,1,0:T(8,128)(2,1)}, u32[]{:S(2)}, u32[]{:S(2)}) %collective-permute-start.3) | collective-permute-done | bytes 1048608 | tf_op jit(solution)/shard_map/ppermute | solution.py:180
  533.4 8.9 fusion.68
  543.8 23.3 %collective-permute-done.4 = bf16[4,128,1024]{2,1,0:T(8,128)(2,1)S(1)} collective-permute-done((bf16[4,128,1024]{2,1,0:T(8,128)(2,1)}, bf16[4,128,1024]{2,1,0:T(8,128)(2,1)S(1)}, u32[]{:S(2)}, u32[]{:S(2)}) %collective-permute-start.4) | collective-permute-done | bytes 1048608 | tf_op jit(solution)/shard_map/ppermute | solution.py:180
  569.9 26.8 %multiply_convert_fusion = bf16[4,128,3584]{2,1,0:T(8,128)(2,1)} fusion(f32[4,128,3584]{2,1,0:T(8,128)} %get-tuple-element.356, bf16[3584,2048]{1,0:T(8,128)(2,1)} %param.39, bf16[4,128,1024]{2,1,0:T(8,128)(2,1)S(1)} %get-tuple-element.307, bf16[4,128,1024]{2,1,0:T(8,128)(2,1)S(1)} %get-tuple-element.306), kind=kOutput, calls=%fused_computation.12 | convolution fusion | flops 7527727104 | bytes 27787264 | tf_op jit(solution)/shard_map/std,fd->stf/dot_general | solution.py:606
  596.7 12.3 fusion.6
  608.9 5.9 multiply_reduce_fusion.1
  626.8 68.8 %collective-permute-done.7 = bf16[4,128,1024]{2,1,0:T(8,128)(2,1)S(1)} collective-permute-done((bf16[4,128,1024]{2,1,0:T(8,128)(2,1)S(1)}, bf16[4,128,1024]{2,1,0:T(8,128)(2,1)S(1)}, u32[]{:S(2)}, u32[]{:S(2)}) %collective-permute-start.7) | collective-permute-done | bytes 1048608 | tf_op jit(solution)/shard_map/ppermute | solution.py:180
  723.8 7.4 pad_maximum_fusion.refs_0_
  748.5 8.5 fusion.105
  759.1 9.6 fusion.55
  772.8 8.1 fusion.53
  786.3 8.2 fusion.57
  794.5 8.8 all-gather.17.cloned.1.call-done
  803.4 9.6 multiply_reduce_fusion.7
  821.9 9.0 fusion.98
  834.9 11.3 fusion.213
  851.1 9.3 fusion.50
  860.5 12.4 fusion.235
  880.0 11.9 convolution_bitcast_fusion.1
  921.7 16.8 %fusion.204 = f32[4,512,2048]{2,1,0:T(8,128)} fusion(bf16[4,2048,1024]{2,1,0:T(8,128)(2,1)} %all-gather.11.cloned.1.call-done, bf16[1,512,1024]{2,1,0:T(8,128)(2,1)} %bitcast.618, bf16[1,512,1024]{2,1,0:T(8,128)(2,1)S(1)} %reshape.922, bf16[1,512,1024]{2,1,0:T(8,128)(2,1)} %reshape.921, bf16[1,512,1024]{2,1,0:T(8,128)(2,1)} %reshape.920), kind=kOutput, calls=%fused_computation.393 | convolution fusion | flops 8596226048 | bytes 37748736 | tf_op jit(solution)/shard_map/nte,nde->ntd/dot_general | solution.py:666
  938.6 12.6 fusion.224
  951.2 15.3 %multiply_bitcast_fusion.4 = (f32[1,4,128,2048]{3,2,1,0:T(8,128)}, f32[1,4,128,2048]{3,2,1,0:T(8,128)}, f32[1,4,128,2048]{3,2,1,0:T(8,128)}, f32[1,4,128,2048]{3,2,1,0:T(8,128)}, f32[1,4,128,2048]{3,2,1,0:T(8,128)}) fusion(f32[4,128,2048]{2,1,0:T(8,128)S(1)} %copy-done.5, f32[4,128,2048]{2,1,0:T(8,128)} %bitcast.561, f32[4,128,2048]{2,1,0:T(8,128)} %fusion.171, ...), kind=kLoop, calls=%fused_computation.257 | loop fusion | flops 5242880 | bytes 46137344 | tf_op jit(solution)/shard_map/transpose(jvp())/broadcast_in_dim | solution.py:69
  966.6 15.6 %convolution_bitcast_fusion.2 = f32[4,128,5,32]{1,3,0,2:T(8,128)S(1)} fusion(bf16[5,32,2048,1]{2,1,0,3:T(8,128)(2,1)S(1)} %copy-done.70, f32[1,4,128,2048]{3,2,1,0:T(8,128)} %get-tuple-element.291, f32[1,4,128,2048]{3,2,1,0:T(8,128)} %get-tuple-element.292, f32[1,4,128,2048]{3,2,1,0:T(8,128)} %get-tuple-element.293, ...), kind=kOutput, calls=%fused_computation.273 | convolution fusion | flops 2034237440 | bytes 21954560 | tf_op jit(solution)/shard_map/transpose(jvp(stri,rid->rstd))/dot_general | solution.py:61
  982.3 14.4 fusion
  997.6 21.1 %multiply_reduce_fusion.14 = (f32[2048]{0:T(1024)S(1)}, f32[2048]{0:T(1024)S(1)}, f32[2048]{0:T(1024)S(1)}, f32[2048]{0:T(1024)S(1)}, f32[2048]{0:T(1024)S(1)}, ...) fusion(f32[4,128,2048]{2,1,0:T(8,128)} %copy-done.4, f32[4,128,2048]{2,1,0:T(8,128)} %bitcast.562, ...), kind=kOutput, calls=%fused_computation.256 | convolution fusion | flops 2042613760 | bytes 55607296 | tf_op jit(solution)/shard_map/transpose(jvp(...i,ij->...j))/dot_general | solution.py:30
  1018.7 11.0 convolution_bitcast_fusion
  1034.7 11.1 pad_add_fusion.1
  1095.6 194.4 %shard_map.355 = (f32[128,3584]{1,0:T(8,128)}, f32[128,3584]{1,0:T(8,128)}, f32[128,1024]{1,0:T(8,128)}) custom-call(bf16[512,2048]{1,0:T(8,128)(2,1)} %bitcast.608, bf16[512,3584]{1,0:T(8,128)(2,1)} %bitcast.715, bf16[512,2048]{1,0:T(8,128)(2,1)} %bitcast.607, bf16[512,3584]{1,0:T(8,128)(2,1)} %bitcast.714, bf16[512,2048]{1,0:T(8,128)(2,1)} %bitcast.609, ...), custom_call_target="tpu_custom_call" | custom-call | flops 17179869184 | bytes 14680064 | tf_op jit(solution)/shard_map/pallas_call | solution.py:401
  1302.0 112.2 %shard_map.354 = (f32[128,1024]{1,0:T(8,128)}, f32[128,1024]{1,0:T(8,128)}, f32[128,1024]{1,0:T(8,128)}, f32[128,1024]{1,0:T(8,128)}, f32[128,1024]{1,0:T(8,128)}) custom-call(bf16[4,512,2048]{2,1,0:T(8,128)(2,1)} %pad_maximum_fusion.refs_0_, bf16[4,512,1024]{2,1,0:T(8,128)(2,1)} %pad_maximum_fusion.1.refs_1_, bf16[512,2048]{1,0:T(8,128)(2,1)} %bitcast.610, ...), custom_call_target="tpu_custom_call" | custom-call | flops 10737418240 | bytes 15728640 | tf_op jit(solution)/shard_map/pallas_call | solution.py:401
  1419.5 10.1 convert_add_fusion.4
  1439.5 9.1 slice.421
  (620 shorter events, 383.2 us)
Async XLA Ops:
  7.2 61.7 %all-gather.19.cloned.1.call-start = ((), (), s32[]{:S(2)}) async-start(), calls=%async_computation.6 | async-start | bytes 3742720 | tf_op jit(solution)/shard_map/all_gather | solution.py:145
  18.9 178.3 %all-gather.11.cloned.1.call-start = ((), (), s32[]{:S(2)}) async-start(), calls=%async_computation.1 | async-start | bytes 17825792 | tf_op jit(solution)/shard_map/all_gather | solution.py:484
  19.7 342.4 %all-gather.15.cloned.1.call-start = ((), (), s32[]{:S(2)}) async-start(), calls=%async_computation.4 | async-start | bytes 9437184 | tf_op jit(solution)/shard_map/all_gather | solution.py:553
  21.7 53.7 %copy-start.132 = (f32[4,128]{1,0:T(4,128)}, f32[4,128]{1,0:T(4,128)S(1)}, u32[]{:S(2)}) copy-start(f32[4,128]{1,0:T(4,128)S(1)} %broadcast_multiply_fusion.5) | copy-start | bytes 6148
  22.4 48.7 %copy-start.162 = (f32[4,128]{1,0:T(4,128)}, f32[4,128]{1,0:T(4,128)S(1)}, u32[]{:S(2)}) copy-start(f32[4,128]{1,0:T(4,128)S(1)} %fusion.20) | copy-start | bytes 6148
  22.4 53.0 %copy-start.140 = (f32[4,128]{1,0:T(4,128)}, f32[4,128]{1,0:T(4,128)S(1)}, u32[]{:S(2)}) copy-start(f32[4,128]{1,0:T(4,128)S(1)} %fusion.186) | copy-start | bytes 6148
  73.9 57.3 %copy-start.90 = (f32[1,16,128]{2,0,1:T(1,128)}, f32[1,16,128]{2,0,1:T(1,128)S(1)}, u32[]{:S(2)}) copy-start(f32[1,16,128]{2,0,1:T(1,128)S(1)} %get-tuple-element.346) | copy-start | bytes 24580
  78.0 18.4 %collective-permute-start = (bf16[4,2048]{1,0:T(4,128)(2,1)}, bf16[4,2048]{1,0:T(4,128)(2,1)}, u32[]{:S(2)}, u32[]{:S(2)}) collective-permute-start(bf16[4,2048]{1,0:T(4,128)(2,1)} %bitcast.553), channel_id=1, source_target_pairs={{0,2},{2,4},{4,6},{6,8},{8,10},{10,12},{12,14},{1,3},{3,5},{5,7},{... | collective-permute-start | bytes 49160 | tf_op jit(solution)/shard_map/ppermute | solution.py:18
  81.4 31.7 %copy-start.96 = (f32[1,16,128]{2,0,1:T(1,128)}, f32[1,16,128]{2,0,1:T(1,128)S(1)}, u32[]{:S(2)}) copy-start(f32[1,16,128]{2,0,1:T(1,128)S(1)} %get-tuple-element.335) | copy-start | bytes 24580
  86.1 27.1 %copy-start.54 = (bf16[2048,64]{1,0:T(8,128)(2,1)}, bf16[2048,64]{1,0:T(8,128)(2,1)S(1)}, u32[]{:S(2)}) copy-start(bf16[2048,64]{1,0:T(8,128)(2,1)S(1)} %reshape_reshape.17) | copy-start | bytes 786436
  96.4 23.7 %copy-start.71 = (bf16[64,16,16,4]{0,3,2,1:T(4,128)(2,1)}, bf16[64,16,16,4]{0,3,2,1:T(4,128)(2,1)S(1)}, u32[]{:S(2)}) copy-start(bf16[64,16,16,4]{0,3,2,1:T(4,128)(2,1)S(1)} %copy.676) | copy-start | bytes 393220
  279.6 136.1 %all-gather.13.cloned.1.call-start = ((), (), s32[]{:S(2)}) async-start(), calls=%async_computation.2 | async-start | bytes 4456448 | tf_op jit(solution)/shard_map/all_gather | solution.py:485
  280.2 523.1 %all-gather.17.cloned.1.call-start = ((), (), s32[]{:S(2)}) async-start(), calls=%async_computation.5 | async-start | bytes 9437184 | tf_op jit(solution)/shard_map/all_gather | solution.py:649
  289.6 94.9 %copy-start.100 = (f32[4,128,16]{1,2,0:T(8,128)}, f32[4,128,16]{1,2,0:T(8,128)S(1)}, u32[]{:S(2)}) copy-start(f32[4,128,16]{1,2,0:T(8,128)S(1)} %copy.694) | copy-start | bytes 98308
  312.3 49.7 %copy-start.104 = (f32[4,16,64]{2,1,0:T(8,128)}, f32[4,16,64]{2,1,0:T(8,128)S(1)}, u32[]{:S(2)}) copy-start(f32[4,16,64]{2,1,0:T(8,128)S(1)} %get-tuple-element.321) | copy-start | bytes 49156
  312.3 49.7 %copy-start.106 = (f32[4,16,64]{2,1,0:T(8,128)}, f32[4,16,64]{2,1,0:T(8,128)S(1)}, u32[]{:S(2)}) copy-start(f32[4,16,64]{2,1,0:T(8,128)S(1)} %get-tuple-element.322) | copy-start | bytes 49156
  312.3 49.7 %copy-start.108 = (f32[4,16,64]{2,1,0:T(8,128)}, f32[4,16,64]{2,1,0:T(8,128)S(1)}, u32[]{:S(2)}) copy-start(f32[4,16,64]{2,1,0:T(8,128)S(1)} %get-tuple-element.323) | copy-start | bytes 49156
  312.3 49.7 %copy-start.110 = (f32[4,16,64]{2,1,0:T(8,128)}, f32[4,16,64]{2,1,0:T(8,128)S(1)}, u32[]{:S(2)}) copy-start(f32[4,16,64]{2,1,0:T(8,128)S(1)} %get-tuple-element.324) | copy-start | bytes 49156
  312.3 49.7 %copy-start.112 = (f32[4,16,64]{2,1,0:T(8,128)}, f32[4,16,64]{2,1,0:T(8,128)S(1)}, u32[]{:S(2)}) copy-start(f32[4,16,64]{2,1,0:T(8,128)S(1)} %get-tuple-element.325) | copy-start | bytes 49156
  312.3 49.7 %copy-start.114 = (f32[4,16,64]{2,1,0:T(8,128)}, f32[4,16,64]{2,1,0:T(8,128)S(1)}, u32[]{:S(2)}) copy-start(f32[4,16,64]{2,1,0:T(8,128)S(1)} %get-tuple-element.326) | copy-start | bytes 49156
  421.6 47.9 %collective-permute-start.1 = (bf16[4,128,2048]{2,1,0:T(8,128)(2,1)S(1)}, bf16[4,128,2048]{2,1,0:T(8,128)(2,1)S(1)}, u32[]{:S(2)}, u32[]{:S(2)}) collective-permute-start(bf16[4,128,2048]{2,1,0:T(8,128)(2,1)S(1)} %get-tuple-element.353), channel_id=1, source_target_pairs={{0,1},{1,0},{2,3},{3,2},{4,5},{5,4},{6,7},{7,6},{8,9},{9,8},{10,11... | collective-permute-start | bytes 6291464 | tf_op jit(solution)/shard_map/ppermute | solution.py:180
  474.8 2.2 collective-permute-start.2
  477.0 19.8 %slice-start = ((s8[14680064]{0:T(1024)(128)(4,1)}), s8[4194304]{0:T(1024)(128)(4,1)S(1)}, s32[]{:S(2)}) async-start(s8[14680064]{0:T(1024)(128)(4,1)} %bitcast.712), calls=%async_computation.7 | async-start | bytes 8388608
  482.4 51.1 %copy-start.76 = (bf16[4,128,2048]{2,1,0:T(8,128)(2,1)}, bf16[4,128,2048]{2,1,0:T(8,128)(2,1)S(1)}, u32[]{:S(2)}) copy-start(bf16[4,128,2048]{2,1,0:T(8,128)(2,1)S(1)} %get-tuple-element.272) | copy-start | bytes 6291460
  507.7 25.7 %collective-permute-start.3 = (bf16[4,128,1024]{2,1,0:T(8,128)(2,1)}, bf16[4,128,1024]{2,1,0:T(8,128)(2,1)}, u32[]{:S(2)}, u32[]{:S(2)}) collective-permute-start(bf16[4,128,1024]{2,1,0:T(8,128)(2,1)} %dynamic-slice_convert_fusion.1), channel_id=1, source_target_pairs={{0,1},{1,0},{2,3},{3,2},{4,5},{5,4},{6,7},{7,6},{8,9},{9,8},{10,11... | collective-permute-start | bytes 3145736 | tf_op jit(solution)/shard_map/ppermute | solution.py:180
  542.3 24.8 %collective-permute-start.4 = (bf16[4,128,1024]{2,1,0:T(8,128)(2,1)}, bf16[4,128,1024]{2,1,0:T(8,128)(2,1)S(1)}, u32[]{:S(2)}, u32[]{:S(2)}) collective-permute-start(bf16[4,128,1024]{2,1,0:T(8,128)(2,1)} %get-tuple-element.303), channel_id=1, source_target_pairs={{0,1},{1,0},{2,3},{3,2},{4,5},{5,4},{6,7},{7,6},{8,9},{9,8},{10,11... | collective-permute-start | bytes 3145736 | tf_op jit(solution)/shard_map/ppermute | solution.py:180
  615.4 3.1 collective-permute-start.5
  622.0 73.7 %copy-start.3 = (f32[4,128,2048]{2,1,0:T(8,128)S(1)}, f32[4,128,2048]{2,1,0:T(8,128)}, u32[]{:S(2)}) copy-start(f32[4,128,2048]{2,1,0:T(8,128)} %copy-done.2) | copy-start | bytes 12582916
  622.0 73.7 %copy-start.11 = (f32[4,128,2048]{2,1,0:T(8,128)S(1)}, f32[4,128,2048]{2,1,0:T(8,128)}, u32[]{:S(2)}) copy-start(f32[4,128,2048]{2,1,0:T(8,128)} %scatter-add.6) | copy-start | bytes 12582916
  624.7 71.0 %collective-permute-start.6 = (bf16[4,128,2048]{2,1,0:T(8,128)(2,1)S(1)}, bf16[4,128,2048]{2,1,0:T(8,128)(2,1)S(1)}, u32[]{:S(2)}, u32[]{:S(2)}) collective-permute-start(bf16[4,128,2048]{2,1,0:T(8,128)(2,1)S(1)} %convert_element_type.339), channel_id=1, source_target_pairs={{0,1},{1,0},{2,3},{3,2},{4,5},{5,4},{6,7},{7,6},{8,9},{9,8},{10,11... | collective-permute-start | bytes 6291464 | tf_op jit(solution)/shard_map/ppermute | solution.py:180
  626.2 69.3 %collective-permute-start.7 = (bf16[4,128,1024]{2,1,0:T(8,128)(2,1)S(1)}, bf16[4,128,1024]{2,1,0:T(8,128)(2,1)S(1)}, u32[]{:S(2)}, u32[]{:S(2)}) collective-permute-start(bf16[4,128,1024]{2,1,0:T(8,128)(2,1)S(1)} %copy-done.86), channel_id=1, source_target_pairs={{0,1},{1,0},{2,3},{3,2},{4,5},{5,4},{6,7},{7,6},{8,9},{9,8},{10,11... | collective-permute-start | bytes 3145736 | tf_op jit(solution)/shard_map/ppermute | solution.py:180
  721.8 709.7 %reduce-scatter.2.cloned.1.call-start = ((), (), s32[]{:S(2)}) async-start(), calls=%async_computation.3 | async-start | bytes 3760128 | tf_op jit(solution)/shard_map/reduce_scatter | solution.py:168
  786.2 17.1 %copy-start.98 = (f32[4,16,64]{2,1,0:T(8,128)S(1)}, f32[4,16,64]{2,1,0:T(8,128)}, u32[]{:S(2)}) copy-start(f32[4,16,64]{2,1,0:T(8,128)} %get-tuple-element.319) | copy-start | bytes 49156
  786.2 17.1 %copy-start.105 = (f32[4,16,64]{2,1,0:T(8,128)S(1)}, f32[4,16,64]{2,1,0:T(8,128)}, u32[]{:S(2)}) copy-start(f32[4,16,64]{2,1,0:T(8,128)} %copy-done.104) | copy-start | bytes 49156
  786.2 17.1 %copy-start.107 = (f32[4,16,64]{2,1,0:T(8,128)S(1)}, f32[4,16,64]{2,1,0:T(8,128)}, u32[]{:S(2)}) copy-start(f32[4,16,64]{2,1,0:T(8,128)} %copy-done.106) | copy-start | bytes 49156
  786.3 17.1 %copy-start.109 = (f32[4,16,64]{2,1,0:T(8,128)S(1)}, f32[4,16,64]{2,1,0:T(8,128)}, u32[]{:S(2)}) copy-start(f32[4,16,64]{2,1,0:T(8,128)} %copy-done.108) | copy-start | bytes 49156
  786.3 17.1 %copy-start.111 = (f32[4,16,64]{2,1,0:T(8,128)S(1)}, f32[4,16,64]{2,1,0:T(8,128)}, u32[]{:S(2)}) copy-start(f32[4,16,64]{2,1,0:T(8,128)} %copy-done.110) | copy-start | bytes 49156
  786.3 17.1 %copy-start.113 = (f32[4,16,64]{2,1,0:T(8,128)S(1)}, f32[4,16,64]{2,1,0:T(8,128)}, u32[]{:S(2)}) copy-start(f32[4,16,64]{2,1,0:T(8,128)} %copy-done.112) | copy-start | bytes 49156
  1032.3 29.2 %collective-permute-start.8 = (bf16[4,2048]{1,0:T(4,128)(2,1)S(1)}, bf16[4,2048]{1,0:T(4,128)(2,1)}, u32[]{:S(2)}, u32[]{:S(2)}) collective-permute-start(bf16[4,2048]{1,0:T(4,128)(2,1)S(1)} %bitcast.704), channel_id=1, source_target_pairs={{2,0},{4,2},{6,4},{8,6},{10,8},{12,10},{14,12},{3,1},{5,3},{7,5},{... | collective-permute-start | bytes 49160 | tf_op jit(solution)/shard_map/ppermute | solution.py:18
  1300.4 129.1 %collective-permute-start.9 = (bf16[4,128,1024]{2,1,0:T(8,128)(2,1)S(1)}, bf16[4,128,1024]{2,1,0:T(8,128)(2,1)S(1)}, u32[]{:S(2)}, u32[]{:S(2)}) collective-permute-start(bf16[4,128,1024]{2,1,0:T(8,128)(2,1)S(1)} %dynamic-slice_convert_fusion), channel_id=1, source_target_pairs={{0,1},{1,0},{2,3},{3,2},{4,5},{5,4},{6,7},{7,6},{8,9},{9,8},{10,11... | collective-permute-start | bytes 3145736 | tf_op jit(solution)/shard_map/ppermute | solution.py:180
  1431.5 17.9 %copy-start.85 = (f32[432,128]{1,0:T(8,128)S(1)}, f32[432,128]{1,0:T(8,128)}, u32[]{:S(2)}) copy-start(f32[432,128]{1,0:T(8,128)} %reduce-scatter.2.cloned.1.call-done) | copy-start | bytes 663556
  1432.4 21.1 %collective-permute-start.11 = (f32[2,128]{1,0:T(2,128)S(1)}, f32[2,128]{1,0:T(2,128)S(1)}, u32[]{:S(2)}, u32[]{:S(2)}) collective-permute-start(f32[2,128]{1,0:T(2,128)S(1)} %get-tuple-element.331), channel_id=1, source_target_pairs={{0,1},{1,0},{2,3},{3,2},{4,5},{5,4},{6,7},{7,6},{8,9},{9,8},{10,11... | collective-permute-start | bytes 3080 | tf_op jit(solution)/shard_map/ppermute | solution.py:180
  1432.9 20.5 %collective-permute-start.10 = (f32[2,128]{1,0:T(2,128)S(1)}, f32[2,128]{1,0:T(2,128)S(1)}, u32[]{:S(2)}, u32[]{:S(2)}) collective-permute-start(f32[2,128]{1,0:T(2,128)S(1)} %get-tuple-element.332), channel_id=1, source_target_pairs={{0,1},{1,0},{2,3},{3,2},{4,5},{5,4},{6,7},{7,6},{8,9},{9,8},{10,11... | collective-permute-start | bytes 3080 | tf_op jit(solution)/shard_map/ppermute | solution.py:180
  1435.1 19.0 %collective-permute-start.12 = (f32[8,128]{1,0:T(8,128)S(1)}, f32[8,128]{1,0:T(8,128)S(1)}, u32[]{:S(2)}, u32[]{:S(2)}) collective-permute-start(f32[8,128]{1,0:T(8,128)S(1)} %slice.512), channel_id=1, source_target_pairs={{0,1},{1,0},{2,3},{3,2},{4,5},{5,4},{6,7},{7,6},{8,9},{9,8},{10,11... | collective-permute-start | bytes 12296 | tf_op jit(solution)/shard_map/ppermute | solution.py:180
  1436.5 21.0 %collective-permute-start.15 = (f32[128,64]{1,0:T(8,128)S(1)}, f32[128,64]{1,0:T(8,128)S(1)}, u32[]{:S(2)}, u32[]{:S(2)}) collective-permute-start(f32[128,64]{1,0:T(8,128)S(1)} %reshape.811), channel_id=1, source_target_pairs={{0,1},{1,0},{2,3},{3,2},{4,5},{5,4},{6,7},{7,6},{8,9},{9,8},{10,11... | collective-permute-start | bytes 98312 | tf_op jit(solution)/shard_map/ppermute | solution.py:180
  1438.9 22.3 %copy-start.81 = (f32[128,3584]{1,0:T(8,128)S(1)}, f32[128,3584]{1,0:T(8,128)}, u32[]{:S(2)}) copy-start(f32[128,3584]{1,0:T(8,128)} %get-tuple-element.405) | copy-start | bytes 5505028
  1438.9 15.7 %collective-permute-start.14 = (f32[160,128]{1,0:T(8,128)S(1)}, f32[160,128]{1,0:T(8,128)S(1)}, u32[]{:S(2)}, u32[]{:S(2)}) collective-permute-start(f32[160,128]{1,0:T(8,128)S(1)} %slice.514), channel_id=1, source_target_pairs={{0,1},{1,0},{2,3},{3,2},{4,5},{5,4},{6,7},{7,6},{8,9},{9,8},{10,11... | collective-permute-start | bytes 245768 | tf_op jit(solution)/shard_map/ppermute | solution.py:180
  1455.3 5.0 collective-permute-start.13
  (145 other events, 1097.6 us)
Sparse Core Ops, SparseCore 0:
  19.0 49.8 all-gather.18
  71.1 125.9 all-gather.10
  279.7 82.2 all-gather.14
  363.9 51.7 all-gather.12
  721.9 81.3 all-gather.16
  1090.2 89.4 reduce-scatter.1

commit v3 on v2

--- a/solution.py
+++ b/solution.py
@@ -7,7 +7,6 @@
 from jax.experimental.pallas import tpu as pltpu
 from jax.sharding import PartitionSpec as P
 
-PRECISION_TOP = lax.Precision.HIGHEST
 NORM_EPS = 1e-05
 GROUP_EPS = 0.00064
 
@@ -28,7 +27,7 @@
 
 def dense_single_float(left, right):
     return jnp.einsum(
-        "...i,ij->...j", left, right, precision=PRECISION_TOP, preferred_element_type=jnp.float32
+        "...i,ij->...j", left, right, preferred_element_type=jnp.float32
     )
 
 
@@ -37,16 +36,6 @@
     centered = values - mean_val
     variance = jnp.mean(centered * centered, axis=-1, keepdims=True)
     return centered * lax.rsqrt(variance + NORM_EPS) * scale_row + shift_row
-
-
-def group_norm(values, scale_rows, shift_rows):
-    mean_val = jnp.mean(values, axis=-1, keepdims=True)
-    centered = values - mean_val
-    variance = jnp.mean(centered * centered, axis=-1, keepdims=True)
-    return (
-        centered * lax.rsqrt(variance + GROUP_EPS) * scale_rows[None, :, None, :]
-        + shift_rows[None, :, None, :]
-    )
 
 
 def token_mixture(
@@ -62,7 +51,6 @@
         "stri,rid->rstd",
         hidden_mixture.reshape(seq_count, length, 5, rank_count),
         lowrank_up.reshape(5, rank_count, feature_columns),
-        precision=PRECISION_TOP,
     )
     mixed_input = [
         normalized_rows
@@ -86,58 +74,420 @@
     )
 
 
-def span_totals(lookup_array_entries, payload_array_entries, natural_log_fading):
-    cumulative = jnp.cumsum(-jnp.exp(natural_log_fading), axis=2)
-    final_cum = cumulative[:, :, -1:, :]
-    carried = jnp.einsum(
-        "shtk,shtv->shkv",
-        lookup_array_entries * jnp.exp(final_cum - cumulative),
-        payload_array_entries,
-        precision=PRECISION_TOP,
-    )
-    return (jnp.exp(final_cum[:, :, 0, :]), carried)
-
-
-def segment_output(
-    acceptance_entries_list,
-    lookup_array_entries,
-    payload_array_entries,
-    natural_log_fading,
-    initial_reward_vector,
-    arriving_carry_tensor,
+WIDE = 256
+PAIR = 128
+EXTRA = 16
+
+
+def halves_dot(left, right, dims):
+    return lax.dot_general(
+        left.astype(jnp.bfloat16),
+        right.astype(jnp.bfloat16),
+        (dims, ((), ())),
+        preferred_element_type=jnp.float32,
+    )
+
+
+def exact_dot(ones, values):
+    high = values.astype(jnp.bfloat16)
+    rest = values - high.astype(jnp.float32)
+    middle = rest.astype(jnp.bfloat16)
+    low = (rest - middle.astype(jnp.float32)).astype(jnp.bfloat16)
+    ones = ones.astype(jnp.bfloat16)
+    dims = ((1,), (0,))
+    return (
+        halves_dot(ones, high, dims) + halves_dot(ones, middle, dims) + halves_dot(ones, low, dims)
+    )
+
+
+def iota(shape, dim):
+    return lax.broadcasted_iota(jnp.int32, shape, dim)
+
+
+def first_head(shape):
+    return iota(shape, len(shape) - 1) < PAIR // 2
+
+
+def compact(full):
+    top, low = full[: PAIR // 2], full[PAIR // 2 :]
+    return jnp.where(first_head(top.shape), top, low)
+
+
+def spread(state):
+    first = first_head(state.shape)
+    return jnp.concatenate([jnp.where(first, state, 0.0), jnp.where(first, 0.0, state)], axis=0)
+
+
+def head_sum(values):
+    first = first_head(values.shape)
+    a = jnp.sum(jnp.where(first, values, 0.0), axis=-1, keepdims=True)
+    b = jnp.sum(jnp.where(first, 0.0, values), axis=-1, keepdims=True)
+    return jnp.where(first, a, b)
+
+
+def running_decay(log_rates):
+    length = log_rates.shape[0]
+    rates = -jnp.exp(log_rates)
+    up_to = iota((length, length), 0) >= iota((length, length), 1)
+    return rates, exact_dot(up_to.astype(jnp.float32), rates)
+
+
+def two_parts(row):
+    high = row.astype(jnp.bfloat16).astype(jnp.float32)
+    return high, row - high
+
+
+def totals_kernel(kv_ref, log_ref, packed_ref):
+    for pair in range(WIDE // PAIR):
+        lanes = slice(pair * PAIR, (pair + 1) * PAIR)
+        keys, values = kv_ref[1, :, lanes], kv_ref[2, :, lanes]
+        rates, total = running_decay(log_ref[:, lanes])
+        length = rates.shape[0]
+        final = total[length - 1 : length]
+        state = compact(halves_dot(keys * jnp.exp(final - total), values, ((0,), (0,))))
+        decay = jnp.exp(rates)
+        rows = [
+            *two_parts(jnp.exp(final)),
+            *two_parts(jnp.min(decay, axis=0, keepdims=True)),
+            *two_parts(jnp.max(decay, axis=0, keepdims=True)),
+        ]
+        row_at = iota((EXTRA, PAIR), 0)
+        extra = jnp.zeros((EXTRA, PAIR), jnp.float32)
+        for at, row in enumerate(rows):
+            extra = jnp.where(row_at == at, row, extra)
+        packed_ref[0, pair] = jnp.concatenate([state, extra], axis=0).astype(jnp.bfloat16)
+
+
+def inner_scores(receive, keys, rates, total):
+    length = receive.shape[0]
+    before = total - rates
+    middle = before[length // 2 : length // 2 + 1]
+    up, down = jnp.exp(before - middle), jnp.exp(middle - total)
+    rows, columns = receive * up, keys * down
+    first = first_head(rows.shape)
+    later = iota((length, length), 0) > iota((length, length), 1)
+    columns = columns.astype(jnp.bfloat16)
+    scores = [
+        jnp.where(
+            later, halves_dot(jnp.where(own, rows, 0.0), columns, ((1,), (1,))), 0.0
+        ).astype(jnp.bfloat16)
+        for own in (first, jnp.logical_not(first))
+    ]
+    return rows.astype(jnp.bfloat16), columns, scores, up, down, before
+
+
+def heads_apply(left, right, side):
+    first = first_head(right.shape)
+    a = halves_dot(left[0], right, ((side,), (0,)))
+    b = halves_dot(left[1], right, ((side,), (0,)))
+    return jnp.where(first, a, b)
+
+
+def inner_kernel(rkv_ref, log_ref, bonus_ref, inner_ref, decayed_ref):
+    for pair in range(WIDE // PAIR):
+        lanes = slice(pair * PAIR, (pair + 1) * PAIR)
+        receive, keys, values = (rkv_ref[n, :, lanes] for n in range(3))
+        rates, total = running_decay(log_ref[:, lanes])
+        _, _, scores, _, _, before = inner_scores(receive, keys, rates, total)
+        now = head_sum(receive * bonus_ref[:, lanes] * keys)
+        inner_ref[:, lanes] = heads_apply(scores, values, 1) + now * values
+        decayed_ref[:, lanes] = (receive * jnp.exp(before)).astype(jnp.bfloat16)
+
+
+def block_decays(extra):
+    blocks = extra.shape[0]
+    flat = extra.astype(jnp.float32)
+    columns = []
+    for start in range(0, blocks, PAIR // EXTRA):
+        some = flat[start : start + PAIR // EXTRA]
+        some = some.reshape(some.shape[0] * EXTRA, PAIR)
+        if some.shape[0] < PAIR:
+            some = jnp.concatenate(
+                [some, jnp.zeros((PAIR - some.shape[0], PAIR), jnp.float32)], axis=0
+            )
+        turned = some.T
+        for k in range(min(PAIR // EXTRA, blocks - start)):
+            both = turned[:, k * EXTRA : k * EXTRA + 1] + turned[:, k * EXTRA + 1 : k * EXTRA + 2]
+            columns.append(compact(jnp.broadcast_to(both, (PAIR, PAIR))))
+    return columns
+
+
+def norm_heads(wkv, count):
+    mean = head_sum(wkv) * (1.0 / count)
+    centered = wkv - mean
+    scale = lax.rsqrt(head_sum(centered * centered) * (1.0 / count) + GROUP_EPS)
+    return centered * scale, scale
+
+
+def join_kernel(
+    place_ref, inner_ref, decayed_ref, gate_ref, packed_ref, start_ref, gain_ref, bias_ref, *outs
 ):
-    decrement = -jnp.exp(natural_log_fading)
-    cumulative = jnp.cumsum(decrement, axis=2)
-    before = cumulative - decrement
-    length = acceptance_entries_list.shape[2]
-    middle = before[:, :, length // 2 : length // 2 + 1, :]
-    carried = jnp.einsum(
-        "shtk,shkv->shtv",
-        acceptance_entries_list * jnp.exp(before),
-        arriving_carry_tensor,
-        precision=PRECISION_TOP,
-    )
-    scores = jnp.einsum(
-        "shtk,shuk->shtu",
-        acceptance_entries_list * jnp.exp(before - middle),
-        lookup_array_entries * jnp.exp(middle - cumulative),
-        precision=PRECISION_TOP,
-    )
-    positions = lax.broadcasted_iota(jnp.int32, (length, length), 0)
-    sources = lax.broadcasted_iota(jnp.int32, (length, length), 1)
-    scores = jnp.where(positions > sources, scores, 0.0)
-    within = jnp.einsum("shtu,shuv->shtv", scores, payload_array_entries, precision=PRECISION_TOP)
-    current = (
-        jnp.sum(
-            acceptance_entries_list
-            * initial_reward_vector[None, :, None, :]
-            * lookup_array_entries,
-            axis=-1,
-            keepdims=True,
+    wkv_ref, mixer_ref, state_ref = outs
+    blocks = packed_ref.shape[0]
+    place = place_ref[0]
+    for pair in range(WIDE // PAIR):
+        lanes = slice(pair * PAIR, (pair + 1) * PAIR)
+        state = start_ref[0, pair]
+        decays = block_decays(packed_ref[:, 0, pair, PAIR // 2 :, :])
+        for k in range(blocks - 1):
+            term = packed_ref[k, 0, pair, : PAIR // 2, :].astype(jnp.float32)
+            state = jnp.where(k < place, decays[k] * state + term, state)
+        state_ref[0, pair] = state
+        wkv = inner_ref[:, lanes] + halves_dot(decayed_ref[:, lanes], spread(state), ((1,), (0,)))
+        wkv_ref[:, lanes] = wkv
+        normed, _ = norm_heads(wkv, PAIR // 2)
+        normed = normed * gain_ref[:, lanes] + bias_ref[:, lanes]
+        gate = gate_ref[0, :, lanes]
+        mixer_ref[:, lanes] = (normed * gate * jax.nn.sigmoid(gate)).astype(jnp.bfloat16)
+
+
+def put_rows(rows):
+    row_at = iota((8, PAIR), 0)
+    out = jnp.zeros((8, PAIR), jnp.float32)
+    for at, row in enumerate(rows):
+        out = jnp.where(row_at == at, row, out)
+    return out
+
+
+def back_join_kernel(grad_ref, wkv_ref, gate_ref, decayed_ref, gain_ref, bias_ref, *outs):
+    grad_wkv_ref, grad_gate_ref, term_ref, sums_ref = outs
+    for pair in range(WIDE // PAIR):
+        lanes = slice(pair * PAIR, (pair + 1) * PAIR)
+        grad, gate = grad_ref[:, lanes], gate_ref[0, :, lanes]
+        gain = gain_ref[:, lanes]
+        hat, scale = norm_heads(wkv_ref[:, lanes], PAIR // 2)
+        sigmoid = jax.nn.sigmoid(gate)
+        normed = hat * gain + bias_ref[:, lanes]
+        grad_gate = grad * normed * sigmoid * (1.0 + gate * (1.0 - sigmoid))
+        grad_gate_ref[:, lanes] = grad_gate.astype(jnp.bfloat16)
+        grad_normed = grad * gate * sigmoid
+        sums_ref[0, :, lanes] = put_rows(
+            [
+                jnp.sum(grad_normed * hat, axis=0, keepdims=True),
+                jnp.sum(grad_normed, axis=0, keepdims=True),
+            ]
         )
-        * payload_array_entries
-    )
-    return carried + within + current
+        q = grad_normed * gain
+        each = 2.0 / PAIR
+        grad_wkv = scale * (q - head_sum(q) * each - hat * (head_sum(q * hat) * each))
+        grad_wkv_ref[:, lanes] = grad_wkv
+        term_ref[0, pair] = compact(
+            halves_dot(decayed_ref[:, lanes], grad_wkv, ((0,), (0,)))
+        ).astype(jnp.bfloat16)
+
+
+def back_inner_kernel(rkv_ref, log_ref, bonus_ref, grad_ref, state_ref, *outs):
+    receive_ref, key_ref, value_ref, running_ref, sums_ref = outs
+    for pair in range(WIDE // PAIR):
+        lanes = slice(pair * PAIR, (pair + 1) * PAIR)
+        receive, keys, values = (rkv_ref[n, :, lanes] for n in range(3))
+        bonus, grad = bonus_ref[:, lanes], grad_ref[:, lanes]
+        rates, total = running_decay(log_ref[:, lanes])
+        rows, columns, scores, up, down, before = inner_scores(receive, keys, rates, total)
+        length = receive.shape[0]
+        first = first_head(values.shape)
+        later = iota((length, length), 0) > iota((length, length), 1)
+        low_values = values.astype(jnp.bfloat16)
+        low_grad = grad.astype(jnp.bfloat16)
+        grad_scores = [
+            jnp.where(
+                later, halves_dot(jnp.where(own, grad, 0.0), low_values, ((1,), (1,))), 0.0
+            ).astype(jnp.bfloat16)
+            for own in (first, jnp.logical_not(first))
+        ]
+        from_state = halves_dot(low_grad, spread(state_ref[0, pair]), ((1,), (1,)))
+        far_receive = heads_apply(grad_scores, columns, 1) * up + jnp.exp(before) * from_state
+        far_keys = heads_apply(grad_scores, rows, 0) * down
+        meet = head_sum(grad * values)
+        receive_ref[:, lanes] = (far_receive + bonus * keys * meet).astype(jnp.bfloat16)
+        key_ref[:, lanes] = far_keys + bonus * receive * meet
+        now = head_sum(receive * bonus * keys)
+        value_ref[:, lanes] = heads_apply(scores, low_grad, 0) + now * grad
+        moved = receive * far_receive
+        moved = pltpu.roll(moved, length - 1, 0)
+        moved = jnp.where(iota(moved.shape, 0) == length - 1, 0.0, moved)
+        running_ref[:, lanes] = moved - keys * far_keys
+        sums_ref[0, :, lanes] = put_rows([jnp.sum(receive * keys * meet, axis=0, keepdims=True)])
+
+
+def back_outer_kernel(
+    place_ref, kv_ref, log_ref, key_ref, value_ref, running_ref, state_ref, packed_ref, terms_ref, *outs
+):
+    grad_key_ref, grad_value_ref, grad_log_ref, start_ref, sums_ref = outs
+    blocks = packed_ref.shape[0]
+    place = place_ref[0]
+    for pair in range(WIDE // PAIR):
+        lanes = slice(pair * PAIR, (pair + 1) * PAIR)
+        keys, values = kv_ref[1, :, lanes], kv_ref[2, :, lanes]
+        rates, total = running_decay(log_ref[:, lanes])
+        length = keys.shape[0]
+        final = total[length - 1 : length]
+        decays = block_decays(packed_ref[:, 0, pair, PAIR // 2 :, :])
+        later = jnp.zeros((PAIR // 2, PAIR), jnp.float32)
+        whole = jnp.zeros((PAIR // 2, PAIR), jnp.float32)
+        for k in range(blocks - 1, -1, -1):
+            term = terms_ref[k, 0, pair].astype(jnp.float32)
+            later = jnp.where(k > place, decays[k] * later + term, later)
+            whole = decays[k] * whole + term
+        start_ref[0, pair] = whole
+        spread_later = spread(later).astype(jnp.bfloat16)
+        fade = jnp.exp(final - total)
+        far_keys = fade * halves_dot(values, spread_later, ((1,), (1,)))
+        grad_key_ref[:, lanes] = (key_ref[:, lanes] + far_keys).astype(jnp.bfloat16)
+        grad_value_ref[:, lanes] = (
+            value_ref[:, lanes] + halves_dot(keys * fade, spread_later, ((1,), (0,)))
+        ).astype(jnp.bfloat16)
+        moved = keys * far_keys
+        met = spread(state_ref[0, pair] * later)
+        high, low = two_parts(met)
+        ones = jnp.ones((8, PAIR), jnp.bfloat16)
+        met_row = (halves_dot(ones, high, ((1,), (1,))) + halves_dot(ones, low, ((1,), (1,))))[:1]
+        last = jnp.sum(moved, axis=0, keepdims=True) + jnp.exp(final) * met_row
+        running = running_ref[:, lanes] - moved
+        running = running + jnp.where(iota(running.shape, 0) == length - 1, last, 0.0)
+        onward = iota((length, length), 0) <= iota((length, length), 1)
+        grad_log = exact_dot(onward.astype(jnp.float32), running) * rates
+        grad_log_ref[:, lanes] = grad_log
+        sums_ref[0, :, lanes] = put_rows([jnp.sum(grad_log, axis=0, keepdims=True)])
+
+
+class Recurrence:
+    def __init__(self, sequences, length, columns):
+        self.sequences, self.length, self.columns = sequences, length, columns
+        self.grid = (sequences, columns // WIDE)
+        self.pairs = columns // PAIR
+        self.tokens = pl.BlockSpec((length, WIDE), lambda s, p: (s, p))
+        self.row = pl.BlockSpec((1, WIDE), lambda s, p: (0, p))
+        self.stack = pl.BlockSpec((3, length, WIDE), lambda s, p: (0, s, p))
+        self.gate = pl.BlockSpec((1, length, WIDE), lambda s, p: (3, s, p))
+        self.state = pl.BlockSpec((1, WIDE // PAIR, PAIR // 2, PAIR), lambda s, p: (s, p, 0, 0))
+        self.sums = pl.BlockSpec((1, 8, WIDE), lambda s, p: (s, 0, p))
+        self.place = pl.BlockSpec(memory_space=pltpu.SMEM)
+
+    def packed(self, blocks=None):
+        rows = PAIR // 2 + EXTRA
+        if blocks is None:
+            return pl.BlockSpec((1, WIDE // PAIR, rows, PAIR), lambda s, p: (s, p, 0, 0))
+        return pl.BlockSpec((blocks, 1, WIDE // PAIR, rows, PAIR), lambda s, p: (0, s, p, 0, 0))
+
+    def terms(self, blocks):
+        return pl.BlockSpec(
+            (blocks, 1, WIDE // PAIR, PAIR // 2, PAIR), lambda s, p: (0, s, p, 0, 0)
+        )
+
+    def token_shape(self, kind):
+        return jax.ShapeDtypeStruct((self.sequences * self.length, self.columns), kind)
+
+    def state_shape(self, kind, rows=PAIR // 2):
+        return jax.ShapeDtypeStruct((self.sequences, self.pairs, rows, PAIR), kind)
+
+    def sums_shape(self):
+        return jax.ShapeDtypeStruct((self.sequences, 8, self.columns), jnp.float32)
+
+    def call(self, kernel, ins, outs, args, flops):
+        size = sum(arg.size * arg.dtype.itemsize for arg in args)
+        return pl.pallas_call(
+            kernel,
+            grid=self.grid,
+            in_specs=ins,
+            out_specs=[spec for spec, _ in outs],
+            out_shape=[shape for _, shape in outs],
+            compiler_params=pltpu.CompilerParams(vmem_limit_bytes=40 * 2**20),
+            cost_estimate=pl.CostEstimate(
+                flops=flops, bytes_accessed=size, transcendentals=6 * args[0].size
+            ),
+        )(*args)
+
+    def totals(self, projected, log_rows):
+        outs = [(self.packed(), self.state_shape(jnp.bfloat16, PAIR // 2 + EXTRA))]
+        return self.call(
+            totals_kernel, [self.stack, self.tokens], outs, (projected, log_rows), 10**9
+        )[0]
+
+    def inner(self, projected, log_rows, bonus):
+        outs = [
+            (self.tokens, self.token_shape(jnp.float32)),
+            (self.tokens, self.token_shape(jnp.bfloat16)),
+        ]
+        ins = [self.stack, self.tokens, self.row]
+        return self.call(inner_kernel, ins, outs, (projected, log_rows, bonus), 2 * 10**9)
+
+    def join(self, place, inner, decayed, projected, packed, start, gain, bias):
+        ins = [
+            self.place,
+            self.tokens,
+            self.tokens,
+            self.gate,
+            self.packed(packed.shape[0]),
+            self.state,
+            self.row,
+            self.row,
+        ]
+        outs = [
+            (self.tokens, self.token_shape(jnp.float32)),
+            (self.tokens, self.token_shape(jnp.bfloat16)),
+            (self.state, self.state_shape(jnp.float32)),
+        ]
+        args = (place, inner, decayed, projected, packed, start, gain, bias)
+        return self.call(join_kernel, ins, outs, args, 10**9)
+
+    def back_join(self, grad, wkv, projected, decayed, gain, bias):
+        ins = [self.tokens, self.tokens, self.gate, self.tokens, self.row, self.row]
+        outs = [
+            (self.tokens, self.token_shape(jnp.float32)),
+            (self.tokens, self.token_shape(jnp.bfloat16)),
+            (self.state, self.state_shape(jnp.bfloat16)),
+            (self.sums, self.sums_shape()),
+        ]
+        args = (grad, wkv, projected, decayed, gain, bias)
+        return self.call(back_join_kernel, ins, outs, args, 10**9)
+
+    def back_inner(self, projected, log_rows, bonus, grad, state):
+        ins = [self.stack, self.tokens, self.row, self.tokens, self.state]
+        outs = [
+            (self.tokens, self.token_shape(jnp.bfloat16)),
+            (self.tokens, self.token_shape(jnp.float32)),
+            (self.tokens, self.token_shape(jnp.float32)),
+            (self.tokens, self.token_shape(jnp.float32)),
+            (self.sums, self.sums_shape()),
+        ]
+        args = (projected, log_rows, bonus, grad, state)
+        return self.call(back_inner_kernel, ins, outs, args, 4 * 10**9)
+
+    def back_outer(self, place, projected, log_rows, keys, values, running, state, packed, terms):
+        blocks = packed.shape[0]
+        ins = [
+            self.place,
+            self.stack,
+            self.tokens,
+            self.tokens,
+            self.tokens,
+            self.tokens,
+            self.state,
+            self.packed(blocks),
+            self.terms(blocks),
+        ]
+        outs = [
+            (self.tokens, self.token_shape(jnp.bfloat16)),
+            (self.tokens, self.token_shape(jnp.bfloat16)),
+            (self.tokens, self.token_shape(jnp.float32)),
+            (self.state, self.state_shape(jnp.float32)),
+            (self.sums, self.sums_shape()),
+        ]
+        args = (place, projected, log_rows, keys, values, running, state, packed, terms)
+        return self.call(back_outer_kernel, ins, outs, args, 3 * 10**9)
+
+
+def paired_states(states):
+    sequences, heads, size, _ = states.shape
+    pairs = states.reshape(sequences, heads // 2, 2, size, size)
+    return pairs.transpose(0, 1, 3, 2, 4).reshape(sequences, heads // 2, size, 2 * size)
+
+
+def single_states(pairs):
+    sequences, count, size, _ = pairs.shape
+    heads = pairs.reshape(sequences, count, size, 2, size).transpose(0, 1, 3, 2, 4)
+    return heads.reshape(sequences, 2 * count, size, size)
 
 
 def packed_gather(pieces):
@@ -489,12 +839,6 @@
     tokens = seq_count * length
     own_cols = channel_recept.shape[1]
 
-    def split_heads(rows):
-        return rows.reshape(seq_count, length, heads_here, head_size).transpose(0, 2, 1, 3)
-
-    def join_heads(rows):
-        return rows.transpose(0, 2, 1, 3).reshape(seq_count, length, head_cols)
-
     def both_halves(own):
         other = other_half(own)
         low = jnp.where(half == 0, own, other)
@@ -531,52 +875,28 @@
     )
     stacked = jnp.stack(mixed_input[:4]).astype(jnp.bfloat16).reshape(4, tokens, feature_columns)
     projected = jnp.einsum("ntd,nde->nte", stacked, projections, preferred_element_type=jnp.float32)
-    acceptance_entries_list = split_heads(projected[0])
-    lookup_array_entries = split_heads(projected[1])
-    payload_array_entries = split_heads(projected[2])
-    gate_pre = projected[3].reshape(seq_count, length, head_cols)
-    gate_act = jax.nn.silu(gate_pre)
-    logarithm_heads = split_heads(log_rows)
-    (decay_prod, carried), totals_back = jax.vjp(
-        span_totals, lookup_array_entries, payload_array_entries, logarithm_heads
-    )
-    decay_heads = jnp.exp(-jnp.exp(logarithm_heads))
-    stat_least = jnp.min(decay_heads, axis=(2, 3))
-    stat_most = jnp.max(decay_heads, axis=(2, 3))
-    small = jnp.concatenate(
-        [decay_prod, stat_least[..., None], stat_most[..., None]], axis=-1
-    )
-    all_small = lax.all_gather(small, "seq")
-    all_decay = all_small[..., :head_size]
-    total_least = jnp.min(all_small[..., head_size], axis=0)
-    total_most = jnp.max(all_small[..., head_size + 1], axis=0)
-    all_carried = lax.all_gather(carried.astype(jnp.bfloat16), "seq")
-    ahead = [jnp.ones_like(decay_prod)]
-    for k in range(blocks):
-        ahead.append(ahead[-1] * all_decay[k])
-    prefix_decay = jnp.ones_like(decay_prod)
-    prefix_state = jnp.zeros_like(carried)
-    for k in range(blocks - 1):
-        reached = k < place
-        prefix_decay = jnp.where(reached, prefix_decay * all_decay[k], prefix_decay)
-        prefix_state = jnp.where(
-            reached,
-            all_decay[k][..., None] * prefix_state + all_carried[k].astype(jnp.float32),
-            prefix_state,
-        )
-    arriving_carry_tensor = prefix_decay[..., None] * initial_state + prefix_state
-    wkv, output_back = jax.vjp(
-        segment_output,
-        acceptance_entries_list,
-        lookup_array_entries,
-        payload_array_entries,
-        logarithm_heads,
-        reward_array_entries,
-        arriving_carry_tensor,
-    )
-    normed_heads, group_back = jax.vjp(group_norm, wkv, group_scale, group_shift)
-    normed_rows = join_heads(normed_heads)
-    mixer_in = (normed_rows * gate_act).astype(jnp.bfloat16)
+    recurrence = Recurrence(seq_count, length, head_cols)
+    log_flat = log_rows.reshape(tokens, head_cols)
+    bonus = reward_array_entries.reshape(1, head_cols)
+    group_scale, group_shift = group_scale.reshape(1, -1), group_shift.reshape(1, -1)
+    where_here = place.astype(jnp.int32).reshape(1)
+    all_packed = lax.all_gather(recurrence.totals(projected, log_flat), "seq")
+    inner, decayed = recurrence.inner(projected, log_flat, bonus)
+    wkv, mixer_rows, state = recurrence.join(
+        where_here,
+        inner,
+        decayed,
+        projected,
+        all_packed,
+        paired_states(initial_state),
+        group_scale,
+        group_shift,
+    )
+    mixer_in = mixer_rows.reshape(seq_count, length, head_cols)
+    extra = all_packed[..., head_size : head_size + 6, :].astype(jnp.float32)
+    extra = extra.reshape(blocks, seq_count, heads_here // 2, 3, 2, 2, head_size).sum(axis=4)
+    total_least = jnp.min(extra[:, :, :, 1], axis=(0, 4)).reshape(seq_count, heads_here)
+    total_most = jnp.max(extra[:, :, :, 2], axis=(0, 4)).reshape(seq_count, heads_here)
     mixer_part = jnp.einsum("std,de->ste", mixer_in, out_proj, preferred_element_type=jnp.float32)
     residual = (
         input_f + mixer_part + other_half(mixer_part.astype(jnp.bfloat16)).astype(jnp.float32)
@@ -603,6 +923,24 @@
     grad_value = (grad_out * gate_chan).astype(jnp.bfloat16)
     grad_recept = (grad_out * kv_rows * gate_chan * (1.0 - gate_chan)).astype(jnp.bfloat16)
     full_value = both_halves(grad_value)
+
+    def weight_terms(left, right):
+        return jnp.einsum(
+            "td,tf->df",
+            left.reshape(tokens, -1),
+            right.reshape(tokens, -1),
+            preferred_element_type=jnp.float32,
+        ).astype(jnp.bfloat16)
+
+    def scattered(whole):
+        return lax.psum_scatter(whole, ("dp", "seq"), scatter_dimension=0, tiled=True).astype(
+            jnp.float32
+        )
+
+    full_value, value_whole = lax.optimization_barrier(
+        (full_value, weight_terms(full_value, hidden))
+    )
+    value_sum = scattered(value_whole)
     grad_hidden = jnp.einsum(
         "std,fd->stf", full_value, channel_value, preferred_element_type=jnp.float32
     )
@@ -615,58 +953,49 @@
     from_next_two = from_behind(for_sending(part_prev_two), "seq", -1).astype(jnp.float32)
     part_normed_two = part_normed_two.at[:, -1, :].add(from_next_two)
     sizes = (lax.axis_size("dp"), blocks)
-    flat_value = full_value.reshape(tokens, -1)
-    key_sum, value_sum, recept_sum = ring_sums(
-        [
-            (chan_key_b.reshape(tokens, -1), grad_key.reshape(tokens, -1), ()),
-            (flat_value, hidden.reshape(tokens, -1), ()),
-            (chan_recept_b.reshape(tokens, -1), grad_recept.reshape(tokens, -1), ()),
-        ],
-        sizes,
-        0,
-    )
+    key_whole = weight_terms(chan_key_b, grad_key)
     grad_normed_two = part_normed_two + other_half(part_normed_two.astype(jnp.bfloat16)).astype(
         jnp.float32
     )
     grad_residual, grad_gain_two, grad_bias_two = norm_two_back(grad_normed_two)
     grad_residual = grad_residual + full_out.astype(jnp.float32)
+    grad_residual, key_whole = lax.optimization_barrier((grad_residual, key_whole))
+    key_sum = scattered(key_whole)
     grad_branch = grad_residual.astype(jnp.bfloat16)
     grad_mixer = jnp.einsum(
         "ste,de->std", grad_branch, out_proj, preferred_element_type=jnp.float32
     )
-    grad_normed_rows = grad_mixer * gate_act
-    gate_sig = jax.nn.sigmoid(gate_pre)
-    grad_gate = grad_mixer * normed_rows * gate_sig * (1.0 + gate_pre * (1.0 - gate_sig))
-    grad_wkv, group_gain_grad, group_bias_grad = group_back(split_heads(grad_normed_rows))
-    (
-        receptance_gradient,
-        key_gradient_output,
-        value_gradient_output,
-        logarithm_gradient_output,
-        reward_cotangent_term,
-        incoming_gradient,
-    ) = output_back(grad_wkv)
-    all_incoming = lax.all_gather(incoming_gradient.astype(jnp.bfloat16), "seq")
-    later_grad = jnp.zeros_like(incoming_gradient)
-    state_grad = jnp.zeros_like(incoming_gradient)
-    for k in range(blocks - 1, -1, -1):
-        term = all_incoming[k].astype(jnp.float32)
-        state_grad = state_grad + ahead[k][..., None] * term
-        later_grad = jnp.where(k > place, all_decay[k][..., None] * later_grad + term, later_grad)
-    grad_decay_prod = jnp.sum(later_grad * arriving_carry_tensor, axis=-1)
-    grad_keys_tot, grad_values_tot, grad_logs_tot = totals_back((grad_decay_prod, later_grad))
-    grad_proj = jnp.stack(
-        [
-            join_heads(receptance_gradient).reshape(tokens, head_cols),
-            join_heads(key_gradient_output + grad_keys_tot).reshape(tokens, head_cols),
-            join_heads(value_gradient_output + grad_values_tot).reshape(tokens, head_cols),
-            grad_gate.reshape(tokens, head_cols),
-        ]
-    ).astype(jnp.bfloat16)
+    grad_wkv, grad_gate, block_term, group_sums = recurrence.back_join(
+        grad_mixer.reshape(tokens, head_cols), wkv, projected, decayed, group_scale, group_shift
+    )
+    all_terms = lax.all_gather(block_term, "seq")
+    grad_receive, near_key, near_value, running, bonus_sums = recurrence.back_inner(
+        projected, log_flat, bonus, grad_wkv, state
+    )
+    grad_keys, grad_values, grad_log, start_pairs, rate_sums = recurrence.back_outer(
+        where_here,
+        projected,
+        log_flat,
+        near_key,
+        near_value,
+        running,
+        state,
+        all_packed,
+        all_terms,
+    )
+    state_grad = single_states(start_pairs)
+
+    def head_rows(sums, row):
+        return jnp.sum(sums[:, row], axis=0).reshape(heads_here, head_size)
+
+    group_gain_grad, group_bias_grad = head_rows(group_sums, 0), head_rows(group_sums, 1)
+    reward_cotangent_term, base_grad = head_rows(bonus_sums, 0), head_rows(rate_sums, 0)
+    grad_proj = jnp.stack([grad_receive, grad_keys, grad_values, grad_gate])
+    grad_proj, value_sum = lax.optimization_barrier((grad_proj, value_sum))
     part_inputs = jnp.einsum(
         "nte,nde->ntd", grad_proj, projections, preferred_element_type=jnp.float32
     )
-    part_hdec, lift_grad, base_grad = decay_back(join_heads(logarithm_gradient_output + grad_logs_tot))
+    part_hdec, lift_grad, _ = decay_back(grad_log.reshape(seq_count, length, head_cols))
     part_normed_one, part_prev_one, grad_coeffs_time, down_grad, up_grad, decay_proj_grad = mix_back(
         (
             part_inputs[0].reshape(seq_count, length, feature_columns),
@@ -697,11 +1026,15 @@
         gathered,
     )
     rest = [part + other_half(part) for part in small_sums[:6]] + small_sums[6:]
-    *proj_sums, out_sum = ring_sums(
+    last_branch, key_sum = lax.optimization_barrier((grad_branch, key_sum))
+    *proj_sums, out_sum, recept_sum = ring_sums(
         [(stacked, grad_proj, (branch,)) for branch in range(4)]
-        + [(grad_branch.reshape(tokens, -1), mixer_in.reshape(tokens, -1), ())],
+        + [
+            (last_branch.reshape(tokens, -1), mixer_in.reshape(tokens, -1), ()),
+            (chan_recept_b.reshape(tokens, -1), grad_recept.reshape(tokens, -1), ()),
+        ],
         sizes,
-        1,
+        0,
     )
     coeff_rows = jnp.concatenate([rest[2][:1], rest[2][2:]], axis=0)
     decay_row = rest[2][1:2]

time: 1480 us -> 1220 us (0.82)
  matrix products: 308 us -> 191 us
  waiting for transfers between devices: 341 us -> 424 us
  other arithmetic: 200 us -> 127 us
  local copies, waits for them, and re-layouts: 260 us -> 192 us
  Pallas kernels: 307 us -> 246 us
  blocking collectives: 16.4 us -> 0 us
    pallas_call x2 -> x1, Pallas kernels: 307 us -> 147 us  [ring_sums(): pl.pallas_call(functools.partial(ring_kernel, dp_size, seq_size, rows, wi...]
    pallas_call x0 -> x6, Pallas kernels: none -> 98.9 us  [call(): pl.pallas_call(kernel, grid=self.grid, in_specs=ins, out_specs=[spec for...]
    reduce_scatter x0 -> x2, waiting for transfers between devices: none -> 94.8 us  [scattered(): lax.psum_scatter(whole, ('dp', 'seq'), scatter_dimension=0, tiled=True)]
    dot_general x21 -> x11, matrix products: 149 us -> 67.9 us  [the longest x9 42.3 us: dense_single_float(): jnp.einsum('...i,ij->...j', left, right, preferred_element_type=jnp.float32)]
    another operation x13 -> x5, local copies, waits for them, and re-layouts: 47.6 us -> 0.89 us  [the longest x4 0.52 us: packed_scatter(): whole.reshape(whole.shape[:dim] + (devices, shape[dim]) + whole.shape[dim...]
    another operation x7 -> x5, other arithmetic: 50.3 us -> 15.6 us  [the longest x2 21 us: segment_output(): cumulative = jnp.cumsum(decrement, axis=2)]
    reduce_sum x7 -> x4, other arithmetic: 36.7 us -> 2.6 us  [the longest x1 2.52 us: per_device(): extra.reshape(blocks, seq_count, heads_here // 2, 3, 2, 2, head_size)]
    ppermute x12, waiting for transfers between devices: 165 us -> 138 us  [other_half(): return lax.ppermute(block, 'tp', [(0, 1), (1, 0)])]
  transfers between devices with their start and end apart: 22 -> 24, of which waited for: 12 -> 13; matrix products, arithmetic and copies ran while one was open for 18% -> 30% of each run, Pallas kernels for 21% -> 18%
where the time goes in v3:
time: 1220 us
  waiting for transfers between devices  424 us (35%)
  Pallas kernels  246 us (20%)
  local copies, waits for them, and re-layouts  192 us (16%)
  matrix products  191 us (16%)
  other arithmetic  127 us (10%)
  starting transfers between devices  22.7 us (2%)
  between operations  16.3 us (1%)
    pallas_call x1, Pallas kernels, ring_sums(): pl.pallas_call(functools.partial(ring_kernel, dp_size, seq_size, rows, wi...  147 us
    ppermute x12, waiting for transfers between devices, other_half(): return lax.ppermute(block, 'tp', [(0, 1), (1, 0)])  138 us
    pallas_call x6, Pallas kernels, call(): pl.pallas_call(kernel, grid=self.grid, in_specs=ins, out_specs=[spec for...  98.9 us
    reduce_scatter x2, waiting for transfers between devices, scattered(): lax.psum_scatter(whole, ('dp', 'seq'), scatter_dimension=0, tiled=True)  94.8 us
    unnamed x308, local copies, waits for them, and re-layouts  83.7 us
    all_gather x1, waiting for transfers between devices, per_device(): lax.all_gather(proj_weights, ('dp', 'seq'), axis=1, tiled=True)  73 us
    all_gather x1, waiting for transfers between devices, packed_gather(): everything = lax.all_gather(flat, ('dp', 'seq'))  46.5 us
    dot_general x9, matrix products, dense_single_float(): jnp.einsum('...i,ij->...j', left, right, preferred_element_type=jnp.float32)  42.3 us
  transfers between devices with their start and end apart: 24, of which 13 were waited for; matrix products, arithmetic and copies ran while one was open for 30% of the time, Pallas kernels for 18%

profile of v3, /device:TPU:0, one launch (start us, length us, event | category | flops | bytes accessed | tf_op | source)
XLA Modules:
  0.0 1218.1 jit_solution(8274108070406283285)
XLA Ops:
  22.4 46.5 %all-gather.18.cloned.1.call-done = bf16[16,1,55040]{2,1,0:T(2,128)(2,1)} async-done(((bf16[1,1,55040]{2,1,0:T(2,128)(2,1)}), bf16[16,1,55040]{2,1,0:T(2,128)(2,1)}) %all-gather.18.cloned.1.call-update) | async-done | bytes 1761296 | tf_op jit(solution)/shard_map/all_gather | solution.py:495
  101.3 8.6 fusion.54
  114.4 10.0 add_convert_fusion.5
  124.4 73.0 %all-gather.10.cloned.1.call-done = bf16[4,2048,1024]{2,1,0:T(8,128)(2,1)} async-done(((bf16[4,128,1024]{2,1,0:T(8,128)(2,1)}), bf16[4,2048,1024]{2,1,0:T(8,128)(2,1)}) %all-gather.10.cloned.1.call-update) | async-done | bytes 16777232 | tf_op jit(solution)/shard_map/all_gather | solution.py:834
  197.4 16.6 %fusion.71.rkv_ref.kv_ref.gate_ref = f32[4,512,1024]{2,1,0:T(8,128)S(1)} fusion(bf16[4,2048,1024]{2,1,0:T(8,128)(2,1)} %all-gather.10.cloned.1.call-done, bf16[1,512,2048]{2,1,0:T(8,128)(2,1)} %bitcast.338, bf16[1,512,2048]{2,1,0:T(8,128)(2,1)} %bitcast.340, bf16[1,512,2048]{2,1,0:T(8,128)(2,1)} %bitcast.342, bf16[1,512,2048]{2,1,0:T(8,128)(2,1)} %bitcast.336), kind=kOutput, calls=%fused_computation.186 | convolution fusion | flops 8602517504 | bytes 33554432 | tf_op jit(solution)/shard_map/ntd,nde->nte/dot_general | solution.py:877
  214.0 11.8 shard_map.355
  229.7 4.6 copy.467
  242.4 14.0 %shard_map.354 = (f32[512,1024]{1,0:T(8,128)S(1)}, bf16[512,1024]{1,0:T(8,128)(2,1)S(1)}) custom-call(f32[4,512,1024]{2,1,0:T(8,128)S(1)} %copy-done.1, f32[512,1024]{1,0:T(8,128)S(1)} %bitcast.308, f32[1,1024]{1,0:T(1,128)S(1)} %reshape.600.bonus_ref), custom_call_target="tpu_custom_call" | custom-call | flops 2000000000 | bytes 10489856 | tf_op jit(solution)/shard_map/pallas_call | solution.py:389
  257.7 25.8 %all-gather.14.cloned.1.call-done = bf16[32,8,80,128]{3,2,1,0:T(8,128)(2,1)} async-done(((bf16[4,8,80,128]{3,2,1,0:T(8,128)(2,1)}), bf16[32,8,80,128]{3,2,1,0:T(8,128)(2,1)}) %all-gather.14.cloned.1.call-update) | async-done | bytes 5242896 | tf_op jit(solution)/shard_map/all_gather | solution.py:883
  288.8 18.2 %shard_map.356 = (f32[512,1024]{1,0:T(8,128)S(1)}, bf16[512,1024]{1,0:T(8,128)(2,1)S(1)}, f32[4,8,64,128]{3,2,1,0:T(8,128)S(1)}) custom-call(s32[1]{0:T(128)} %bitcast.place_ref, f32[512,1024]{1,0:T(8,128)S(1)} %copy-done.11, bf16[512,1024]{1,0:T(8,128)(2,1)S(1)} %get-tuple-element.80.decayed_ref, f32[4,512,1024]{2,1,0:T(8,128)} %copy-done, ...), custom_call_target="tpu_custom_call" | custom-call | flops 1000000000 | bytes 17833988 | tf_op jit(solution)/shard_map/pallas_call | solution.py:389
  310.3 27.1 %all-gather.12.cloned.1.call-done = bf16[1024,2048]{1,0:T(8,128)(2,1)} async-done(((bf16[1024,128]{1,0:T(8,128)(2,1)}), bf16[1024,2048]{1,0:T(8,128)(2,1)}) %all-gather.12.cloned.1.call-update) | async-done | bytes 4194320 | tf_op jit(solution)/shard_map/all_gather | solution.py:835
  337.4 5.0 fusion.85
  344.0 46.3 %collective-permute-done.1 = bf16[4,128,2048]{2,1,0:T(8,128)(2,1)S(1)} collective-permute-done((bf16[4,128,2048]{2,1,0:T(8,128)(2,1)S(1)}, bf16[4,128,2048]{2,1,0:T(8,128)(2,1)S(1)}, u32[]{:S(2)}, u32[]{:S(2)}) %collective-permute-start.1) | collective-permute-done | bytes 2097184 | tf_op jit(solution)/shard_map/ppermute | solution.py:530
  397.7 6.4 add_convert_fusion
  405.4 13.0 %fusion.8 = f32[4,128,3584]{2,1,0:T(8,128)} fusion(bf16[4,128,2048]{2,1,0:T(8,128)(2,1)S(1)} %get-tuple-element.274, bf16[2048,3584]{1,0:T(8,128)(2,1)} %param.38), kind=kOutput, calls=%fused_computation.11 | convolution fusion | flops 7516192768 | bytes 24117248 | tf_op jit(solution)/shard_map/std,df->stf/dot_general | solution.py:911
  418.5 10.0 fusion.4
  433.1 24.3 %collective-permute-done.3 = bf16[4,128,1024]{2,1,0:T(8,128)(2,1)} collective-permute-done((bf16[4,128,1024]{2,1,0:T(8,128)(2,1)}, bf16[4,128,1024]{2,1,0:T(8,128)(2,1)}, u32[]{:S(2)}, u32[]{:S(2)}) %collective-permute-start.3) | collective-permute-done | bytes 1048608 | tf_op jit(solution)/shard_map/ppermute | solution.py:530
  457.3 9.6 fusion.38
  468.9 24.4 %collective-permute-done.4 = bf16[4,128,1024]{2,1,0:T(8,128)(2,1)} collective-permute-done((bf16[4,128,1024]{2,1,0:T(8,128)(2,1)}, bf16[4,128,1024]{2,1,0:T(8,128)(2,1)}, u32[]{:S(2)}, u32[]{:S(2)}) %collective-permute-start.4) | collective-permute-done | bytes 1048608 | tf_op jit(solution)/shard_map/ppermute | solution.py:530
  496.5 14.5 %bitcast_convert_fusion.1 = bf16[2048,3584]{1,0:T(8,128)(2,1)} fusion(f32[4,128,3584]{2,1,0:T(8,128)} %fusion.8, bf16[4,128,1024]{2,1,0:T(8,128)(2,1)S(1)} %get-tuple-element.290, bf16[4,128,1024]{2,1,0:T(8,128)(2,1)S(1)} %get-tuple-element.289), kind=kOutput, calls=%fused_computation.1 | convolution fusion | flops 7533232128 | bytes 24117248 | tf_op jit(solution)/shard_map/td,tf->df/dot_general | solution.py:928
  511.0 14.3 %multiply_convert_fusion = bf16[4,128,3584]{2,1,0:T(8,128)(2,1)} fusion(f32[4,128,3584]{2,1,0:T(8,128)} %fusion.8, bf16[4,128,2048]{2,1,0:T(8,128)(2,1)} %pad_maximum_fusion.2, bf16[3584,2048]{1,0:T(8,128)(2,1)} %param.39), kind=kOutput, calls=%fused_computation.14 | convolution fusion | flops 7523532800 | bytes 27787264 | tf_op jit(solution)/shard_map/std,fd->stf/dot_general | solution.py:944
  525.4 12.3 %fusion.6 = f32[4,128,2048]{2,1,0:T(8,128)S(1)} fusion(bf16[4,128,3584]{2,1,0:T(8,128)(2,1)} %multiply_convert_fusion, bf16[2048,3584]{1,0:T(8,128)(2,1)} %param.38), kind=kOutput, calls=%fused_computation.9 | convolution fusion | flops 7516192768 | bytes 22544384 | tf_op jit(solution)/shard_map/stf,df->std/dot_general | solution.py:948
  537.6 7.9 multiply_reduce_fusion.1
  557.4 4.0 convert_element_type.243
  566.0 11.1 bitcast_convert_fusion
  577.1 33.0 %collective-permute-done.6 = bf16[4,128,2048]{2,1,0:T(8,128)(2,1)} collective-permute-done((bf16[4,128,2048]{2,1,0:T(8,128)(2,1)}, bf16[4,128,2048]{2,1,0:T(8,128)(2,1)}, u32[]{:S(2)}, u32[]{:S(2)}) %collective-permute-start.6) | collective-permute-done | bytes 2097184 | tf_op jit(solution)/shard_map/ppermute | solution.py:530
  610.1 5.0 multiply_reduce_fusion.4
  627.9 12.7 %shard_map.357 = (f32[512,1024]{1,0:T(8,128)S(1)}, bf16[512,1024]{1,0:T(8,128)(2,1)S(1)}, bf16[4,8,64,128]{3,2,1,0:T(8,128)(2,1)S(1)}, f32[4,8,1024]{2,1,0:T(8,128)S(1)}) custom-call(f32[512,1024]{1,0:T(8,128)S(1)} %bitcast.313, f32[512,1024]{1,0:T(8,128)S(1)} %copy-done.13, f32[4,512,1024]{2,1,0:T(8,128)} %copy-done, ...), custom_call_target="tpu_custom_call" | custom-call | flops 1000000000 | bytes 13639680 | tf_op jit(solution)/shard_map/pallas_call | solution.py:389
  647.9 19.7 %shard_map.358 = (bf16[512,1024]{1,0:T(8,128)(2,1)S(1)}, f32[512,1024]{1,0:T(8,128)S(1)}, f32[512,1024]{1,0:T(8,128)S(1)}, f32[512,1024]{1,0:T(8,128)S(1)}, f32[4,8,1024]{2,1,0:T(8,128)S(1)}) custom-call(f32[4,512,1024]{2,1,0:T(8,128)} %copy-done, f32[512,1024]{1,0:T(8,128)S(1)} %bitcast.309, f32[1,1024]{1,0:T(1,128)S(1)} %copy-done.25, ...), custom_call_target="tpu_custom_call" | custom-call | flops 4000000000 | bytes 13635584 | tf_op jit(solution)/shard_map/pallas_call | solution.py:389
  674.2 16.2 %all-gather.16.cloned.1.call-done = bf16[32,8,64,128]{3,2,1,0:T(8,128)(2,1)} async-done(((bf16[4,8,64,128]{3,2,1,0:T(8,128)(2,1)}), bf16[32,8,64,128]{3,2,1,0:T(8,128)(2,1)}) %all-gather.16.cloned.1.call-update) | async-done | bytes 4194320 | tf_op jit(solution)/shard_map/all_gather | solution.py:971
  694.9 22.5 %shard_map.359 = (bf16[512,1024]{1,0:T(8,128)(2,1)S(1)}, bf16[512,1024]{1,0:T(8,128)(2,1)S(1)}, f32[512,1024]{1,0:T(8,128)S(1)}, f32[4,8,64,128]{3,2,1,0:T(8,128)S(1)}, f32[4,8,1024]{2,1,0:T(8,128)S(1)}) custom-call(s32[1]{0:T(128)} %bitcast.place_ref, f32[4,512,1024]{2,1,0:T(8,128)} %copy-done, f32[512,1024]{1,0:T(8,128)S(1)} %bitcast.310, ...), custom_call_target="tpu_custom_call" | custom-call | flops 3000000000 | bytes 27262980 | tf_op jit(solution)/shard_map/pallas_call | solution.py:389
  723.8 6.2 convolution_bitcast_fusion.1
  748.3 94.8 %reduce-scatter.4.cloned.1.call-done = bf16[128,3584]{1,0:T(8,128)(2,1)} async-done(((bf16[2048,3584]{1,0:T(8,128)(2,1)}), bf16[128,3584]{1,0:T(8,128)(2,1)}) %reduce-scatter.4.cloned.1.call-update) | async-done | bytes 917520 | tf_op jit(solution)/shard_map/reduce_scatter | solution.py:936
  845.7 18.0 %fusion.88 = f32[4,512,2048]{2,1,0:T(8,128)} fusion(bf16[4,512,1024]{2,1,0:T(8,128)(2,1)} %pad_maximum_fusion.1.refs_1_, bf16[4,2048,1024]{2,1,0:T(8,128)(2,1)} %all-gather.10.cloned.1.call-done), kind=kOutput, calls=%fused_computation.200 | convolution fusion | flops 8589934592 | bytes 37748736 | tf_op jit(solution)/shard_map/nte,nde->ntd/dot_general | solution.py:995
  863.7 15.2 %fusion.76 = (f32[1,512,2048]{2,1,0:T(8,128)}, f32[1,512,2048]{2,1,0:T(8,128)}, f32[1,512,2048]{2,1,0:T(8,128)}, f32[1,512,2048]{2,1,0:T(8,128)}) fusion(f32[4,512,2048]{2,1,0:T(8,128)} %fusion.88), kind=kLoop, calls=%fused_computation.189 | loop fusion | bytes 33554432 | tf_op jit(solution)/shard_map/slice | solution.py:1004
  879.8 14.3 %multiply_bitcast_fusion.4 = (f32[1,4,128,2048]{3,2,1,0:T(8,128)}, f32[1,4,128,2048]{3,2,1,0:T(8,128)}, f32[1,4,128,2048]{3,2,1,0:T(8,128)}, f32[1,4,128,2048]{3,2,1,0:T(8,128)}, f32[1,4,128,2048]{3,2,1,0:T(8,128)}) fusion(f32[4,128,2048]{2,1,0:T(8,128)S(1)} %copy-done.37, f32[4,128,2048]{2,1,0:T(8,128)} %bitcast.321, f32[4,128,2048]{2,1,0:T(8,128)S(1)} %copy-done.46, ...), kind=kLoop, calls=%fused_computation.104 | loop fusion | flops 5242880 | bytes 46137344 | tf_op jit(solution)/shard_map/transpose(jvp())/broadcast_in_dim | solution.py:57
  894.1 8.6 pad_add_fusion
  906.8 20.5 %multiply_reduce_fusion.10 = (f32[2048]{0:T(1024)S(1)}, f32[2048]{0:T(1024)S(1)}, f32[2048]{0:T(1024)S(1)}, f32[2048]{0:T(1024)S(1)}, f32[2048]{0:T(1024)S(1)}, ...) fusion(f32[4,128,2048]{2,1,0:T(8,128)} %copy-done.36, f32[4,128,2048]{2,1,0:T(8,128)} %bitcast.322, ...), kind=kOutput, calls=%fused_computation.103 | convolution fusion | flops 364892160 | bytes 55443456 | tf_op jit(solution)/shard_map/transpose(jvp(...i,ij->...j))/dot_general | solution.py:29
  928.2 5.3 split.20
  935.7 4.2 convolution_bitcast_fusion
  943.6 10.9 pad_add_fusion.1
  956.3 4.3 reshape_reshape.27
  981.5 4.0 pad.68
  995.6 3.9 pad_maximum_fusion.refs_0_
  1013.2 6.6 collective-permute-done.9
  1019.8 4.6 add_add_fusion.2
  1027.0 147.4 %shard_map.360 = (f32[128,1024]{1,0:T(8,128)}, f32[128,1024]{1,0:T(8,128)}, f32[128,1024]{1,0:T(8,128)}, f32[128,1024]{1,0:T(8,128)}, f32[128,1024]{1,0:T(8,128)}, /*index=5*/f32[128,1024]{1,0:T(8,128)}) custom-call(bf16[4,512,2048]{2,1,0:T(8,128)(2,1)} %pad_maximum_fusion.refs_0_, bf16[4,512,1024]{2,1,0:T(8,128)(2,1)} %pad_maximum_fusion.1.refs_1_, ...), custom_call_target="tpu_custom_call" | custom-call | flops 12884901888 | bytes 18874368 | tf_op jit(solution)/shard_map/pallas_call | solution.py:751
  1188.4 9.1 slice.302
  (499 shorter events, 255.4 us)
Async XLA Ops:
  7.2 14.5 %copy-start.29 = (bf16[4,128,2048]{2,1,0:T(8,128)(2,1)S(1)}, bf16[4,128,2048]{2,1,0:T(8,128)(2,1)}, u32[]{:S(2)}) copy-start(bf16[4,128,2048]{2,1,0:T(8,128)(2,1)} %param.23) | copy-start | bytes 6291460
  7.2 61.7 %all-gather.18.cloned.1.call-start = ((), (), s32[]{:S(2)}) async-start(), calls=%async_computation.10 | async-start | bytes 3742720 | tf_op jit(solution)/shard_map/all_gather | solution.py:495
  18.9 178.5 %all-gather.10.cloned.1.call-start = ((), (), s32[]{:S(2)}) async-start(), calls=%async_computation.3 | async-start | bytes 17825792 | tf_op jit(solution)/shard_map/all_gather | solution.py:834
  19.7 263.8 %all-gather.14.cloned.1.call-start = ((), (), s32[]{:S(2)}) async-start(), calls=%async_computation.8 | async-start | bytes 5898240 | tf_op jit(solution)/shard_map/all_gather | solution.py:883
  21.7 53.7 %copy-start.103 = (f32[4,128]{1,0:T(4,128)}, f32[4,128]{1,0:T(4,128)S(1)}, u32[]{:S(2)}) copy-start(f32[4,128]{1,0:T(4,128)S(1)} %broadcast_multiply_fusion.3) | copy-start | bytes 6148
  22.4 48.7 %copy-start.126 = (f32[4,128]{1,0:T(4,128)}, f32[4,128]{1,0:T(4,128)S(1)}, u32[]{:S(2)}) copy-start(f32[4,128]{1,0:T(4,128)S(1)} %fusion.20) | copy-start | bytes 6148
  22.4 52.9 %copy-start.110 = (f32[4,128]{1,0:T(4,128)}, f32[4,128]{1,0:T(4,128)S(1)}, u32[]{:S(2)}) copy-start(f32[4,128]{1,0:T(4,128)S(1)} %fusion.66) | copy-start | bytes 6148
  73.9 40.5 %copy-start.83 = (f32[1,16,128]{2,0,1:T(1,128)}, f32[1,16,128]{2,0,1:T(1,128)S(1)}, u32[]{:S(2)}) copy-start(f32[1,16,128]{2,0,1:T(1,128)S(1)} %get-tuple-element.318) | copy-start | bytes 24580
  78.0 17.2 %collective-permute-start = (bf16[4,2048]{1,0:T(4,128)(2,1)}, bf16[4,2048]{1,0:T(4,128)(2,1)}, u32[]{:S(2)}, u32[]{:S(2)}) collective-permute-start(bf16[4,2048]{1,0:T(4,128)(2,1)} %bitcast.298), channel_id=1, source_target_pairs={{0,2},{2,4},{4,6},{6,8},{8,10},{10,12},{12,14},{1,3},{3,5},{5,7},{... | collective-permute-start | bytes 49160 | tf_op jit(solution)/shard_map/ppermute | solution.py:17
  81.6 28.3 %copy-start.88 = (f32[1,16,128]{2,0,1:T(1,128)}, f32[1,16,128]{2,0,1:T(1,128)S(1)}, u32[]{:S(2)}) copy-start(f32[1,16,128]{2,0,1:T(1,128)S(1)} %get-tuple-element.311) | copy-start | bytes 24580
  85.4 24.5 %copy-start.65 = (bf16[2048,64]{1,0:T(8,128)(2,1)}, bf16[2048,64]{1,0:T(8,128)(2,1)S(1)}, u32[]{:S(2)}) copy-start(bf16[2048,64]{1,0:T(8,128)(2,1)S(1)} %reshape_reshape.26) | copy-start | bytes 786436
  95.2 18.7 %copy-start.70 = (bf16[64,16,16,4]{0,3,2,1:T(4,128)(2,1)}, bf16[64,16,16,4]{0,3,2,1:T(4,128)(2,1)S(1)}, u32[]{:S(2)}) copy-start(bf16[64,16,16,4]{0,3,2,1:T(4,128)(2,1)S(1)} %copy.366) | copy-start | bytes 393220
  99.7 14.7 %copy-start.36 = (f32[4,128,2048]{2,1,0:T(8,128)}, f32[4,128,2048]{2,1,0:T(8,128)S(1)}, u32[]{:S(2)}) copy-start(f32[4,128,2048]{2,1,0:T(8,128)S(1)} %maximum_subtract_fusion) | copy-start | bytes 12582916
  229.1 108.3 %all-gather.12.cloned.1.call-start = ((), (), s32[]{:S(2)}) async-start(), calls=%async_computation.4 | async-start | bytes 4456448 | tf_op jit(solution)/shard_map/all_gather | solution.py:835
  229.7 460.8 %all-gather.16.cloned.1.call-start = ((), (), s32[]{:S(2)}) async-start(), calls=%async_computation.9 | async-start | bytes 4718592 | tf_op jit(solution)/shard_map/all_gather | solution.py:971
  238.3 18.0 %copy-start.24 = (f32[1,1024]{1,0:T(1,128)}, f32[1,1024]{1,0:T(1,128)S(1)}, u32[]{:S(2)}) copy-start(f32[1,1024]{1,0:T(1,128)S(1)} %reshape.600.bonus_ref) | copy-start | bytes 12292
  337.4 52.9 %copy-start.31 = (bf16[4,128,2048]{2,1,0:T(8,128)(2,1)S(1)}, bf16[4,128,2048]{2,1,0:T(8,128)(2,1)}, u32[]{:S(2)}) copy-start(bf16[4,128,2048]{2,1,0:T(8,128)(2,1)} %param.23) | copy-start | bytes 6291460
  342.4 47.9 %collective-permute-start.1 = (bf16[4,128,2048]{2,1,0:T(8,128)(2,1)S(1)}, bf16[4,128,2048]{2,1,0:T(8,128)(2,1)S(1)}, u32[]{:S(2)}, u32[]{:S(2)}) collective-permute-start(bf16[4,128,2048]{2,1,0:T(8,128)(2,1)S(1)} %get-tuple-element.323), channel_id=1, source_target_pairs={{0,1},{1,0},{2,3},{3,2},{4,5},{5,4},{6,7},{7,6},{8,9},{9,8},{10,11... | collective-permute-start | bytes 6291464 | tf_op jit(solution)/shard_map/ppermute | solution.py:530
  395.5 2.2 collective-permute-start.2
  397.7 20.7 %slice-start = ((s8[14680064]{0:T(1024)(128)(4,1)}), s8[4194304]{0:T(1024)(128)(4,1)S(1)}, s32[]{:S(2)}) async-start(s8[14680064]{0:T(1024)(128)(4,1)} %bitcast.454), calls=%async_computation.11 | async-start | bytes 8388608
  405.4 13.0 %slice-start.1 = ((s8[14680064]{0:T(1024)(128)(4,1)}), s8[4194304]{0:T(1024)(128)(4,1)S(1)}, s32[]{:S(2)}) async-start(s8[14680064]{0:T(1024)(128)(4,1)} %bitcast.454), calls=%async_computation.12 | async-start | bytes 8388608
  405.4 13.0 %slice-start.2 = ((s8[14680064]{0:T(1024)(128)(4,1)}), s8[4194304]{0:T(1024)(128)(4,1)S(1)}, s32[]{:S(2)}) async-start(s8[14680064]{0:T(1024)(128)(4,1)} %bitcast.454), calls=%async_computation.13 | async-start | bytes 8388608
  405.4 13.0 %slice-start.3 = ((s8[14680064]{0:T(1024)(128)(4,1)}), s8[2097152]{0:T(1024)(128)(4,1)S(1)}, s32[]{:S(2)}) async-start(s8[14680064]{0:T(1024)(128)(4,1)} %bitcast.454), calls=%async_computation.14 | async-start | bytes 4194304
  431.6 25.7 %collective-permute-start.3 = (bf16[4,128,1024]{2,1,0:T(8,128)(2,1)}, bf16[4,128,1024]{2,1,0:T(8,128)(2,1)}, u32[]{:S(2)}, u32[]{:S(2)}) collective-permute-start(bf16[4,128,1024]{2,1,0:T(8,128)(2,1)} %dynamic-slice_convert_fusion.1), channel_id=1, source_target_pairs={{0,1},{1,0},{2,3},{3,2},{4,5},{5,4},{6,7},{7,6},{8,9},{9,8},{10,11... | collective-permute-start | bytes 3145736 | tf_op jit(solution)/shard_map/ppermute | solution.py:530
  466.9 26.4 %collective-permute-start.4 = (bf16[4,128,1024]{2,1,0:T(8,128)(2,1)}, bf16[4,128,1024]{2,1,0:T(8,128)(2,1)}, u32[]{:S(2)}, u32[]{:S(2)}) collective-permute-start(bf16[4,128,1024]{2,1,0:T(8,128)(2,1)} %get-tuple-element.288), channel_id=1, source_target_pairs={{0,1},{1,0},{2,3},{3,2},{4,5},{5,4},{6,7},{7,6},{8,9},{9,8},{10,11... | collective-permute-start | bytes 3145736 | tf_op jit(solution)/shard_map/ppermute | solution.py:530
  468.4 94.5 %collective-permute-start.7 = (bf16[4,128,1024]{2,1,0:T(8,128)(2,1)}, bf16[4,128,1024]{2,1,0:T(8,128)(2,1)}, u32[]{:S(2)}, u32[]{:S(2)}) collective-permute-start(bf16[4,128,1024]{2,1,0:T(8,128)(2,1)} %param.41), channel_id=1, source_target_pairs={{0,1},{1,0},{2,3},{3,2},{4,5},{5,4},{6,7},{7,6},{8,9},{9,8},{10,11... | collective-permute-start | bytes 3145736 | tf_op jit(solution)/shard_map/ppermute | solution.py:530
  548.2 5.4 collective-permute-start.5
  561.4 48.7 %collective-permute-start.6 = (bf16[4,128,2048]{2,1,0:T(8,128)(2,1)}, bf16[4,128,2048]{2,1,0:T(8,128)(2,1)}, u32[]{:S(2)}, u32[]{:S(2)}) collective-permute-start(bf16[4,128,2048]{2,1,0:T(8,128)(2,1)} %convert_element_type.243), channel_id=1, source_target_pairs={{0,1},{1,0},{2,3},{3,2},{4,5},{5,4},{6,7},{7,6},{8,9},{9,8},{10,11... | collective-permute-start | bytes 6291464 | tf_op jit(solution)/shard_map/ppermute | solution.py:530
  577.1 38.0 %copy-start.35 = (f32[4,128,2048]{2,1,0:T(8,128)S(1)}, f32[4,128,2048]{2,1,0:T(8,128)}, u32[]{:S(2)}) copy-start(f32[4,128,2048]{2,1,0:T(8,128)} %copy-done.34) | copy-start | bytes 12582916
  577.1 38.0 %copy-start.40 = (f32[4,128,2048]{2,1,0:T(8,128)S(1)}, f32[4,128,2048]{2,1,0:T(8,128)}, u32[]{:S(2)}) copy-start(f32[4,128,2048]{2,1,0:T(8,128)} %scatter-add.6) | copy-start | bytes 12582916
  643.7 199.4 %reduce-scatter.4.cloned.1.call-start = ((), (), s32[]{:S(2)}) async-start(), calls=%async_computation.5 | async-start | bytes 15597568 | tf_op jit(solution)/shard_map/reduce_scatter | solution.py:936
  644.3 380.1 %reduce-scatter.8.cloned.1.call-start = ((), (), s32[]{:S(2)}) async-start(), calls=%async_computation.7 | async-start | bytes 15597568 | tf_op jit(solution)/shard_map/reduce_scatter | solution.py:936
  674.2 505.4 %reduce-scatter.6.cloned.1.call-start = ((), (), s32[]{:S(2)}) async-start(), calls=%async_computation.6 | async-start | bytes 3760128 | tf_op jit(solution)/shard_map/reduce_scatter | solution.py:518
  694.9 25.8 %copy-start.71 = (bf16[64,16,16,4]{0,3,2,1:T(4,128)(2,1)S(1)}, bf16[64,16,16,4]{0,3,2,1:T(4,128)(2,1)}, u32[]{:S(2)}) copy-start(bf16[64,16,16,4]{0,3,2,1:T(4,128)(2,1)} %copy-done.70) | copy-start | bytes 393220
  694.9 25.8 %copy-start.75 = (f32[4,128,64]{1,2,0:T(8,128)S(1)}, f32[4,128,64]{1,2,0:T(8,128)}, u32[]{:S(2)}) copy-start(f32[4,128,64]{1,2,0:T(8,128)} %copy-done.74) | copy-start | bytes 393220
  863.7 15.2 %copy-start.37 = (f32[4,128,2048]{2,1,0:T(8,128)S(1)}, f32[4,128,2048]{2,1,0:T(8,128)}, u32[]{:S(2)}) copy-start(f32[4,128,2048]{2,1,0:T(8,128)} %copy-done.36) | copy-start | bytes 12582916
  863.7 16.1 %copy-start.46 = (f32[4,128,2048]{2,1,0:T(8,128)S(1)}, f32[4,128,2048]{2,1,0:T(8,128)}, u32[]{:S(2)}) copy-start(f32[4,128,2048]{2,1,0:T(8,128)} %fusion.57) | copy-start | bytes 12582916
  906.7 20.5 %copy-start.85 = (bf16[4,128,160]{1,2,0:T(8,128)(2,1)}, bf16[4,128,160]{1,2,0:T(8,128)(2,1)S(1)}, u32[]{:S(2)}) copy-start(bf16[4,128,160]{1,2,0:T(8,128)(2,1)S(1)} %bitcast_multiply_fusion) | copy-start | bytes 491524
  934.1 26.5 %collective-permute-start.8 = (bf16[4,2048]{1,0:T(4,128)(2,1)}, bf16[4,2048]{1,0:T(4,128)(2,1)}, u32[]{:S(2)}, u32[]{:S(2)}) collective-permute-start(bf16[4,2048]{1,0:T(4,128)(2,1)} %bitcast.300), channel_id=1, source_target_pairs={{2,0},{4,2},{6,4},{8,6},{10,8},{12,10},{14,12},{3,1},{5,3},{7,5},{... | collective-permute-start | bytes 49160 | tf_op jit(solution)/shard_map/ppermute | solution.py:17
  993.4 26.4 %collective-permute-start.9 = (bf16[4,128,1024]{2,1,0:T(8,128)(2,1)}, bf16[4,128,1024]{2,1,0:T(8,128)(2,1)}, u32[]{:S(2)}, u32[]{:S(2)}) collective-permute-start(bf16[4,128,1024]{2,1,0:T(8,128)(2,1)} %dynamic-slice_convert_fusion), channel_id=1, source_target_pairs={{0,1},{1,0},{2,3},{3,2},{4,5},{5,4},{6,7},{7,6},{8,9},{9,8},{10,11... | collective-permute-start | bytes 3145736 | tf_op jit(solution)/shard_map/ppermute | solution.py:530
  1179.6 18.7 %copy-start.80 = (f32[432,128]{1,0:T(8,128)S(1)}, f32[432,128]{1,0:T(8,128)}, u32[]{:S(2)}) copy-start(f32[432,128]{1,0:T(8,128)} %reduce-scatter.6.cloned.1.call-done) | copy-start | bytes 663556
  1180.4 21.9 %collective-permute-start.11 = (f32[2,128]{1,0:T(2,128)S(1)}, f32[2,128]{1,0:T(2,128)S(1)}, u32[]{:S(2)}, u32[]{:S(2)}) collective-permute-start(f32[2,128]{1,0:T(2,128)S(1)} %get-tuple-element.307), channel_id=1, source_target_pairs={{0,1},{1,0},{2,3},{3,2},{4,5},{5,4},{6,7},{7,6},{8,9},{9,8},{10,11... | collective-permute-start | bytes 3080 | tf_op jit(solution)/shard_map/ppermute | solution.py:530
  1181.9 20.5 %collective-permute-start.10 = (f32[2,128]{1,0:T(2,128)S(1)}, f32[2,128]{1,0:T(2,128)S(1)}, u32[]{:S(2)}, u32[]{:S(2)}) collective-permute-start(f32[2,128]{1,0:T(2,128)S(1)} %get-tuple-element.308), channel_id=1, source_target_pairs={{0,1},{1,0},{2,3},{3,2},{4,5},{5,4},{6,7},{7,6},{8,9},{9,8},{10,11... | collective-permute-start | bytes 3080 | tf_op jit(solution)/shard_map/ppermute | solution.py:530
  1183.1 19.8 %collective-permute-start.12 = (f32[8,128]{1,0:T(8,128)S(1)}, f32[8,128]{1,0:T(8,128)S(1)}, u32[]{:S(2)}, u32[]{:S(2)}) collective-permute-start(f32[8,128]{1,0:T(8,128)S(1)} %slice.350), channel_id=1, source_target_pairs={{0,1},{1,0},{2,3},{3,2},{4,5},{5,4},{6,7},{7,6},{8,9},{9,8},{10,11... | collective-permute-start | bytes 12296 | tf_op jit(solution)/shard_map/ppermute | solution.py:530
  1185.4 20.0 %collective-permute-start.15 = (f32[128,64]{1,0:T(8,128)S(1)}, f32[128,64]{1,0:T(8,128)S(1)}, u32[]{:S(2)}, u32[]{:S(2)}) collective-permute-start(f32[128,64]{1,0:T(8,128)S(1)} %reshape.589), channel_id=1, source_target_pairs={{0,1},{1,0},{2,3},{3,2},{4,5},{5,4},{6,7},{7,6},{8,9},{9,8},{10,11... | collective-permute-start | bytes 98312 | tf_op jit(solution)/shard_map/ppermute | solution.py:530
  1186.9 23.1 %copy-start.87 = (f32[128,1024]{1,0:T(8,128)S(1)}, f32[128,1024]{1,0:T(8,128)}, u32[]{:S(2)}) copy-start(f32[128,1024]{1,0:T(8,128)} %get-tuple-element.370) | copy-start | bytes 1572868
  1186.9 16.5 %collective-permute-start.14 = (f32[160,128]{1,0:T(8,128)S(1)}, f32[160,128]{1,0:T(8,128)S(1)}, u32[]{:S(2)}, u32[]{:S(2)}) collective-permute-start(f32[160,128]{1,0:T(8,128)S(1)} %slice.352), channel_id=1, source_target_pairs={{0,1},{1,0},{2,3},{3,2},{4,5},{5,4},{6,7},{7,6},{8,9},{9,8},{10,11... | collective-permute-start | bytes 245768 | tf_op jit(solution)/shard_map/ppermute | solution.py:530
  1204.2 5.0 collective-permute-start.13
  (111 other events, 533.3 us)
Sparse Core Ops, SparseCore 0:
  19.0 49.8 all-gather.17
  71.1 126.2 all-gather.9
  229.2 54.2 all-gather.13
  285.4 51.9 all-gather.11
  643.8 46.6 all-gather.15
  694.4 148.7 reduce-scatter.3
  847.2 148.7 reduce-scatter.7
  999.8 77.4 reduce-scatter.5

commit v4 on v3

--- a/solution.py
+++ b/solution.py
@@ -25,44 +25,11 @@
     return jax.tree.map(short, array)
 
 
-def dense_single_float(left, right):
-    return jnp.einsum(
-        "...i,ij->...j", left, right, preferred_element_type=jnp.float32
-    )
-
-
 def layer_norm(values, scale_row, shift_row):
     mean_val = jnp.mean(values, axis=-1, keepdims=True)
     centered = values - mean_val
     variance = jnp.mean(centered * centered, axis=-1, keepdims=True)
     return centered * lax.rsqrt(variance + NORM_EPS) * scale_row + shift_row
-
-
-def token_mixture(
-    normalized_rows, preceding_row, shift_coefficient, lowrank_down, lowrank_up, decay_projection
-):
-    earlier = jnp.concatenate([preceding_row[:, None, :], normalized_rows[:, :-1, :]], axis=1)
-    shift_difference = earlier - normalized_rows
-    base_value = normalized_rows + shift_difference * shift_coefficient[0]
-    hidden_mixture = jnp.tanh(dense_single_float(base_value, lowrank_down))
-    seq_count, length, feature_columns = normalized_rows.shape
-    rank_count = lowrank_up.shape[0] // 5
-    lowrank_map = jnp.einsum(
-        "stri,rid->rstd",
-        hidden_mixture.reshape(seq_count, length, 5, rank_count),
-        lowrank_up.reshape(5, rank_count, feature_columns),
-    )
-    mixed_input = [
-        normalized_rows
-        + shift_difference * (shift_coefficient[1 + branch_output] + lowrank_map[branch_output])
-        for branch_output in range(5)
-    ]
-    hidden_decay = jnp.tanh(dense_single_float(mixed_input[0], decay_projection))
-    return (mixed_input[3], mixed_input[1], mixed_input[2], mixed_input[4], hidden_decay)
-
-
-def decay_rates(hidden_decay, decay_lift, decay_base):
-    return decay_base + dense_single_float(hidden_decay, decay_lift)
 
 
 def channel_mix(normalized_rows, preceding_row, shift_coefficient):
@@ -222,13 +189,21 @@
 def join_kernel(
     place_ref, inner_ref, decayed_ref, gate_ref, packed_ref, start_ref, gain_ref, bias_ref, *outs
 ):
-    wkv_ref, mixer_ref, state_ref = outs
+    wkv_ref, mixer_ref, state_ref, range_ref = outs
     blocks = packed_ref.shape[0]
     place = place_ref[0]
     for pair in range(WIDE // PAIR):
         lanes = slice(pair * PAIR, (pair + 1) * PAIR)
         state = start_ref[0, pair]
-        decays = block_decays(packed_ref[:, 0, pair, PAIR // 2 :, :])
+        extra = packed_ref[:, 0, pair, PAIR // 2 :, :]
+        decays = block_decays(extra)
+        extra = extra.astype(jnp.float32)
+        range_ref[0, :, lanes] = put_rows(
+            [
+                jnp.min(extra[:, 2] + extra[:, 3], axis=0, keepdims=True),
+                jnp.max(extra[:, 4] + extra[:, 5], axis=0, keepdims=True),
+            ]
+        )
         for k in range(blocks - 1):
             term = packed_ref[k, 0, pair, : PAIR // 2, :].astype(jnp.float32)
             state = jnp.where(k < place, decays[k] * state + term, state)
@@ -401,7 +376,7 @@
     def totals(self, projected, log_rows):
         outs = [(self.packed(), self.state_shape(jnp.bfloat16, PAIR // 2 + EXTRA))]
         return self.call(
-            totals_kernel, [self.stack, self.tokens], outs, (projected, log_rows), 10**9
+            totals_kernel, [self.stack, self.tokens], outs, (projected, log_rows), 14 * 10**9
         )[0]
 
     def inner(self, projected, log_rows, bonus):
@@ -410,7 +385,7 @@
             (self.tokens, self.token_shape(jnp.bfloat16)),
         ]
         ins = [self.stack, self.tokens, self.row]
-        return self.call(inner_kernel, ins, outs, (projected, log_rows, bonus), 2 * 10**9)
+        return self.call(inner_kernel, ins, outs, (projected, log_rows, bonus), 16 * 10**9)
 
     def join(self, place, inner, decayed, projected, packed, start, gain, bias):
         ins = [
@@ -427,9 +402,10 @@
             (self.tokens, self.token_shape(jnp.float32)),
             (self.tokens, self.token_shape(jnp.bfloat16)),
             (self.state, self.state_shape(jnp.float32)),
+            (self.sums, self.sums_shape()),
         ]
         args = (place, inner, decayed, projected, packed, start, gain, bias)
-        return self.call(join_kernel, ins, outs, args, 10**9)
+        return self.call(join_kernel, ins, outs, args, 21 * 10**9)
 
     def back_join(self, grad, wkv, projected, decayed, gain, bias):
         ins = [self.tokens, self.tokens, self.gate, self.tokens, self.row, self.row]
@@ -440,7 +416,7 @@
             (self.sums, self.sums_shape()),
         ]
         args = (grad, wkv, projected, decayed, gain, bias)
-        return self.call(back_join_kernel, ins, outs, args, 10**9)
+        return self.call(back_join_kernel, ins, outs, args, 15 * 10**9)
 
     def back_inner(self, projected, log_rows, bonus, grad, state):
         ins = [self.stack, self.tokens, self.row, self.tokens, self.state]
@@ -452,7 +428,7 @@
             (self.sums, self.sums_shape()),
         ]
         args = (projected, log_rows, bonus, grad, state)
-        return self.call(back_inner_kernel, ins, outs, args, 4 * 10**9)
+        return self.call(back_inner_kernel, ins, outs, args, 22 * 10**9)
 
     def back_outer(self, place, projected, log_rows, keys, values, running, state, packed, terms):
         blocks = packed.shape[0]
@@ -475,7 +451,7 @@
             (self.sums, self.sums_shape()),
         ]
         args = (place, projected, log_rows, keys, values, running, state, packed, terms)
-        return self.call(back_outer_kernel, ins, outs, args, 3 * 10**9)
+        return self.call(back_outer_kernel, ins, outs, args, 24 * 10**9)
 
 
 def paired_states(states):
@@ -490,40 +466,216 @@
     return heads.reshape(sequences, 2 * count, size, size)
 
 
-def packed_gather(pieces):
-    flat = jnp.concatenate([part.reshape(-1) for part, _ in pieces])
-    everything = lax.all_gather(flat, ("dp", "seq"))
-    devices = everything.shape[0]
-    out, at = [], 0
-    for part, dim in pieces:
-        piece = everything[:, at : at + part.size].reshape((devices,) + part.shape)
-        at += part.size
-        piece = jnp.moveaxis(piece, 0, dim)
-        shape = list(part.shape)
-        shape[dim] *= devices
-        out.append(piece.reshape(shape))
-    return out
-
-
-def packed_scatter(pieces, devices):
-    rows, shapes = [], []
-    for whole, dim in pieces:
-        shape = list(whole.shape)
-        shape[dim] //= devices
-        shapes.append(tuple(shape))
-        cut = whole.reshape(whole.shape[:dim] + (devices, shape[dim]) + whole.shape[dim + 1 :])
-        rows.append(jnp.moveaxis(cut, dim, 0).reshape(devices, -1))
-    rows = jnp.concatenate(rows, axis=1)
-    rows = jnp.pad(rows, ((0, 0), (0, -rows.shape[1] % 1024))).reshape(-1, 128)
-    flat = lax.psum_scatter(rows, ("dp", "seq"), scatter_dimension=0, tiled=True).reshape(-1)
-    out, at = [], 0
-    for shape in shapes:
-        size = 1
-        for extent in shape:
-            size *= extent
-        out.append(flat[at : at + size].reshape(shape))
-        at += size
-    return out
+BRANCHES = (3, 1, 2, 4)
+STRIP = 512
+
+
+def mix_back_kernel(
+    x_ref,
+    before_ref,
+    grad_ref,
+    log_ref,
+    hidden_ref,
+    decay_ref,
+    proj_ref,
+    coeff_ref,
+    norm_ref,
+    down_ref,
+    up_ref,
+    decay_down_ref,
+    decay_up_ref,
+    block_ref,
+    edge_ref,
+    sums_ref,
+    grad_up_ref,
+    grad_down_ref,
+    grad_decay_down_ref,
+    grad_decay_up_ref,
+    hat_ref,
+    grad_diff_ref,
+    grad_all_ref,
+):
+    length, columns = x_ref.shape[1:]
+    ranks = up_ref.shape[0] // 5
+    strips = columns // STRIP
+    low = jnp.bfloat16
+    last = length - 1
+
+    @pl.when(pl.program_id(0) == 0)
+    def _():
+        for ref in (sums_ref, grad_up_ref, grad_down_ref, grad_decay_down_ref, grad_decay_up_ref):
+            ref[...] = jnp.zeros_like(ref)
+
+    x = x_ref[0].astype(jnp.float32)
+    mean = jnp.mean(x, axis=-1, keepdims=True)
+    variance = jnp.mean((x - mean) * (x - mean), axis=-1, keepdims=True)
+    scale = lax.rsqrt(variance + NORM_EPS)
+    hidden, hidden_decay = hidden_ref[...], decay_ref[...]
+    low_hidden, low_decay = hidden.astype(low), hidden_decay.astype(low)
+    grad_log = log_ref[...].astype(low)
+    grad_decay = halves_dot(grad_log, decay_up_ref[...], ((1,), (1,)))
+    grad_decay = grad_decay * (1.0 - hidden_decay * hidden_decay)
+    low_grad_decay = grad_decay.astype(low)
+    grad_decay_up_ref[...] += halves_dot(low_decay, grad_log, ((0,), (0,)))
+
+    def strip_of(strip):
+        return pl.ds(pl.multiple_of(strip * STRIP, STRIP), STRIP)
+
+    def normed_and_diff(at, hat):
+        normed = hat * norm_ref[0:1, at] + norm_ref[1:2, at]
+        earlier = pltpu.roll(normed, 1, 0)
+        earlier = jnp.where(iota(normed.shape, 0) == 0, before_ref[0, :, at], earlier)
+        return normed, earlier - normed
+
+    def first(strip, grad_pre):
+        at = strip_of(strip)
+        hat = (x_ref[0, :, at].astype(jnp.float32) - mean) * scale
+        hat_ref[:, at] = hat
+        normed, diff = normed_and_diff(at, hat)
+        grad_diff = jnp.zeros_like(diff)
+        grad_all = jnp.zeros_like(diff)
+        parts = []
+        for branch in range(5):
+            rows = slice(branch * ranks, (branch + 1) * ranks)
+            up = up_ref[rows, at]
+            weight = coeff_ref[1 + branch : 2 + branch, at] + halves_dot(
+                low_hidden[:, rows], up, ((1,), (0,))
+            )
+            if branch == 0:
+                mixed = normed + diff * weight
+                grad_decay_down_ref[:, at] += halves_dot(low_grad_decay, mixed, ((0,), (0,)))
+                grad = halves_dot(low_grad_decay, decay_down_ref[:, at], ((1,), (0,)))
+            else:
+                n = BRANCHES.index(branch)
+                grad = halves_dot(grad_ref[n], proj_ref[n, at, :], ((1,), (1,)))
+            grad_all += grad
+            grad_diff += grad * weight
+            moved = grad * diff
+            sums_ref[1 + branch : 2 + branch, at] += jnp.sum(moved, axis=0, keepdims=True)
+            moved = moved.astype(low)
+            grad_up_ref[rows, at] += halves_dot(low_hidden[:, rows], moved, ((0,), (0,)))
+            parts.append(halves_dot(moved, up, ((1,), (1,))))
+        grad_diff_ref[:, at] = grad_diff
+        grad_all_ref[:, at] = grad_all
+        return grad_pre + jnp.concatenate(parts, axis=1)
+
+    grad_pre = lax.fori_loop(0, strips, first, jnp.zeros(hidden.shape, jnp.float32))
+    grad_pre = (grad_pre * (1.0 - hidden * hidden)).astype(low)
+
+    def second(strip, carry):
+        total, against = carry
+        at = strip_of(strip)
+        hat = hat_ref[:, at]
+        normed, diff = normed_and_diff(at, hat)
+        coeff = coeff_ref[0:1, at]
+        grad_base = halves_dot(grad_pre, down_ref[:, at], ((1,), (0,)))
+        grad_down_ref[:, at] += halves_dot(grad_pre, normed + diff * coeff, ((0,), (0,)))
+        sums_ref[0:1, at] += jnp.sum(grad_base * diff, axis=0, keepdims=True)
+        grad_diff = grad_diff_ref[:, at] + grad_base * coeff
+        edge_ref[0, :, at] = grad_diff[0:1]
+        onward = pltpu.roll(grad_diff, last, 0)
+        onward = jnp.where(iota(onward.shape, 0) == last, 0.0, onward)
+        grad = grad_base + grad_all_ref[:, at] - grad_diff + onward
+        sums_ref[6:7, at] += jnp.sum(grad * hat, axis=0, keepdims=True)
+        sums_ref[7:8, at] += jnp.sum(grad, axis=0, keepdims=True)
+        q = grad * norm_ref[0:1, at]
+        grad_all_ref[:, at] = q
+        total += jnp.sum(q, axis=-1, keepdims=True)
+        against += jnp.sum(q * hat, axis=-1, keepdims=True)
+        return total, against
+
+    zero = jnp.zeros((length, 1), jnp.float32)
+    total, against = lax.fori_loop(0, strips, second, (zero, zero))
+    total, against = total * (1.0 / columns), against * (1.0 / columns)
+
+    def third(strip, carry):
+        at = strip_of(strip)
+        block_ref[0, :, at] = scale * (grad_all_ref[:, at] - total - hat_ref[:, at] * against)
+        return carry
+
+    lax.fori_loop(0, strips, third, 0)
+
+
+def mix_back(
+    block_input,
+    before,
+    grad_proj,
+    grad_log,
+    hidden,
+    hidden_decay,
+    projections,
+    coeffs,
+    norm,
+    down,
+    up,
+    decay_down,
+    decay_up,
+):
+    sequences, length, columns = block_input.shape
+    heads = grad_proj.shape[-1]
+    ranks, decay_ranks = up.shape[0], decay_up.shape[0]
+
+    def whole(array):
+        return pl.BlockSpec(array.shape, lambda s: (0,) * array.ndim)
+
+    def kept(shape):
+        return pl.BlockSpec(shape, lambda s: (0, 0)), jax.ShapeDtypeStruct(shape, jnp.float32)
+
+    block = pl.BlockSpec((1, length, columns), lambda s: (s, 0, 0))
+    edge = pl.BlockSpec((1, 1, columns), lambda s: (s, 0, 0))
+    outs = [
+        (block, jax.ShapeDtypeStruct(block_input.shape, jnp.float32)),
+        (edge, jax.ShapeDtypeStruct((sequences, 1, columns), jnp.float32)),
+        kept((8, columns)),
+        kept((ranks, columns)),
+        kept((ranks, columns)),
+        kept((decay_ranks, columns)),
+        kept((decay_ranks, heads)),
+    ]
+    args = (
+        block_input,
+        before,
+        grad_proj,
+        grad_log,
+        hidden,
+        hidden_decay,
+        projections,
+        coeffs,
+        norm,
+        down,
+        up,
+        decay_down,
+        decay_up,
+    )
+    return pl.pallas_call(
+        mix_back_kernel,
+        grid=(sequences,),
+        in_specs=[
+            block,
+            edge,
+            pl.BlockSpec((4, length, heads), lambda s: (0, s, 0)),
+            pl.BlockSpec((length, heads), lambda s: (s, 0)),
+            pl.BlockSpec((length, hidden.shape[1]), lambda s: (s, 0)),
+            pl.BlockSpec((length, decay_ranks), lambda s: (s, 0)),
+            pl.BlockSpec(projections.shape, lambda s: (0, 0, 0), pipeline_mode=pl.Buffered(1)),
+        ]
+        + [whole(array) for array in args[7:]],
+        out_specs=[spec for spec, _ in outs],
+        out_shape=[shape for _, shape in outs],
+        scratch_shapes=[pltpu.VMEM((length, columns), jnp.float32)] * 3,
+        compiler_params=pltpu.CompilerParams(vmem_limit_bytes=58 * 2**20),
+        cost_estimate=pl.CostEstimate(
+            flops=7 * 10**10, bytes_accessed=40 * 2**20, transcendentals=0
+        ),
+    )(*args)
+
+
+def sum_columns(rows):
+    shards = lax.axis_size("dp") * lax.axis_size("seq")
+    parts = rows.reshape(rows.shape[0], shards, -1).transpose(1, 0, 2)
+    return lax.psum_scatter(
+        parts.reshape(-1, parts.shape[2]), ("dp", "seq"), scatter_dimension=0, tiled=True
+    )
 
 
 def other_half(block):
@@ -770,11 +922,180 @@
             collective_id=collective_id, has_side_effects=True, vmem_limit_bytes=60 * 2**20
         ),
         cost_estimate=pl.CostEstimate(
-            flops=2 * tokens * rows * dp_size * seq_size * sum(widths),
+            flops=int(28 * 10**6 * sum(widths)),
             bytes_accessed=2 * tokens * (2048 * len(pairs) + sum(widths)),
             transcendentals=0,
         ),
     )(*operands)
+
+
+def spread_kernel(dp_size, seq_size, part_ref, whole_ref, local, send, recv, pair_send, pair_recv):
+    count = dp_size * seq_size // CORES
+    per_row, width = seq_size // CORES, part_ref.shape[1]
+    row, core = lax.axis_index("dp"), lax.rem(lax.axis_index("seq"), CORES)
+    position = row * per_row + lax.div(lax.axis_index("seq"), CORES)
+
+    def device(place, which):
+        place = lax.rem(place + count, count)
+        return {"dp": lax.div(place, per_row), "seq": lax.rem(place, per_row) * CORES + which}
+
+    def columns(place, which):
+        place = lax.rem(place + count, count)
+        return pl.ds(pl.multiple_of((place * CORES + which) * width, width), width)
+
+    barrier = pltpu.get_barrier_semaphore()
+    sibling = device(position, 1 - core)
+    for other in [sibling] + [device(position + k, core) for k in range(1, count)]:
+        pl.semaphore_signal(barrier, inc=1, device_id=other, device_id_type=pl.DeviceIdType.MESH)
+    pl.semaphore_wait(barrier, count)
+
+    own = whole_ref.at[:, columns(position, core)]
+    keep = pltpu.make_async_copy(part_ref, own, local)
+    keep.start()
+    copies = [
+        pltpu.make_async_remote_copy(
+            src_ref=part_ref,
+            dst_ref=own,
+            send_sem=send.at[k],
+            recv_sem=recv.at[k],
+            device_id=device(position + k, core),
+            device_id_type=pl.DeviceIdType.MESH,
+        )
+        for k in range(1, count)
+    ]
+    passed = []
+    for k in range(count):
+        at = whole_ref.at[:, columns(position - k, core)]
+        passed.append(
+            pltpu.make_async_remote_copy(
+                src_ref=part_ref if k == 0 else at,
+                dst_ref=at,
+                send_sem=pair_send.at[k],
+                recv_sem=pair_recv.at[k],
+                device_id=sibling,
+                device_id_type=pl.DeviceIdType.MESH,
+            )
+        )
+    for copy in copies:
+        copy.start()
+    passed[0].start()
+    for k in range(1, count):
+        copies[k - 1].wait_recv()
+        passed[k].start()
+    keep.wait()
+    for copy in copies:
+        copy.wait_send()
+    for copy in passed:
+        copy.wait()
+
+
+def spread_columns(part, sizes, collective_id):
+    if part.shape[1] % 128:
+        return lax.all_gather(part, ("dp", "seq"), axis=1, tiled=True)
+    dp_size, seq_size = sizes
+    count = dp_size * seq_size // CORES
+    rows, width = part.shape
+    return pl.pallas_call(
+        functools.partial(spread_kernel, dp_size, seq_size),
+        out_shape=jax.ShapeDtypeStruct((rows, width * dp_size * seq_size), part.dtype),
+        in_specs=[pl.BlockSpec(memory_space=pltpu.VMEM)],
+        out_specs=pl.BlockSpec(memory_space=pltpu.VMEM),
+        scratch_shapes=[pltpu.SemaphoreType.DMA(())] + [pltpu.SemaphoreType.DMA((count,))] * 4,
+        compiler_params=pltpu.CompilerParams(
+            collective_id=collective_id, has_side_effects=True, vmem_limit_bytes=16 * 2**20
+        ),
+        cost_estimate=pl.CostEstimate(
+            flops=50 * 10**9, bytes_accessed=4 * 2**20, transcendentals=0
+        ),
+    )(part)
+
+
+def mix_kernel(
+    x_ref,
+    before_ref,
+    coeff_ref,
+    norm_ref,
+    down_ref,
+    up_ref,
+    decay_down_ref,
+    decay_up_ref,
+    base_ref,
+    mixed_ref,
+    hidden_ref,
+    decay_ref,
+    log_ref,
+):
+    length, columns = x_ref.shape[1:]
+    ranks = up_ref.shape[0] // 5
+    strips = columns // STRIP
+    x = x_ref[0].astype(jnp.float32)
+    mean = jnp.mean(x, axis=-1, keepdims=True)
+    variance = jnp.mean((x - mean) * (x - mean), axis=-1, keepdims=True)
+    scale = lax.rsqrt(variance + NORM_EPS)
+
+    def normed_and_diff(strip):
+        at = pl.ds(pl.multiple_of(strip * STRIP, STRIP), STRIP)
+        hat = (x_ref[0, :, at].astype(jnp.float32) - mean) * scale
+        normed = hat * norm_ref[0:1, at] + norm_ref[1:2, at]
+        earlier = pltpu.roll(normed, 1, 0)
+        earlier = jnp.where(iota(normed.shape, 0) == 0, before_ref[0, :, at], earlier)
+        return at, normed, earlier - normed
+
+    def first(strip, hidden):
+        at, normed, diff = normed_and_diff(strip)
+        return hidden + halves_dot(normed + diff * coeff_ref[0:1, at], down_ref[:, at], ((1,), (1,)))
+
+    hidden = lax.fori_loop(0, strips, first, jnp.zeros(hidden_ref.shape, jnp.float32))
+    hidden = jnp.tanh(hidden)
+    hidden_ref[...] = hidden
+    hidden = hidden.astype(jnp.bfloat16)
+
+    def second(strip, decay):
+        at, normed, diff = normed_and_diff(strip)
+        for branch in range(5):
+            rows = slice(branch * ranks, (branch + 1) * ranks)
+            weight = coeff_ref[1 + branch : 2 + branch, at] + halves_dot(
+                hidden[:, rows], up_ref[rows, at], ((1,), (0,))
+            )
+            mixed = (normed + diff * weight).astype(jnp.bfloat16)
+            if branch == 0:
+                decay += halves_dot(mixed, decay_down_ref[:, at], ((1,), (1,)))
+            else:
+                mixed_ref[BRANCHES.index(branch), :, at] = mixed
+        return decay
+
+    decay = lax.fori_loop(0, strips, second, jnp.zeros(decay_ref.shape, jnp.float32))
+    decay = jnp.tanh(decay)
+    decay_ref[...] = decay
+    log_ref[...] = base_ref[...] + halves_dot(decay, decay_up_ref[...], ((1,), (0,)))
+
+
+def mix_forward(block_input, before, coeffs, norm, down, up, decay_down, decay_up, base):
+    sequences, length, columns = block_input.shape
+    heads, tokens = decay_up.shape[1], sequences * length
+    args = (block_input, before, coeffs, norm, down, up, decay_down, decay_up, base)
+
+    def rows(wide):
+        return pl.BlockSpec((length, wide), lambda s: (s, 0))
+
+    outs = [(down.shape[0], jnp.float32), (decay_up.shape[0], jnp.float32), (heads, jnp.float32)]
+    return pl.pallas_call(
+        mix_kernel,
+        grid=(sequences,),
+        in_specs=[
+            pl.BlockSpec((1, length, columns), lambda s: (s, 0, 0)),
+            pl.BlockSpec((1, 1, columns), lambda s: (s, 0, 0)),
+        ]
+        + [pl.BlockSpec(array.shape, lambda s: (0, 0)) for array in args[2:]],
+        out_specs=[pl.BlockSpec((4, length, columns), lambda s: (0, s, 0))]
+        + [rows(wide) for wide, _ in outs],
+        out_shape=[jax.ShapeDtypeStruct((4, tokens, columns), jnp.bfloat16)]
+        + [jax.ShapeDtypeStruct((tokens, wide), kind) for wide, kind in outs],
+        compiler_params=pltpu.CompilerParams(vmem_limit_bytes=40 * 2**20),
+        cost_estimate=pl.CostEstimate(
+            flops=17 * 10**9, bytes_accessed=16 * 2**20, transcendentals=10**5
+        ),
+    )(*args)
 
 
 def per_device(
@@ -799,43 +1120,58 @@
     out_grad,
 ):
     blocks, place = lax.axis_size("seq"), lax.axis_index("seq")
-    gathered = lax.axis_size("dp") * blocks
     half = lax.axis_index("tp")
-    (
-        gains_all,
-        biases_all,
-        shift_coefficient,
-        lowrank_down,
-        lowrank_up,
-        decay_projection,
-        decay_lift,
-        decay_base,
-        reward_array_entries,
-        group_scale,
-        group_shift,
-    ) = [
-        part.astype(jnp.float32)
-        for part in packed_gather(
-            [
-                (norm_gains, 1),
-                (norm_biases, 1),
-                (mixing_coefficients, 1),
-                (mix_down, 0),
-                (mixing_up_weight, 1),
-                (decay_down, 0),
-                (decay_up, 2),
-                (time_decay, 1),
-                (time_first, 1),
-                (group_gain, 1),
-                (group_bias, 1),
-            ]
-        )
-    ]
+    sizes = (lax.axis_size("dp"), blocks)
+    width = norm_gains.shape[1]
+    heads_here, each = time_decay.shape
+    head_size = initial_state.shape[-1]
+    head_cols = heads_here * head_size
+    ranks, decay_ranks = mix_down.shape[1], decay_down.shape[1]
+
+    def narrow_rows(part):
+        part = part.reshape(-1, heads_here * each)
+        return jnp.pad(part, ((0, 0), (0, width - part.shape[1])))
+
+    up_at = 16
+    down_at = up_at + ranks
+    decay_at = down_at + ranks
+    narrow_at = decay_at + decay_ranks
+    own_rows = jnp.concatenate(
+        [
+            norm_gains,
+            norm_biases,
+            mixing_coefficients,
+            jnp.zeros((4, width), jnp.bfloat16),
+            mixing_up_weight,
+            mix_down.T,
+            decay_down.T,
+            narrow_rows(decay_up),
+            narrow_rows(time_decay),
+            narrow_rows(time_first),
+            narrow_rows(group_gain),
+            narrow_rows(group_bias),
+            jnp.zeros((12, width), jnp.bfloat16),
+        ]
+    )
+    spread_rows = spread_columns(own_rows, sizes, 1)
+    channel = jnp.arange(head_cols)
+    lane = (channel % head_size) // each * width + channel // head_size * each + channel % each
+    choose = (jnp.arange(spread_rows.shape[1])[:, None] == lane[None, :]).astype(jnp.bfloat16)
+    narrow_all = jnp.dot(
+        spread_rows[narrow_at:], choose, preferred_element_type=jnp.float32
+    )
+    gains_all, biases_all = (spread_rows[k : k + 2].astype(jnp.float32) for k in (0, 2))
+    shift_coefficient = spread_rows[4:12].astype(jnp.float32)
+    lowrank_up = spread_rows[up_at:down_at]
+    lowrank_down = spread_rows[down_at:decay_at]
+    decay_projection = spread_rows[decay_at:narrow_at]
+    lift_rows = narrow_all[:decay_ranks].astype(jnp.bfloat16)
+    base_row, bonus, group_scale, group_shift = (
+        narrow_all[decay_ranks + k : decay_ranks + k + 1] for k in range(4)
+    )
     projections = lax.all_gather(proj_weights, ("dp", "seq"), axis=1, tiled=True)
     out_proj = lax.all_gather(out_weight, ("dp", "seq"), axis=1, tiled=True)
     seq_count, length, feature_columns = block_input.shape
-    heads_here, head_size = decay_base.shape
-    head_cols = heads_here * head_size
     tokens = seq_count * length
     own_cols = channel_recept.shape[1]
 
@@ -854,35 +1190,27 @@
 
     full_out = both_halves(out_grad)
     input_f = block_input.astype(jnp.float32)
-    normalized_first, norm_one_back = jax.vjp(layer_norm, input_f, gains_all[0], biases_all[0])
-    preceding_first = from_behind(normalized_first[:, -1, :].astype(jnp.bfloat16), "seq", 1).astype(
-        jnp.float32
-    )
-    mixed_input, mix_back = jax.vjp(
-        token_mixture,
-        normalized_first,
+    last_one = layer_norm(input_f[:, -1], gains_all[0], biases_all[0])
+    preceding_first = from_behind(last_one.astype(jnp.bfloat16), "seq", 1)
+    preceding_first = preceding_first.astype(jnp.float32)[:, None, :]
+    norm_one = jnp.stack([gains_all[0], biases_all[0]])
+    stacked, hidden_mixture, hidden_decay, log_flat = mix_forward(
+        block_input,
         preceding_first,
         shift_coefficient,
+        norm_one,
         lowrank_down,
         lowrank_up,
         decay_projection,
-    )
-    log_rows, decay_back = jax.vjp(
-        decay_rates,
-        mixed_input[4],
-        decay_lift.reshape(decay_lift.shape[0], head_cols),
-        decay_base.reshape(head_cols),
-    )
-    stacked = jnp.stack(mixed_input[:4]).astype(jnp.bfloat16).reshape(4, tokens, feature_columns)
+        lift_rows,
+        base_row,
+    )
     projected = jnp.einsum("ntd,nde->nte", stacked, projections, preferred_element_type=jnp.float32)
     recurrence = Recurrence(seq_count, length, head_cols)
-    log_flat = log_rows.reshape(tokens, head_cols)
-    bonus = reward_array_entries.reshape(1, head_cols)
-    group_scale, group_shift = group_scale.reshape(1, -1), group_shift.reshape(1, -1)
     where_here = place.astype(jnp.int32).reshape(1)
     all_packed = lax.all_gather(recurrence.totals(projected, log_flat), "seq")
     inner, decayed = recurrence.inner(projected, log_flat, bonus)
-    wkv, mixer_rows, state = recurrence.join(
+    wkv, mixer_rows, state, decay_range = recurrence.join(
         where_here,
         inner,
         decayed,
@@ -893,10 +1221,9 @@
         group_shift,
     )
     mixer_in = mixer_rows.reshape(seq_count, length, head_cols)
-    extra = all_packed[..., head_size : head_size + 6, :].astype(jnp.float32)
-    extra = extra.reshape(blocks, seq_count, heads_here // 2, 3, 2, 2, head_size).sum(axis=4)
-    total_least = jnp.min(extra[:, :, :, 1], axis=(0, 4)).reshape(seq_count, heads_here)
-    total_most = jnp.max(extra[:, :, :, 2], axis=(0, 4)).reshape(seq_count, heads_here)
+    decay_range = decay_range[:, :2].reshape(seq_count, 2, heads_here, head_size)
+    total_least = jnp.min(decay_range[:, 0], axis=-1)
+    total_most = jnp.max(decay_range[:, 1], axis=-1)
     mixer_part = jnp.einsum("std,de->ste", mixer_in, out_proj, preferred_element_type=jnp.float32)
     residual = (
         input_f + mixer_part + other_half(mixer_part.astype(jnp.bfloat16)).astype(jnp.float32)
@@ -953,7 +1280,9 @@
     from_next_two = from_behind(for_sending(part_prev_two), "seq", -1).astype(jnp.float32)
     part_normed_two = part_normed_two.at[:, -1, :].add(from_next_two)
     sizes = (lax.axis_size("dp"), blocks)
-    key_whole = weight_terms(chan_key_b, grad_key)
+    grad_key_rows = grad_key.reshape(tokens, -1)
+    key_cut = grad_key_rows.shape[1] * 4 // 7
+    key_whole = weight_terms(chan_key_b, grad_key_rows[:, :key_cut])
     grad_normed_two = part_normed_two + other_half(part_normed_two.astype(jnp.bfloat16)).astype(
         jnp.float32
     )
@@ -969,6 +1298,7 @@
         grad_mixer.reshape(tokens, head_cols), wkv, projected, decayed, group_scale, group_shift
     )
     all_terms = lax.all_gather(block_term, "seq")
+    grad_wkv, value_sum = lax.optimization_barrier((grad_wkv, value_sum))
     grad_receive, near_key, near_value, running, bonus_sums = recurrence.back_inner(
         projected, log_flat, bonus, grad_wkv, state
     )
@@ -985,78 +1315,88 @@
     )
     state_grad = single_states(start_pairs)
 
-    def head_rows(sums, row):
-        return jnp.sum(sums[:, row], axis=0).reshape(heads_here, head_size)
-
-    group_gain_grad, group_bias_grad = head_rows(group_sums, 0), head_rows(group_sums, 1)
-    reward_cotangent_term, base_grad = head_rows(bonus_sums, 0), head_rows(rate_sums, 0)
     grad_proj = jnp.stack([grad_receive, grad_keys, grad_values, grad_gate])
-    grad_proj, value_sum = lax.optimization_barrier((grad_proj, value_sum))
-    part_inputs = jnp.einsum(
-        "nte,nde->ntd", grad_proj, projections, preferred_element_type=jnp.float32
-    )
-    part_hdec, lift_grad, _ = decay_back(grad_log.reshape(seq_count, length, head_cols))
-    part_normed_one, part_prev_one, grad_coeffs_time, down_grad, up_grad, decay_proj_grad = mix_back(
-        (
-            part_inputs[0].reshape(seq_count, length, feature_columns),
-            part_inputs[1].reshape(seq_count, length, feature_columns),
-            part_inputs[2].reshape(seq_count, length, feature_columns),
-            part_inputs[3].reshape(seq_count, length, feature_columns),
-            part_hdec,
-        )
-    )
-    from_next_one = from_behind(for_sending(part_prev_one), "seq", -1).astype(jnp.float32)
-    part_normed_one = part_normed_one.at[:, -1, :].add(from_next_one)
-    part_block, grad_gain_one, grad_bias_one = norm_one_back(part_normed_one)
-    input_grad = own_half(grad_residual) + half_sum(part_block)
-    small_sums = packed_scatter(
+    part_block, edge, mix_sums, up_grad, down_grad, decay_down_grad, lift_grad = mix_back(
+        block_input,
+        preceding_first,
+        grad_proj,
+        grad_log,
+        hidden_mixture,
+        hidden_decay,
+        projections,
+        shift_coefficient,
+        norm_one,
+        lowrank_down,
+        lowrank_up,
+        decay_projection,
+        lift_rows,
+    )
+    from_next_one = from_behind(edge[:, 0].astype(jnp.bfloat16), "seq", -1).astype(jnp.float32)
+    _, last_back = jax.vjp(layer_norm, input_f[:, -1], gains_all[0], biases_all[0])
+    part_last, gain_last, bias_last = last_back(from_next_one)
+    part_block = part_block.at[:, -1].add(part_last)
+    head_rows = jnp.concatenate(
         [
-            (jnp.stack([grad_gain_one, 0.5 * grad_gain_two]), 1),
-            (jnp.stack([grad_bias_one, 0.5 * grad_bias_two]), 1),
-            (grad_coeffs_time + grad_coeffs_chan, 1),
-            (down_grad, 0),
-            (up_grad, 1),
-            (decay_proj_grad, 0),
-            (lift_grad.reshape(decay_lift.shape), 2),
-            (base_grad.reshape(decay_base.shape), 1),
-            (reward_cotangent_term, 1),
-            (group_gain_grad, 1),
-            (group_bias_grad, 1),
-        ],
-        gathered,
-    )
-    rest = [part + other_half(part) for part in small_sums[:6]] + small_sums[6:]
-    last_branch, key_sum = lax.optimization_barrier((grad_branch, key_sum))
-    *proj_sums, out_sum, recept_sum = ring_sums(
+            lift_grad,
+            jnp.sum(rate_sums[:, :1], axis=0),
+            jnp.sum(bonus_sums[:, :1], axis=0),
+            jnp.sum(group_sums[:, :2], axis=0),
+            jnp.zeros((12, head_cols), jnp.float32),
+        ]
+    )
+    head_rows = lax.dot_general(
+        head_rows,
+        choose.astype(jnp.float32),
+        (((1,), (1,)), ((), ())),
+        precision=lax.Precision.HIGHEST,
+    )
+    small_rows = jnp.concatenate(
+        [
+            jnp.stack([mix_sums[6] + gain_last, 0.5 * grad_gain_two]),
+            jnp.stack([mix_sums[7] + bias_last, 0.5 * grad_bias_two]),
+            mix_sums[:6],
+            grad_coeffs_chan[6:],
+            jnp.zeros((4, feature_columns), jnp.float32),
+            up_grad,
+            down_grad,
+            decay_down_grad,
+            head_rows,
+        ]
+    )
+    half_block = half_sum(part_block)
+    small_sums = sum_columns(small_rows)
+    input_grad = own_half(grad_residual) + half_block
+    *proj_sums, out_sum, recept_sum, key_rest = ring_sums(
         [(stacked, grad_proj, (branch,)) for branch in range(4)]
         + [
-            (last_branch.reshape(tokens, -1), mixer_in.reshape(tokens, -1), ()),
+            (grad_branch.reshape(tokens, -1), mixer_in.reshape(tokens, -1), ()),
             (chan_recept_b.reshape(tokens, -1), grad_recept.reshape(tokens, -1), ()),
+            (chan_key_b.reshape(tokens, -1), grad_key_rows[:, key_cut:], ()),
         ],
         sizes,
         0,
     )
-    coeff_rows = jnp.concatenate([rest[2][:1], rest[2][2:]], axis=0)
-    decay_row = rest[2][1:2]
+    shared = small_sums[:narrow_at] + other_half(small_sums[:narrow_at])
+    narrow = small_sums[narrow_at:, : heads_here * each]
+    head_sums = [
+        narrow[decay_ranks + k].reshape(heads_here, each) for k in range(4)
+    ]
     return (
         output,
         input_grad,
         state_grad,
-        rest[0],
-        rest[1],
-        coeff_rows,
-        decay_row,
-        rest[3],
-        rest[4],
-        rest[5],
-        rest[6],
+        shared[:2],
+        shared[2:4],
+        jnp.concatenate([shared[4:5], shared[6:12]], axis=0),
+        shared[5:6],
+        shared[down_at:decay_at].T,
+        shared[up_at:down_at],
+        shared[decay_at:].T,
+        narrow[:decay_ranks].reshape(decay_ranks, heads_here, each),
         jnp.stack(proj_sums),
         out_sum.T,
-        rest[7],
-        rest[8],
-        rest[9],
-        rest[10],
-        key_sum,
+        *head_sums,
+        jnp.concatenate([key_sum, key_rest], axis=1),
         value_sum.T,
         recept_sum,
         total_least,

time: 1220 us -> 1290 us (1.057)
  Pallas kernels: 246 us -> 412 us
  waiting for transfers between devices: 424 us -> 499 us
  local copies, waits for them, and re-layouts: 192 us -> 120 us
  matrix products: 191 us -> 122 us
  other arithmetic: 127 us -> 92.4 us
    reduce_scatter x2, waiting for transfers between devices: 94.8 us -> 218 us  [scattered(): lax.psum_scatter(whole, ('dp', 'seq'), scatter_dimension=0, tiled=True)]
    pallas_call x0 -> x3, Pallas kernels: none -> 123 us  [the longest x1 63.1 us: mix_back(): pl.pallas_call(mix_back_kernel, grid=(sequences,), in_specs=[block, edge,...]
    dot_general x13 -> x2, matrix products: 74 us -> 6.02 us  [the longest x1 4.35 us: per_device(): lax.dot_general(head_rows, choose.astype(jnp.float32), (((1,), (1,)), (()...]
    all_gather x1 -> x0, waiting for transfers between devices: 46.5 us -> none  [packed_gather(): everything = lax.all_gather(flat, ('dp', 'seq'))]
    pallas_call x1, Pallas kernels: 147 us -> 190 us  [ring_sums(): pl.pallas_call(functools.partial(ring_kernel, dp_size, seq_size, rows, wi...]
    slice x18 -> x16, local copies, waits for them, and re-layouts: 33.1 us -> 8.89 us  [the longest x1 2.67 us: per_device(): grad_key_rows[:, key_cut:]]
    add_any x3 -> x0, other arithmetic: 22.6 us -> none  [the longest x1 10.9 us: token_mixture(): normalized_rows[:, :-1, :]]
    reshape x21 -> x6, local copies, waits for them, and re-layouts: 19.7 us -> 1.29 us  [the longest x5 1.19 us: narrow_rows(): part = part.reshape(-1, heads_here * each)]
  transfers between devices with their start and end apart: 24 -> 18, of which waited for: 13 -> 11; matrix products, arithmetic and copies ran while one was open for 30% -> 14% of each run, Pallas kernels for 18% -> 25%
where the time goes in v4:
time: 1290 us; the launch traced here: 1280 us
  waiting for transfers between devices  499 us (39%)
  Pallas kernels  412 us (32%)
  matrix products  122 us (9%)
  local copies, waits for them, and re-layouts  120 us (9%)
  other arithmetic  92.4 us (7%)
  between operations  15.9 us (1%)
  starting transfers between devices  15.8 us (1%)
    reduce_scatter x2, waiting for transfers between devices, scattered(): lax.psum_scatter(whole, ('dp', 'seq'), scatter_dimension=0, tiled=True)  218 us
    pallas_call x1, Pallas kernels, ring_sums(): pl.pallas_call(functools.partial(ring_kernel, dp_size, seq_size, rows, wi...  190 us
    ppermute x7, waiting for transfers between devices, other_half(): return lax.ppermute(block, 'tp', [(0, 1), (1, 0)])  139 us
    pallas_call x6, Pallas kernels, call(): pl.pallas_call(kernel, grid=self.grid, in_specs=ins, out_specs=[spec for...  98.8 us
    all_gather x1, waiting for transfers between devices, per_device(): lax.all_gather(proj_weights, ('dp', 'seq'), axis=1, tiled=True)  70.5 us
    unnamed x216, local copies, waits for them, and re-layouts  67.6 us
    pallas_call x1, Pallas kernels, mix_back(): pl.pallas_call(mix_back_kernel, grid=(sequences,), in_specs=[block, edge,...  63.1 us
    pallas_call x1, Pallas kernels, spread_columns(): pl.pallas_call(functools.partial(spread_kernel, dp_size, seq_size), out_s...  45.2 us
  transfers between devices with their start and end apart: 18, of which 11 were waited for; matrix products, arithmetic and copies ran while one was open for 14% of the time, Pallas kernels for 25%

profile of v4, /device:TPU:0, one launch (start us, length us, event | category | flops | bytes accessed | tf_op | source)
XLA Modules:
  0.0 1276.5 jit_solution(7210247083268511132)
XLA Ops:
  12.3 4.0 concatenate.48.part_ref
  20.7 45.2 %shard_map.354 = bf16[480,2048]{1,0:T(8,128)(2,1)S(1)} custom-call(bf16[480,128]{1,0:T(8,128)(2,1)S(1)} %concatenate.48.part_ref), custom_call_target="tpu_custom_call" | custom-call | flops 49999998976 | bytes 4194304 | tf_op jit(solution)/shard_map/pallas_call | solution.py:998
  71.2 15.0 %shard_map.355 = (bf16[4,512,2048]{2,1,0:T(8,128)(2,1)}, f32[512,160]{1,0:T(8,128)S(1)}, f32[512,64]{1,0:T(8,128)S(1)}, f32[512,1024]{1,0:T(8,128)S(1)}) custom-call(bf16[4,128,2048]{2,1,0:T(8,128)(2,1)S(1)} %copy-done, f32[4,1,2048]{2,1,0:T(1,128)S(1)} %reshape.354.before_ref, f32[8,2048]{1,0:T(8,128)S(1)} %slice_convert_fusion.3.coeff_ref, ...), custom_call_target="tpu_custom_call" | custom-call | flops 16999999488 | bytes 16777216 | tf_op jit(solution)/shard_map/pallas_call | solution.py:1082
  90.5 70.5 %all-gather.7.cloned.1.call-done.proj_ref = bf16[4,2048,1024]{2,1,0:T(8,128)(2,1)} async-done(((bf16[4,128,1024]{2,1,0:T(8,128)(2,1)}), bf16[4,2048,1024]{2,1,0:T(8,128)(2,1)}) %all-gather.7.cloned.1.call-update) | async-done | bytes 16777232 | tf_op jit(solution)/shard_map/all_gather | solution.py:1172
  161.0 16.9 %fusion.88.rkv_ref.kv_ref.gate_ref = f32[4,512,1024]{2,1,0:T(8,128)} fusion(bf16[4,512,2048]{2,1,0:T(8,128)(2,1)} %get-tuple-element.90.refs_0_, bf16[4,2048,1024]{2,1,0:T(8,128)(2,1)} %all-gather.7.cloned.1.call-done.proj_ref), kind=kOutput, calls=%fused_computation.192 | convolution fusion | flops 8589934592 | bytes 33554432 | tf_op jit(solution)/shard_map/ntd,nde->nte/dot_general | solution.py:1208
  177.9 3.4 copy-done.12
  181.3 11.8 shard_map.357
  193.9 4.6 copy.345
  206.4 14.0 %shard_map.356 = (f32[512,1024]{1,0:T(8,128)S(1)}, bf16[512,1024]{1,0:T(8,128)(2,1)S(1)}) custom-call(f32[4,512,1024]{2,1,0:T(8,128)S(1)} %copy-done.13, f32[512,1024]{1,0:T(8,128)S(1)} %copy-done.16, f32[1,1024]{1,0:T(1,128)S(1)} %get-tuple-element.282.bonus_ref), custom_call_target="tpu_custom_call" | custom-call | flops 16000000000 | bytes 10489856 | tf_op jit(solution)/shard_map/pallas_call | solution.py:364
  222.7 24.8 %all-gather.11.cloned.1.call-done = bf16[32,8,80,128]{3,2,1,0:T(8,128)(2,1)} async-done(((bf16[4,8,80,128]{3,2,1,0:T(8,128)(2,1)}), bf16[32,8,80,128]{3,2,1,0:T(8,128)(2,1)}) %all-gather.11.cloned.1.call-update) | async-done | bytes 5242896 | tf_op jit(solution)/shard_map/all_gather | solution.py:1211
  252.8 18.3 %shard_map.358 = (f32[512,1024]{1,0:T(8,128)S(1)}, bf16[512,1024]{1,0:T(8,128)(2,1)S(1)}, f32[4,8,64,128]{3,2,1,0:T(8,128)S(1)}, f32[4,8,1024]{2,1,0:T(8,128)S(1)}) custom-call(s32[1]{0:T(128)} %bitcast.place_ref, f32[512,1024]{1,0:T(8,128)S(1)} %copy-done.24, bf16[512,1024]{1,0:T(8,128)(2,1)S(1)} %copy-done.26, ...), custom_call_target="tpu_custom_call" | custom-call | flops 20999999488 | bytes 17833988 | tf_op jit(solution)/shard_map/pallas_call | solution.py:364
  274.4 27.3 %all-gather.9.cloned.1.call-done = bf16[1024,2048]{1,0:T(8,128)(2,1)} async-done(((bf16[1024,128]{1,0:T(8,128)(2,1)}), bf16[1024,2048]{1,0:T(8,128)(2,1)}) %all-gather.9.cloned.1.call-update) | async-done | bytes 4194320 | tf_op jit(solution)/shard_map/all_gather | solution.py:1173
  301.7 4.8 fusion.18
  310.7 46.3 %collective-permute-done.1 = bf16[4,128,2048]{2,0,1:T(4,128)(2,1)S(1)} collective-permute-done((bf16[4,128,2048]{2,0,1:T(4,128)(2,1)S(1)}, bf16[4,128,2048]{2,0,1:T(4,128)(2,1)S(1)}, u32[]{:S(2)}, u32[]{:S(2)}) %collective-permute-start.1) | collective-permute-done | bytes 2097184 | tf_op jit(solution)/shard_map/ppermute | solution.py:682
  357.1 6.9 fusion.77
  367.4 4.8 multiply_add_fusion.1
  377.8 4.4 add_convert_fusion.1
  382.3 16.2 %fusion.6 = f32[4,128,3584]{2,1,0:T(8,128)S(1)} fusion(bf16[2048,3584]{1,0:T(8,128)(2,1)} %param.38, bf16[4,128,2048]{2,0,1:T(4,128)(2,1)S(1)} %get-tuple-element.266), kind=kOutput, calls=%fused_computation.7 | convolution fusion | flops 7516192768 | bytes 24117248 | tf_op jit(solution)/shard_map/std,df->stf/dot_general | solution.py:1238
  398.5 14.0 %fusion.2 = f32[4,128,2048]{2,1,0:T(8,128)S(1)} fusion(bf16[3584,2048]{1,0:T(8,128)(2,1)} %param.39, f32[4,128,3584]{2,1,0:T(8,128)S(1)} %fusion.6), kind=kOutput, calls=%fused_computation.3 | convolution fusion | flops 7521697792 | bytes 26214400 | tf_op jit(solution)/shard_map/stf,fd->std/dot_general | solution.py:1240
  419.2 3.9 fusion.14
  423.1 17.5 %collective-permute-done.3 = bf16[4,128,1024]{2,0,1:T(4,128)(2,1)} collective-permute-done((bf16[4,128,1024]{2,0,1:T(4,128)(2,1)}, bf16[4,128,1024]{2,0,1:T(4,128)(2,1)}, u32[]{:S(2)}, u32[]{:S(2)}) %collective-permute-start.3) | collective-permute-done | bytes 1048608 | tf_op jit(solution)/shard_map/ppermute | solution.py:682
  440.6 7.6 fusion.25
  452.1 22.6 %collective-permute-done.4 = bf16[4,128,1024]{2,0,1:T(4,128)(2,1)} collective-permute-done((bf16[4,128,1024]{2,0,1:T(4,128)(2,1)}, bf16[4,128,1024]{2,0,1:T(4,128)(2,1)}, u32[]{:S(2)}, u32[]{:S(2)}) %collective-permute-start.4) | collective-permute-done | bytes 1048608 | tf_op jit(solution)/shard_map/ppermute | solution.py:682
  478.9 15.6 %bitcast_convert_fusion = bf16[2048,3584]{1,0:T(8,128)(2,1)} fusion(bf16[4,128,2048]{2,0,1:T(4,128)(2,1)S(1)} %pad_maximum_fusion.1, f32[4,128,3584]{2,1,0:T(8,128)} %copy-done.93), kind=kOutput, calls=%fused_computation | convolution fusion | flops 7529037824 | bytes 24117248 | tf_op jit(solution)/shard_map/td,tf->df/dot_general | solution.py:1255
  494.5 16.4 %multiply_convert_fusion = bf16[4,128,3584]{2,1,0:T(8,128)(2,1)S(1)} fusion(f32[4,128,3584]{2,1,0:T(8,128)} %copy-done.93, bf16[3584,2048]{1,0:T(8,128)(2,1)} %param.39, bf16[4,128,2048]{2,0,1:T(4,128)(2,1)} %copy-done.60), kind=kOutput, calls=%fused_computation.13 | convolution fusion | flops 7523532800 | bytes 27787264 | tf_op jit(solution)/shard_map/std,fd->stf/dot_general | solution.py:1271
  511.0 12.4 fusion.4
  523.4 4.8 fusion.87
  528.2 11.0 multiply_reduce_fusion.1
  541.1 3.5 fusion.20
  548.5 3.8 broadcast_select_fusion.1
  554.9 6.9 convolution_convert_fusion
  561.7 34.0 %collective-permute-done.6 = bf16[4,128,2048]{2,0,1:T(4,128)(2,1)} collective-permute-done((bf16[4,128,2048]{2,0,1:T(4,128)(2,1)}, bf16[4,128,2048]{2,0,1:T(4,128)(2,1)}, u32[]{:S(2)}, u32[]{:S(2)}) %collective-permute-start.6) | collective-permute-done | bytes 2097184 | tf_op jit(solution)/shard_map/ppermute | solution.py:682
  595.7 7.0 multiply_reduce_fusion.2
  602.9 5.7 fusion.76
  612.2 3.4 convert_element_type.135
  615.7 3.8 fusion.16
  619.5 13.6 %shard_map.359 = (f32[512,1024]{1,0:T(8,128)S(1)}, bf16[512,1024]{1,0:T(8,128)(2,1)S(1)}, bf16[4,8,64,128]{3,2,1,0:T(8,128)(2,1)}, f32[4,8,1024]{2,1,0:T(8,128)S(1)}) custom-call(f32[512,1024]{1,0:T(8,128)S(1)} %bitcast.140, f32[512,1024]{1,0:T(8,128)S(1)} %copy-done.20, f32[4,512,1024]{2,1,0:T(8,128)} %fusion.88.rkv_ref.kv_ref.gate_ref, ...), custom_call_target="tpu_custom_call" | custom-call | flops 15000000512 | bytes 13639680 | tf_op jit(solution)/shard_map/pallas_call | solution.py:364
  635.4 4.1 copy.237
  648.5 67.1 %reduce-scatter.8.cloned.1.call-done = bf16[128,2048]{1,0:T(8,128)(2,1)} async-done(((bf16[2048,2048]{1,0:T(8,128)(2,1)}), bf16[128,2048]{1,0:T(8,128)(2,1)}) %reduce-scatter.8.cloned.1.call-update) | async-done | bytes 524304 | tf_op jit(solution)/shard_map/reduce_scatter | solution.py:1263
  717.8 151.2 %reduce-scatter.4.cloned.1.call-done = bf16[128,3584]{1,0:T(8,128)(2,1)} async-done(((bf16[2048,3584]{1,0:T(8,128)(2,1)}), bf16[128,3584]{1,0:T(8,128)(2,1)}) %reduce-scatter.4.cloned.1.call-update) | async-done | bytes 917520 | tf_op jit(solution)/shard_map/reduce_scatter | solution.py:1263
  875.9 19.7 %shard_map.360 = (bf16[512,1024]{1,0:T(8,128)(2,1)S(1)}, f32[512,1024]{1,0:T(8,128)S(1)}, f32[512,1024]{1,0:T(8,128)S(1)}, f32[512,1024]{1,0:T(8,128)S(1)}, f32[4,8,1024]{2,1,0:T(8,128)S(1)}) custom-call(f32[4,512,1024]{2,1,0:T(8,128)} %fusion.88.rkv_ref.kv_ref.gate_ref, f32[512,1024]{1,0:T(8,128)S(1)} %copy-done.17, f32[1,1024]{1,0:T(1,128)S(1)} %copy-done.9, ...), custom_call_target="tpu_custom_call" | custom-call | flops 22000001024 | bytes 13635584 | tf_op jit(solution)/shard_map/pallas_call | solution.py:364
  899.7 17.6 %all-gather.13.cloned.1.call-done = bf16[32,8,64,128]{3,2,1,0:T(8,128)(2,1)} async-done(((bf16[4,8,64,128]{3,2,1,0:T(8,128)(2,1)}), bf16[32,8,64,128]{3,2,1,0:T(8,128)(2,1)}) %all-gather.13.cloned.1.call-update) | async-done | bytes 4194320 | tf_op jit(solution)/shard_map/all_gather | solution.py:1300
  923.2 21.3 %shard_map.361 = (bf16[512,1024]{1,0:T(8,128)(2,1)S(1)}, bf16[512,1024]{1,0:T(8,128)(2,1)S(1)}, f32[512,1024]{1,0:T(8,128)S(1)}, f32[4,8,64,128]{3,2,1,0:T(8,128)S(1)}, f32[4,8,1024]{2,1,0:T(8,128)S(1)}) custom-call(s32[1]{0:T(128)} %bitcast.place_ref, f32[4,512,1024]{2,1,0:T(8,128)} %fusion.88.rkv_ref.kv_ref.gate_ref, f32[512,1024]{1,0:T(8,128)S(1)} %copy-done.18, ...), custom_call_target="tpu_custom_call" | custom-call | flops 24000000000 | bytes 27262980 | tf_op jit(solution)/shard_map/pallas_call | solution.py:364
  947.2 63.1 %shard_map.362 = (f32[4,128,2048]{2,1,0:T(8,128)}, f32[4,1,2048]{2,1,0:T(1,128)}, f32[8,2048]{1,0:T(8,128)}, f32[160,2048]{1,0:T(8,128)}, f32[160,2048]{1,0:T(8,...) custom-call(bf16[4,128,2048]{2,1,0:T(8,128)(2,1)} %x_ref.3, f32[4,1,2048]{2,1,0:T(1,128)} %copy-done.6, ...), custom_call_target="tpu_custom_call" | custom-call | flops 70000001024 | bytes 41943040 | tf_op jit(solution)/shard_map/pallas_call | solution.py:650
  1014.7 4.4 fusion.33
  1026.0 189.6 %shard_map.363 = (f32[128,1024]{1,0:T(8,128)}, f32[128,1024]{1,0:T(8,128)}, f32[128,1024]{1,0:T(8,128)}, f32[128,1024]{1,0:T(8,128)}, f32[128,1024]{1,0:T(8,128)...) custom-call(bf16[4,512,2048]{2,1,0:T(8,128)(2,1)} %get-tuple-element.90.refs_0_, ...), custom_call_target="tpu_custom_call" | custom-call | flops 215040000000 | bytes 22544384 | tf_op jit(solution)/shard_map/pallas_call | solution.py:903
  1217.5 6.9 copy.260
  1237.8 18.3 %collective-permute-done.9 = bf16[4,128,1024]{2,0,1:T(4,128)(2,1)S(1)} collective-permute-done((bf16[4,128,1024]{2,0,1:T(4,128)(2,1)S(1)}, bf16[4,128,1024]{2,0,1:T(4,128)(2,1)S(1)}, u32[]{:S(2)}, u32[]{:S(2)}) %collective-permute-start.9) | collective-permute-done | bytes 1048608 | tf_op jit(solution)/shard_map/ppermute | solution.py:682
  (348 shorter events, 150.8 us)
Async XLA Ops:
  7.2 153.8 %all-gather.7.cloned.1.call-start = ((), (), s32[]{:S(2)}) async-start(), calls=%async_computation.3 | async-start | bytes 17825792 | tf_op jit(solution)/shard_map/all_gather | solution.py:1172
  7.9 239.6 %all-gather.11.cloned.1.call-start = ((), (), s32[]{:S(2)}) async-start(), calls=%async_computation.8 | async-start | bytes 5898240 | tf_op jit(solution)/shard_map/all_gather | solution.py:1211
  19.5 46.4 %copy-start.53 = (f32[4,128,2048]{2,0,1:T(4,128)}, f32[4,128,2048]{2,0,1:T(4,128)S(1)}, u32[]{:S(2)}) copy-start(f32[4,128,2048]{2,0,1:T(4,128)S(1)} %copy_convert_fusion.2) | copy-start | bytes 12582916
  19.7 46.3 %copy-start.81 = (f32[4]{0:T(128)}, f32[4]{0:T(128)S(1)}, u32[]{:S(2)}) copy-start(f32[4]{0:T(128)S(1)} %broadcast_multiply_fusion.1) | copy-start | bytes 52
  20.7 45.3 %copy-start.84 = (f32[4]{0:T(128)}, f32[4]{0:T(128)S(1)}, u32[]{:S(2)}) copy-start(f32[4]{0:T(128)S(1)} %fusion.67) | copy-start | bytes 52
  66.1 4.4 collective-permute-start
  68.5 17.7 %copy-start.87 = (s32[1024]{0:T(1024)}, s32[1024]{0:T(1024)S(1)}, u32[]{:S(2)}) copy-start(s32[1024]{0:T(1024)S(1)} %fusion.58) | copy-start | bytes 12292
  70.2 131.2 %copy-start.8 = (f32[1,1024]{1,0:T(1,128)}, f32[1,1024]{1,0:T(1,128)S(1)}, u32[]{:S(2)}) copy-start(f32[1,1024]{1,0:T(1,128)S(1)} %get-tuple-element.282.bonus_ref) | copy-start | bytes 12292
  70.3 304.1 %copy-start.5 = (f32[8,2048]{1,0:T(8,128)}, f32[8,2048]{1,0:T(8,128)S(1)}, u32[]{:S(2)}) copy-start(f32[8,2048]{1,0:T(8,128)S(1)} %slice_convert_fusion.3.coeff_ref) | copy-start | bytes 196612
  70.4 15.8 %copy-start.7 = (f32[2,2048]{1,0:T(2,128)}, f32[2,2048]{1,0:T(2,128)S(1)}, u32[]{:S(2)}) copy-start(f32[2,2048]{1,0:T(2,128)S(1)} %pad_maximum_fusion.5.norm_ref) | copy-start | bytes 49156
  70.5 15.7 %copy-start.6 = (f32[4,1,2048]{2,1,0:T(1,128)}, f32[4,1,2048]{2,1,0:T(1,128)S(1)}, u32[]{:S(2)}) copy-start(f32[4,1,2048]{2,1,0:T(1,128)S(1)} %reshape.354.before_ref) | copy-start | bytes 98308
  90.5 87.4 %copy-start.38 = (f32[512,64]{1,0:T(8,128)}, f32[512,64]{1,0:T(8,128)S(1)}, u32[]{:S(2)}) copy-start(f32[512,64]{1,0:T(8,128)S(1)} %get-tuple-element.112.decay_ref) | copy-start | bytes 393220
  161.0 16.9 %copy-start.15 = (f32[512,1024]{1,0:T(8,128)S(1)}, f32[512,1024]{1,0:T(8,128)}, u32[]{:S(2)}) copy-start(f32[512,1024]{1,0:T(8,128)} %copy-done.14) | copy-start | bytes 6291460
  193.1 108.5 %all-gather.9.cloned.1.call-start = ((), (), s32[]{:S(2)}) async-start(), calls=%async_computation.4 | async-start | bytes 4456448 | tf_op jit(solution)/shard_map/all_gather | solution.py:1173
  193.9 521.7 %reduce-scatter.8.cloned.1.call-start = ((), (), s32[]{:S(2)}) async-start(), calls=%async_computation.7 | async-start | bytes 8912896 | tf_op jit(solution)/shard_map/reduce_scatter | solution.py:1263
  309.2 47.9 %collective-permute-start.1 = (bf16[4,128,2048]{2,0,1:T(4,128)(2,1)S(1)}, bf16[4,128,2048]{2,0,1:T(4,128)(2,1)S(1)}, u32[]{:S(2)}, u32[]{:S(2)}) collective-permute-start(bf16[4,128,2048]{2,0,1:T(4,128)(2,1)S(1)} %copy.339), channel_id=1, source_target_pairs={{0,1},{1,0},{2,3},{3,2},{4,5},{5,4},{6,7},{7,6},{8,9},{9,8},{10,11... | collective-permute-start | bytes 6291464 | tf_op jit(solution)/shard_map/ppermute | solution.py:682
  373.0 4.1 collective-permute-start.2
  382.3 16.2 %copy-start.48 = (bf16[4,128,2048]{2,0,1:T(4,128)(2,1)}, bf16[4,128,2048]{2,0,1:T(4,128)(2,1)S(1)}, u32[]{:S(2)}) copy-start(bf16[4,128,2048]{2,0,1:T(4,128)(2,1)S(1)} %get-tuple-element.266) | copy-start | bytes 6291460
  382.3 36.0 %copy-start.47 = (bf16[4,128,2048]{2,0,1:T(4,128)(2,1)}, bf16[4,128,2048]{2,0,1:T(4,128)(2,1)S(1)}, u32[]{:S(2)}) copy-start(bf16[4,128,2048]{2,0,1:T(4,128)(2,1)S(1)} %get-tuple-element.265) | copy-start | bytes 6291460
  398.5 14.0 %copy-start.93 = (f32[4,128,3584]{2,1,0:T(8,128)}, f32[4,128,3584]{2,1,0:T(8,128)S(1)}, u32[]{:S(2)}) copy-start(f32[4,128,3584]{2,1,0:T(8,128)S(1)} %fusion.6) | copy-start | bytes 22020100
  414.9 25.7 %collective-permute-start.3 = (bf16[4,128,1024]{2,0,1:T(4,128)(2,1)}, bf16[4,128,1024]{2,0,1:T(4,128)(2,1)}, u32[]{:S(2)}, u32[]{:S(2)}) collective-permute-start(bf16[4,128,1024]{2,0,1:T(4,128)(2,1)} %copy.340), channel_id=1, source_target_pairs={{0,1},{1,0},{2,3},{3,2},{4,5},{5,4},{6,7},{7,6},{8,9},{9,8},{10,11... | collective-permute-start | bytes 3145736 | tf_op jit(solution)/shard_map/ppermute | solution.py:682
  419.2 21.4 %copy-start.41 = (f32[4,128,2048]{2,0,1:T(4,128)S(1)}, f32[4,128,2048]{2,0,1:T(4,128)}, u32[]{:S(2)}) copy-start(f32[4,128,2048]{2,0,1:T(4,128)} %copy-done.39) | copy-start | bytes 12582916
  419.2 21.4 %copy-start.46 = (bf16[4,128,1024]{2,1,0:T(8,128)(2,1)S(1)}, bf16[4,128,1024]{2,1,0:T(8,128)(2,1)}, u32[]{:S(2)}) copy-start(bf16[4,128,1024]{2,1,0:T(8,128)(2,1)} %param.41) | copy-start | bytes 3145732
  448.2 26.4 %collective-permute-start.4 = (bf16[4,128,1024]{2,0,1:T(4,128)(2,1)}, bf16[4,128,1024]{2,0,1:T(4,128)(2,1)}, u32[]{:S(2)}, u32[]{:S(2)}) collective-permute-start(bf16[4,128,1024]{2,0,1:T(4,128)(2,1)} %get-tuple-element.269), channel_id=1, source_target_pairs={{0,1},{1,0},{2,3},{3,2},{4,5},{5,4},{6,7},{7,6},{8,9},{9,8},{10,11... | collective-permute-start | bytes 3145736 | tf_op jit(solution)/shard_map/ppermute | solution.py:682
  451.5 97.0 %collective-permute-start.7 = (bf16[4,128,1024]{2,0,1:T(4,128)(2,1)}, bf16[4,128,1024]{2,0,1:T(4,128)(2,1)}, u32[]{:S(2)}, u32[]{:S(2)}) collective-permute-start(bf16[4,128,1024]{2,0,1:T(4,128)(2,1)} %copy.242), channel_id=1, source_target_pairs={{0,1},{1,0},{2,3},{3,2},{4,5},{5,4},{6,7},{7,6},{8,9},{9,8},{10,11... | collective-permute-start | bytes 3145736 | tf_op jit(solution)/shard_map/ppermute | solution.py:682
  511.0 12.4 copy-start.65
  539.8 4.8 collective-permute-start.5
  547.0 7.8 copy-start.66
  547.0 48.7 %collective-permute-start.6 = (bf16[4,128,2048]{2,0,1:T(4,128)(2,1)}, bf16[4,128,2048]{2,0,1:T(4,128)(2,1)}, u32[]{:S(2)}, u32[]{:S(2)}) collective-permute-start(bf16[4,128,2048]{2,0,1:T(4,128)(2,1)} %convert_element_type.131), channel_id=1, source_target_pairs={{0,1},{1,0},{2,3},{3,2},{4,5},{5,4},{6,7},{7,6},{8,9},{9,8},{10,11... | collective-permute-start | bytes 6291464 | tf_op jit(solution)/shard_map/ppermute | solution.py:682
  611.6 257.4 %reduce-scatter.4.cloned.1.call-start = ((), (), s32[]{:S(2)}) async-start(), calls=%async_computation.5 | async-start | bytes 15597568 | tf_op jit(solution)/shard_map/reduce_scatter | solution.py:1263
  612.2 305.1 %all-gather.13.cloned.1.call-start = ((), (), s32[]{:S(2)}) async-start(), calls=%async_computation.9 | async-start | bytes 4718592 | tf_op jit(solution)/shard_map/all_gather | solution.py:1300
  634.5 601.7 %reduce-scatter.6.cloned.1.call-start = ((), (), s32[]{:S(2)}) async-start(), calls=%async_computation.6 | async-start | bytes 4177920 | tf_op jit(solution)/shard_map/reduce_scatter | solution.py:676
  645.9 225.6 %copy-start.9 = (f32[1,1024]{1,0:T(1,128)S(1)}, f32[1,1024]{1,0:T(1,128)}, u32[]{:S(2)}) copy-start(f32[1,1024]{1,0:T(1,128)} %copy-done.8) | copy-start | bytes 12292
  947.2 67.5 %copy-start.88 = (s32[1024]{0:T(1024)S(1)}, s32[1024]{0:T(1024)}, u32[]{:S(2)}) copy-start(s32[1024]{0:T(1024)} %copy-done.87) | copy-start | bytes 12292
  1010.3 9.0 copy-start.68
  1010.3 9.1 copy-start.62
  1011.2 8.6 collective-permute-start.8
  1026.0 189.6 %copy-start.52 = (f32[128,3584]{1,0:T(8,128)S(1)}, f32[128,3584]{1,0:T(8,128)}, u32[]{:S(2)}) copy-start(f32[128,3584]{1,0:T(8,128)} %convert_element_type.136) | copy-start | bytes 5505028
  1217.5 8.0 copy-start.90
  1217.5 8.0 copy-start.91
  1217.5 8.0 copy-start.76
  1217.5 8.0 copy-start.78
  1217.5 8.0 copy-start.83
  1217.5 8.0 copy-start.86
  1230.0 26.1 %collective-permute-start.9 = (bf16[4,128,1024]{2,0,1:T(4,128)(2,1)S(1)}, bf16[4,128,1024]{2,0,1:T(4,128)(2,1)S(1)}, u32[]{:S(2)}, u32[]{:S(2)}) collective-permute-start(bf16[4,128,1024]{2,0,1:T(4,128)(2,1)S(1)} %dynamic-slice_convert_fusion), channel_id=1, source_target_pairs={{0,1},{1,0},{2,3},{3,2},{4,5},{5,4},{6,7},{7,6},{8,9},{9,8},{10,11... | collective-permute-start | bytes 3145736 | tf_op jit(solution)/shard_map/ppermute | solution.py:682
  1237.1 24.8 %copy-start.63 = (f32[480,128]{1,0:T(8,128)S(1)}, f32[480,128]{1,0:T(8,128)}, u32[]{:S(2)}) copy-start(f32[480,128]{1,0:T(8,128)} %reduce-scatter.6.cloned.1.call-done) | copy-start | bytes 737284
  1237.1 28.5 %collective-permute-start.10 = (f32[400,128]{1,0:T(8,128)S(1)}, f32[400,128]{1,0:T(8,128)S(1)}, u32[]{:S(2)}, u32[]{:S(2)}) collective-permute-start(f32[400,128]{1,0:T(8,128)S(1)} %slice.272), channel_id=1, source_target_pairs={{0,1},{1,0},{2,3},{3,2},{4,5},{5,4},{6,7},{7,6},{8,9},{9,8},{10,11... | collective-permute-start | bytes 614408 | tf_op jit(solution)/shard_map/ppermute | solution.py:682
  1259.4 9.3 copy-start.67
  (64 other events, 170.4 us)
Sparse Core Ops, SparseCore 0:
  10.3 150.6 all-gather.6
  193.3 54.1 all-gather.10
  249.6 52.0 all-gather.8
  611.7 103.8 reduce-scatter.7
  719.5 149.3 reduce-scatter.3
  871.0 46.2 all-gather.12
  1026.1 94.2 reduce-scatter.5

commit v5 on v4

--- a/solution.py
+++ b/solution.py
@@ -194,7 +194,7 @@
     place = place_ref[0]
     for pair in range(WIDE // PAIR):
         lanes = slice(pair * PAIR, (pair + 1) * PAIR)
-        state = start_ref[0, pair]
+        state = jnp.concatenate([start_ref[0, 2 * pair], start_ref[0, 2 * pair + 1]], axis=1)
         extra = packed_ref[:, 0, pair, PAIR // 2 :, :]
         decays = block_decays(extra)
         extra = extra.astype(jnp.float32)
@@ -304,7 +304,8 @@
             term = terms_ref[k, 0, pair].astype(jnp.float32)
             later = jnp.where(k > place, decays[k] * later + term, later)
             whole = decays[k] * whole + term
-        start_ref[0, pair] = whole
+        start_ref[0, 2 * pair] = whole[:, : PAIR // 2]
+        start_ref[0, 2 * pair + 1] = whole[:, PAIR // 2 :]
         spread_later = spread(later).astype(jnp.bfloat16)
         fade = jnp.exp(final - total)
         far_keys = fade * halves_dot(values, spread_later, ((1,), (1,)))
@@ -336,6 +337,9 @@
         self.stack = pl.BlockSpec((3, length, WIDE), lambda s, p: (0, s, p))
         self.gate = pl.BlockSpec((1, length, WIDE), lambda s, p: (3, s, p))
         self.state = pl.BlockSpec((1, WIDE // PAIR, PAIR // 2, PAIR), lambda s, p: (s, p, 0, 0))
+        self.heads = pl.BlockSpec(
+            (1, 2 * WIDE // PAIR, PAIR // 2, PAIR // 2), lambda s, p: (s, p, 0, 0)
+        )
         self.sums = pl.BlockSpec((1, 8, WIDE), lambda s, p: (s, 0, p))
         self.place = pl.BlockSpec(memory_space=pltpu.SMEM)
 
@@ -376,7 +380,7 @@
     def totals(self, projected, log_rows):
         outs = [(self.packed(), self.state_shape(jnp.bfloat16, PAIR // 2 + EXTRA))]
         return self.call(
-            totals_kernel, [self.stack, self.tokens], outs, (projected, log_rows), 14 * 10**9
+            totals_kernel, [self.stack, self.tokens], outs, (projected, log_rows), 10**9
         )[0]
 
     def inner(self, projected, log_rows, bonus):
@@ -385,7 +389,7 @@
             (self.tokens, self.token_shape(jnp.bfloat16)),
         ]
         ins = [self.stack, self.tokens, self.row]
-        return self.call(inner_kernel, ins, outs, (projected, log_rows, bonus), 16 * 10**9)
+        return self.call(inner_kernel, ins, outs, (projected, log_rows, bonus), 2 * 10**9)
 
     def join(self, place, inner, decayed, projected, packed, start, gain, bias):
         ins = [
@@ -394,7 +398,7 @@
             self.tokens,
             self.gate,
             self.packed(packed.shape[0]),
-            self.state,
+            self.heads,
             self.row,
             self.row,
         ]
@@ -405,7 +409,7 @@
             (self.sums, self.sums_shape()),
         ]
         args = (place, inner, decayed, projected, packed, start, gain, bias)
-        return self.call(join_kernel, ins, outs, args, 21 * 10**9)
+        return self.call(join_kernel, ins, outs, args, 10**9)
 
     def back_join(self, grad, wkv, projected, decayed, gain, bias):
         ins = [self.tokens, self.tokens, self.gate, self.tokens, self.row, self.row]
@@ -416,7 +420,7 @@
             (self.sums, self.sums_shape()),
         ]
         args = (grad, wkv, projected, decayed, gain, bias)
-        return self.call(back_join_kernel, ins, outs, args, 15 * 10**9)
+        return self.call(back_join_kernel, ins, outs, args, 10**9)
 
     def back_inner(self, projected, log_rows, bonus, grad, state):
         ins = [self.stack, self.tokens, self.row, self.tokens, self.state]
@@ -428,7 +432,7 @@
             (self.sums, self.sums_shape()),
         ]
         args = (projected, log_rows, bonus, grad, state)
-        return self.call(back_inner_kernel, ins, outs, args, 22 * 10**9)
+        return self.call(back_inner_kernel, ins, outs, args, 4 * 10**9)
 
     def back_outer(self, place, projected, log_rows, keys, values, running, state, packed, terms):
         blocks = packed.shape[0]
@@ -447,23 +451,16 @@
             (self.tokens, self.token_shape(jnp.bfloat16)),
             (self.tokens, self.token_shape(jnp.bfloat16)),
             (self.tokens, self.token_shape(jnp.float32)),
-            (self.state, self.state_shape(jnp.float32)),
+            (
+                self.heads,
+                jax.ShapeDtypeStruct(
+                    (self.sequences, 2 * self.pairs, PAIR // 2, PAIR // 2), jnp.float32
+                ),
+            ),
             (self.sums, self.sums_shape()),
         ]
         args = (place, projected, log_rows, keys, values, running, state, packed, terms)
-        return self.call(back_outer_kernel, ins, outs, args, 24 * 10**9)
-
-
-def paired_states(states):
-    sequences, heads, size, _ = states.shape
-    pairs = states.reshape(sequences, heads // 2, 2, size, size)
-    return pairs.transpose(0, 1, 3, 2, 4).reshape(sequences, heads // 2, size, 2 * size)
-
-
-def single_states(pairs):
-    sequences, count, size, _ = pairs.shape
-    heads = pairs.reshape(sequences, count, size, 2, size).transpose(0, 1, 3, 2, 4)
-    return heads.reshape(sequences, 2 * count, size, size)
+        return self.call(back_outer_kernel, ins, outs, args, 3 * 10**9)
 
 
 BRANCHES = (3, 1, 2, 4)
@@ -486,27 +483,29 @@
     decay_up_ref,
     block_ref,
     edge_ref,
-    sums_ref,
-    grad_up_ref,
-    grad_down_ref,
-    grad_decay_down_ref,
+    all_ref,
     grad_decay_up_ref,
     hat_ref,
     grad_diff_ref,
     grad_all_ref,
 ):
-    length, columns = x_ref.shape[1:]
+    together, length, columns = x_ref.shape
+    tokens = together * length
     ranks = up_ref.shape[0] // 5
+    up_rows, decay_rows = up_ref.shape[0], decay_down_ref.shape[0]
+    sums_ref = all_ref.at[0:8]
+    grad_up_ref = all_ref.at[16 : 16 + up_rows]
+    grad_down_ref = all_ref.at[16 + up_rows : 16 + 2 * up_rows]
+    grad_decay_down_ref = all_ref.at[16 + 2 * up_rows : 16 + 2 * up_rows + decay_rows]
     strips = columns // STRIP
     low = jnp.bfloat16
-    last = length - 1
 
     @pl.when(pl.program_id(0) == 0)
     def _():
-        for ref in (sums_ref, grad_up_ref, grad_down_ref, grad_decay_down_ref, grad_decay_up_ref):
+        for ref in (all_ref, grad_decay_up_ref):
             ref[...] = jnp.zeros_like(ref)
 
-    x = x_ref[0].astype(jnp.float32)
+    x = x_ref[...].reshape(tokens, columns).astype(jnp.float32)
     mean = jnp.mean(x, axis=-1, keepdims=True)
     variance = jnp.mean((x - mean) * (x - mean), axis=-1, keepdims=True)
     scale = lax.rsqrt(variance + NORM_EPS)
@@ -524,12 +523,15 @@
     def normed_and_diff(at, hat):
         normed = hat * norm_ref[0:1, at] + norm_ref[1:2, at]
         earlier = pltpu.roll(normed, 1, 0)
-        earlier = jnp.where(iota(normed.shape, 0) == 0, before_ref[0, :, at], earlier)
+        for k in range(together):
+            earlier = jnp.where(
+                iota(normed.shape, 0) == k * length, before_ref[k, :, at], earlier
+            )
         return normed, earlier - normed
 
     def first(strip, grad_pre):
         at = strip_of(strip)
-        hat = (x_ref[0, :, at].astype(jnp.float32) - mean) * scale
+        hat = (x_ref[:, :, at].reshape(tokens, STRIP).astype(jnp.float32) - mean) * scale
         hat_ref[:, at] = hat
         normed, diff = normed_and_diff(at, hat)
         grad_diff = jnp.zeros_like(diff)
@@ -572,9 +574,10 @@
         grad_down_ref[:, at] += halves_dot(grad_pre, normed + diff * coeff, ((0,), (0,)))
         sums_ref[0:1, at] += jnp.sum(grad_base * diff, axis=0, keepdims=True)
         grad_diff = grad_diff_ref[:, at] + grad_base * coeff
-        edge_ref[0, :, at] = grad_diff[0:1]
-        onward = pltpu.roll(grad_diff, last, 0)
-        onward = jnp.where(iota(onward.shape, 0) == last, 0.0, onward)
+        onward = pltpu.roll(grad_diff, tokens - 1, 0)
+        for k in range(together):
+            edge_ref[k, :, at] = grad_diff[k * length : k * length + 1]
+            onward = jnp.where(iota(onward.shape, 0) == (k + 1) * length - 1, 0.0, onward)
         grad = grad_base + grad_all_ref[:, at] - grad_diff + onward
         sums_ref[6:7, at] += jnp.sum(grad * hat, axis=0, keepdims=True)
         sums_ref[7:8, at] += jnp.sum(grad, axis=0, keepdims=True)
@@ -584,13 +587,14 @@
         against += jnp.sum(q * hat, axis=-1, keepdims=True)
         return total, against
 
-    zero = jnp.zeros((length, 1), jnp.float32)
+    zero = jnp.zeros((tokens, 1), jnp.float32)
     total, against = lax.fori_loop(0, strips, second, (zero, zero))
     total, against = total * (1.0 / columns), against * (1.0 / columns)
 
     def third(strip, carry):
         at = strip_of(strip)
-        block_ref[0, :, at] = scale * (grad_all_ref[:, at] - total - hat_ref[:, at] * against)
+        block = scale * (grad_all_ref[:, at] - total - hat_ref[:, at] * against)
+        block_ref[:, :, at] = block.reshape(together, length, STRIP)
         return carry
 
     lax.fori_loop(0, strips, third, 0)
@@ -610,6 +614,7 @@
     up,
     decay_down,
     decay_up,
+    sum_rows,
 ):
     sequences, length, columns = block_input.shape
     heads = grad_proj.shape[-1]
@@ -621,15 +626,14 @@
     def kept(shape):
         return pl.BlockSpec(shape, lambda s: (0, 0)), jax.ShapeDtypeStruct(shape, jnp.float32)
 
-    block = pl.BlockSpec((1, length, columns), lambda s: (s, 0, 0))
-    edge = pl.BlockSpec((1, 1, columns), lambda s: (s, 0, 0))
+    together = 2 - sequences % 2
+    tokens = together * length
+    block = pl.BlockSpec((together, length, columns), lambda s: (s, 0, 0))
+    edge = pl.BlockSpec((together, 1, columns), lambda s: (s, 0, 0))
     outs = [
         (block, jax.ShapeDtypeStruct(block_input.shape, jnp.float32)),
         (edge, jax.ShapeDtypeStruct((sequences, 1, columns), jnp.float32)),
-        kept((8, columns)),
-        kept((ranks, columns)),
-        kept((ranks, columns)),
-        kept((decay_ranks, columns)),
+        kept((sum_rows, columns)),
         kept((decay_ranks, heads)),
     ]
     args = (
@@ -649,33 +653,25 @@
     )
     return pl.pallas_call(
         mix_back_kernel,
-        grid=(sequences,),
+        grid=(sequences // together,),
         in_specs=[
             block,
             edge,
-            pl.BlockSpec((4, length, heads), lambda s: (0, s, 0)),
-            pl.BlockSpec((length, heads), lambda s: (s, 0)),
-            pl.BlockSpec((length, hidden.shape[1]), lambda s: (s, 0)),
-            pl.BlockSpec((length, decay_ranks), lambda s: (s, 0)),
+            pl.BlockSpec((4, tokens, heads), lambda s: (0, s, 0)),
+            pl.BlockSpec((tokens, heads), lambda s: (s, 0)),
+            pl.BlockSpec((tokens, hidden.shape[1]), lambda s: (s, 0)),
+            pl.BlockSpec((tokens, decay_ranks), lambda s: (s, 0)),
             pl.BlockSpec(projections.shape, lambda s: (0, 0, 0), pipeline_mode=pl.Buffered(1)),
         ]
         + [whole(array) for array in args[7:]],
         out_specs=[spec for spec, _ in outs],
         out_shape=[shape for _, shape in outs],
-        scratch_shapes=[pltpu.VMEM((length, columns), jnp.float32)] * 3,
+        scratch_shapes=[pltpu.VMEM((tokens, columns), jnp.float32)] * 3,
         compiler_params=pltpu.CompilerParams(vmem_limit_bytes=58 * 2**20),
         cost_estimate=pl.CostEstimate(
-            flops=7 * 10**10, bytes_accessed=40 * 2**20, transcendentals=0
+            flops=10**10, bytes_accessed=40 * 2**20, transcendentals=0
         ),
     )(*args)
-
-
-def sum_columns(rows):
-    shards = lax.axis_size("dp") * lax.axis_size("seq")
-    parts = rows.reshape(rows.shape[0], shards, -1).transpose(1, 0, 2)
-    return lax.psum_scatter(
-        parts.reshape(-1, parts.shape[2]), ("dp", "seq"), scatter_dimension=0, tiled=True
-    )
 
 
 def other_half(block):
@@ -721,13 +717,16 @@
 def ring_kernel(dp_size, seq_size, rows, widths, runs, places, operands, *refs):
     products = len(widths)
     lefts = [(refs[left], lead) for left, _, lead in places]
-    rights = [(refs[right], lead) for _, right, lead in places]
-    totals, refs = refs[operands : operands + products], refs[operands + products :]
+    rights = [(None if right is None else refs[right], lead) for _, right, lead in places]
+    sent_ref, received_ref = refs[operands - 1], refs[operands + products]
+    totals, refs = refs[operands : operands + products], refs[operands + products + 1 :]
     rings = len(runs)
     mine, pair_out, pair_in, ring_out, ring_in = [
         refs[k * rings : (k + 1) * rings] for k in range(5)
     ]
-    pair_send, pair_recv, pair_free, ring_send, ring_recv, ring_free = refs[5 * rings :]
+    pair_send, pair_recv, pair_free, ring_send, ring_recv, ring_free, half_send, half_recv = refs[
+        5 * rings :
+    ]
     count, chip, own = ring_places(dp_size, seq_size)
     position, core = own(), lax.rem(lax.axis_index("seq"), CORES)
 
@@ -738,9 +737,19 @@
     sibling = device(position, 1 - core)
     after, before = device(position + 1, core), device(position - 1, core)
     barrier = pltpu.get_barrier_semaphore()
-    for other in (sibling, after, before):
+    partner = {"tp": 1 - lax.axis_index("tp")}
+    for other in (sibling, after, before, partner):
         pl.semaphore_signal(barrier, inc=1, device_id=other, device_id_type=pl.DeviceIdType.MESH)
-    pl.semaphore_wait(barrier, 3)
+    pl.semaphore_wait(barrier, 4)
+    halves = pltpu.make_async_remote_copy(
+        src_ref=sent_ref,
+        dst_ref=received_ref,
+        send_sem=half_send,
+        recv_sem=half_recv,
+        device_id=partner,
+        device_id_type=pl.DeviceIdType.MESH,
+    )
+    halves.start()
 
     def pair_copy(ring):
         return pltpu.make_async_remote_copy(
@@ -769,6 +778,13 @@
         at = 0
         for product, first, wide in runs[ring]:
             ref, lead = lefts[product]
+            if rights[product][0] is None:
+                if rows % 128 == 0:
+                    put(at, wide, ref[pl.ds(first, wide), pl.ds(start, rows)].T)
+                else:
+                    put(at, wide, ref[pl.ds(start, rows), pl.ds(first, wide)])
+                at += wide
+                continue
             if rows % 128 == 0:
                 left = ref[(*lead, slice(None), pl.ds(start, rows))]
             else:
@@ -879,9 +895,10 @@
         pair_copy(ring).wait_send()
         for step in (count - 3, count - 2):
             ring_copy(ring, step % 2).wait_send()
-
-
-def ring_sums(pairs, sizes, collective_id):
+    halves.wait()
+
+
+def ring_sums(pairs, given, sent, sizes, collective_id):
     dp_size, seq_size = sizes
     rows = pairs[0][0].shape[-1] // (dp_size * seq_size)
     tokens = pairs[0][1].shape[-2]
@@ -895,7 +912,9 @@
 
     for left, right, lead in pairs:
         places.append((place_of(left, rows % 128 != 0), place_of(right, False), lead))
-    widths = [right.shape[-1] for _, right, _ in pairs]
+    places.append((place_of(given, rows % 128 != 0), None, ()))
+    operands.append(sent)
+    widths = [right.shape[-1] for _, right, _ in pairs] + [given.shape[0]]
     rings = 4
     runs = cut_rings(widths, rings)
     each = sum(widths) // rings
@@ -904,9 +923,10 @@
         functools.partial(
             ring_kernel, dp_size, seq_size, rows, widths, runs, places, len(operands)
         ),
-        out_shape=[jax.ShapeDtypeStruct((rows, wide), jnp.float32) for wide in widths],
+        out_shape=[jax.ShapeDtypeStruct((rows, wide), jnp.float32) for wide in widths]
+        + [jax.ShapeDtypeStruct(sent.shape, sent.dtype)],
         in_specs=[pl.BlockSpec(memory_space=pltpu.VMEM)] * len(operands),
-        out_specs=[pl.BlockSpec(memory_space=pltpu.VMEM)] * len(pairs),
+        out_specs=[pl.BlockSpec(memory_space=pltpu.VMEM)] * (len(widths) + 1),
         scratch_shapes=[pltpu.VMEM((rows, each), jnp.float32)] * rings
         + [pltpu.VMEM((rows, each), low)] * (2 * rings)
         + [pltpu.VMEM((2, rows, each), low)] * (2 * rings)
@@ -917,97 +937,144 @@
             pltpu.SemaphoreType.DMA((rings, 2)),
             pltpu.SemaphoreType.DMA((rings, 2)),
             pltpu.SemaphoreType.REGULAR((rings,)),
+            pltpu.SemaphoreType.DMA(()),
+            pltpu.SemaphoreType.DMA(()),
         ],
         compiler_params=pltpu.CompilerParams(
             collective_id=collective_id, has_side_effects=True, vmem_limit_bytes=60 * 2**20
         ),
         cost_estimate=pl.CostEstimate(
-            flops=int(28 * 10**6 * sum(widths)),
+            flops=2 * tokens * rows * dp_size * seq_size * sum(widths),
             bytes_accessed=2 * tokens * (2048 * len(pairs) + sum(widths)),
             transcendentals=0,
         ),
     )(*operands)
 
 
-def spread_kernel(dp_size, seq_size, part_ref, whole_ref, local, send, recv, pair_send, pair_recv):
-    count = dp_size * seq_size // CORES
-    per_row, width = seq_size // CORES, part_ref.shape[1]
-    row, core = lax.axis_index("dp"), lax.rem(lax.axis_index("seq"), CORES)
-    position = row * per_row + lax.div(lax.axis_index("seq"), CORES)
+def gather_kernel(
+    dp_size,
+    seq_size,
+    small_ref,
+    proj_ref,
+    out_ref,
+    small_all,
+    proj_all,
+    out_all,
+    keep,
+    send,
+    recv,
+    pair_send,
+    pair_recv,
+):
+    width = small_ref.shape[1]
+    count, chip, own = ring_places(dp_size, seq_size)
+    position, core = own(), lax.rem(lax.axis_index("seq"), CORES)
+    far = count // 2
+    hops = [(far, far - 1), (far, far - 1), (far - 1, far), (far - 1, far)]
+    halfway = proj_ref.shape[0] // 2
 
     def device(place, which):
-        place = lax.rem(place + count, count)
-        return {"dp": lax.div(place, per_row), "seq": lax.rem(place, per_row) * CORES + which}
-
-    def columns(place, which):
-        place = lax.rem(place + count, count)
-        return pl.ds(pl.multiple_of((place * CORES + which) * width, width), width)
-
+        row, column = chip(place)
+        return {"dp": row, "seq": column * CORES + which}
+
+    def regions(place, which):
+        row, column = chip(place)
+        start = (row * seq_size + column * CORES + which) * width
+        at = pl.ds(pl.multiple_of(start, width), width)
+        return [
+            small_all.at[:, at],
+            proj_all.at[:halfway, at, :],
+            proj_all.at[halfway:, at, :],
+            out_all.at[:, at],
+        ]
+
+    sources = [small_ref, proj_ref.at[:halfway], proj_ref.at[halfway:], out_ref]
+    sibling = device(position, 1 - core)
+    ways = [device(position + 1, core), device(position - 1, core)]
     barrier = pltpu.get_barrier_semaphore()
-    sibling = device(position, 1 - core)
-    for other in [sibling] + [device(position + k, core) for k in range(1, count)]:
+    for other in [sibling] + ways:
         pl.semaphore_signal(barrier, inc=1, device_id=other, device_id_type=pl.DeviceIdType.MESH)
-    pl.semaphore_wait(barrier, count)
-
-    own = whole_ref.at[:, columns(position, core)]
-    keep = pltpu.make_async_copy(part_ref, own, local)
-    keep.start()
-    copies = [
-        pltpu.make_async_remote_copy(
-            src_ref=part_ref,
-            dst_ref=own,
-            send_sem=send.at[k],
-            recv_sem=recv.at[k],
-            device_id=device(position + k, core),
+    pl.semaphore_wait(barrier, 3)
+
+    def place_of(way, hop):
+        return position - hop if way == 0 else position + hop
+
+    def onward(part, way, hop):
+        at = regions(place_of(way, hop - 1), core)[part]
+        return pltpu.make_async_remote_copy(
+            src_ref=sources[part] if hop == 1 else at,
+            dst_ref=at,
+            send_sem=send.at[part, way, hop - 1],
+            recv_sem=recv.at[part, way, hop - 1],
+            device_id=ways[way],
             device_id_type=pl.DeviceIdType.MESH,
         )
-        for k in range(1, count)
+
+    def across(part, way, hop):
+        at = regions(place_of(way, hop), core)[part]
+        return pltpu.make_async_remote_copy(
+            src_ref=sources[part] if hop == 0 else at,
+            dst_ref=at,
+            send_sem=pair_send.at[part, way, hop],
+            recv_sem=pair_recv.at[part, way, hop],
+            device_id=sibling,
+            device_id_type=pl.DeviceIdType.MESH,
+        )
+
+    parts = range(len(sources))
+    kept = []
+    for part in parts:
+        for way in range(2):
+            onward(part, way, 1).start()
+        across(part, 0, 0).start()
+        copy = pltpu.make_async_copy(
+            sources[part], regions(position, core)[part], keep.at[part]
+        )
+        copy.start()
+        kept.append(copy)
+    for hop in range(1, far + 1):
+        for part in parts:
+            for way in range(2):
+                if hop <= hops[part][way]:
+                    onward(part, way, hop).wait_recv()
+                    if hop < hops[part][way]:
+                        onward(part, way, hop + 1).start()
+                    across(part, way, hop).start()
+    for part in parts:
+        kept[part].wait()
+        across(part, 0, 0).wait()
+        for way in range(2):
+            for hop in range(1, hops[part][way] + 1):
+                onward(part, way, hop).wait_send()
+                across(part, way, hop).wait()
+
+
+def gather_weights(small, proj, out, sizes, collective_id):
+    if small.shape[1] % 128:
+        return (
+            lax.all_gather(small, ("dp", "seq"), axis=1, tiled=True),
+            lax.all_gather(proj, ("dp", "seq"), axis=1, tiled=True),
+            lax.all_gather(out, ("dp", "seq"), axis=1, tiled=True),
+        )
+    dp_size, seq_size = sizes
+    every = dp_size * seq_size
+    far = every // CORES // 2
+    rows, width = small.shape
+    shapes = [
+        (rows, width * every),
+        (proj.shape[0], width * every, proj.shape[2]),
+        (out.shape[0], width * every),
     ]
-    passed = []
-    for k in range(count):
-        at = whole_ref.at[:, columns(position - k, core)]
-        passed.append(
-            pltpu.make_async_remote_copy(
-                src_ref=part_ref if k == 0 else at,
-                dst_ref=at,
-                send_sem=pair_send.at[k],
-                recv_sem=pair_recv.at[k],
-                device_id=sibling,
-                device_id_type=pl.DeviceIdType.MESH,
-            )
-        )
-    for copy in copies:
-        copy.start()
-    passed[0].start()
-    for k in range(1, count):
-        copies[k - 1].wait_recv()
-        passed[k].start()
-    keep.wait()
-    for copy in copies:
-        copy.wait_send()
-    for copy in passed:
-        copy.wait()
-
-
-def spread_columns(part, sizes, collective_id):
-    if part.shape[1] % 128:
-        return lax.all_gather(part, ("dp", "seq"), axis=1, tiled=True)
-    dp_size, seq_size = sizes
-    count = dp_size * seq_size // CORES
-    rows, width = part.shape
     return pl.pallas_call(
-        functools.partial(spread_kernel, dp_size, seq_size),
-        out_shape=jax.ShapeDtypeStruct((rows, width * dp_size * seq_size), part.dtype),
-        in_specs=[pl.BlockSpec(memory_space=pltpu.VMEM)],
-        out_specs=pl.BlockSpec(memory_space=pltpu.VMEM),
-        scratch_shapes=[pltpu.SemaphoreType.DMA(())] + [pltpu.SemaphoreType.DMA((count,))] * 4,
-        compiler_params=pltpu.CompilerParams(
-            collective_id=collective_id, has_side_effects=True, vmem_limit_bytes=16 * 2**20
-        ),
-        cost_estimate=pl.CostEstimate(
-            flops=50 * 10**9, bytes_accessed=4 * 2**20, transcendentals=0
-        ),
-    )(part)
+        functools.partial(gather_kernel, dp_size, seq_size),
+        out_shape=[jax.ShapeDtypeStruct(shape, small.dtype) for shape in shapes],
+        in_specs=[pl.BlockSpec(memory_space=pl.ANY)] * 3,
+        out_specs=[pl.BlockSpec(memory_space=pl.ANY)] * 3,
+        scratch_shapes=[pltpu.SemaphoreType.DMA((4,))]
+        + [pltpu.SemaphoreType.DMA((4, 2, far))] * 2
+        + [pltpu.SemaphoreType.DMA((4, 2, far + 1))] * 2,
+        compiler_params=pltpu.CompilerParams(collective_id=collective_id, has_side_effects=True),
+    )(small, proj, out)
 
 
 def mix_kernel(
@@ -1093,7 +1160,7 @@
         + [jax.ShapeDtypeStruct((tokens, wide), kind) for wide, kind in outs],
         compiler_params=pltpu.CompilerParams(vmem_limit_bytes=40 * 2**20),
         cost_estimate=pl.CostEstimate(
-            flops=17 * 10**9, bytes_accessed=16 * 2**20, transcendentals=10**5
+            flops=2 * 10**9, bytes_accessed=16 * 2**20, transcendentals=10**5
         ),
     )(*args)
 
@@ -1136,16 +1203,11 @@
     down_at = up_at + ranks
     decay_at = down_at + ranks
     narrow_at = decay_at + decay_ranks
-    own_rows = jnp.concatenate(
+    top_rows = jnp.concatenate(
+        [norm_gains, norm_biases, mixing_coefficients, jnp.zeros((4, width), jnp.bfloat16)]
+    )
+    low_rows = jnp.concatenate(
         [
-            norm_gains,
-            norm_biases,
-            mixing_coefficients,
-            jnp.zeros((4, width), jnp.bfloat16),
-            mixing_up_weight,
-            mix_down.T,
-            decay_down.T,
-            narrow_rows(decay_up),
             narrow_rows(time_decay),
             narrow_rows(time_first),
             narrow_rows(group_gain),
@@ -1153,7 +1215,20 @@
             jnp.zeros((12, width), jnp.bfloat16),
         ]
     )
-    spread_rows = spread_columns(own_rows, sizes, 1)
+    top_rows, low_rows = lax.optimization_barrier((top_rows, low_rows))
+    own_rows = jnp.concatenate(
+        [
+            top_rows,
+            mixing_up_weight,
+            mix_down.T,
+            decay_down.T,
+            narrow_rows(decay_up),
+            low_rows,
+        ]
+    )
+    spread_rows, projections, out_proj = gather_weights(
+        own_rows, proj_weights, out_weight, sizes, 1
+    )
     channel = jnp.arange(head_cols)
     lane = (channel % head_size) // each * width + channel // head_size * each + channel % each
     choose = (jnp.arange(spread_rows.shape[1])[:, None] == lane[None, :]).astype(jnp.bfloat16)
@@ -1169,8 +1244,6 @@
     base_row, bonus, group_scale, group_shift = (
         narrow_all[decay_ranks + k : decay_ranks + k + 1] for k in range(4)
     )
-    projections = lax.all_gather(proj_weights, ("dp", "seq"), axis=1, tiled=True)
-    out_proj = lax.all_gather(out_weight, ("dp", "seq"), axis=1, tiled=True)
     seq_count, length, feature_columns = block_input.shape
     tokens = seq_count * length
     own_cols = channel_recept.shape[1]
@@ -1184,13 +1257,13 @@
     def own_half(rows):
         return lax.dynamic_slice_in_dim(rows, half * own_cols, own_cols, rows.ndim - 1)
 
-    def half_sum(part):
-        sent = lax.dynamic_slice_in_dim(part, (1 - half) * own_cols, own_cols, part.ndim - 1)
-        return own_half(part) + other_half(sent.astype(jnp.bfloat16)).astype(jnp.float32)
+    def add_last(rows, last):
+        at_last = jnp.arange(length)[None, :, None] == length - 1
+        return rows + jnp.where(at_last, last[:, None, :], 0.0)
 
     full_out = both_halves(out_grad)
-    input_f = block_input.astype(jnp.float32)
-    last_one = layer_norm(input_f[:, -1], gains_all[0], biases_all[0])
+    last_input = block_input[:, -1].astype(jnp.float32)
+    last_one = layer_norm(last_input, gains_all[0], biases_all[0])
     preceding_first = from_behind(last_one.astype(jnp.bfloat16), "seq", 1)
     preceding_first = preceding_first.astype(jnp.float32)[:, None, :]
     norm_one = jnp.stack([gains_all[0], biases_all[0]])
@@ -1216,7 +1289,7 @@
         decayed,
         projected,
         all_packed,
-        paired_states(initial_state),
+        initial_state,
         group_scale,
         group_shift,
     )
@@ -1225,8 +1298,9 @@
     total_least = jnp.min(decay_range[:, 0], axis=-1)
     total_most = jnp.max(decay_range[:, 1], axis=-1)
     mixer_part = jnp.einsum("std,de->ste", mixer_in, out_proj, preferred_element_type=jnp.float32)
+    late_input, mixer_part = lax.optimization_barrier((block_input, mixer_part))
     residual = (
-        input_f + mixer_part + other_half(mixer_part.astype(jnp.bfloat16)).astype(jnp.float32)
+        late_input.astype(jnp.float32) + mixer_part + other_half(mixer_part.astype(jnp.bfloat16)).astype(jnp.float32)
     )
     normed_two, norm_two_back = jax.vjp(layer_norm, residual, gains_all[1], biases_all[1])
     prev_two = from_behind(normed_two[:, -1, :].astype(jnp.bfloat16), "seq", 1).astype(jnp.float32)
@@ -1237,13 +1311,18 @@
     chan_recept_b = chan_recept.astype(jnp.bfloat16)
     key_pre = jnp.einsum("std,df->stf", chan_key_b, channel_key, preferred_element_type=jnp.float32)
     hidden = jnp.square(jnp.maximum(key_pre, 0.0)).astype(jnp.bfloat16)
-    value_part = jnp.einsum(
-        "stf,fd->std", hidden, channel_value, preferred_element_type=jnp.float32
-    )
+    own_value, sent_value = (
+        lax.dynamic_slice_in_dim(channel_value, which * own_cols, own_cols, 1)
+        for which in (half, 1 - half)
+    )
+    sent_part = jnp.einsum("stf,fd->std", hidden, sent_value, preferred_element_type=jnp.float32)
+    other_part = other_half(sent_part.astype(jnp.bfloat16)).astype(jnp.float32)
+    own_part = jnp.einsum("stf,fd->std", hidden, own_value, preferred_element_type=jnp.float32)
     recept_pre = jnp.einsum(
         "std,de->ste", chan_recept_b, channel_recept, preferred_element_type=jnp.float32
     )
-    kv_rows = half_sum(value_part)
+    own_part, recept_pre = lax.optimization_barrier((own_part, recept_pre))
+    kv_rows = own_part + other_part
     gate_chan = jax.nn.sigmoid(recept_pre)
     output = (own_half(residual) + gate_chan * kv_rows).astype(jnp.bfloat16)
     grad_out = out_grad.astype(jnp.float32)
@@ -1278,10 +1357,10 @@
     )
     part_normed_two, part_prev_two, grad_coeffs_chan = chan_back((part_key, part_recept))
     from_next_two = from_behind(for_sending(part_prev_two), "seq", -1).astype(jnp.float32)
-    part_normed_two = part_normed_two.at[:, -1, :].add(from_next_two)
+    part_normed_two = add_last(part_normed_two, from_next_two)
     sizes = (lax.axis_size("dp"), blocks)
     grad_key_rows = grad_key.reshape(tokens, -1)
-    key_cut = grad_key_rows.shape[1] * 4 // 7
+    key_cut = grad_key_rows.shape[1] * 5 // 7
     key_whole = weight_terms(chan_key_b, grad_key_rows[:, :key_cut])
     grad_normed_two = part_normed_two + other_half(part_normed_two.astype(jnp.bfloat16)).astype(
         jnp.float32
@@ -1289,7 +1368,6 @@
     grad_residual, grad_gain_two, grad_bias_two = norm_two_back(grad_normed_two)
     grad_residual = grad_residual + full_out.astype(jnp.float32)
     grad_residual, key_whole = lax.optimization_barrier((grad_residual, key_whole))
-    key_sum = scattered(key_whole)
     grad_branch = grad_residual.astype(jnp.bfloat16)
     grad_mixer = jnp.einsum(
         "ste,de->std", grad_branch, out_proj, preferred_element_type=jnp.float32
@@ -1298,11 +1376,12 @@
         grad_mixer.reshape(tokens, head_cols), wkv, projected, decayed, group_scale, group_shift
     )
     all_terms = lax.all_gather(block_term, "seq")
-    grad_wkv, value_sum = lax.optimization_barrier((grad_wkv, value_sum))
+    grad_wkv, value_sum, key_whole = lax.optimization_barrier((grad_wkv, value_sum, key_whole))
+    key_sum = scattered(key_whole)
     grad_receive, near_key, near_value, running, bonus_sums = recurrence.back_inner(
         projected, log_flat, bonus, grad_wkv, state
     )
-    grad_keys, grad_values, grad_log, start_pairs, rate_sums = recurrence.back_outer(
+    grad_keys, grad_values, grad_log, state_grad, rate_sums = recurrence.back_outer(
         where_here,
         projected,
         log_flat,
@@ -1313,10 +1392,9 @@
         all_packed,
         all_terms,
     )
-    state_grad = single_states(start_pairs)
 
     grad_proj = jnp.stack([grad_receive, grad_keys, grad_values, grad_gate])
-    part_block, edge, mix_sums, up_grad, down_grad, decay_down_grad, lift_grad = mix_back(
+    part_block, edge, small_rows, lift_grad = mix_back(
         block_input,
         preceding_first,
         grad_proj,
@@ -1330,11 +1408,12 @@
         lowrank_up,
         decay_projection,
         lift_rows,
+        narrow_at + 112,
     )
     from_next_one = from_behind(edge[:, 0].astype(jnp.bfloat16), "seq", -1).astype(jnp.float32)
-    _, last_back = jax.vjp(layer_norm, input_f[:, -1], gains_all[0], biases_all[0])
+    _, last_back = jax.vjp(layer_norm, last_input, gains_all[0], biases_all[0])
     part_last, gain_last, bias_last = last_back(from_next_one)
-    part_block = part_block.at[:, -1].add(part_last)
+    part_block = add_last(part_block, part_last)
     head_rows = jnp.concatenate(
         [
             lift_grad,
@@ -1344,38 +1423,43 @@
             jnp.zeros((12, head_cols), jnp.float32),
         ]
     )
-    head_rows = lax.dot_general(
-        head_rows,
-        choose.astype(jnp.float32),
-        (((1,), (1,)), ((), ())),
-        precision=lax.Precision.HIGHEST,
-    )
-    small_rows = jnp.concatenate(
+    thirds = []
+    for _ in range(3):
+        thirds.append(head_rows.astype(jnp.bfloat16))
+        head_rows = head_rows - lax.optimization_barrier(thirds[-1]).astype(jnp.float32)
+    head_rows = jnp.sum(
+        lax.dot_general(
+            jnp.stack(thirds),
+            choose,
+            (((2,), (1,)), ((), ())),
+            preferred_element_type=jnp.float32,
+        ),
+        axis=0,
+    )
+    other_rows = jnp.concatenate(
         [
-            jnp.stack([mix_sums[6] + gain_last, 0.5 * grad_gain_two]),
-            jnp.stack([mix_sums[7] + bias_last, 0.5 * grad_bias_two]),
-            mix_sums[:6],
             grad_coeffs_chan[6:],
-            jnp.zeros((4, feature_columns), jnp.float32),
-            up_grad,
-            down_grad,
-            decay_down_grad,
-            head_rows,
+            jnp.stack([0.5 * grad_gain_two, 0.5 * grad_bias_two, gain_last, bias_last]),
+            jnp.zeros((2, feature_columns), jnp.float32),
         ]
     )
-    half_block = half_sum(part_block)
-    small_sums = sum_columns(small_rows)
-    input_grad = own_half(grad_residual) + half_block
-    *proj_sums, out_sum, recept_sum, key_rest = ring_sums(
+    small_rows = lax.dynamic_update_slice(small_rows, other_rows, (8, 0))
+    small_rows = lax.dynamic_update_slice(small_rows, head_rows, (narrow_at, 0))
+    sent_block = lax.dynamic_slice_in_dim(part_block, (1 - half) * own_cols, own_cols, 2)
+    *proj_sums, out_sum, recept_sum, key_rest, small_sums, other_block = ring_sums(
         [(stacked, grad_proj, (branch,)) for branch in range(4)]
         + [
             (grad_branch.reshape(tokens, -1), mixer_in.reshape(tokens, -1), ()),
             (chan_recept_b.reshape(tokens, -1), grad_recept.reshape(tokens, -1), ()),
             (chan_key_b.reshape(tokens, -1), grad_key_rows[:, key_cut:], ()),
         ],
+        small_rows,
+        sent_block.astype(jnp.bfloat16),
         sizes,
         0,
     )
+    small_sums = small_sums.T
+    input_grad = own_half(grad_residual) + own_half(part_block) + other_block.astype(jnp.float32)
     shared = small_sums[:narrow_at] + other_half(small_sums[:narrow_at])
     narrow = small_sums[narrow_at:, : heads_here * each]
     head_sums = [
@@ -1385,10 +1469,10 @@
         output,
         input_grad,
         state_grad,
-        shared[:2],
-        shared[2:4],
-        jnp.concatenate([shared[4:5], shared[6:12]], axis=0),
-        shared[5:6],
+        jnp.stack([shared[6] + shared[12], shared[10]]),
+        jnp.stack([shared[7] + shared[13], shared[11]]),
+        jnp.concatenate([shared[:1], shared[2:6], shared[8:10]], axis=0),
+        shared[1:2],
         shared[down_at:decay_at].T,
         shared[up_at:down_at],
         shared[decay_at:].T,

time: 1290 us -> 931 us (0.72)
  waiting for transfers between devices: 499 us -> 199 us
  local copies, waits for them, and re-layouts: 120 us -> 70.1 us
  Pallas kernels: 412 us -> 457 us
  other arithmetic: 92.4 us -> 56.1 us
    reduce_scatter x2, waiting for transfers between devices: 218 us -> 27.1 us  [scattered(): lax.psum_scatter(whole, ('dp', 'seq'), scatter_dimension=0, tiled=True)]
    all_gather x2 -> x0, waiting for transfers between devices: 97.7 us -> none  [the longest x1 70.5 us: per_device(): lax.all_gather(proj_weights, ('dp', 'seq'), axis=1, tiled=True)]
    pallas_call x2, Pallas kernels: 108 us -> 161 us  [the longest x1 117 us: gather_weights(): pl.pallas_call(functools.partial(gather_kernel, dp_size, seq_size), out_s...]
    ppermute x7 -> x6, waiting for transfers between devices: 139 us -> 119 us  [other_half(): return lax.ppermute(block, 'tp', [(0, 1), (1, 0)])]
    unnamed x216 -> x192, local copies, waits for them, and re-layouts: 67.6 us -> 53.3 us
  transfers between devices with their start and end apart: 18 -> 14, of which waited for: 11 -> 9; matrix products, arithmetic and copies ran while one was open for 14% -> 13% of each run, Pallas kernels for 25% -> 32%
where the time goes in v5:
time: 931 us; the launch traced here: 922 us
  Pallas kernels  457 us (49%)
  waiting for transfers between devices  199 us (21%)
  matrix products  110 us (12%)
  local copies, waits for them, and re-layouts  70.1 us (8%)
  other arithmetic  56.1 us (6%)
  between operations  15.3 us (2%)
  starting transfers between devices  14.8 us (2%)
    pallas_call x1, Pallas kernels, ring_sums(): pl.pallas_call(functools.partial(ring_kernel, dp_size, seq_size, rows, wi...  180 us
    ppermute x6, waiting for transfers between devices, other_half(): return lax.ppermute(block, 'tp', [(0, 1), (1, 0)])  119 us
    pallas_call x1, Pallas kernels, gather_weights(): pl.pallas_call(functools.partial(gather_kernel, dp_size, seq_size), out_s...  117 us
    pallas_call x6, Pallas kernels, call(): pl.pallas_call(kernel, grid=self.grid, in_specs=ins, out_specs=[spec for...  100 us
    unnamed x192, local copies, waits for them, and re-layouts  53.3 us
    pallas_call x1, Pallas kernels, mix_back(): pl.pallas_call(mix_back_kernel, grid=(sequences // together,), in_specs=[...  44 us
    all_gather x1, waiting for transfers between devices, per_device(): all_packed = lax.all_gather(recurrence.totals(projected, log_flat), 'seq')  35.5 us
    reduce_scatter x2, waiting for transfers between devices, scattered(): lax.psum_scatter(whole, ('dp', 'seq'), scatter_dimension=0, tiled=True)  27.1 us
  transfers between devices with their start and end apart: 14, of which 9 were waited for; matrix products, arithmetic and copies ran while one was open for 13% of the time, Pallas kernels for 32%

profile of v5, /device:TPU:0, one launch (start us, length us, event | category | flops | bytes accessed | tf_op | source)
XLA Modules:
  0.0 922.2 jit_solution(7785782188696536779)
XLA Ops:
  17.4 117.2 %shard_map.354 = (bf16[480,2048]{1,0:T(8,128)(2,1)}, bf16[4,2048,1024]{2,1,0:T(8,128)(2,1)}, bf16[1024,2048]{1,0:T(8,128)(2,1)}) custom-call(bf16[480,128]{1,0:T(8,128)(2,1)} %copy-done.69, bf16[4,128,1024]{2,1,0:T(8,128)(2,1)} %proj_ref.1, bf16[1024,128]{1,0:T(8,128)(2,1)} %out_ref.1), custom_call_target="tpu_custom_call" | custom-call | tf_op jit(solution)/shard_map/pallas_call | solution.py:1068
  135.6 2.3 collective-permute-start
  140.2 2.9 fusion.7
  144.3 14.9 %shard_map.355 = (bf16[4,512,2048]{2,1,0:T(8,128)(2,1)}, f32[512,160]{1,0:T(8,128)S(1)}, f32[512,64]{1,0:T(8,128)S(1)}, f32[512,1024]{1,0:T(8,128)S(1)}) custom-call(bf16[4,128,2048]{2,1,0:T(8,128)(2,1)S(1)} %copy-done.2, f32[4,1,2048]{2,1,0:T(1,128)S(1)} %reshape.331.before_ref, f32[8,2048]{1,0:T(8,128)S(1)} %slice_convert_fusion.2.coeff_ref, ...), custom_call_target="tpu_custom_call" | custom-call | flops 2000000000 | bytes 16777216 | tf_op jit(solution)/shard_map/pallas_call | solution.py:1149
  161.4 13.8 %fusion.99.rkv_ref.kv_ref.gate_ref = f32[4,512,1024]{2,1,0:T(8,128)S(1)} fusion(bf16[4,512,2048]{2,1,0:T(8,128)(2,1)} %get-tuple-element.78.refs_0_, bf16[4,2048,1024]{2,1,0:T(8,128)(2,1)} %get-tuple-element.79.proj_ref), kind=kOutput, calls=%fused_computation.193 | convolution fusion | flops 8589934592 | bytes 33554432 | tf_op jit(solution)/shard_map/ntd,nde->nte/dot_general | solution.py:1281
  176.7 11.8 %shard_map.357 = bf16[4,8,80,128]{3,2,1,0:T(8,128)(2,1)} custom-call(f32[4,512,1024]{2,1,0:T(8,128)S(1)} %fusion.99.rkv_ref.kv_ref.gate_ref, f32[512,1024]{1,0:T(8,128)S(1)} %copy-done.6), custom_call_target="tpu_custom_call" | custom-call | flops 1000000000 | bytes 10485760 | tf_op jit(solution)/shard_map/pallas_call | solution.py:368
  188.5 3.3 copy-done
  192.4 3.4 copy-done.1
  197.4 14.0 %shard_map.356 = (f32[512,1024]{1,0:T(8,128)S(1)}, bf16[512,1024]{1,0:T(8,128)(2,1)S(1)}) custom-call(f32[4,512,1024]{2,1,0:T(8,128)S(1)} %copy-done.1, f32[512,1024]{1,0:T(8,128)S(1)} %copy-done.7, f32[1,1024]{1,0:T(1,128)S(1)} %get-tuple-element.232.bonus_ref), custom_call_target="tpu_custom_call" | custom-call | flops 2000000000 | bytes 10489856 | tf_op jit(solution)/shard_map/pallas_call | solution.py:368
  212.7 35.5 %all-gather.5.cloned.1.call-done = bf16[32,8,80,128]{3,2,1,0:T(8,128)(2,1)} async-done(((bf16[4,8,80,128]{3,2,1,0:T(8,128)(2,1)}), bf16[32,8,80,128]{3,2,1,0:T(8,128)(2,1)}) %all-gather.5.cloned.1.call-update) | async-done | bytes 5242896 | tf_op jit(solution)/shard_map/all_gather | solution.py:1284
  249.7 18.9 %shard_map.358 = (f32[512,1024]{1,0:T(8,128)S(1)}, bf16[512,1024]{1,0:T(8,128)(2,1)S(1)}, f32[4,8,64,128]{3,2,1,0:T(8,128)S(1)}, f32[4,8,1024]{2,1,0:T(8,128)S(1)}) custom-call(s32[1]{0:T(128)} %bitcast.place_ref, f32[512,1024]{1,0:T(8,128)S(1)} %copy-done.16, bf16[512,1024]{1,0:T(8,128)(2,1)S(1)} %get-tuple-element.82.decayed_ref, f32[4,512,1024]{2,1,0:T(8,128)} %copy-done, ...), custom_call_target="tpu_custom_call" | custom-call | flops 1000000000 | bytes 17833988 | tf_op jit(solution)/shard_map/pallas_call | solution.py:368
  268.7 2.4 fusion.24
  273.0 46.3 %collective-permute-done.1 = bf16[4,128,2048]{2,1,0:T(8,128)(2,1)S(1)} collective-permute-done((bf16[4,128,2048]{2,1,0:T(8,128)(2,1)S(1)}, bf16[4,128,2048]{2,1,0:T(8,128)(2,1)S(1)}, u32[]{:S(2)}, u32[]{:S(2)}) %collective-permute-start.1) | collective-permute-done | bytes 2097184 | tf_op jit(solution)/shard_map/ppermute | solution.py:678
  322.4 2.8 multiply_add_fusion.1
  328.4 4.9 add_convert_fusion
  334.6 13.0 %fusion.4 = f32[4,128,3584]{2,1,0:T(8,128)} fusion(bf16[4,128,2048]{2,1,0:T(8,128)(2,1)S(1)} %get-tuple-element.217, bf16[2048,3584]{1,0:T(8,128)(2,1)} %param.34), kind=kOutput, calls=%fused_computation.5 | convolution fusion | flops 7516192768 | bytes 24117248 | tf_op jit(solution)/shard_map/std,df->stf/dot_general | solution.py:1312
  347.7 6.5 fusion.33
  355.7 2.3 fusion.20
  358.8 6.4 fusion.12
  365.2 14.7 %collective-permute-done.3 = bf16[4,128,1024]{2,1,0:T(8,128)(2,1)S(1)} collective-permute-done((bf16[4,128,1024]{2,1,0:T(8,128)(2,1)S(1)}, bf16[4,128,1024]{2,1,0:T(8,128)(2,1)S(1)}, u32[]{:S(2)}, u32[]{:S(2)}) %collective-permute-start.3) | collective-permute-done | bytes 1048608 | tf_op jit(solution)/shard_map/ppermute | solution.py:678
  379.9 3.5 fusion.31
  384.9 23.4 %collective-permute-done.4 = bf16[4,128,1024]{2,1,0:T(8,128)(2,1)} collective-permute-done((bf16[4,128,1024]{2,1,0:T(8,128)(2,1)S(1)}, bf16[4,128,1024]{2,1,0:T(8,128)(2,1)}, u32[]{:S(2)}, u32[]{:S(2)}) %collective-permute-start.4) | collective-permute-done | bytes 1048608 | tf_op jit(solution)/shard_map/ppermute | solution.py:678
  411.2 14.6 %bitcast_convert_fusion = bf16[2048,3584]{1,0:T(8,128)(2,1)} fusion(bf16[4,128,1024]{2,1,0:T(8,128)(2,1)S(1)} %get-tuple-element.223, bf16[4,128,1024]{2,1,0:T(8,128)(2,1)S(1)} %get-tuple-element.222, f32[4,128,3584]{2,1,0:T(8,128)} %fusion.4), kind=kOutput, calls=%fused_computation | convolution fusion | flops 7533232128 | bytes 24117248 | tf_op jit(solution)/shard_map/td,tf->df/dot_general | solution.py:1334
  427.5 15.9 %multiply_convert_fusion = bf16[4,128,3584]{2,1,0:T(8,128)(2,1)} fusion(f32[4,128,3584]{2,1,0:T(8,128)} %fusion.4, bf16[4,128,2048]{2,1,0:T(8,128)(2,1)} %pad_maximum_fusion.1, bf16[3584,2048]{1,0:T(8,128)(2,1)} %param.35), kind=kOutput, calls=%fused_computation.16 | convolution fusion | flops 7523532800 | bytes 27787264 | tf_op jit(solution)/shard_map/std,fd->stf/dot_general | solution.py:1350
  443.4 13.9 %fusion.2 = f32[4,128,2048]{2,1,0:T(8,128)S(1)} fusion(bf16[4,128,3584]{2,1,0:T(8,128)(2,1)} %multiply_convert_fusion, bf16[2048,3584]{1,0:T(8,128)(2,1)} %param.34), kind=kOutput, calls=%fused_computation.3 | convolution fusion | flops 7516192768 | bytes 22544384 | tf_op jit(solution)/shard_map/stf,df->std/dot_general | solution.py:1354
  457.4 6.0 multiply_reduce_fusion.2
  466.5 4.0 fusion.90
  470.5 3.1 broadcast_select_fusion.1
  473.7 8.4 convolution_convert_fusion
  482.0 34.4 %collective-permute-done.6 = bf16[4,128,2048]{2,1,0:T(8,128)(2,1)S(1)} collective-permute-done((bf16[4,128,2048]{2,1,0:T(8,128)(2,1)}, bf16[4,128,2048]{2,1,0:T(8,128)(2,1)S(1)}, u32[]{:S(2)}, u32[]{:S(2)}) %collective-permute-start.6) | collective-permute-done | bytes 2097184 | tf_op jit(solution)/shard_map/ppermute | solution.py:678
  516.4 4.5 multiply_reduce_fusion.3
  522.6 2.2 multiply_reduce_fusion
  527.0 3.4 copy-done.79
  530.4 2.4 fusion.22
  532.8 13.4 %shard_map.359 = (f32[512,1024]{1,0:T(8,128)S(1)}, bf16[512,1024]{1,0:T(8,128)(2,1)S(1)}, bf16[4,8,64,128]{3,2,1,0:T(8,128)(2,1)}, f32[4,8,1024]{2,1,0:T(8,128)S(1)}) custom-call(f32[512,1024]{1,0:T(8,128)S(1)} %bitcast.137, f32[512,1024]{1,0:T(8,128)S(1)} %copy-done.18, f32[4,512,1024]{2,1,0:T(8,128)} %copy-done, ...), custom_call_target="tpu_custom_call" | custom-call | flops 1000000000 | bytes 13639680 | tf_op jit(solution)/shard_map/pallas_call | solution.py:368
  547.2 27.1 %reduce-scatter.3.cloned.1.call-done = bf16[128,3584]{1,0:T(8,128)(2,1)} async-done(((bf16[2048,3584]{1,0:T(8,128)(2,1)}), bf16[128,3584]{1,0:T(8,128)(2,1)}) %reduce-scatter.3.cloned.1.call-update) | async-done | bytes 917520 | tf_op jit(solution)/shard_map/reduce_scatter | solution.py:1342
  574.4 2.6 convert_element_type.168
  577.8 2.5 slice.222.refs_7_
  582.0 19.9 %shard_map.360 = (bf16[512,1024]{1,0:T(8,128)(2,1)S(1)}, f32[512,1024]{1,0:T(8,128)S(1)}, f32[512,1024]{1,0:T(8,128)S(1)}, f32[512,1024]{1,0:T(8,128)S(1)}, f32[4,8,1024]{2,1,0:T(8,128)S(1)}) custom-call(f32[4,512,1024]{2,1,0:T(8,128)} %copy-done, f32[512,1024]{1,0:T(8,128)S(1)} %copy-done.8, f32[1,1024]{1,0:T(1,128)S(1)} %copy-done.33, ...), custom_call_target="tpu_custom_call" | custom-call | flops 4000000000 | bytes 13635584 | tf_op jit(solution)/shard_map/pallas_call | solution.py:368
  606.8 16.1 %all-gather.7.cloned.1.call-done = bf16[32,8,64,128]{3,2,1,0:T(8,128)(2,1)} async-done(((bf16[4,8,64,128]{3,2,1,0:T(8,128)(2,1)}), bf16[32,8,64,128]{3,2,1,0:T(8,128)(2,1)}) %all-gather.7.cloned.1.call-update) | async-done | bytes 4194320 | tf_op jit(solution)/shard_map/all_gather | solution.py:1378
  627.6 22.4 %shard_map.361 = (bf16[512,1024]{1,0:T(8,128)(2,1)S(1)}, bf16[512,1024]{1,0:T(8,128)(2,1)S(1)}, f32[512,1024]{1,0:T(8,128)S(1)}, f32[4,16,64,64]{3,2,1,0:T(8,128)}, f32[4,8,1024]{2,1,0:T(8,128)S(1)}) custom-call(s32[1]{0:T(128)} %bitcast.place_ref, f32[4,512,1024]{2,1,0:T(8,128)} %copy-done, f32[512,1024]{1,0:T(8,128)S(1)} %copy-done.8, ...), custom_call_target="tpu_custom_call" | custom-call | flops 3000000000 | bytes 27262980 | tf_op jit(solution)/shard_map/pallas_call | solution.py:368
  650.1 2.6 pad_maximum_fusion.grad_ref.refs_1_
  652.8 44.0 %shard_map.362 = (f32[4,128,2048]{2,1,0:T(8,128)}, f32[4,1,2048]{2,1,0:T(1,128)}, f32[512,2048]{1,0:T(8,128)}, f32[64,1024]{1,0:T(8,128)}) custom-call(bf16[4,128,2048]{2,1,0:T(8,128)(2,1)} %x_ref.3, f32[4,1,2048]{2,1,0:T(1,128)} %copy-done.30, bf16[4,512,1024]{2,1,0:T(8,128)(2,1)} %pad_maximum_fusion.grad_ref.refs_1_, f32[512,1024]{1,0:T(8,128)} %copy-done.36, ...), custom_call_target="tpu_custom_call" | custom-call | flops 10000000000 | bytes 41943040 | tf_op jit(solution)/shard_map/pallas_call | solution.py:654
  701.8 1.9 fusion.36
  706.0 2.7 select_add_fusion
  708.8 2.0 copy-done.45
  713.4 180.0 %shard_map.363 = (f32[128,1024]{1,0:T(8,128)}, f32[128,1024]{1,0:T(8,128)}, f32[128,1024]{1,0:T(8,128)}, f32[128,1024]{1,0:T(8,128)}, f32[128,1024]{1,0:T(8,128)...) custom-call(bf16[4,512,2048]{2,1,0:T(8,128)(2,1)} %get-tuple-element.78.refs_0, ...), custom_call_target="tpu_custom_call" | custom-call | flops 16106127360 | bytes 22544384 | tf_op jit(solution)/shard_map/pallas_call | solution.py:922
  895.0 4.8 convert_add_fusion.3
  (324 shorter events, 88.1 us)
Async XLA Ops:
  7.2 241.0 %all-gather.5.cloned.1.call-start = ((), (), s32[]{:S(2)}) async-start(), calls=%async_computation.4 | async-start | bytes 5898240 | tf_op jit(solution)/shard_map/all_gather | solution.py:1284
  13.7 130.5 %copy-start.64 = (bf16[4,1,2048]{2,0,1:T(4,128)(2,1)}, bf16[4,1,2048]{2,0,1:T(4,128)(2,1)S(1)}, u32[]{:S(2)}) copy-start(bf16[4,1,2048]{2,0,1:T(4,128)(2,1)S(1)} %get-tuple-element.215) | copy-start | bytes 49156
  13.7 125.1 %copy-start.70 = (f32[4]{0:T(128)}, f32[4]{0:T(128)S(1)}, u32[]{:S(2)}) copy-start(f32[4]{0:T(128)S(1)} %broadcast_multiply_fusion.3) | copy-start | bytes 52
  14.4 124.4 %copy-start.72 = (f32[4]{0:T(128)}, f32[4]{0:T(128)S(1)}, u32[]{:S(2)}) copy-start(f32[4]{0:T(128)S(1)} %fusion.86) | copy-start | bytes 52
  17.4 126.9 %copy-start.2 = (bf16[4,128,2048]{2,1,0:T(8,128)(2,1)S(1)}, bf16[4,128,2048]{2,1,0:T(8,128)(2,1)}, u32[]{:S(2)}) copy-start(bf16[4,128,2048]{2,1,0:T(8,128)(2,1)} %x_ref.3) | copy-start | bytes 6291460
  135.5 23.7 %copy-start.67 = (f32[1,2048]{1,0:T(1,128)}, f32[1,2048]{1,0:T(1,128)S(1)}, u32[]{:S(2)}) copy-start(f32[1,2048]{1,0:T(1,128)S(1)} %get-tuple-element.247) | copy-start | bytes 24580
  135.6 8.6 collective-permute-start
  138.8 188.9 %copy-start.29 = (f32[8,2048]{1,0:T(8,128)}, f32[8,2048]{1,0:T(8,128)S(1)}, u32[]{:S(2)}) copy-start(f32[8,2048]{1,0:T(8,128)S(1)} %slice_convert_fusion.2.coeff_ref) | copy-start | bytes 196612
  140.2 19.0 %copy-start.25 = (bf16[160,2048]{1,0:T(8,128)(2,1)}, bf16[160,2048]{1,0:T(8,128)(2,1)S(1)}, u32[]{:S(2)}) copy-start(bf16[160,2048]{1,0:T(8,128)(2,1)S(1)} %get-tuple-element.226.up_ref) | copy-start | bytes 1966084
  140.2 19.0 %copy-start.26 = (bf16[160,2048]{1,0:T(8,128)(2,1)}, bf16[160,2048]{1,0:T(8,128)(2,1)S(1)}, u32[]{:S(2)}) copy-start(bf16[160,2048]{1,0:T(8,128)(2,1)S(1)} %get-tuple-element.227.down_ref) | copy-start | bytes 1966084
  143.1 49.3 %copy-start.32 = (f32[1,1024]{1,0:T(1,128)}, f32[1,1024]{1,0:T(1,128)S(1)}, u32[]{:S(2)}) copy-start(f32[1,1024]{1,0:T(1,128)S(1)} %get-tuple-element.232.bonus_ref) | copy-start | bytes 12292
  143.2 18.2 %copy-start.31 = (f32[2,2048]{1,0:T(2,128)}, f32[2,2048]{1,0:T(2,128)S(1)}, u32[]{:S(2)}) copy-start(f32[2,2048]{1,0:T(2,128)S(1)} %pad_maximum_fusion.4.norm_ref) | copy-start | bytes 49156
  144.2 17.2 %copy-start.27 = (bf16[64,2048]{1,0:T(8,128)(2,1)}, bf16[64,2048]{1,0:T(8,128)(2,1)S(1)}, u32[]{:S(2)}) copy-start(bf16[64,2048]{1,0:T(8,128)(2,1)S(1)} %slice.167.decay_down_ref) | copy-start | bytes 786436
  144.2 17.1 %copy-start.28 = (bf16[64,1024]{1,0:T(8,128)(2,1)}, bf16[64,1024]{1,0:T(8,128)(2,1)S(1)}, u32[]{:S(2)}) copy-start(bf16[64,1024]{1,0:T(8,128)(2,1)S(1)} %slice.264.decay_up_ref) | copy-start | bytes 393220
  144.3 17.1 %copy-start.30 = (f32[4,1,2048]{2,1,0:T(1,128)}, f32[4,1,2048]{2,1,0:T(1,128)S(1)}, u32[]{:S(2)}) copy-start(f32[4,1,2048]{2,1,0:T(1,128)S(1)} %reshape.331.before_ref) | copy-start | bytes 98308
  161.3 13.8 %copy-start.39 = (f32[512,64]{1,0:T(8,128)}, f32[512,64]{1,0:T(8,128)S(1)}, u32[]{:S(2)}) copy-start(f32[512,64]{1,0:T(8,128)S(1)} %get-tuple-element.107.decay_ref) | copy-start | bytes 393220
  191.8 382.6 %reduce-scatter.3.cloned.1.call-start = ((), (), s32[]{:S(2)}) async-start(), calls=%async_computation.2 | async-start | bytes 15597568 | tf_op jit(solution)/shard_map/reduce_scatter | solution.py:1342
  197.4 50.8 %copy-start.4 = (f32[4,16,64,64]{3,2,1,0:T(8,128)S(1)}, f32[4,16,64,64]{3,2,1,0:T(8,128)}, u32[]{:S(2)}) copy-start(f32[4,16,64,64]{3,2,1,0:T(8,128)} %start_ref.1) | copy-start | bytes 3145732
  249.7 19.0 %copy-start.78 = (bf16[1024,2048]{1,0:T(8,128)(2,1)S(1)}, bf16[1024,2048]{1,0:T(8,128)(2,1)}, u32[]{:S(2)}) copy-start(bf16[1024,2048]{1,0:T(8,128)(2,1)} %get-tuple-element.84) | copy-start | bytes 12582916
  271.1 48.2 %copy-start.3 = (bf16[4,128,2048]{2,1,0:T(8,128)(2,1)S(1)}, bf16[4,128,2048]{2,1,0:T(8,128)(2,1)}, u32[]{:S(2)}) copy-start(bf16[4,128,2048]{2,1,0:T(8,128)(2,1)} %x_ref.3) | copy-start | bytes 6291460
  271.5 47.8 %collective-permute-start.1 = (bf16[4,128,2048]{2,1,0:T(8,128)(2,1)S(1)}, bf16[4,128,2048]{2,1,0:T(8,128)(2,1)S(1)}, u32[]{:S(2)}, u32[]{:S(2)}) collective-permute-start(bf16[4,128,2048]{2,1,0:T(8,128)(2,1)S(1)} %convert_element_type.147), channel_id=1, source_target_pairs={{0,1},{1,0},{2,3},{3,2},{4,5},{5,4},{6,7},{7,6},{8,9},{9,8},{10,11... | collective-permute-start | bytes 6291464 | tf_op jit(solution)/shard_map/ppermute | solution.py:678
  326.2 2.2 collective-permute-start.2
  328.4 19.3 %slice-start = ((s8[14680064]{0:T(1024)(128)(4,1)}), s8[4194304]{0:T(1024)(128)(4,1)S(1)}, s32[]{:S(2)}) async-start(s8[14680064]{0:T(1024)(128)(4,1)} %bitcast.194), calls=%async_computation.6 | async-start | bytes 8388608
  333.3 22.4 %copy-start.53 = (bf16[4,128,2048]{2,1,0:T(8,128)(2,1)}, bf16[4,128,2048]{2,1,0:T(8,128)(2,1)S(1)}, u32[]{:S(2)}) copy-start(bf16[4,128,2048]{2,1,0:T(8,128)(2,1)S(1)} %get-tuple-element.216) | copy-start | bytes 6291460
  334.6 13.0 %slice-start.1 = ((s8[14680064]{0:T(1024)(128)(4,1)}), s8[4194304]{0:T(1024)(128)(4,1)S(1)}, s32[]{:S(2)}) async-start(s8[14680064]{0:T(1024)(128)(4,1)} %bitcast.194), calls=%async_computation.7 | async-start | bytes 8388608
  334.6 13.0 %slice-start.2 = ((s8[14680064]{0:T(1024)(128)(4,1)}), s8[4194304]{0:T(1024)(128)(4,1)S(1)}, s32[]{:S(2)}) async-start(s8[14680064]{0:T(1024)(128)(4,1)} %bitcast.194), calls=%async_computation.8 | async-start | bytes 8388608
  334.6 13.0 %slice-start.3 = ((s8[14680064]{0:T(1024)(128)(4,1)}), s8[2097152]{0:T(1024)(128)(4,1)S(1)}, s32[]{:S(2)}) async-start(s8[14680064]{0:T(1024)(128)(4,1)} %bitcast.194), calls=%async_computation.9 | async-start | bytes 4194304
  354.2 25.7 %collective-permute-start.3 = (bf16[4,128,1024]{2,1,0:T(8,128)(2,1)S(1)}, bf16[4,128,1024]{2,1,0:T(8,128)(2,1)S(1)}, u32[]{:S(2)}, u32[]{:S(2)}) collective-permute-start(bf16[4,128,1024]{2,1,0:T(8,128)(2,1)S(1)} %fusion.33), channel_id=1, source_target_pairs={{0,1},{1,0},{2,3},{3,2},{4,5},{5,4},{6,7},{7,6},{8,9},{9,8},{10,11... | collective-permute-start | bytes 3145736 | tf_op jit(solution)/shard_map/ppermute | solution.py:678
  358.8 21.1 %copy-start.41 = (f32[4,128,2048]{2,1,0:T(8,128)S(1)}, f32[4,128,2048]{2,1,0:T(8,128)}, u32[]{:S(2)}) copy-start(f32[4,128,2048]{2,1,0:T(8,128)} %copy-done.40) | copy-start | bytes 12582916
  383.4 73.9 %copy-start.49 = (bf16[4,128,1024]{2,1,0:T(8,128)(2,1)}, bf16[4,128,1024]{2,1,0:T(8,128)(2,1)S(1)}, u32[]{:S(2)}) copy-start(bf16[4,128,1024]{2,1,0:T(8,128)(2,1)S(1)} %get-tuple-element.219) | copy-start | bytes 3145732
  383.4 24.9 %collective-permute-start.4 = (bf16[4,128,1024]{2,1,0:T(8,128)(2,1)S(1)}, bf16[4,128,1024]{2,1,0:T(8,128)(2,1)}, u32[]{:S(2)}, u32[]{:S(2)}) collective-permute-start(bf16[4,128,1024]{2,1,0:T(8,128)(2,1)S(1)} %get-tuple-element.221), channel_id=1, source_target_pairs={{0,1},{1,0},{2,3},{3,2},{4,5},{5,4},{6,7},{7,6},{8,9},{9,8},{10,11... | collective-permute-start | bytes 3145736 | tf_op jit(solution)/shard_map/ppermute | solution.py:678
  425.8 197.0 %all-gather.7.cloned.1.call-start = ((), (), s32[]{:S(2)}) async-start(), calls=%async_computation.5 | async-start | bytes 4718592 | tf_op jit(solution)/shard_map/all_gather | solution.py:1378
  425.9 44.6 %collective-permute-start.7 = (bf16[4,128,1024]{2,1,0:T(8,128)(2,1)}, bf16[4,128,1024]{2,1,0:T(8,128)(2,1)}, u32[]{:S(2)}, u32[]{:S(2)}) collective-permute-start(bf16[4,128,1024]{2,1,0:T(8,128)(2,1)} %param.37), channel_id=1, source_target_pairs={{0,1},{1,0},{2,3},{3,2},{4,5},{5,4},{6,7},{7,6},{8,9},{9,8},{10,11... | collective-permute-start | bytes 3145736 | tf_op jit(solution)/shard_map/ppermute | solution.py:678
  443.4 14.0 %copy-start.48 = (bf16[2048,1024]{1,0:T(8,128)(2,1)S(1)}, bf16[2048,1024]{1,0:T(8,128)(2,1)}, u32[]{:S(2)}) copy-start(bf16[2048,1024]{1,0:T(8,128)(2,1)} %param.36) | copy-start | bytes 12582916
  463.4 3.1 collective-permute-start.5
  470.5 46.0 %collective-permute-start.6 = (bf16[4,128,2048]{2,1,0:T(8,128)(2,1)}, bf16[4,128,2048]{2,1,0:T(8,128)(2,1)S(1)}, u32[]{:S(2)}, u32[]{:S(2)}) collective-permute-start(bf16[4,128,2048]{2,1,0:T(8,128)(2,1)} %get-tuple-element.210), channel_id=1, source_target_pairs={{0,1},{1,0},{2,3},{3,2},{4,5},{5,4},{6,7},{7,6},{8,9},{9,8},{10,11... | collective-permute-start | bytes 6291464 | tf_op jit(solution)/shard_map/ppermute | solution.py:678
  547.2 29.8 %copy-start.34 = (f32[512,1024]{1,0:T(8,128)}, f32[512,1024]{1,0:T(8,128)S(1)}, u32[]{:S(2)}) copy-start(f32[512,1024]{1,0:T(8,128)S(1)} %get-tuple-element.95.grad_ref) | copy-start | bytes 6291460
  547.2 364.9 %reduce-scatter.5.cloned.1.call-start = ((), (), s32[]{:S(2)}) async-start(), calls=%async_computation.3 | async-start | bytes 11141120 | tf_op jit(solution)/shard_map/reduce_scatter | solution.py:1342
  627.6 22.5 %copy-start.22 = (bf16[512,1024]{1,0:T(8,128)(2,1)S(1)}, bf16[512,1024]{1,0:T(8,128)(2,1)}, u32[]{:S(2)}) copy-start(bf16[512,1024]{1,0:T(8,128)(2,1)} %copy-done.21) | copy-start | bytes 3145732
  627.6 22.5 %copy-start.24 = (bf16[512,1024]{1,0:T(8,128)(2,1)S(1)}, bf16[512,1024]{1,0:T(8,128)(2,1)}, u32[]{:S(2)}) copy-start(bf16[512,1024]{1,0:T(8,128)(2,1)} %copy-done.23) | copy-start | bytes 3145732
  652.8 49.0 %copy-start.75 = (s32[1024]{0:T(1024)S(1)}, s32[1024]{0:T(1024)}, u32[]{:S(2)}) copy-start(s32[1024]{0:T(1024)} %copy-done.74) | copy-start | bytes 12292
  697.6 7.8 collective-permute-start.8
  893.5 10.3 %copy-start.59 = (f32[128,1024]{1,0:T(8,128)S(1)}, f32[128,1024]{1,0:T(8,128)}, u32[]{:S(2)}) copy-start(f32[128,1024]{1,0:T(8,128)} %get-tuple-element.122) | copy-start | bytes 1572868
  893.5 12.7 %collective-permute-start.9 = (f32[400,128]{0,1:T(8,128)}, f32[400,128]{0,1:T(8,128)S(1)}, u32[]{:S(2)}, u32[]{:S(2)}) collective-permute-start(f32[400,128]{0,1:T(8,128)} %bitcast.152), channel_id=1, source_target_pairs={{0,1},{1,0},{2,3},{3,2},{4,5},{5,4},{6,7},{7,6},{8,9},{9,8},{10,11... | collective-permute-start | bytes 614408 | tf_op jit(solution)/shard_map/ppermute | solution.py:678
  895.0 9.7 %copy-start.60 = (f32[128,1024]{1,0:T(8,128)S(1)}, f32[128,1024]{1,0:T(8,128)}, u32[]{:S(2)}) copy-start(f32[128,1024]{1,0:T(8,128)} %get-tuple-element.118) | copy-start | bytes 1572868
  895.0 9.7 %copy-start.61 = (f32[128,1024]{1,0:T(8,128)S(1)}, f32[128,1024]{1,0:T(8,128)}, u32[]{:S(2)}) copy-start(f32[128,1024]{1,0:T(8,128)} %get-tuple-element.119) | copy-start | bytes 1572868
  895.0 9.7 %copy-start.62 = (f32[128,1024]{1,0:T(8,128)S(1)}, f32[128,1024]{1,0:T(8,128)}, u32[]{:S(2)}) copy-start(f32[128,1024]{1,0:T(8,128)} %get-tuple-element.120) | copy-start | bytes 1572868
  895.0 9.7 %copy-start.63 = (f32[128,1024]{1,0:T(8,128)S(1)}, f32[128,1024]{1,0:T(8,128)}, u32[]{:S(2)}) copy-start(f32[128,1024]{1,0:T(8,128)} %get-tuple-element.121) | copy-start | bytes 1572868
  (51 other events, 152.5 us)
Sparse Core Ops, SparseCore 0:
  191.9 56.1 all-gather.4
  426.0 148.3 reduce-scatter.2
  576.6 46.2 all-gather.6
  626.8 127.2 reduce-scatter.4

commit v6 on v5

--- a/solution.py
+++ b/solution.py
@@ -1297,75 +1297,102 @@
     decay_range = decay_range[:, :2].reshape(seq_count, 2, heads_here, head_size)
     total_least = jnp.min(decay_range[:, 0], axis=-1)
     total_most = jnp.max(decay_range[:, 1], axis=-1)
-    mixer_part = jnp.einsum("std,de->ste", mixer_in, out_proj, preferred_element_type=jnp.float32)
-    late_input, mixer_part = lax.optimization_barrier((block_input, mixer_part))
-    residual = (
-        late_input.astype(jnp.float32) + mixer_part + other_half(mixer_part.astype(jnp.bfloat16)).astype(jnp.float32)
-    )
-    normed_two, norm_two_back = jax.vjp(layer_norm, residual, gains_all[1], biases_all[1])
-    prev_two = from_behind(normed_two[:, -1, :].astype(jnp.bfloat16), "seq", 1).astype(jnp.float32)
-    (chan_key, chan_recept), chan_back = jax.vjp(
-        channel_mix, normed_two, prev_two, shift_coefficient
-    )
-    chan_key_b = chan_key.astype(jnp.bfloat16)
-    chan_recept_b = chan_recept.astype(jnp.bfloat16)
-    key_pre = jnp.einsum("std,df->stf", chan_key_b, channel_key, preferred_element_type=jnp.float32)
-    hidden = jnp.square(jnp.maximum(key_pre, 0.0)).astype(jnp.bfloat16)
+    runs = 2 - seq_count % 2
+    each_run = seq_count // runs
+    parts = range(runs)
+
+    def run_of(rows):
+        return [rows[k * each_run : (k + 1) * each_run] for k in parts]
+
+    def flat(rows):
+        return jnp.concatenate([part.reshape(-1, part.shape[-1]) for part in rows])
+
+    def product(pattern, left, right):
+        return jnp.einsum(pattern, left, right, preferred_element_type=jnp.float32)
+
+    def summed(part):
+        return part + other_half(part.astype(jnp.bfloat16)).astype(jnp.float32)
+
+    mixer_part = [product("std,de->ste", rows, out_proj) for rows in run_of(mixer_in)]
+    late_input, *mixer_part = lax.optimization_barrier((block_input, *mixer_part))
+    residual = [
+        rows.astype(jnp.float32) + summed(part)
+        for rows, part in zip(run_of(late_input), mixer_part)
+    ]
+    normed_two, norm_two_back = zip(
+        *[jax.vjp(layer_norm, rows, gains_all[1], biases_all[1]) for rows in residual]
+    )
+    prev_two = [
+        from_behind(rows[:, -1, :].astype(jnp.bfloat16), "seq", 1).astype(jnp.float32)
+        for rows in normed_two
+    ]
+    chan_inputs, chan_back = zip(
+        *[
+            jax.vjp(channel_mix, rows, prev, shift_coefficient)
+            for rows, prev in zip(normed_two, prev_two)
+        ]
+    )
+    chan_key_b = [rows.astype(jnp.bfloat16) for rows, _ in chan_inputs]
+    chan_recept_b = [rows.astype(jnp.bfloat16) for _, rows in chan_inputs]
     own_value, sent_value = (
         lax.dynamic_slice_in_dim(channel_value, which * own_cols, own_cols, 1)
         for which in (half, 1 - half)
     )
-    sent_part = jnp.einsum("stf,fd->std", hidden, sent_value, preferred_element_type=jnp.float32)
-    other_part = other_half(sent_part.astype(jnp.bfloat16)).astype(jnp.float32)
-    own_part = jnp.einsum("stf,fd->std", hidden, own_value, preferred_element_type=jnp.float32)
-    recept_pre = jnp.einsum(
-        "std,de->ste", chan_recept_b, channel_recept, preferred_element_type=jnp.float32
-    )
-    own_part, recept_pre = lax.optimization_barrier((own_part, recept_pre))
-    kv_rows = own_part + other_part
-    gate_chan = jax.nn.sigmoid(recept_pre)
-    output = (own_half(residual) + gate_chan * kv_rows).astype(jnp.bfloat16)
-    grad_out = out_grad.astype(jnp.float32)
-    grad_value = (grad_out * gate_chan).astype(jnp.bfloat16)
-    grad_recept = (grad_out * kv_rows * gate_chan * (1.0 - gate_chan)).astype(jnp.bfloat16)
-    full_value = both_halves(grad_value)
+    out_grads = run_of(out_grad.astype(jnp.float32))
+    key_pre, hidden, own_part, other_part, recept_pre = [], [], [], [], []
+    for k in parts:
+        key_pre.append(product("std,df->stf", chan_key_b[k], channel_key))
+        hidden.append(jnp.square(jnp.maximum(key_pre[k], 0.0)).astype(jnp.bfloat16))
+        sent_part = product("stf,fd->std", hidden[k], sent_value).astype(jnp.bfloat16)
+        other_part.append(other_half(sent_part).astype(jnp.float32))
+        own, recept = lax.optimization_barrier(
+            (
+                product("stf,fd->std", hidden[k], own_value),
+                product("std,de->ste", chan_recept_b[k], channel_recept),
+            )
+        )
+        own_part.append(own)
+        recept_pre.append(recept)
+    output, grad_recept, full_value = [], [], []
+    for k in parts:
+        kv_rows = own_part[k] + other_part[k]
+        gate_chan = jax.nn.sigmoid(recept_pre[k])
+        output.append((own_half(residual[k]) + gate_chan * kv_rows).astype(jnp.bfloat16))
+        grad_recept.append(
+            (out_grads[k] * kv_rows * gate_chan * (1.0 - gate_chan)).astype(jnp.bfloat16)
+        )
+        full_value.append(both_halves((out_grads[k] * gate_chan).astype(jnp.bfloat16)))
+    output = jnp.concatenate(output)
 
     def weight_terms(left, right):
-        return jnp.einsum(
-            "td,tf->df",
-            left.reshape(tokens, -1),
-            right.reshape(tokens, -1),
-            preferred_element_type=jnp.float32,
-        ).astype(jnp.bfloat16)
+        return product("td,tf->df", left, right).astype(jnp.bfloat16)
 
     def scattered(whole):
         return lax.psum_scatter(whole, ("dp", "seq"), scatter_dimension=0, tiled=True).astype(
             jnp.float32
         )
 
-    full_value, value_whole = lax.optimization_barrier(
-        (full_value, weight_terms(full_value, hidden))
-    )
+    flat_value, flat_hidden = flat(full_value), flat(hidden)
+    value_cut = flat_hidden.shape[1] * 5 // 7
+    value_whole = weight_terms(flat_value, flat_hidden[:, :value_cut])
+    full_value[-1], value_whole = lax.optimization_barrier((full_value[-1], value_whole))
     value_sum = scattered(value_whole)
-    grad_hidden = jnp.einsum(
-        "std,fd->stf", full_value, channel_value, preferred_element_type=jnp.float32
-    )
-    grad_key = (grad_hidden * 2.0 * jnp.maximum(key_pre, 0.0)).astype(jnp.bfloat16)
-    part_key = jnp.einsum("stf,df->std", grad_key, channel_key, preferred_element_type=jnp.float32)
-    part_recept = jnp.einsum(
-        "ste,de->std", grad_recept, channel_recept, preferred_element_type=jnp.float32
-    )
-    part_normed_two, part_prev_two, grad_coeffs_chan = chan_back((part_key, part_recept))
-    from_next_two = from_behind(for_sending(part_prev_two), "seq", -1).astype(jnp.float32)
-    part_normed_two = add_last(part_normed_two, from_next_two)
-    sizes = (lax.axis_size("dp"), blocks)
-    grad_key_rows = grad_key.reshape(tokens, -1)
-    key_cut = grad_key_rows.shape[1] * 5 // 7
-    key_whole = weight_terms(chan_key_b, grad_key_rows[:, :key_cut])
-    grad_normed_two = part_normed_two + other_half(part_normed_two.astype(jnp.bfloat16)).astype(
-        jnp.float32
-    )
-    grad_residual, grad_gain_two, grad_bias_two = norm_two_back(grad_normed_two)
+    grad_key, part_normed_two, grad_coeffs_chan = [], [], 0.0
+    for k in parts:
+        grad_hidden = product("std,fd->stf", full_value[k], channel_value)
+        grad_key.append((grad_hidden * 2.0 * jnp.maximum(key_pre[k], 0.0)).astype(jnp.bfloat16))
+        part_key = product("stf,df->std", grad_key[k], channel_key)
+        part_recept = product("ste,de->std", grad_recept[k], channel_recept)
+        part_two, part_prev_two, coeffs = chan_back[k]((part_key, part_recept))
+        from_next_two = from_behind(for_sending(part_prev_two), "seq", -1).astype(jnp.float32)
+        part_normed_two.append(add_last(part_two, from_next_two))
+        grad_coeffs_chan += coeffs
+    flat_chan_key, flat_grad_key = flat(chan_key_b), flat(grad_key)
+    key_cut = flat_grad_key.shape[1] * 5 // 7
+    key_whole = weight_terms(flat_chan_key, flat_grad_key[:, :key_cut])
+    two_back = [back(summed(part)) for back, part in zip(norm_two_back, part_normed_two)]
+    grad_gain_two, grad_bias_two = (sum(back[k] for back in two_back) for k in (1, 2))
+    grad_residual = jnp.concatenate([back[0] for back in two_back])
     grad_residual = grad_residual + full_out.astype(jnp.float32)
     grad_residual, key_whole = lax.optimization_barrier((grad_residual, key_whole))
     grad_branch = grad_residual.astype(jnp.bfloat16)
@@ -1446,12 +1473,13 @@
     small_rows = lax.dynamic_update_slice(small_rows, other_rows, (8, 0))
     small_rows = lax.dynamic_update_slice(small_rows, head_rows, (narrow_at, 0))
     sent_block = lax.dynamic_slice_in_dim(part_block, (1 - half) * own_cols, own_cols, 2)
-    *proj_sums, out_sum, recept_sum, key_rest, small_sums, other_block = ring_sums(
+    *proj_sums, out_sum, recept_sum, key_rest, value_rest, small_sums, other_block = ring_sums(
         [(stacked, grad_proj, (branch,)) for branch in range(4)]
         + [
             (grad_branch.reshape(tokens, -1), mixer_in.reshape(tokens, -1), ()),
-            (chan_recept_b.reshape(tokens, -1), grad_recept.reshape(tokens, -1), ()),
-            (chan_key_b.reshape(tokens, -1), grad_key_rows[:, key_cut:], ()),
+            (flat(chan_recept_b), flat(grad_recept), ()),
+            (flat_chan_key, flat_grad_key[:, key_cut:], ()),
+            (flat_value, flat_hidden[:, value_cut:], ()),
         ],
         small_rows,
         sent_block.astype(jnp.bfloat16),
@@ -1481,7 +1509,7 @@
         out_sum.T,
         *head_sums,
         jnp.concatenate([key_sum, key_rest], axis=1),
-        value_sum.T,
+        jnp.concatenate([value_sum, value_rest], axis=1).T,
         recept_sum,
         total_least,
         total_most,

time: 931 us -> 971 us (1.043)
  waiting for transfers between devices: 199 us -> 162 us
  matrix products: 110 us -> 146 us
  Pallas kernels: 457 us -> 479 us
  other arithmetic: 56.1 us -> 66.4 us
    dot_general x10 -> x18, matrix products: 89.3 us -> 126 us  [product(): return jnp.einsum(pattern, left, right, preferred_element_type=jnp.float32)]
    reduce_scatter x2, waiting for transfers between devices: 27.1 us -> 0.02 us  [scattered(): lax.psum_scatter(whole, ('dp', 'seq'), scatter_dimension=0, tiled=True)]
    pallas_call x1, Pallas kernels: 180 us -> 203 us  [ring_sums(): pl.pallas_call(functools.partial(ring_kernel, dp_size, seq_size, rows, wi...]
    all_gather x1, waiting for transfers between devices: 16.1 us -> 5.12 us  [per_device(): all_terms = lax.all_gather(block_term, 'seq')]
    concatenate x0 -> x7, other arithmetic: none -> 10.3 us  [the longest x6 9.26 us: flat(): return jnp.concatenate([part.reshape(-1, part.shape[-1]) for part in rows])]
    unnamed x192 -> x252, local copies, waits for them, and re-layouts: 53.3 us -> 56.4 us
    ppermute x6 -> x10, waiting for transfers between devices: 119 us -> 119 us  [other_half(): return lax.ppermute(block, 'tp', [(0, 1), (1, 0)])]
  transfers between devices with their start and end apart: 14 -> 20, of which waited for: 9 -> 11; matrix products, arithmetic and copies ran while one was open for 13% -> 18% of each run, Pallas kernels for 32% -> 33%
where the time goes in v6:
time: 971 us; the launch traced here: 962 us
  Pallas kernels  479 us (49%)
  waiting for transfers between devices  162 us (17%)
  matrix products  146 us (15%)
  local copies, waits for them, and re-layouts  69.2 us (7%)
  other arithmetic  66.4 us (7%)
  starting transfers between devices  22.7 us (2%)
  between operations  15.6 us (2%)
    pallas_call x1, Pallas kernels, ring_sums(): pl.pallas_call(functools.partial(ring_kernel, dp_size, seq_size, rows, wi...  203 us
    dot_general x18, matrix products, product(): return jnp.einsum(pattern, left, right, preferred_element_type=jnp.float32)  126 us
    ppermute x10, waiting for transfers between devices, other_half(): return lax.ppermute(block, 'tp', [(0, 1), (1, 0)])  119 us
    pallas_call x1, Pallas kernels, gather_weights(): pl.pallas_call(functools.partial(gather_kernel, dp_size, seq_size), out_s...  117 us
    pallas_call x6, Pallas kernels, call(): pl.pallas_call(kernel, grid=self.grid, in_specs=ins, out_specs=[spec for...  100 us
    unnamed x252, local copies, waits for them, and re-layouts  56.4 us
    pallas_call x1, Pallas kernels, mix_back(): pl.pallas_call(mix_back_kernel, grid=(sequences // together,), in_specs=[...  43.9 us
    all_gather x1, waiting for transfers between devices, per_device(): all_packed = lax.all_gather(recurrence.totals(projected, log_flat), 'seq')  35.8 us
  transfers between devices with their start and end apart: 20, of which 11 were waited for; matrix products, arithmetic and copies ran while one was open for 18% of the time, Pallas kernels for 33%

profile of v6, /device:TPU:0, one launch (start us, length us, event | category | flops | bytes accessed | tf_op | source)
XLA Modules:
  0.0 961.7 jit_solution(10787981475233300479)
XLA Ops:
  16.7 117.2 %shard_map.354 = (bf16[480,2048]{1,0:T(8,128)(2,1)}, bf16[4,2048,1024]{2,1,0:T(8,128)(2,1)}, bf16[1024,2048]{1,0:T(8,128)(2,1)}) custom-call(bf16[480,128]{1,0:T(8,128)(2,1)} %copy-done.105, bf16[4,128,1024]{2,1,0:T(8,128)(2,1)} %proj_ref.1, bf16[1024,128]{1,0:T(8,128)(2,1)} %out_ref.1), custom_call_target="tpu_custom_call" | custom-call | tf_op jit(solution)/shard_map/pallas_call | solution.py:1068
  140.4 2.8 fusion.13
  144.4 14.9 %shard_map.355 = (bf16[4,512,2048]{2,1,0:T(8,128)(2,1)}, f32[512,160]{1,0:T(8,128)S(1)}, f32[512,64]{1,0:T(8,128)S(1)}, f32[512,1024]{1,0:T(8,128)S(1)}) custom-call(bf16[4,128,2048]{2,1,0:T(8,128)(2,1)S(1)} %copy-done.2, f32[4,1,2048]{2,1,0:T(1,128)S(1)} %reshape.417.before_ref, f32[8,2048]{1,0:T(8,128)S(1)} %slice_convert_fusion.1.coeff_ref, ...), custom_call_target="tpu_custom_call" | custom-call | flops 2000000000 | bytes 16777216 | tf_op jit(solution)/shard_map/pallas_call | solution.py:1149
  162.2 13.7 %fusion.153.rkv_ref.kv_ref.gate_ref = f32[4,512,1024]{2,1,0:T(8,128)S(1)} fusion(bf16[4,512,2048]{2,1,0:T(8,128)(2,1)} %get-tuple-element.82.refs_0_, bf16[4,2048,1024]{2,1,0:T(8,128)(2,1)} %get-tuple-element.83.proj_ref), kind=kOutput, calls=%fused_computation.273 | convolution fusion | flops 8589934592 | bytes 33554432 | tf_op jit(solution)/shard_map/ntd,nde->nte/dot_general | solution.py:1281
  177.4 11.8 %shard_map.357 = bf16[4,8,80,128]{3,2,1,0:T(8,128)(2,1)} custom-call(f32[4,512,1024]{2,1,0:T(8,128)S(1)} %fusion.153.rkv_ref.kv_ref.gate_ref, f32[512,1024]{1,0:T(8,128)S(1)} %copy-done.6), custom_call_target="tpu_custom_call" | custom-call | flops 1000000000 | bytes 10485760 | tf_op jit(solution)/shard_map/pallas_call | solution.py:368
  189.3 3.3 copy-done
  192.9 3.4 copy-done.1
  197.8 14.0 %shard_map.356 = (f32[512,1024]{1,0:T(8,128)S(1)}, bf16[512,1024]{1,0:T(8,128)(2,1)S(1)}) custom-call(f32[4,512,1024]{2,1,0:T(8,128)S(1)} %copy-done.1, f32[512,1024]{1,0:T(8,128)S(1)} %copy-done.7, f32[1,1024]{1,0:T(1,128)S(1)} %get-tuple-element.266.bonus_ref), custom_call_target="tpu_custom_call" | custom-call | flops 2000000000 | bytes 10489856 | tf_op jit(solution)/shard_map/pallas_call | solution.py:368
  213.2 35.8 %all-gather.5.cloned.1.call-done = bf16[32,8,80,128]{3,2,1,0:T(8,128)(2,1)} async-done(((bf16[4,8,80,128]{3,2,1,0:T(8,128)(2,1)}), bf16[32,8,80,128]{3,2,1,0:T(8,128)(2,1)}) %all-gather.5.cloned.1.call-update) | async-done | bytes 5242896 | tf_op jit(solution)/shard_map/all_gather | solution.py:1284
  250.6 18.9 %shard_map.358 = (f32[512,1024]{1,0:T(8,128)S(1)}, bf16[512,1024]{1,0:T(8,128)(2,1)S(1)}, f32[4,8,64,128]{3,2,1,0:T(8,128)S(1)}, f32[4,8,1024]{2,1,0:T(8,128)S(1)}) custom-call(s32[1]{0:T(128)} %bitcast.place_ref, f32[512,1024]{1,0:T(8,128)S(1)} %copy-done.16, bf16[512,1024]{1,0:T(8,128)(2,1)S(1)} %get-tuple-element.86.decayed_ref, f32[4,512,1024]{2,1,0:T(8,128)} %copy-done, ...), custom_call_target="tpu_custom_call" | custom-call | flops 1000000000 | bytes 17833988 | tf_op jit(solution)/shard_map/pallas_call | solution.py:368
  278.9 21.6 %collective-permute-done.1 = bf16[2,128,2048]{2,1,0:T(8,128)(2,1)} collective-permute-done((bf16[2,128,2048]{2,1,0:T(8,128)(2,1)}, bf16[2,128,2048]{2,1,0:T(8,128)(2,1)}, u32[]{:S(2)}, u32[]{:S(2)}) %collective-permute-start.1) | collective-permute-done | bytes 1048608 | tf_op jit(solution)/shard_map/ppermute | solution.py:678
  300.6 22.5 %collective-permute-done.4 = bf16[2,128,2048]{2,1,0:T(8,128)(2,1)} collective-permute-done((bf16[2,128,2048]{2,1,0:T(8,128)(2,1)}, bf16[2,128,2048]{2,1,0:T(8,128)(2,1)}, u32[]{:S(2)}, u32[]{:S(2)}) %collective-permute-start.4) | collective-permute-done | bytes 1048608 | tf_op jit(solution)/shard_map/ppermute | solution.py:678
  323.0 3.6 fusion.143
  331.8 13.0 %collective-permute-done.13 = bf16[4,128,1024]{2,1,0:T(8,128)(2,1)} collective-permute-done((bf16[4,128,1024]{2,1,0:T(8,128)(2,1)}, bf16[4,128,1024]{2,1,0:T(8,128)(2,1)}, u32[]{:S(2)}, u32[]{:S(2)}) %collective-permute-start.13) | collective-permute-done | bytes 1048608 | tf_op jit(solution)/shard_map/ppermute | solution.py:678
  344.8 3.5 broadcast_select_fusion.1
  350.0 12.5 %multiply_convert_fusion.1 = (bf16[2,128,3584]{2,1,0:T(8,128)(2,1)S(1)}, f32[2,128,3584]{2,1,0:T(8,128)}) fusion(bf16[2,128,2048]{2,1,0:T(8,128)(2,1)S(1)} %get-tuple-element.282, bf16[2048,3584]{1,0:T(8,128)(2,1)} %param.34), kind=kOutput, calls=%fused_computation.62 | convolution fusion | flops 3760848896 | bytes 21233664 | tf_op jit(solution)/shard_map/std,df->stf/dot_general | solution.py:1311
  363.7 5.3 fusion.22
  369.0 5.3 fusion.75
  375.9 11.1 %multiply_convert_fusion = (bf16[2,128,3584]{2,1,0:T(8,128)(2,1)S(1)}, f32[2,128,3584]{2,1,0:T(8,128)}) fusion(bf16[2,128,2048]{2,1,0:T(8,128)(2,1)S(1)} %get-tuple-element.237, bf16[2048,3584]{1,0:T(8,128)(2,1)} %param.34), kind=kOutput, calls=%fused_computation.61 | convolution fusion | flops 3760848896 | bytes 21233664 | tf_op jit(solution)/shard_map/std,df->stf/dot_general | solution.py:1311
  388.3 5.8 fusion.78
  394.7 5.3 fusion.20
  400.0 7.2 collective-permute-done.6
  411.6 12.8 %collective-permute-done.10 = bf16[2,128,1024]{2,1,0:T(8,128)(2,1)S(1)} collective-permute-done((bf16[2,128,1024]{2,1,0:T(8,128)(2,1)S(1)}, bf16[2,128,1024]{2,1,0:T(8,128)(2,1)S(1)}, u32[]{:S(2)}, u32[]{:S(2)}) %collective-permute-start.10) | collective-permute-done | bytes 524320 | tf_op jit(solution)/shard_map/ppermute | solution.py:678
  424.6 8.2 collective-permute-done.7
  434.9 8.2 convolution_convert_fusion.1
  443.4 13.1 %fusion.46 = bf16[2,128,3584]{2,1,0:T(8,128)(2,1)} fusion(f32[2,128,3584]{2,1,0:T(8,128)} %get-tuple-element.292, bf16[3584,2048]{1,0:T(8,128)(2,1)} %param.35, bf16[2,128,1024]{2,1,0:T(8,128)(2,1)} %copy-done.86, bf16[2,128,1024]{2,1,0:T(8,128)(2,1)} %copy-done.85), kind=kOutput, calls=%fused_computation.36 | convolution fusion | flops 3762946048 | bytes 21233664 | tf_op jit(solution)/shard_map/std,fd->stf/dot_general | solution.py:1311
  456.4 13.0 %fusion.6 = f32[2,128,2048]{2,1,0:T(8,128)} fusion(bf16[2,128,3584]{2,1,0:T(8,128)(2,1)} %fusion.46, bf16[2048,3584]{1,0:T(8,128)(2,1)} %param.34), kind=kOutput, calls=%fused_computation.6 | convolution fusion | flops 3758096384 | bytes 18612224 | tf_op jit(solution)/shard_map/stf,df->std/dot_general | solution.py:1311
  469.5 6.0 multiply_reduce_fusion.5
  478.4 11.8 %fusion.49 = bf16[2,128,3584]{2,1,0:T(8,128)(2,1)} fusion(f32[2,128,3584]{2,1,0:T(8,128)} %get-tuple-element.294, bf16[2,128,2048]{2,1,0:T(8,128)(2,1)} %copy-done.78, bf16[3584,2048]{1,0:T(8,128)(2,1)} %param.35), kind=kOutput, calls=%fused_computation.37 | convolution fusion | flops 3760848896 | bytes 21233664 | tf_op jit(solution)/shard_map/std,fd->stf/dot_general | solution.py:1311
  490.2 11.2 %fusion.4 = f32[2,128,2048]{2,1,0:T(8,128)} fusion(bf16[2,128,3584]{2,1,0:T(8,128)(2,1)} %fusion.49, bf16[2048,3584]{1,0:T(8,128)(2,1)} %param.34), kind=kOutput, calls=%fused_computation.4 | convolution fusion | flops 3758096384 | bytes 18612224 | tf_op jit(solution)/shard_map/stf,df->std/dot_general | solution.py:1311
  501.4 3.6 multiply_reduce_fusion.3
  509.6 4.0 fusion.141
  515.6 8.5 convolution_convert_fusion
  524.1 14.2 %collective-permute-done.9 = bf16[2,128,2048]{2,1,0:T(8,128)(2,1)} collective-permute-done((bf16[2,128,2048]{2,1,0:T(8,128)(2,1)}, bf16[2,128,2048]{2,1,0:T(8,128)(2,1)}, u32[]{:S(2)}, u32[]{:S(2)}) %collective-permute-start.9) | collective-permute-done | bytes 1048608 | tf_op jit(solution)/shard_map/ppermute | solution.py:678
  538.3 2.5 multiply_reduce_fusion.7
  540.8 19.9 %collective-permute-done.12 = bf16[2,128,2048]{2,1,0:T(8,128)(2,1)} collective-permute-done((bf16[2,128,2048]{2,1,0:T(8,128)(2,1)}, bf16[2,128,2048]{2,1,0:T(8,128)(2,1)}, u32[]{:S(2)}, u32[]{:S(2)}) %collective-permute-start.12) | collective-permute-done | bytes 1048608 | tf_op jit(solution)/shard_map/ppermute | solution.py:678
  560.8 3.9 multiply_reduce_fusion.1
  564.7 3.1 multiply_reduce_fusion
  571.1 3.4 copy-done.52
  576.9 13.4 %shard_map.359 = (f32[512,1024]{1,0:T(8,128)S(1)}, bf16[512,1024]{1,0:T(8,128)(2,1)S(1)}, bf16[4,8,64,128]{3,2,1,0:T(8,128)(2,1)}, f32[4,8,1024]{2,1,0:T(8,128)S(1)}) custom-call(f32[512,1024]{1,0:T(8,128)S(1)} %bitcast.200, f32[512,1024]{1,0:T(8,128)S(1)} %copy-done.18, f32[4,512,1024]{2,1,0:T(8,128)} %copy-done, ...), custom_call_target="tpu_custom_call" | custom-call | flops 1000000000 | bytes 13639680 | tf_op jit(solution)/shard_map/pallas_call | solution.py:368
  608.9 19.7 %shard_map.360 = (bf16[512,1024]{1,0:T(8,128)(2,1)S(1)}, f32[512,1024]{1,0:T(8,128)S(1)}, f32[512,1024]{1,0:T(8,128)S(1)}, f32[512,1024]{1,0:T(8,128)S(1)}, f32[4,8,1024]{2,1,0:T(8,128)S(1)}) custom-call(f32[4,512,1024]{2,1,0:T(8,128)} %copy-done, f32[512,1024]{1,0:T(8,128)S(1)} %copy-done.8, f32[1,1024]{1,0:T(1,128)S(1)} %copy-done.34, ...), custom_call_target="tpu_custom_call" | custom-call | flops 4000000000 | bytes 13635584 | tf_op jit(solution)/shard_map/pallas_call | solution.py:368
  633.5 5.1 all-gather.7.cloned.1.call-done
  643.4 22.4 %shard_map.361 = (bf16[512,1024]{1,0:T(8,128)(2,1)S(1)}, bf16[512,1024]{1,0:T(8,128)(2,1)S(1)}, f32[512,1024]{1,0:T(8,128)S(1)}, f32[4,16,64,64]{3,2,1,0:T(8,128)}, f32[4,8,1024]{2,1,0:T(8,128)S(1)}) custom-call(s32[1]{0:T(128)} %bitcast.place_ref, f32[4,512,1024]{2,1,0:T(8,128)} %copy-done, f32[512,1024]{1,0:T(8,128)S(1)} %copy-done.8, ...), custom_call_target="tpu_custom_call" | custom-call | flops 3000000000 | bytes 27262980 | tf_op jit(solution)/shard_map/pallas_call | solution.py:368
  668.4 43.9 %shard_map.362 = (f32[4,128,2048]{2,1,0:T(8,128)}, f32[4,1,2048]{2,1,0:T(1,128)}, f32[512,2048]{1,0:T(8,128)}, f32[64,1024]{1,0:T(8,128)}) custom-call(bf16[4,128,2048]{2,1,0:T(8,128)(2,1)} %x_ref.3, f32[4,1,2048]{2,1,0:T(1,128)} %copy-done.31, bf16[4,512,1024]{2,1,0:T(8,128)(2,1)} %pad_maximum_fusion.grad_ref.refs_1_, f32[512,1024]{1,0:T(8,128)} %copy-done.37, ...), custom_call_target="tpu_custom_call" | custom-call | flops 10000000000 | bytes 41943040 | tf_op jit(solution)/shard_map/pallas_call | solution.py:654
  719.0 2.7 select_add_fusion
  726.3 202.8 %shard_map.363 = (f32[128,1024]{1,0:T(8,128)}, f32[128,1024]{1,0:T(8,128)}, f32[128,1024]{1,0:T(8,128)}, f32[128,1024]{1,0:T(8,128)}, f32[128,1024]{1,0:T(8,128)...) custom-call(bf16[4,512,2048]{2,1,0:T(8,128)(2,1)} %get-tuple-element, ...), custom_call_target="tpu_custom_call" | custom-call | flops 18253611008 | bytes 25690112 | tf_op jit(solution)/shard_map/pallas_call | solution.py:922
  930.7 4.8 convert_add_fusion
  943.0 2.7 pad_maximum_fusion.4
  (426 shorter events, 128.7 us)
Async XLA Ops:
  7.2 241.8 %all-gather.5.cloned.1.call-start = ((), (), s32[]{:S(2)}) async-start(), calls=%async_computation.4 | async-start | bytes 5898240 | tf_op jit(solution)/shard_map/all_gather | solution.py:1284
  8.3 131.4 %copy-start.101 = (bf16[4,1,2048]{2,0,1:T(4,128)(2,1)}, bf16[4,1,2048]{2,0,1:T(4,128)(2,1)S(1)}, u32[]{:S(2)}) copy-start(bf16[4,1,2048]{2,0,1:T(4,128)(2,1)S(1)} %get-tuple-element.233) | copy-start | bytes 49156
  135.1 9.2 collective-permute-start
  138.3 140.7 %copy-start.30 = (f32[8,2048]{1,0:T(8,128)}, f32[8,2048]{1,0:T(8,128)S(1)}, u32[]{:S(2)}) copy-start(f32[8,2048]{1,0:T(8,128)S(1)} %slice_convert_fusion.1.coeff_ref) | copy-start | bytes 196612
  143.2 49.6 %copy-start.33 = (f32[1,1024]{1,0:T(1,128)}, f32[1,1024]{1,0:T(1,128)S(1)}, u32[]{:S(2)}) copy-start(f32[1,1024]{1,0:T(1,128)S(1)} %get-tuple-element.266.bonus_ref) | copy-start | bytes 12292
  143.3 16.1 %copy-start.32 = (f32[2,2048]{1,0:T(2,128)}, f32[2,2048]{1,0:T(2,128)S(1)}, u32[]{:S(2)}) copy-start(f32[2,2048]{1,0:T(2,128)S(1)} %pad_maximum_fusion.12.norm_ref) | copy-start | bytes 49156
  144.3 15.1 %copy-start.28 = (bf16[64,2048]{1,0:T(8,128)(2,1)}, bf16[64,2048]{1,0:T(8,128)(2,1)S(1)}, u32[]{:S(2)}) copy-start(bf16[64,2048]{1,0:T(8,128)(2,1)S(1)} %slice.208.decay_down_ref) | copy-start | bytes 786436
  144.3 15.0 %copy-start.29 = (bf16[64,1024]{1,0:T(8,128)(2,1)}, bf16[64,1024]{1,0:T(8,128)(2,1)S(1)}, u32[]{:S(2)}) copy-start(bf16[64,1024]{1,0:T(8,128)(2,1)S(1)} %slice.343.decay_up_ref) | copy-start | bytes 393220
  144.3 15.0 %copy-start.31 = (f32[4,1,2048]{2,1,0:T(1,128)}, f32[4,1,2048]{2,1,0:T(1,128)S(1)}, u32[]{:S(2)}) copy-start(f32[4,1,2048]{2,1,0:T(1,128)S(1)} %reshape.417.before_ref) | copy-start | bytes 98308
  192.6 399.2 %reduce-scatter.3.cloned.1.call-start = ((), (), s32[]{:S(2)}) async-start(), calls=%async_computation.2 | async-start | bytes 11141120 | tf_op jit(solution)/shard_map/reduce_scatter | solution.py:1371
  197.8 51.1 %copy-start.4 = (f32[4,16,64,64]{3,2,1,0:T(8,128)S(1)}, f32[4,16,64,64]{3,2,1,0:T(8,128)}, u32[]{:S(2)}) copy-start(f32[4,16,64,64]{3,2,1,0:T(8,128)} %start_ref.1) | copy-start | bytes 3145732
  250.6 19.1 %copy-start.51 = (bf16[1024,2048]{1,0:T(8,128)(2,1)S(1)}, bf16[1024,2048]{1,0:T(8,128)(2,1)}, u32[]{:S(2)}) copy-start(bf16[1024,2048]{1,0:T(8,128)(2,1)} %get-tuple-element.88) | copy-start | bytes 12582916
  274.3 48.8 %copy-start.3 = (bf16[4,128,2048]{2,1,0:T(8,128)(2,1)S(1)}, bf16[4,128,2048]{2,1,0:T(8,128)(2,1)}, u32[]{:S(2)}) copy-start(bf16[4,128,2048]{2,1,0:T(8,128)(2,1)} %x_ref.3) | copy-start | bytes 6291460
  274.3 26.3 %collective-permute-start.1 = (bf16[2,128,2048]{2,1,0:T(8,128)(2,1)}, bf16[2,128,2048]{2,1,0:T(8,128)(2,1)}, u32[]{:S(2)}, u32[]{:S(2)}) collective-permute-start(bf16[2,128,2048]{2,1,0:T(8,128)(2,1)} %convert_element_type.201), channel_id=1, source_target_pairs={{0,1},{1,0},{2,3},{3,2},{4,5},{5,4},{6,7},{7,6},{8,9},{9,8},{10,11... | collective-permute-start | bytes 3145736 | tf_op jit(solution)/shard_map/ppermute | solution.py:678
  276.9 46.1 %collective-permute-start.4 = (bf16[2,128,2048]{2,1,0:T(8,128)(2,1)}, bf16[2,128,2048]{2,1,0:T(8,128)(2,1)}, u32[]{:S(2)}, u32[]{:S(2)}) collective-permute-start(bf16[2,128,2048]{2,1,0:T(8,128)(2,1)} %convert_element_type.211), channel_id=1, source_target_pairs={{0,1},{1,0},{2,3},{3,2},{4,5},{5,4},{6,7},{7,6},{8,9},{9,8},{10,11... | collective-permute-start | bytes 3145736 | tf_op jit(solution)/shard_map/ppermute | solution.py:678
  277.4 67.4 %collective-permute-start.13 = (bf16[4,128,1024]{2,1,0:T(8,128)(2,1)}, bf16[4,128,1024]{2,1,0:T(8,128)(2,1)}, u32[]{:S(2)}, u32[]{:S(2)}) collective-permute-start(bf16[4,128,1024]{2,1,0:T(8,128)(2,1)} %param.37), channel_id=1, source_target_pairs={{0,1},{1,0},{2,3},{3,2},{4,5},{5,4},{6,7},{7,6},{8,9},{9,8},{10,11... | collective-permute-start | bytes 3145736 | tf_op jit(solution)/shard_map/ppermute | solution.py:678
  326.6 80.5 %copy-start.40 = (f32[2,128,2048]{2,1,0:T(8,128)}, f32[2,128,2048]{2,1,0:T(8,128)S(1)}, u32[]{:S(2)}) copy-start(f32[2,128,2048]{2,1,0:T(8,128)S(1)} %get-tuple-element.229) | copy-start | bytes 6291460
  326.6 80.5 %copy-start.42 = (f32[2,128,2048]{2,1,0:T(8,128)}, f32[2,128,2048]{2,1,0:T(8,128)S(1)}, u32[]{:S(2)}) copy-start(f32[2,128,2048]{2,1,0:T(8,128)S(1)} %get-tuple-element.252) | copy-start | bytes 6291460
  328.1 20.2 %copy-start.44 = (f32[2,128,2048]{2,1,0:T(8,128)}, f32[2,128,2048]{2,1,0:T(8,128)S(1)}, u32[]{:S(2)}) copy-start(f32[2,128,2048]{2,1,0:T(8,128)S(1)} %get-tuple-element.284) | copy-start | bytes 6291460
  328.2 20.1 %collective-permute-start.5 = (bf16[2,2048]{1,0:T(2,128)(2,1)S(1)}, bf16[2,2048]{1,0:T(2,128)(2,1)S(1)}, u32[]{:S(2)}, u32[]{:S(2)}) collective-permute-start(bf16[2,2048]{1,0:T(2,128)(2,1)S(1)} %bitcast.277), channel_id=1, source_target_pairs={{0,2},{2,4},{4,6},{6,8},{8,10},{10,12},{12,14},{1,3},{3,5},{5,7},{... | collective-permute-start | bytes 24584 | tf_op jit(solution)/shard_map/ppermute | solution.py:17
  329.5 18.8 %collective-permute-start.2 = (bf16[2,2048]{1,0:T(2,128)(2,1)S(1)}, bf16[2,2048]{1,0:T(2,128)(2,1)S(1)}, u32[]{:S(2)}, u32[]{:S(2)}) collective-permute-start(bf16[2,2048]{1,0:T(2,128)(2,1)S(1)} %bitcast.278), channel_id=1, source_target_pairs={{0,2},{2,4},{4,6},{6,8},{8,10},{10,12},{12,14},{1,3},{3,5},{5,7},{... | collective-permute-start | bytes 24584 | tf_op jit(solution)/shard_map/ppermute | solution.py:17
  349.9 12.5 %copy-start.75 = (bf16[2,128,2048]{2,1,0:T(8,128)(2,1)}, bf16[2,128,2048]{2,1,0:T(8,128)(2,1)S(1)}, u32[]{:S(2)}) copy-start(bf16[2,128,2048]{2,1,0:T(8,128)(2,1)S(1)} %get-tuple-element.282) | copy-start | bytes 3145732
  349.9 12.5 %copy-start.70 = (bf16[2,128,2048]{2,1,0:T(8,128)(2,1)}, bf16[2,128,2048]{2,1,0:T(8,128)(2,1)S(1)}, u32[]{:S(2)}) copy-start(bf16[2,128,2048]{2,1,0:T(8,128)(2,1)S(1)} %get-tuple-element.283) | copy-start | bytes 3145732
  349.9 26.0 %copy-start.72 = (bf16[2,128,2048]{2,1,0:T(8,128)(2,1)}, bf16[2,128,2048]{2,1,0:T(8,128)(2,1)S(1)}, u32[]{:S(2)}) copy-start(bf16[2,128,2048]{2,1,0:T(8,128)(2,1)S(1)} %get-tuple-element.237) | copy-start | bytes 3145732
  349.9 37.1 %copy-start.68 = (bf16[2,128,2048]{2,1,0:T(8,128)(2,1)}, bf16[2,128,2048]{2,1,0:T(8,128)(2,1)S(1)}, u32[]{:S(2)}) copy-start(bf16[2,128,2048]{2,1,0:T(8,128)(2,1)S(1)} %get-tuple-element.236) | copy-start | bytes 3145732
  350.0 12.5 %copy-start.53 = (bf16[2048,1024]{1,0:T(8,128)(2,1)S(1)}, bf16[2048,1024]{1,0:T(8,128)(2,1)}, u32[]{:S(2)}) copy-start(bf16[2048,1024]{1,0:T(8,128)(2,1)} %param.36) | copy-start | bytes 12582916
  362.5 71.5 %copy-start.87 = (bf16[2,128,3584]{2,1,0:T(8,128)(2,1)}, bf16[2,128,3584]{2,1,0:T(8,128)(2,1)S(1)}, u32[]{:S(2)}) copy-start(bf16[2,128,3584]{2,1,0:T(8,128)(2,1)S(1)} %get-tuple-element.291) | copy-start | bytes 5505028
  374.4 25.6 %collective-permute-start.3 = (bf16[2,128,1024]{2,1,0:T(8,128)(2,1)S(1)}, bf16[2,128,1024]{2,1,0:T(8,128)(2,1)S(1)}, u32[]{:S(2)}, u32[]{:S(2)}) collective-permute-start(bf16[2,128,1024]{2,1,0:T(8,128)(2,1)S(1)} %fusion.75), channel_id=1, source_target_pairs={{0,1},{1,0},{2,3},{3,2},{4,5},{5,4},{6,7},{7,6},{8,9},{9,8},{10,11... | collective-permute-start | bytes 1572872 | tf_op jit(solution)/shard_map/ppermute | solution.py:678
  387.0 46.9 %copy-start.88 = (bf16[2,128,3584]{2,1,0:T(8,128)(2,1)}, bf16[2,128,3584]{2,1,0:T(8,128)(2,1)S(1)}, u32[]{:S(2)}) copy-start(bf16[2,128,3584]{2,1,0:T(8,128)(2,1)S(1)} %get-tuple-element.293) | copy-start | bytes 5505028
  394.1 13.0 %collective-permute-start.6 = (bf16[2,128,1024]{2,1,0:T(8,128)(2,1)S(1)}, bf16[2,128,1024]{2,1,0:T(8,128)(2,1)S(1)}, u32[]{:S(2)}, u32[]{:S(2)}) collective-permute-start(bf16[2,128,1024]{2,1,0:T(8,128)(2,1)S(1)} %fusion.78), channel_id=1, source_target_pairs={{0,1},{1,0},{2,3},{3,2},{4,5},{5,4},{6,7},{7,6},{8,9},{9,8},{10,11... | collective-permute-start | bytes 1572872 | tf_op jit(solution)/shard_map/ppermute | solution.py:678
  409.6 14.9 %collective-permute-start.10 = (bf16[2,128,1024]{2,1,0:T(8,128)(2,1)S(1)}, bf16[2,128,1024]{2,1,0:T(8,128)(2,1)S(1)}, u32[]{:S(2)}, u32[]{:S(2)}) collective-permute-start(bf16[2,128,1024]{2,1,0:T(8,128)(2,1)S(1)} %get-tuple-element.249), channel_id=1, source_target_pairs={{0,1},{1,0},{2,3},{3,2},{4,5},{5,4},{6,7},{7,6},{8,9},{9,8},{10,11... | collective-permute-start | bytes 1572872 | tf_op jit(solution)/shard_map/ppermute | solution.py:678
  410.1 22.8 %collective-permute-start.7 = (bf16[2,128,1024]{2,1,0:T(8,128)(2,1)S(1)}, bf16[2,128,1024]{2,1,0:T(8,128)(2,1)S(1)}, u32[]{:S(2)}, u32[]{:S(2)}) collective-permute-start(bf16[2,128,1024]{2,1,0:T(8,128)(2,1)S(1)} %get-tuple-element.241), channel_id=1, source_target_pairs={{0,1},{1,0},{2,3},{3,2},{4,5},{5,4},{6,7},{7,6},{8,9},{9,8},{10,11... | collective-permute-start | bytes 1572872 | tf_op jit(solution)/shard_map/ppermute | solution.py:678
  443.1 195.5 %all-gather.7.cloned.1.call-start = ((), (), s32[]{:S(2)}) async-start(), calls=%async_computation.5 | async-start | bytes 4718592 | tf_op jit(solution)/shard_map/all_gather | solution.py:1405
  456.4 13.0 %copy-start.45 = (f32[2,128,2048]{2,1,0:T(8,128)S(1)}, f32[2,128,2048]{2,1,0:T(8,128)}, u32[]{:S(2)}) copy-start(f32[2,128,2048]{2,1,0:T(8,128)} %copy-done.44) | copy-start | bytes 6291460
  456.4 13.0 %copy-start.62 = (bf16[2,128,1024]{2,1,0:T(8,128)(2,1)S(1)}, bf16[2,128,1024]{2,1,0:T(8,128)(2,1)}, u32[]{:S(2)}) copy-start(bf16[2,128,1024]{2,1,0:T(8,128)(2,1)} %get-tuple-element.240) | copy-start | bytes 1572868
  476.9 30.1 %collective-permute-start.8 = (bf16[2,2048]{1,0:T(2,128)(2,1)S(1)}, bf16[2,2048]{1,0:T(2,128)(2,1)S(1)}, u32[]{:S(2)}, u32[]{:S(2)}) collective-permute-start(bf16[2,2048]{1,0:T(2,128)(2,1)S(1)} %bitcast.276), channel_id=1, source_target_pairs={{2,0},{4,2},{6,4},{8,6},{10,8},{12,10},{14,12},{3,1},{5,3},{7,5},{... | collective-permute-start | bytes 24584 | tf_op jit(solution)/shard_map/ppermute | solution.py:17
  490.2 11.2 %copy-start.64 = (bf16[2,128,1024]{2,1,0:T(8,128)(2,1)S(1)}, bf16[2,128,1024]{2,1,0:T(8,128)(2,1)}, u32[]{:S(2)}) copy-start(bf16[2,128,1024]{2,1,0:T(8,128)(2,1)} %get-tuple-element.250) | copy-start | bytes 1572868
  505.1 3.9 collective-permute-start.11
  513.6 24.7 %collective-permute-start.9 = (bf16[2,128,2048]{2,1,0:T(8,128)(2,1)}, bf16[2,128,2048]{2,1,0:T(8,128)(2,1)}, u32[]{:S(2)}, u32[]{:S(2)}) collective-permute-start(bf16[2,128,2048]{2,1,0:T(8,128)(2,1)} %get-tuple-element.224), channel_id=1, source_target_pairs={{0,1},{1,0},{2,3},{3,2},{4,5},{5,4},{6,7},{7,6},{8,9},{9,8},{10,11... | collective-permute-start | bytes 3145736 | tf_op jit(solution)/shard_map/ppermute | solution.py:678
  513.6 47.2 %collective-permute-start.12 = (bf16[2,128,2048]{2,1,0:T(8,128)(2,1)}, bf16[2,128,2048]{2,1,0:T(8,128)(2,1)}, u32[]{:S(2)}, u32[]{:S(2)}) collective-permute-start(bf16[2,128,2048]{2,1,0:T(8,128)(2,1)} %get-tuple-element.280), channel_id=1, source_target_pairs={{0,1},{1,0},{2,3},{3,2},{4,5},{5,4},{6,7},{7,6},{8,9},{9,8},{10,11... | collective-permute-start | bytes 3145736 | tf_op jit(solution)/shard_map/ppermute | solution.py:678
  515.6 22.7 %copy-start.41 = (f32[2,128,2048]{2,1,0:T(8,128)S(1)}, f32[2,128,2048]{2,1,0:T(8,128)}, u32[]{:S(2)}) copy-start(f32[2,128,2048]{2,1,0:T(8,128)} %copy-done.40) | copy-start | bytes 6291460
  538.3 22.5 %copy-start.43 = (f32[2,128,2048]{2,1,0:T(8,128)S(1)}, f32[2,128,2048]{2,1,0:T(8,128)}, u32[]{:S(2)}) copy-start(f32[2,128,2048]{2,1,0:T(8,128)} %copy-done.42) | copy-start | bytes 6291460
  538.3 22.5 %copy-start.46 = (f32[2,128,2048]{2,1,0:T(8,128)S(1)}, f32[2,128,2048]{2,1,0:T(8,128)}, u32[]{:S(2)}) copy-start(f32[2,128,2048]{2,1,0:T(8,128)} %get-tuple-element.225) | copy-start | bytes 6291460
  591.3 360.3 %reduce-scatter.5.cloned.1.call-start = ((), (), s32[]{:S(2)}) async-start(), calls=%async_computation.3 | async-start | bytes 11141120 | tf_op jit(solution)/shard_map/reduce_scatter | solution.py:1371
  643.4 22.4 %copy-start.23 = (bf16[512,1024]{1,0:T(8,128)(2,1)S(1)}, bf16[512,1024]{1,0:T(8,128)(2,1)}, u32[]{:S(2)}) copy-start(bf16[512,1024]{1,0:T(8,128)(2,1)} %copy-done.22) | copy-start | bytes 3145732
  643.4 22.4 %copy-start.25 = (bf16[512,1024]{1,0:T(8,128)(2,1)S(1)}, bf16[512,1024]{1,0:T(8,128)(2,1)}, u32[]{:S(2)}) copy-start(bf16[512,1024]{1,0:T(8,128)(2,1)} %copy-done.24) | copy-start | bytes 3145732
  713.2 5.1 collective-permute-start.14
  929.1 16.5 %collective-permute-start.15 = (f32[400,128]{0,1:T(8,128)}, f32[400,128]{0,1:T(8,128)S(1)}, u32[]{:S(2)}, u32[]{:S(2)}) collective-permute-start(f32[400,128]{0,1:T(8,128)} %bitcast.235), channel_id=1, source_target_pairs={{0,1},{1,0},{2,3},{3,2},{4,5},{5,4},{6,7},{7,6},{8,9},{9,8},{10,11... | collective-permute-start | bytes 614408 | tf_op jit(solution)/shard_map/ppermute | solution.py:678
  (86 other events, 260.8 us)
Sparse Core Ops, SparseCore 0:
  192.7 56.1 all-gather.4
  443.3 116.8 reduce-scatter.2
  591.4 47.1 all-gather.6
  642.5 128.4 reduce-scatter.4

commit v7 on v5

--- a/solution.py
+++ b/solution.py
@@ -1283,6 +1283,7 @@
     where_here = place.astype(jnp.int32).reshape(1)
     all_packed = lax.all_gather(recurrence.totals(projected, log_flat), "seq")
     inner, decayed = recurrence.inner(projected, log_flat, bonus)
+    inner, full_out = lax.optimization_barrier((inner, full_out))
     wkv, mixer_rows, state, decay_range = recurrence.join(
         where_here,
         inner,
@@ -1304,11 +1305,17 @@
     )
     normed_two, norm_two_back = jax.vjp(layer_norm, residual, gains_all[1], biases_all[1])
     prev_two = from_behind(normed_two[:, -1, :].astype(jnp.bfloat16), "seq", 1).astype(jnp.float32)
-    (chan_key, chan_recept), chan_back = jax.vjp(
-        channel_mix, normed_two, prev_two, shift_coefficient
-    )
+    chan_key, chan_recept = channel_mix(normed_two, prev_two, shift_coefficient)
     chan_key_b = chan_key.astype(jnp.bfloat16)
     chan_recept_b = chan_recept.astype(jnp.bfloat16)
+    recept_pre = jnp.einsum(
+        "std,de->ste", chan_recept_b, channel_recept, preferred_element_type=jnp.float32
+    )
+    gate_chan = jax.nn.sigmoid(recept_pre)
+    grad_out = out_grad.astype(jnp.float32)
+    grad_value = (grad_out * gate_chan).astype(jnp.bfloat16)
+    chan_key_b, grad_value = lax.optimization_barrier((chan_key_b, grad_value))
+    full_value = both_halves(grad_value)
     key_pre = jnp.einsum("std,df->stf", chan_key_b, channel_key, preferred_element_type=jnp.float32)
     hidden = jnp.square(jnp.maximum(key_pre, 0.0)).astype(jnp.bfloat16)
     own_value, sent_value = (
@@ -1316,26 +1323,13 @@
         for which in (half, 1 - half)
     )
     sent_part = jnp.einsum("stf,fd->std", hidden, sent_value, preferred_element_type=jnp.float32)
-    other_part = other_half(sent_part.astype(jnp.bfloat16)).astype(jnp.float32)
+    hidden, sent_part = lax.optimization_barrier((hidden, sent_part.astype(jnp.bfloat16)))
+    other_part = other_half(sent_part).astype(jnp.float32)
     own_part = jnp.einsum("stf,fd->std", hidden, own_value, preferred_element_type=jnp.float32)
-    recept_pre = jnp.einsum(
-        "std,de->ste", chan_recept_b, channel_recept, preferred_element_type=jnp.float32
-    )
-    own_part, recept_pre = lax.optimization_barrier((own_part, recept_pre))
-    kv_rows = own_part + other_part
-    gate_chan = jax.nn.sigmoid(recept_pre)
-    output = (own_half(residual) + gate_chan * kv_rows).astype(jnp.bfloat16)
-    grad_out = out_grad.astype(jnp.float32)
-    grad_value = (grad_out * gate_chan).astype(jnp.bfloat16)
-    grad_recept = (grad_out * kv_rows * gate_chan * (1.0 - gate_chan)).astype(jnp.bfloat16)
-    full_value = both_halves(grad_value)
 
     def weight_terms(left, right):
         return jnp.einsum(
-            "td,tf->df",
-            left.reshape(tokens, -1),
-            right.reshape(tokens, -1),
-            preferred_element_type=jnp.float32,
+            "td,tf->df", left, right, preferred_element_type=jnp.float32
         ).astype(jnp.bfloat16)
 
     def scattered(whole):
@@ -1343,28 +1337,47 @@
             jnp.float32
         )
 
-    full_value, value_whole = lax.optimization_barrier(
-        (full_value, weight_terms(full_value, hidden))
+    flat_value, flat_hidden = full_value.reshape(tokens, -1), hidden.reshape(tokens, -1)
+    value_cut = flat_hidden.shape[1] * 5 // 7
+    full_value, own_part, value_whole = lax.optimization_barrier(
+        (full_value, own_part, weight_terms(flat_value, flat_hidden[:, :value_cut]))
     )
     value_sum = scattered(value_whole)
     grad_hidden = jnp.einsum(
         "std,fd->stf", full_value, channel_value, preferred_element_type=jnp.float32
     )
     grad_key = (grad_hidden * 2.0 * jnp.maximum(key_pre, 0.0)).astype(jnp.bfloat16)
-    part_key = jnp.einsum("stf,df->std", grad_key, channel_key, preferred_element_type=jnp.float32)
-    part_recept = jnp.einsum(
-        "ste,de->std", grad_recept, channel_recept, preferred_element_type=jnp.float32
-    )
-    part_normed_two, part_prev_two, grad_coeffs_chan = chan_back((part_key, part_recept))
-    from_next_two = from_behind(for_sending(part_prev_two), "seq", -1).astype(jnp.float32)
-    part_normed_two = add_last(part_normed_two, from_next_two)
-    sizes = (lax.axis_size("dp"), blocks)
-    grad_key_rows = grad_key.reshape(tokens, -1)
-    key_cut = grad_key_rows.shape[1] * 5 // 7
-    key_whole = weight_terms(chan_key_b, grad_key_rows[:, :key_cut])
-    grad_normed_two = part_normed_two + other_half(part_normed_two.astype(jnp.bfloat16)).astype(
-        jnp.float32
-    )
+    grad_key, own_part = lax.optimization_barrier((grad_key, own_part))
+    kv_rows = own_part + other_part
+    output = (own_half(residual) + gate_chan * kv_rows).astype(jnp.bfloat16)
+    grad_recept = (grad_out * kv_rows * gate_chan * (1.0 - gate_chan)).astype(jnp.bfloat16)
+    grad_normed_two, grad_coeffs_chan = [], []
+    for k in range(2):
+        at = slice(k * own_cols, (k + 1) * own_cols)
+        part_key = jnp.einsum(
+            "stf,df->std", grad_key, channel_key[at], preferred_element_type=jnp.float32
+        )
+        part_recept = jnp.einsum(
+            "ste,de->std", grad_recept, channel_recept[at], preferred_element_type=jnp.float32
+        )
+        _, chan_back = jax.vjp(
+            channel_mix, normed_two[..., at], prev_two[..., at], shift_coefficient[:, at]
+        )
+        part_two, part_prev_two, coeffs = chan_back((part_key, part_recept))
+        grad_coeffs_chan.append(coeffs)
+        sent_two = part_two.astype(jnp.bfloat16)
+        grad_key, sent_two = lax.optimization_barrier((grad_key, sent_two))
+        other_two = other_half(sent_two).astype(jnp.float32)
+        from_next_two = from_behind(for_sending(part_prev_two), "seq", -1)
+        from_next_two = from_next_two.astype(jnp.float32) + other_half(from_next_two).astype(
+            jnp.float32
+        )
+        grad_normed_two.append(add_last(part_two + other_two, from_next_two))
+    grad_coeffs_chan = jnp.concatenate(grad_coeffs_chan, axis=1)
+    grad_normed_two = jnp.concatenate(grad_normed_two, axis=-1)
+    flat_key, flat_grad_key = chan_key_b.reshape(tokens, -1), grad_key.reshape(tokens, -1)
+    key_cut = flat_grad_key.shape[1] * 5 // 7
+    key_whole = weight_terms(flat_key, flat_grad_key[:, :key_cut])
     grad_residual, grad_gain_two, grad_bias_two = norm_two_back(grad_normed_two)
     grad_residual = grad_residual + full_out.astype(jnp.float32)
     grad_residual, key_whole = lax.optimization_barrier((grad_residual, key_whole))
@@ -1446,12 +1459,13 @@
     small_rows = lax.dynamic_update_slice(small_rows, other_rows, (8, 0))
     small_rows = lax.dynamic_update_slice(small_rows, head_rows, (narrow_at, 0))
     sent_block = lax.dynamic_slice_in_dim(part_block, (1 - half) * own_cols, own_cols, 2)
-    *proj_sums, out_sum, recept_sum, key_rest, small_sums, other_block = ring_sums(
+    *proj_sums, out_sum, recept_sum, key_rest, value_rest, small_sums, other_block = ring_sums(
         [(stacked, grad_proj, (branch,)) for branch in range(4)]
         + [
             (grad_branch.reshape(tokens, -1), mixer_in.reshape(tokens, -1), ()),
             (chan_recept_b.reshape(tokens, -1), grad_recept.reshape(tokens, -1), ()),
-            (chan_key_b.reshape(tokens, -1), grad_key_rows[:, key_cut:], ()),
+            (flat_key, flat_grad_key[:, key_cut:], ()),
+            (flat_value, flat_hidden[:, value_cut:], ()),
         ],
         small_rows,
         sent_block.astype(jnp.bfloat16),
@@ -1481,7 +1495,7 @@
         out_sum.T,
         *head_sums,
         jnp.concatenate([key_sum, key_rest], axis=1),
-        value_sum.T,
+        jnp.concatenate([value_sum, value_rest], axis=1).T,
         recept_sum,
         total_least,
         total_most,

time: 931 us -> 905 us (0.972)
  waiting for transfers between devices: 199 us -> 130 us
  Pallas kernels: 457 us -> 476 us
  local copies, waits for them, and re-layouts: 70.1 us -> 79.5 us
    ppermute x6 -> x9, waiting for transfers between devices: 119 us -> 87.8 us  [other_half(): return lax.ppermute(block, 'tp', [(0, 1), (1, 0)])]
    reduce_scatter x2, waiting for transfers between devices: 27.1 us -> 0.02 us  [scattered(): lax.psum_scatter(whole, ('dp', 'seq'), scatter_dimension=0, tiled=True)]
    pallas_call x1, Pallas kernels: 180 us -> 200 us  [ring_sums(): pl.pallas_call(functools.partial(ring_kernel, dp_size, seq_size, rows, wi...]
    dot_general x1, matrix products: 15.9 us -> 28.7 us  [per_device(): jnp.einsum('std,fd->stf', full_value, channel_value, preferred_element_ty...]
    dot_general x4 -> x6, matrix products: 42.9 us -> 35.8 us  [the longest x2 17.1 us: weight_terms(): jnp.einsum('td,tf->df', left, right, preferred_element_type=jnp.float32)]
    unnamed x192 -> x207, local copies, waits for them, and re-layouts: 53.3 us -> 54.3 us
  transfers between devices with their start and end apart: 14 -> 18, of which waited for: 9 -> 8; matrix products, arithmetic and copies ran while one was open for 13% -> 18% of each run, Pallas kernels for 32% -> 35%
where the time goes in v7:
time: 905 us; the launch traced here: 896 us
  Pallas kernels  476 us (53%)
  waiting for transfers between devices  130 us (14%)
  matrix products  115 us (13%)
  local copies, waits for them, and re-layouts  79.5 us (9%)
  other arithmetic  58.2 us (6%)
  starting transfers between devices  20.9 us (2%)
  between operations  15.4 us (2%)
    pallas_call x1, Pallas kernels, ring_sums(): pl.pallas_call(functools.partial(ring_kernel, dp_size, seq_size, rows, wi...  200 us
    pallas_call x1, Pallas kernels, gather_weights(): pl.pallas_call(functools.partial(gather_kernel, dp_size, seq_size), out_s...  117 us
    pallas_call x6, Pallas kernels, call(): pl.pallas_call(kernel, grid=self.grid, in_specs=ins, out_specs=[spec for...  100 us
    ppermute x9, waiting for transfers between devices, other_half(): return lax.ppermute(block, 'tp', [(0, 1), (1, 0)])  87.8 us
    unnamed x207, local copies, waits for them, and re-layouts  54.3 us
    pallas_call x1, Pallas kernels, mix_back(): pl.pallas_call(mix_back_kernel, grid=(sequences // together,), in_specs=[...  43.9 us
    dot_general x1, matrix products, per_device(): jnp.einsum('std,fd->stf', full_value, channel_value, preferred_element_ty...  28.7 us
    all_gather x1, waiting for transfers between devices, per_device(): all_packed = lax.all_gather(recurrence.totals(projected, log_flat), 'seq')  27.2 us
  transfers between devices with their start and end apart: 18, of which 8 were waited for; matrix products, arithmetic and copies ran while one was open for 18% of the time, Pallas kernels for 35%

profile of v7, /device:TPU:0, one launch (start us, length us, event | category | flops | bytes accessed | tf_op | source)
XLA Modules:
  0.0 895.6 jit_solution(13916545568896370189)
XLA Ops:
  17.4 117.2 %shard_map.354 = (bf16[480,2048]{1,0:T(8,128)(2,1)}, bf16[4,2048,1024]{2,1,0:T(8,128)(2,1)}, bf16[1024,2048]{1,0:T(8,128)(2,1)}) custom-call(bf16[480,128]{1,0:T(8,128)(2,1)} %copy-done.75, bf16[4,128,1024]{2,1,0:T(8,128)(2,1)} %proj_ref.1, bf16[1024,128]{1,0:T(8,128)(2,1)} %out_ref.1), custom_call_target="tpu_custom_call" | custom-call | tf_op jit(solution)/shard_map/pallas_call | solution.py:1068
  135.6 2.3 collective-permute-start
  140.2 3.1 fusion.5
  144.4 14.9 %shard_map.355 = (bf16[4,512,2048]{2,1,0:T(8,128)(2,1)}, f32[512,160]{1,0:T(8,128)S(1)}, f32[512,64]{1,0:T(8,128)S(1)}, f32[512,1024]{1,0:T(8,128)S(1)}) custom-call(bf16[4,128,2048]{2,1,0:T(8,128)(2,1)S(1)} %copy-done.2, f32[4,1,2048]{2,1,0:T(1,128)S(1)} %reshape.351.before_ref, f32[8,2048]{1,0:T(8,128)S(1)} %slice_convert_fusion.1.coeff_ref, ...), custom_call_target="tpu_custom_call" | custom-call | flops 2000000000 | bytes 16777216 | tf_op jit(solution)/shard_map/pallas_call | solution.py:1149
  162.2 13.7 %fusion.114.rkv_ref.kv_ref.gate_ref = f32[4,512,1024]{2,1,0:T(8,128)S(1)} fusion(bf16[4,512,2048]{2,1,0:T(8,128)(2,1)} %get-tuple-element.90.refs_0_, bf16[4,2048,1024]{2,1,0:T(8,128)(2,1)} %get-tuple-element.91.proj_ref), kind=kOutput, calls=%fused_computation.224 | convolution fusion | flops 8589934592 | bytes 33554432 | tf_op jit(solution)/shard_map/ntd,nde->nte/dot_general | solution.py:1281
  177.5 11.8 %shard_map.357 = bf16[4,8,80,128]{3,2,1,0:T(8,128)(2,1)} custom-call(f32[4,512,1024]{2,1,0:T(8,128)S(1)} %fusion.114.rkv_ref.kv_ref.gate_ref, f32[512,1024]{1,0:T(8,128)S(1)} %copy-done.6), custom_call_target="tpu_custom_call" | custom-call | flops 1000000000 | bytes 10485760 | tf_op jit(solution)/shard_map/pallas_call | solution.py:368
  189.3 3.3 copy-done
  194.5 3.4 copy-done.1
  199.5 14.0 %shard_map.356 = (f32[512,1024]{1,0:T(8,128)S(1)}, bf16[512,1024]{1,0:T(8,128)(2,1)S(1)}) custom-call(f32[4,512,1024]{2,1,0:T(8,128)S(1)} %copy-done.1, f32[512,1024]{1,0:T(8,128)S(1)} %copy-done.7, f32[1,1024]{1,0:T(1,128)S(1)} %get-tuple-element.263.bonus_ref), custom_call_target="tpu_custom_call" | custom-call | flops 2000000000 | bytes 10489856 | tf_op jit(solution)/shard_map/pallas_call | solution.py:368
  213.5 5.3 collective-permute-done.1
  221.7 27.2 %all-gather.5.cloned.1.call-done = bf16[32,8,80,128]{3,2,1,0:T(8,128)(2,1)} async-done(((bf16[4,8,80,128]{3,2,1,0:T(8,128)(2,1)}), bf16[32,8,80,128]{3,2,1,0:T(8,128)(2,1)}) %all-gather.5.cloned.1.call-update) | async-done | bytes 5242896 | tf_op jit(solution)/shard_map/all_gather | solution.py:1284
  250.6 18.9 %shard_map.358 = (f32[512,1024]{1,0:T(8,128)S(1)}, bf16[512,1024]{1,0:T(8,128)(2,1)S(1)}, f32[4,8,64,128]{3,2,1,0:T(8,128)S(1)}, f32[4,8,1024]{2,1,0:T(8,128)S(1)}) custom-call(s32[1]{0:T(128)} %bitcast.place_ref, f32[512,1024]{1,0:T(8,128)S(1)} %copy-done.10, bf16[512,1024]{1,0:T(8,128)(2,1)S(1)} %get-tuple-element.95.decayed_ref, f32[4,512,1024]{2,1,0:T(8,128)} %copy-done, ...), custom_call_target="tpu_custom_call" | custom-call | flops 1000000000 | bytes 17833988 | tf_op jit(solution)/shard_map/pallas_call | solution.py:368
  269.6 2.4 fusion.26
  273.8 46.3 %collective-permute-done.2 = bf16[4,128,2048]{2,1,0:T(8,128)(2,1)S(1)} collective-permute-done((bf16[4,128,2048]{2,1,0:T(8,128)(2,1)S(1)}, bf16[4,128,2048]{2,1,0:T(8,128)(2,1)S(1)}, u32[]{:S(2)}, u32[]{:S(2)}) %collective-permute-start.2) | collective-permute-done | bytes 2097184 | tf_op jit(solution)/shard_map/ppermute | solution.py:678
  323.4 2.8 multiply_add_fusion
  329.4 4.9 add_convert_fusion
  334.4 3.9 fusion.32
  339.8 13.5 %multiply_convert_fusion.1 = (bf16[4,128,3584]{2,1,0:T(8,128)(2,1)S(1)}, f32[4,128,3584]{2,1,0:T(8,128)}) fusion(bf16[4,128,2048]{2,1,0:T(8,128)(2,1)S(1)} %get-tuple-element.101, bf16[2048,3584]{1,0:T(8,128)(2,1)} %param.34), kind=kOutput, calls=%fused_computation.23 | convolution fusion | flops 7521697792 | bytes 27787264 | tf_op jit(solution)/shard_map/std,df->stf/dot_general | solution.py:1319
  353.4 4.9 fusion.45
  358.4 5.3 fusion.12
  365.7 8.6 convolution_convert_fusion.1
  374.5 5.0 fusion.104
  380.9 28.7 %multiply_convert_fusion = bf16[4,128,3584]{2,1,0:T(8,128)(2,1)} fusion(f32[4,128,3584]{2,1,0:T(8,128)} %get-tuple-element.292, bf16[4,128,2048]{2,1,0:T(8,128)(2,1)S(1)} %copy-done.51, bf16[3584,2048]{1,0:T(8,128)(2,1)} %param.35), kind=kOutput, calls=%fused_computation.20 | convolution fusion | flops 7523532800 | bytes 27787264 | tf_op jit(solution)/shard_map/std,fd->stf/dot_general | solution.py:1346
  410.6 4.7 fusion.35
  417.7 6.3 multiply_add_fusion.2
  425.8 2.4 fusion.102
  430.5 9.9 %multiply_reduce_fusion.6 = (f32[1024]{0:T(1024)S(1)}, f32[1024]{0:T(1024)S(1)}, f32[1024]{0:T(1024)S(1)}, f32[1024]{0:T(1024)S(1)}, f32[4,128,1024]{2,1,0:T(8,128)S(1)}, /*index=5*/f32[4,128,1024]{2,1,0:T(8,128)S(1)}) fusion(f32[4,128,1024]{2,1,0:T(8,128)S(1)} %fusion.38, f32[4,128,2048]{2,1,0:T(8,128)} %multiply_add_fusion, ...), kind=kOutput, calls=%fused_computation.67 | convolution fusion | flops 3765956608 | bytes 29908992 | tf_op jit(solution)/shard_map/stf,df->std/dot_general | solution.py:1357
  440.6 2.4 fusion.101
  446.9 8.4 convolution_convert_fusion
  457.1 35.6 %collective-permute-done.8 = bf16[4,1024]{1,0:T(4,128)(2,1)S(1)} collective-permute-done((bf16[4,1024]{1,0:T(4,128)(2,1)S(1)}, bf16[4,1024]{1,0:T(4,128)(2,1)S(1)}, u32[]{:S(2)}, u32[]{:S(2)}) %collective-permute-start.8) | collective-permute-done | bytes 8224 | tf_op jit(solution)/shard_map/ppermute | solution.py:678
  494.2 3.7 select_add_fusion.2
  499.0 1.9 multiply_reduce_fusion
  502.9 3.4 copy-done.87
  506.2 2.4 fusion.24
  508.6 13.4 %shard_map.359 = (f32[512,1024]{1,0:T(8,128)S(1)}, bf16[512,1024]{1,0:T(8,128)(2,1)S(1)}, bf16[4,8,64,128]{3,2,1,0:T(8,128)(2,1)}, f32[4,8,1024]{2,1,0:T(8,128)S(1)}) custom-call(f32[512,1024]{1,0:T(8,128)S(1)} %bitcast.172, f32[512,1024]{1,0:T(8,128)S(1)} %copy-done.18, f32[4,512,1024]{2,1,0:T(8,128)} %copy-done, ...), custom_call_target="tpu_custom_call" | custom-call | flops 1000000000 | bytes 13639680 | tf_op jit(solution)/shard_map/pallas_call | solution.py:368
  523.5 2.5 convert_element_type.196
  526.9 2.4 slice.300.refs_9_
  529.3 2.3 slice.299.refs_7_
  533.5 19.7 %shard_map.360 = (bf16[512,1024]{1,0:T(8,128)(2,1)S(1)}, f32[512,1024]{1,0:T(8,128)S(1)}, f32[512,1024]{1,0:T(8,128)S(1)}, f32[512,1024]{1,0:T(8,128)S(1)}, f32[4,8,1024]{2,1,0:T(8,128)S(1)}) custom-call(f32[4,512,1024]{2,1,0:T(8,128)} %copy-done, f32[512,1024]{1,0:T(8,128)S(1)} %copy-done.8, f32[1,1024]{1,0:T(1,128)S(1)} %copy-done.33, ...), custom_call_target="tpu_custom_call" | custom-call | flops 4000000000 | bytes 13635584 | tf_op jit(solution)/shard_map/pallas_call | solution.py:368
  558.2 14.4 %all-gather.7.cloned.1.call-done = bf16[32,8,64,128]{3,2,1,0:T(8,128)(2,1)} async-done(((bf16[4,8,64,128]{3,2,1,0:T(8,128)(2,1)}), bf16[32,8,64,128]{3,2,1,0:T(8,128)(2,1)}) %all-gather.7.cloned.1.call-update) | async-done | bytes 4194320 | tf_op jit(solution)/shard_map/all_gather | solution.py:1391
  577.4 22.4 %shard_map.361 = (bf16[512,1024]{1,0:T(8,128)(2,1)S(1)}, bf16[512,1024]{1,0:T(8,128)(2,1)S(1)}, f32[512,1024]{1,0:T(8,128)S(1)}, f32[4,16,64,64]{3,2,1,0:T(8,128)}, f32[4,8,1024]{2,1,0:T(8,128)S(1)}) custom-call(s32[1]{0:T(128)} %bitcast.place_ref, f32[4,512,1024]{2,1,0:T(8,128)} %copy-done, f32[512,1024]{1,0:T(8,128)S(1)} %copy-done.8, ...), custom_call_target="tpu_custom_call" | custom-call | flops 3000000000 | bytes 27262980 | tf_op jit(solution)/shard_map/pallas_call | solution.py:368
  599.9 2.6 pad_maximum_fusion.1.grad_ref.refs_1_
  602.5 43.9 %shard_map.362 = (f32[4,128,2048]{2,1,0:T(8,128)}, f32[4,1,2048]{2,1,0:T(1,128)}, f32[512,2048]{1,0:T(8,128)}, f32[64,1024]{1,0:T(8,128)}) custom-call(bf16[4,128,2048]{2,1,0:T(8,128)(2,1)} %x_ref.3, f32[4,1,2048]{2,1,0:T(1,128)} %copy-done.30, bf16[4,512,1024]{2,1,0:T(8,128)(2,1)} %pad_maximum_fusion.1.grad_ref.refs_1_, f32[512,1024]{1,0:T(8,128)} %copy-done.36, ...), custom_call_target="tpu_custom_call" | custom-call | flops 10000000000 | bytes 41943040 | tf_op jit(solution)/shard_map/pallas_call | solution.py:654
  653.8 5.1 select_add_fusion
  658.9 2.7 dynamic-slice_convert_fusion.refs_11_
  663.1 199.9 %shard_map.363 = (f32[128,1024]{1,0:T(8,128)}, f32[128,1024]{1,0:T(8,128)}, f32[128,1024]{1,0:T(8,128)}, f32[128,1024]{1,0:T(8,128)}, f32[128,1024]{1,0:T(8,128)...) custom-call(bf16[4,512,2048]{2,1,0:T(8,128)(2,1)} %get-tuple-element, ...), custom_call_target="tpu_custom_call" | custom-call | flops 18253611008 | bytes 25690112 | tf_op jit(solution)/shard_map/pallas_call | solution.py:922
  864.6 4.8 convert_add_fusion.2
  876.9 2.7 pad_maximum_fusion.4
  (366 shorter events, 98.9 us)
Async XLA Ops:
  7.2 241.8 %all-gather.5.cloned.1.call-start = ((), (), s32[]{:S(2)}) async-start(), calls=%async_computation.4 | async-start | bytes 5898240 | tf_op jit(solution)/shard_map/all_gather | solution.py:1284
  13.7 129.6 %copy-start.68 = (bf16[4,1,2048]{2,0,1:T(4,128)(2,1)}, bf16[4,1,2048]{2,0,1:T(4,128)(2,1)S(1)}, u32[]{:S(2)}) copy-start(bf16[4,1,2048]{2,0,1:T(4,128)(2,1)S(1)} %get-tuple-element.245) | copy-start | bytes 49156
  13.7 129.6 %copy-start.76 = (f32[4]{0:T(128)}, f32[4]{0:T(128)S(1)}, u32[]{:S(2)}) copy-start(f32[4]{0:T(128)S(1)} %broadcast_multiply_fusion.3) | copy-start | bytes 52
  14.4 128.9 %copy-start.78 = (f32[4]{0:T(128)}, f32[4]{0:T(128)S(1)}, u32[]{:S(2)}) copy-start(f32[4]{0:T(128)S(1)} %fusion.97) | copy-start | bytes 52
  135.5 7.8 copy-start.73
  135.6 8.8 collective-permute-start
  138.8 235.7 %copy-start.28 = (f32[8,2048]{1,0:T(8,128)}, f32[8,2048]{1,0:T(8,128)S(1)}, u32[]{:S(2)}) copy-start(f32[8,2048]{1,0:T(8,128)S(1)} %slice_convert_fusion.1.coeff_ref) | copy-start | bytes 196612
  140.2 19.2 %copy-start.25 = (bf16[160,2048]{1,0:T(8,128)(2,1)}, bf16[160,2048]{1,0:T(8,128)(2,1)S(1)}, u32[]{:S(2)}) copy-start(bf16[160,2048]{1,0:T(8,128)(2,1)S(1)} %get-tuple-element.257.up_ref) | copy-start | bytes 1966084
  140.2 19.2 %copy-start.26 = (bf16[160,2048]{1,0:T(8,128)(2,1)}, bf16[160,2048]{1,0:T(8,128)(2,1)S(1)}, u32[]{:S(2)}) copy-start(bf16[160,2048]{1,0:T(8,128)(2,1)S(1)} %get-tuple-element.258.down_ref) | copy-start | bytes 1966084
  143.3 51.2 %copy-start.32 = (f32[1,1024]{1,0:T(1,128)}, f32[1,1024]{1,0:T(1,128)S(1)}, u32[]{:S(2)}) copy-start(f32[1,1024]{1,0:T(1,128)S(1)} %get-tuple-element.263.bonus_ref) | copy-start | bytes 12292
  143.4 16.0 %copy-start.31 = (f32[2,2048]{1,0:T(2,128)}, f32[2,2048]{1,0:T(2,128)S(1)}, u32[]{:S(2)}) copy-start(f32[2,2048]{1,0:T(2,128)S(1)} %pad_maximum_fusion.7.norm_ref) | copy-start | bytes 49156
  144.3 15.0 %copy-start.27 = (bf16[64,2048]{1,0:T(8,128)(2,1)}, bf16[64,2048]{1,0:T(8,128)(2,1)S(1)}, u32[]{:S(2)}) copy-start(bf16[64,2048]{1,0:T(8,128)(2,1)S(1)} %slice.223.decay_down_ref) | copy-start | bytes 786436
  144.4 15.0 %copy-start.29 = (bf16[64,1024]{1,0:T(8,128)(2,1)}, bf16[64,1024]{1,0:T(8,128)(2,1)S(1)}, u32[]{:S(2)}) copy-start(bf16[64,1024]{1,0:T(8,128)(2,1)S(1)} %slice.377.decay_up_ref) | copy-start | bytes 393220
  144.4 15.0 %copy-start.30 = (f32[4,1,2048]{2,1,0:T(1,128)}, f32[4,1,2048]{2,1,0:T(1,128)S(1)}, u32[]{:S(2)}) copy-start(f32[4,1,2048]{2,1,0:T(1,128)S(1)} %reshape.351.before_ref) | copy-start | bytes 98308
  177.5 15.4 %copy-start.46 = (bf16[4,128,1024]{2,1,0:T(8,128)(2,1)S(1)}, bf16[4,128,1024]{2,1,0:T(8,128)(2,1)}, u32[]{:S(2)}) copy-start(bf16[4,128,1024]{2,1,0:T(8,128)(2,1)} %param.37) | copy-start | bytes 3145732
  192.6 330.8 %reduce-scatter.3.cloned.1.call-start = ((), (), s32[]{:S(2)}) async-start(), calls=%async_computation.2 | async-start | bytes 11141120 | tf_op jit(solution)/shard_map/reduce_scatter | solution.py:1336
  192.9 25.9 %collective-permute-start.1 = (bf16[4,128,1024]{2,1,0:T(8,128)(2,1)S(1)}, bf16[4,128,1024]{2,1,0:T(8,128)(2,1)}, u32[]{:S(2)}, u32[]{:S(2)}) collective-permute-start(bf16[4,128,1024]{2,1,0:T(8,128)(2,1)S(1)} %copy-done.46), channel_id=1, source_target_pairs={{0,1},{1,0},{2,3},{3,2},{4,5},{5,4},{6,7},{7,6},{8,9},{9,8},{10,11... | collective-permute-start | bytes 3145736 | tf_op jit(solution)/shard_map/ppermute | solution.py:678
  213.5 8.2 copy-start.9
  220.2 28.7 %copy-start.4 = (f32[4,16,64,64]{3,2,1,0:T(8,128)S(1)}, f32[4,16,64,64]{3,2,1,0:T(8,128)}, u32[]{:S(2)}) copy-start(f32[4,16,64,64]{3,2,1,0:T(8,128)} %start_ref.1) | copy-start | bytes 3145732
  250.6 19.0 %copy-start.86 = (bf16[1024,2048]{1,0:T(8,128)(2,1)S(1)}, bf16[1024,2048]{1,0:T(8,128)(2,1)}, u32[]{:S(2)}) copy-start(bf16[1024,2048]{1,0:T(8,128)(2,1)} %get-tuple-element.97) | copy-start | bytes 12582916
  271.9 48.2 %copy-start.3 = (bf16[4,128,2048]{2,1,0:T(8,128)(2,1)S(1)}, bf16[4,128,2048]{2,1,0:T(8,128)(2,1)}, u32[]{:S(2)}) copy-start(bf16[4,128,2048]{2,1,0:T(8,128)(2,1)} %x_ref.3) | copy-start | bytes 6291460
  272.3 47.8 %collective-permute-start.2 = (bf16[4,128,2048]{2,1,0:T(8,128)(2,1)S(1)}, bf16[4,128,2048]{2,1,0:T(8,128)(2,1)S(1)}, u32[]{:S(2)}, u32[]{:S(2)}) collective-permute-start(bf16[4,128,2048]{2,1,0:T(8,128)(2,1)S(1)} %convert_element_type.168), channel_id=1, source_target_pairs={{0,1},{1,0},{2,3},{3,2},{4,5},{5,4},{6,7},{7,6},{8,9},{9,8},{10,11... | collective-permute-start | bytes 6291464 | tf_op jit(solution)/shard_map/ppermute | solution.py:678
  327.2 2.2 collective-permute-start.3
  338.3 15.1 %slice-start = ((s8[14680064]{0:T(1024)(128)(4,1)}), s8[4194304]{0:T(1024)(128)(4,1)S(1)}, s32[]{:S(2)}) async-start(s8[14680064]{0:T(1024)(128)(4,1)} %bitcast.239), calls=%async_computation.6 | async-start | bytes 8388608
  338.3 15.1 %slice-start.1 = ((s8[14680064]{0:T(1024)(128)(4,1)}), s8[4194304]{0:T(1024)(128)(4,1)S(1)}, s32[]{:S(2)}) async-start(s8[14680064]{0:T(1024)(128)(4,1)} %bitcast.239), calls=%async_computation.7 | async-start | bytes 8388608
  338.3 15.1 %slice-start.2 = ((s8[14680064]{0:T(1024)(128)(4,1)}), s8[4194304]{0:T(1024)(128)(4,1)S(1)}, s32[]{:S(2)}) async-start(s8[14680064]{0:T(1024)(128)(4,1)} %bitcast.239), calls=%async_computation.8 | async-start | bytes 8388608
  338.3 15.1 %slice-start.3 = ((s8[14680064]{0:T(1024)(128)(4,1)}), s8[2097152]{0:T(1024)(128)(4,1)S(1)}, s32[]{:S(2)}) async-start(s8[14680064]{0:T(1024)(128)(4,1)} %bitcast.239), calls=%async_computation.9 | async-start | bytes 4194304
  338.3 25.7 %collective-permute-start.4 = (bf16[4,128,1024]{2,1,0:T(8,128)(2,1)S(1)}, bf16[4,128,1024]{2,1,0:T(8,128)(2,1)S(1)}, u32[]{:S(2)}, u32[]{:S(2)}) collective-permute-start(bf16[4,128,1024]{2,1,0:T(8,128)(2,1)S(1)} %get-tuple-element.100), channel_id=1, source_target_pairs={{0,1},{1,0},{2,3},{3,2},{4,5},{5,4},{6,7},{7,6},{8,9},{9,8},{10,11... | collective-permute-start | bytes 3145736 | tf_op jit(solution)/shard_map/ppermute | solution.py:678
  353.4 11.0 %copy-start.70 = (bf16[4,128,3584]{2,1,0:T(8,128)(2,1)}, bf16[4,128,3584]{2,1,0:T(8,128)(2,1)S(1)}, u32[]{:S(2)}) copy-start(bf16[4,128,3584]{2,1,0:T(8,128)(2,1)S(1)} %get-tuple-element.102) | copy-start | bytes 11010052
  374.4 198.2 %all-gather.7.cloned.1.call-start = ((), (), s32[]{:S(2)}) async-start(), calls=%async_computation.5 | async-start | bytes 4718592 | tf_op jit(solution)/shard_map/all_gather | solution.py:1391
  374.5 6.5 copy-start.51
  379.5 30.1 %collective-permute-start.5 = (bf16[4,128,1024]{2,1,0:T(8,128)(2,1)}, bf16[4,128,1024]{2,1,0:T(8,128)(2,1)S(1)}, u32[]{:S(2)}, u32[]{:S(2)}) collective-permute-start(bf16[4,128,1024]{2,1,0:T(8,128)(2,1)} %fusion.45), channel_id=1, source_target_pairs={{0,1},{1,0},{2,3},{3,2},{4,5},{5,4},{6,7},{7,6},{8,9},{9,8},{10,11... | collective-permute-start | bytes 3145736 | tf_op jit(solution)/shard_map/ppermute | solution.py:678
  380.9 29.7 %copy-start.41 = (f32[4,128,2048]{2,1,0:T(8,128)S(1)}, f32[4,128,2048]{2,1,0:T(8,128)}, u32[]{:S(2)}) copy-start(f32[4,128,2048]{2,1,0:T(8,128)} %copy-done.40) | copy-start | bytes 12582916
  380.9 29.7 %copy-start.48 = (bf16[4,128,1024]{2,1,0:T(8,128)(2,1)S(1)}, bf16[4,128,1024]{2,1,0:T(8,128)(2,1)}, u32[]{:S(2)}) copy-start(bf16[4,128,1024]{2,1,0:T(8,128)(2,1)} %param.37) | copy-start | bytes 3145732
  415.3 13.0 %copy-start.57 = (bf16[4,128,1024]{2,1,0:T(8,128)(2,1)}, bf16[4,128,1024]{2,1,0:T(8,128)(2,1)S(1)}, u32[]{:S(2)}) copy-start(bf16[4,128,1024]{2,1,0:T(8,128)(2,1)S(1)} %get-tuple-element.248) | copy-start | bytes 3145732
  424.3 22.3 %collective-permute-start.7 = (bf16[4,1024]{1,0:T(4,128)(2,1)S(1)}, bf16[4,1024]{1,0:T(4,128)(2,1)S(1)}, u32[]{:S(2)}, u32[]{:S(2)}) collective-permute-start(bf16[4,1024]{1,0:T(4,128)(2,1)S(1)} %bitcast.233), channel_id=1, source_target_pairs={{2,0},{4,2},{6,4},{8,6},{10,8},{12,10},{14,12},{3,1},{5,3},{7,5},{... | collective-permute-start | bytes 24584 | tf_op jit(solution)/shard_map/ppermute | solution.py:17
  443.1 12.3 %collective-permute-start.10 = (bf16[4,1024]{1,0:T(4,128)(2,1)S(1)}, bf16[4,1024]{1,0:T(4,128)(2,1)S(1)}, u32[]{:S(2)}, u32[]{:S(2)}) collective-permute-start(bf16[4,1024]{1,0:T(4,128)(2,1)S(1)} %bitcast.234), channel_id=1, source_target_pairs={{2,0},{4,2},{6,4},{8,6},{10,8},{12,10},{14,12},{3,1},{5,3},{7,5},{... | collective-permute-start | bytes 24584 | tf_op jit(solution)/shard_map/ppermute | solution.py:17
  444.5 48.3 %collective-permute-start.9 = (bf16[4,128,1024]{2,1,0:T(8,128)(2,1)}, bf16[4,128,1024]{2,1,0:T(8,128)(2,1)S(1)}, u32[]{:S(2)}, u32[]{:S(2)}) collective-permute-start(bf16[4,128,1024]{2,1,0:T(8,128)(2,1)} %get-tuple-element.110), channel_id=1, source_target_pairs={{0,1},{1,0},{2,3},{3,2},{4,5},{5,4},{6,7},{7,6},{8,9},{9,8},{10,11... | collective-permute-start | bytes 3145736 | tf_op jit(solution)/shard_map/ppermute | solution.py:678
  444.9 48.0 %collective-permute-start.6 = (bf16[4,128,1024]{2,1,0:T(8,128)(2,1)}, bf16[4,128,1024]{2,1,0:T(8,128)(2,1)S(1)}, u32[]{:S(2)}, u32[]{:S(2)}) collective-permute-start(bf16[4,128,1024]{2,1,0:T(8,128)(2,1)} %get-tuple-element.108), channel_id=1, source_target_pairs={{0,1},{1,0},{2,3},{3,2},{4,5},{5,4},{6,7},{7,6},{8,9},{9,8},{10,11... | collective-permute-start | bytes 3145736 | tf_op jit(solution)/shard_map/ppermute | solution.py:678
  446.6 46.0 %collective-permute-start.8 = (bf16[4,1024]{1,0:T(4,128)(2,1)S(1)}, bf16[4,1024]{1,0:T(4,128)(2,1)S(1)}, u32[]{:S(2)}, u32[]{:S(2)}) collective-permute-start(bf16[4,1024]{1,0:T(4,128)(2,1)S(1)} %collective-permute-done.7), channel_id=1, source_target_pairs={{0,1},{1,0},{2,3},{3,2},{4,5},{5,4},{6,7},{7,6},{8,9},{9,8},{10,11... | collective-permute-start | bytes 24584 | tf_op jit(solution)/shard_map/ppermute | solution.py:678
  455.4 37.5 %collective-permute-start.11 = (bf16[4,1024]{1,0:T(4,128)(2,1)S(1)}, bf16[4,1024]{1,0:T(4,128)(2,1)S(1)}, u32[]{:S(2)}, u32[]{:S(2)}) collective-permute-start(bf16[4,1024]{1,0:T(4,128)(2,1)S(1)} %collective-permute-done.10), channel_id=1, source_target_pairs={{0,1},{1,0},{2,3},{3,2},{4,5},{5,4},{6,7},{7,6},{8,9},{9,8},{10,11... | collective-permute-start | bytes 24584 | tf_op jit(solution)/shard_map/ppermute | solution.py:678
  523.0 362.4 %reduce-scatter.5.cloned.1.call-start = ((), (), s32[]{:S(2)}) async-start(), calls=%async_computation.3 | async-start | bytes 11141120 | tf_op jit(solution)/shard_map/reduce_scatter | solution.py:1336
  577.4 22.5 %copy-start.22 = (bf16[512,1024]{1,0:T(8,128)(2,1)S(1)}, bf16[512,1024]{1,0:T(8,128)(2,1)}, u32[]{:S(2)}) copy-start(bf16[512,1024]{1,0:T(8,128)(2,1)} %copy-done.21) | copy-start | bytes 3145732
  577.4 22.5 %copy-start.24 = (bf16[512,1024]{1,0:T(8,128)(2,1)S(1)}, bf16[512,1024]{1,0:T(8,128)(2,1)}, u32[]{:S(2)}) copy-start(bf16[512,1024]{1,0:T(8,128)(2,1)} %copy-done.23) | copy-start | bytes 3145732
  647.2 5.9 collective-permute-start.12
  863.0 16.5 %collective-permute-start.13 = (f32[400,128]{0,1:T(8,128)}, f32[400,128]{0,1:T(8,128)S(1)}, u32[]{:S(2)}, u32[]{:S(2)}) collective-permute-start(f32[400,128]{0,1:T(8,128)} %bitcast.188), channel_id=1, source_target_pairs={{0,1},{1,0},{2,3},{3,2},{4,5},{5,4},{6,7},{7,6},{8,9},{9,8},{10,11... | collective-permute-start | bytes 614408 | tf_op jit(solution)/shard_map/ppermute | solution.py:678
  870.3 6.6 copy-start.66
  879.6 7.1 copy-start.62
  (62 other events, 169.3 us)
Sparse Core Ops, SparseCore 0:
  192.8 56.1 all-gather.4
  374.5 119.4 reduce-scatter.2
  523.1 49.4 all-gather.6
  576.5 125.8 reduce-scatter.4
